TPU v7x, 32 devices: a whole 2x2x4 slice. The times are simulated.
32 devices in a mesh: seq: 16 (over z, y, x), rows: 2 (over core).
Axes of the slice: x: 2, y: 2, z: 4, core: 2. Of those that a mesh axis runs over, the one named last changes fastest.
Arguments:
- inputs: float32 [2, 8192, 1024], P('rows', 'seq'), may hold values from -6 to 6
- lengths: int32 [2, 8], P('rows'), may hold values from 1 to 7681, as said below
- norm_gain: float32 [2, 1024], replicated, may hold values from 0.5 to 1.5
- in_weight: bfloat16 [2, 1024, 4384], replicated, may hold values from -0.1875 to 0.1875
- conv_weight: float32 [2, 2304, 4], replicated, may hold values from -3 to 3
- conv_bias: float32 [2, 2304], replicated, may hold values from -3 to 3
- log_decay: float32 [2, 32], replicated, may hold values from -0.7 to 0.7
- dt_bias: float32 [2, 32], replicated, may hold values from -11 to -3
- skip: float32 [2, 32], replicated, may hold values from 0.5 to 1.5
- gate_gain: float32 [2, 2048], replicated, may hold values from 0.5 to 1.5
- out_weight: bfloat16 [2, 2048, 1024], replicated, may hold values from -0.125 to 0.125
- cotangent: float32 [2, 8192, 1024], P('rows', 'seq'), may hold values from -6 to 6
Outputs:
- output: float32 [2, 8192, 1024], P('rows', 'seq')
- input_grad: float32 [2, 8192, 1024], P('rows', 'seq')
- norm_gain_grad: float32 [2, 1024], P(None, ('seq', 'rows'))
- in_weight_grad: float32 [2, 1024, 4384], P(None, ('seq', 'rows'))
- conv_weight_grad: float32 [2, 2304, 4], P(None, ('seq', 'rows'))
- conv_bias_grad: float32 [2, 2304], P(None, ('seq', 'rows'))
- log_decay_grad: float32 [2, 32], replicated
- dt_bias_grad: float32 [2, 32], replicated
- skip_grad: float32 [2, 32], replicated
- gate_gain_grad: float32 [2, 2048], P(None, ('seq', 'rows'))
- out_weight_grad: float32 [2, 2048, 1024], P(None, ('seq', 'rows'))
Inputs may be any that keep to these rules, and one draw needn't show every extreme that they name: Each row's lengths sum to 8192; one of them is 7681, the others add up to 511; its place in the row varies.
All inputs are finite; a program needn't handle non-finite values.
Results may differ from a plain program's by a relative error of at most 0.0074.
Values sent between devices are 32-bit elements; how exact they have to be, the bound alone decides.
A program may use at most 320 MiB of HBM per device.

v0:
```python
from functools import partial

import jax
import jax.numpy as jnp
from jax import lax
from jax.sharding import PartitionSpec as P

DI = 2048
STATE = 128
HEAD_DIM = 64
KW = 4
GROUP = 256
LAYERS = 2


EPS = 1e-05
HIGHEST = lax.Precision.HIGHEST


def shifted(value, axis, steps):
    count = lax.axis_size(axis)
    leading, last = (max(0, -steps), min(count, count - steps))
    return lax.ppermute(value, axis, [(source, source + steps) for source in range(leading, last)])


def entering_2(value, axis, combine, identity, reverse):
    peers, mine = (lax.axis_size(axis), lax.axis_index(axis))
    everything = jax.tree.map(lambda part: lax.all_gather(part, axis), value)
    start = jax.tree.map(
        lambda part, zero: jnp.broadcast_to(jnp.asarray(zero, part.dtype), part.shape),
        value,
        identity,
    )

    def lap(k, before):
        at = peers - 1 - k if reverse else k
        reached = at > mine if reverse else at < mine
        new = combine(before, jax.tree.map(lambda part: part[at], everything))
        return jax.tree.map(lambda a, b: jnp.where(reached, a, b), new, before)

    return lax.fori_loop(0, peers, lap, start)


def norm_rows(values, gain):
    return values * lax.rsqrt(jnp.mean(values * values, -1, keepdims=True) + EPS) * gain


def doc_table(lengths, first, count):
    starts = jnp.cumsum(lengths, -1) - lengths
    places = first + jnp.arange(count, dtype=jnp.int32)
    return jnp.sum((starts[:, None, :] <= places[None, :, None]).astype(jnp.int32), -1) - 1


def combine(earlier, later):
    return (earlier[0] * later[0], later[0][..., None, None] * earlier[1] + later[1])


def local_scan(values, in_map, out_map, step_size, log_rate, docs, before_doc):
    row_count, span = docs.shape
    count = span // GROUP

    def blocks(array):
        return array.reshape((row_count, count, GROUP) + array.shape[2:])

    values_c = blocks(values)
    in_c = blocks(in_map)
    out_c = blocks(out_map)
    step_c = blocks(step_size)
    docs_c = blocks(docs)
    cumul = jnp.cumsum(blocks(log_rate), 2)
    prior = jnp.concatenate([before_doc[:, None], docs_c[:, :-1, -1]], 1)
    lower = jnp.tri(GROUP, dtype=bool)
    same = (docs_c[:, :, :, None] == docs_c[:, :, None, :]) & lower
    masks = same[..., None]
    spread = cumul[:, :, :, None, :] - cumul[:, :, None, :, :]
    weights = jnp.where(masks, jnp.exp(jnp.where(masks, spread, 0.0)), 0.0)
    scores = jnp.einsum("rcin,rcjn->rcij", out_c, in_c, precision=HIGHEST)
    mixing = scores[..., None] * weights * step_c[:, :, None, :, :]
    inner = jnp.einsum("rcijh,rcjhp->rcihp", mixing, values_c, precision=HIGHEST)
    final_doc = docs_c[:, :, -1:]
    tail = (
        jnp.exp(cumul[:, :, -1:, :] - cumul)
        * (docs_c == final_doc).astype(jnp.float32)[..., None]
        * step_c
    )
    made = jnp.einsum("rcjh,rcjhp,rcjn->rchpn", tail, values_c, in_c, precision=HIGHEST)
    keeping = (
        jnp.exp(cumul[:, :, -1, :]) * (final_doc[:, :, 0] == prior).astype(jnp.float32)[..., None]
    )
    entering = jnp.exp(cumul) * (docs_c == prior[:, :, None]).astype(jnp.float32)[..., None]
    carried = jnp.zeros(made.shape[:1] + made.shape[2:], jnp.float32)
    through = jnp.ones(keeping.shape[:1] + keeping.shape[2:], jnp.float32)
    carried_list = []
    through_list = []
    for block_index in range(count):
        carried_list.append(carried)
        through_list.append(through)
        carried = keeping[:, block_index, :, None, None] * carried + made[:, block_index]
        through = through * keeping[:, block_index]
    before_blocks = jnp.stack(carried_list, 1)
    through_blocks = jnp.stack(through_list, 1)
    outer = (
        jnp.einsum("rcin,rchpn->rcihp", out_c, before_blocks, precision=HIGHEST)
        * entering[..., None]
    )
    scanned = (inner + outer).reshape(values.shape)
    entering_all = (entering * through_blocks[:, :, None, :]).reshape(step_size.shape)
    return (scanned, carried, through, entering_all)


def mixer_local(docs_ext, extended, conv_weight, conv_bias, rate_in, dt_bias, log_decay):
    row_count, span = (rate_in.shape[0], rate_in.shape[1])
    docs = docs_ext[:, KW - 1 :]
    conv = jnp.zeros((row_count, span, conv_bias.shape[0]), jnp.float32) + conv_bias
    for offset in range(KW):
        match = (docs_ext[:, offset : offset + span] == docs).astype(jnp.float32)[..., None]
        conv = conv + conv_weight[:, offset] * extended[:, offset : offset + span] * match
    active = jax.nn.silu(conv)
    values = active[..., :DI].reshape(row_count, span, DI // HEAD_DIM, HEAD_DIM)
    in_map = active[..., DI : DI + STATE]
    out_map = active[..., DI + STATE :]
    step_size = jax.nn.softplus(rate_in + dt_bias)
    log_rate = -jnp.exp(log_decay) * step_size
    scanned, final_state, total_keep, entering = local_scan(
        values, in_map, out_map, step_size, log_rate, docs, docs_ext[:, KW - 2]
    )
    return (values, out_map, scanned, final_state, total_keep, entering)


def finish(values, out_map, scanned, entering, state_in, gate_in, skip, gate_gain):
    carried_part = (
        jnp.einsum("rtn,rhpn->rthp", out_map, state_in, precision=HIGHEST) * entering[..., None]
    )
    result = scanned + carried_part + skip[:, None] * values
    gated = result.reshape(gate_in.shape) * jax.nn.silu(gate_in)
    return norm_rows(gated, gate_gain)


def local(
    inputs,
    lengths,
    norm_gain,
    in_weight,
    conv_weight,
    conv_bias,
    log_decay,
    dt_bias,
    skip,
    gate_gain,
    out_weight,
    cotangent,
):
    row_count, span, width = inputs.shape
    position = lax.axis_index("seq")
    docs_ext = doc_table(lengths, position * span - (KW - 1), span + KW - 1)
    channels = DI + 2 * STATE
    hidden = inputs
    saved = []
    for depth in range(LAYERS):
        normed, norm_pull = jax.vjp(norm_rows, hidden, norm_gain[depth])
        normed_low = normed.astype(jnp.bfloat16).reshape(row_count * span, width)
        projected = jnp.dot(
            normed_low, in_weight[depth], preferred_element_type=jnp.float32
        ).reshape(row_count, span, -1)
        gate_in = projected[..., :DI]
        mixed_in = projected[..., DI : DI + channels]
        rate_in = projected[..., DI + channels :]
        before = shifted(mixed_in[:, span - (KW - 1) :], "seq", 1)
        extended = jnp.concatenate([before, mixed_in], 1)
        mixer_out, mixer_pull = jax.vjp(
            partial(mixer_local, docs_ext),
            extended,
            conv_weight[depth],
            conv_bias[depth],
            rate_in,
            dt_bias[depth],
            log_decay[depth],
        )
        values, out_map, scanned, final_state, total_keep, entering = mixer_out
        identity = (jnp.ones_like(total_keep), jnp.zeros_like(final_state))
        _, state_in = entering_2((total_keep, final_state), "seq", combine, identity, False)
        normed_out, finish_pull = jax.vjp(
            finish,
            values,
            out_map,
            scanned,
            entering,
            state_in,
            gate_in,
            skip[depth],
            gate_gain[depth],
        )
        out_low = normed_out.astype(jnp.bfloat16).reshape(row_count * span, DI)
        branch = jnp.dot(out_low, out_weight[depth], preferred_element_type=jnp.float32).reshape(
            row_count, span, width
        )
        saved.append(
            (
                norm_pull,
                normed_low,
                mixer_pull,
                total_keep,
                state_in,
                finish_pull,
                out_low,
                identity,
            )
        )
        hidden = hidden + branch
    gradient = cotangent
    collected = [None] * LAYERS
    for depth in reversed(range(LAYERS)):
        norm_pull, normed_low, mixer_pull, total_keep, state_in, finish_pull, out_low, identity = (
            saved[depth]
        )
        grad_low = gradient.astype(jnp.bfloat16).reshape(row_count * span, width)
        out_weight_grad = jnp.einsum(
            "te,td->ed", out_low, grad_low, preferred_element_type=jnp.float32
        )
        grad_normed = jnp.einsum(
            "td,ed->te", grad_low, out_weight[depth], preferred_element_type=jnp.float32
        ).reshape(row_count, span, DI)
        (
            grad_values,
            grad_map,
            grad_scanned,
            grad_entering,
            grad_state,
            grad_gate,
            grad_skip,
            grad_gain,
        ) = finish_pull(grad_normed)
        _, grad_final = entering_2((total_keep, grad_state), "seq", combine, identity, True)
        grad_total = jnp.sum(grad_final * state_in, axis=(2, 3))
        grad_ext, grad_conv_w, grad_conv_b, grad_rate, grad_bias, grad_decay = mixer_pull(
            (grad_values, grad_map, grad_scanned, grad_final, grad_total, grad_entering)
        )
        returned = shifted(grad_ext[:, : KW - 1], "seq", -1)
        grad_mixed = grad_ext[:, KW - 1 :] + jnp.pad(
            returned, ((0, 0), (span - (KW - 1), 0), (0, 0))
        )
        grad_proj = (
            jnp.concatenate([grad_gate, grad_mixed, grad_rate], -1)
            .astype(jnp.bfloat16)
            .reshape(row_count * span, -1)
        )
        in_weight_grad = jnp.einsum(
            "td,tp->dp", normed_low, grad_proj, preferred_element_type=jnp.float32
        )
        grad_normed_in = jnp.einsum(
            "tp,dp->td", grad_proj, in_weight[depth], preferred_element_type=jnp.float32
        ).reshape(row_count, span, width)
        grad_hidden, grad_norm_gain = norm_pull(grad_normed_in)
        gradient = gradient + grad_hidden
        members = (
            grad_norm_gain,
            in_weight_grad,
            grad_conv_w,
            grad_conv_b,
            grad_gain,
            out_weight_grad,
        )
        collected[depth] = members + (grad_decay, grad_bias, grad_skip)
    stacked = [
        jnp.stack([collected[level][member] for level in range(LAYERS)]) for member in range(9)
    ]
    summed = (
        lax.psum_scatter(stacked[0], ("seq", "rows"), scatter_dimension=1, tiled=True),
        lax.psum_scatter(stacked[1], ("seq", "rows"), scatter_dimension=1, tiled=True),
        lax.psum_scatter(stacked[2], ("seq", "rows"), scatter_dimension=1, tiled=True),
        lax.psum_scatter(stacked[3], ("seq", "rows"), scatter_dimension=1, tiled=True),
        lax.psum_scatter(stacked[4], ("seq", "rows"), scatter_dimension=1, tiled=True),
        lax.psum_scatter(stacked[5], ("seq", "rows"), scatter_dimension=1, tiled=True),
    )
    head_sums = lax.psum((stacked[6], stacked[7], stacked[8]), ("seq", "rows"))
    return (
        hidden,
        gradient,
        summed[0],
        summed[1],
        summed[2],
        summed[3],
        head_sums[0],
        head_sums[1],
        head_sums[2],
        summed[4],
        summed[5],
    )


def solution(mesh):
    in_specs = (
        P("rows", "seq", None),
        P("rows", None),
        P(),
        P(),
        P(),
        P(),
        P(),
        P(),
        P(),
        P(),
        P(),
        P("rows", "seq", None),
    )
    out_specs = (
        P("rows", "seq", None),
        P("rows", "seq", None),
        P(None, ("seq", "rows")),
        P(None, ("seq", "rows"), None),
        P(None, ("seq", "rows"), None),
        P(None, ("seq", "rows")),
        P(),
        P(),
        P(),
        P(None, ("seq", "rows")),
        P(None, ("seq", "rows"), None),
    )
    return jax.shard_map(local, mesh=mesh, in_specs=in_specs, out_specs=out_specs, check_vma=False)
```

profile of v0, /device:TPU:1, one launch (start us, length us, event | category | flops | bytes accessed | tf_op | source)
XLA Modules:
  0.0 2287.4 jit_solution(2258518244852918929)
XLA Ops:
  10.5 8.5 fusion.48
  42.8 14.2 fusion.69
  60.7 6.0 reshape.1733
  66.7 6.0 fusion.172
  76.3 32.5 %all_gather.32 = f32[16,1,32]{2,1,0:T(1,128)S(1)} all-gather(f32[1,1,32]{2,1,0:T(1,128)S(1)} %get-tuple-element.876), channel_id=1, replica_groups=mesh['seq'=16,'rows'=2] {'seq'}, dimensions={0}, use_global_device_ids=true | all-gather | bytes 2176 | tf_op jit(solution)/shard_map/all_gather | solution.py:28
  117.2 19.3 bitcast_add_fusion.7
  141.7 6.6 reshape.1746
  148.4 119.0 %all-gather.7.cloned.1.call-done = f32[16,1,32,64,128]{4,3,2,1,0:T(8,128)} async-done(((f32[1,1,32,64,128]{4,3,2,1,0:T(8,128)}), f32[16,1,32,64,128]{4,3,2,1,0:T(8,128)}) %all-gather.7.cloned.1.call-update) | async-done | bytes 16777232 | tf_op jit(solution)/shard_map/all_gather | solution.py:28
  267.3 24.0 %while.60 = (s32[]{:T(128)}, f32[1,32,64,128]{3,2,1,0:T(8,128)S(1)}, s32[]{:T(128)}, f32[16,1,32]{2,1,0:T(1,128)S(1)}, f32[16,1,32,64,128]{4,3,2,1,0:T(8,128)}, /*index=5*/s32[]{:T(128)}, s32[]{:T(128)}) while((s32[]{:T(128)}, f32[1,32,64,128]{3,2,1,0:T(8,128)S(1)}, s32[]{:T(128)}, f32[16,1,32]{2,1,0:T(1,128)S(1)}, ...), condition=%wide.region_6.8_spmd.clone, body=%wide.region_5.7_spmd.clone.sunk | while | flops 1048580 | bytes 3146225 | solution.py:41
  296.3 5.5 multiply_add_fusion.5
  307.5 5.8 multiply_reduce_fusion.20
  313.4 8.3 fusion.51
  340.4 13.9 fusion.68
  358.1 5.9 reshape.1755
  364.0 6.0 fusion.175
  373.4 30.0 %all_gather.34 = f32[16,1,32]{2,1,0:T(1,128)S(1)} all-gather(f32[1,1,32]{2,1,0:T(1,128)S(1)} %copy-done.245), channel_id=1, replica_groups=mesh['seq'=16,'rows'=2] {'seq'}, dimensions={0}, use_global_device_ids=true | all-gather | bytes 2176 | tf_op jit(solution)/shard_map/all_gather | solution.py:28
  410.8 19.5 bitcast_add_fusion.6
  435.5 6.6 reshape.1767
  442.1 120.8 %all-gather.9.cloned.1.call-done = f32[16,1,32,64,128]{4,3,2,1,0:T(8,128)} async-done(((f32[1,1,32,64,128]{4,3,2,1,0:T(8,128)}), f32[16,1,32,64,128]{4,3,2,1,0:T(8,128)}) %all-gather.9.cloned.1.call-update) | async-done | bytes 16777232 | tf_op jit(solution)/shard_map/all_gather | solution.py:28
  562.9 24.0 %while.61 = (s32[]{:T(128)}, f32[1,32,64,128]{3,2,1,0:T(8,128)S(1)}, s32[]{:T(128)}, f32[16,1,32]{2,1,0:T(1,128)S(1)}, f32[16,1,32,64,128]{4,3,2,1,0:T(8,128)}, /*index=5*/s32[]{:T(128)}, s32[]{:T(128)}) while((s32[]{:T(128)}, f32[1,32,64,128]{3,2,1,0:T(8,128)S(1)}, s32[]{:T(128)}, f32[16,1,32]{2,1,0:T(1,128)S(1)}, ...), condition=%wide.region_12.14_spmd.clone, body=%wide.region_11.13_spmd.clone.sunk | while | flops 1048580 | bytes 3146225 | solution.py:41
  586.9 6.0 fusion.231
  593.0 5.4 multiply_add_fusion.4
  600.0 9.6 fusion.76
  609.7 6.9 multiply_reduce_fusion.12
  625.8 5.9 reshape.1775
  631.6 6.2 reshape.1776
  637.9 5.3 multiply_reduce_fusion.17
  644.7 8.7 fusion.181
  653.5 29.9 %fusion.21 = (f32[2,256,32]{1,2,0:T(8,128)}, f32[2,256,32]{1,2,0:T(8,128)}, f32[2,256,32]{1,2,0:T(8,128)}, f32[2,256,256]{2,1,0:T(8,128)S(1)}) fusion(f32[2,256,256]{2,1,0:T(8,128)S(1)} %copy-done.105, f32[2,256,32]{1,2,0:T(8,128)S(1)} %copy-done.159, f32[2,256,32]{1,2,0:T(8,128)S(1)} %copy-done.167, pred[2,256,256]{2,1,0:T(8,128)(4,1)S(1)} %copy-done.122, ...), kind=kOutput, calls=%fused_computation.45 | convolution fusion | flops 3283959808 | bytes 9895936 | tf_op jit(solution)/shard_map/transpose(jvp(rcijh,rcjhp->rcihp))/dot_general | solution.py:79
  686.9 7.4 fusion.171
  698.8 116.2 %all-gather.11.cloned.1.call-done = f32[512,64,128]{2,1,0:T(8,128)} async-done(((f32[32,64,128]{2,1,0:T(8,128)}), f32[512,64,128]{2,1,0:T(8,128)}) %all-gather.11.cloned.1.call-update) | async-done | bytes 16777232 | tf_op jit(solution)/shard_map/all_gather | solution.py:28
  814.9 24.5 %while.62 = (s32[]{:T(128)}, f32[1,32,64,128]{3,2,1,0:T(8,128)S(1)}, s32[]{:T(128)}, f32[16,1,32]{2,1,0:T(1,128)S(1)}, f32[16,1,32,64,128]{4,3,2,1,0:T(8,128)}, ...) while((s32[]{:T(128)}, f32[1,32,64,128]{3,2,1,0:T(8,128)S(1)}, s32[]{:T(128)}, ...), condition=%wide.region_17.19_spmd.clone, body=%wide.region_16.18_spmd.clone.sunk | while | flops 1048584 | bytes 3146287 | solution.py:41
  850.9 16.2 bitcast_add_fusion.5
  874.0 6.0 fusion.199
  880.1 5.3 copy.640
  885.4 6.5 reshape.1782
  896.9 13.9 multiply_reduce_fusion.4
  915.8 6.8 pad_add_fusion.1
  932.6 12.2 fusion.130
  952.4 7.1 multiply_reduce_fusion.13
  969.5 6.3 reshape.1793
  975.8 6.2 reshape.1794
  988.2 8.7 fusion.178
  997.0 29.9 %fusion.23 = (f32[2,256,32]{1,2,0:T(8,128)}, f32[2,256,32]{1,2,0:T(8,128)}, f32[2,256,32]{1,2,0:T(8,128)}, f32[2,256,256]{2,1,0:T(8,128)S(1)}) fusion(f32[2,256,256]{2,1,0:T(8,128)} %copy-done.102, f32[2,256,32]{1,2,0:T(8,128)S(1)} %copy-done.156, f32[2,256,32]{1,2,0:T(8,128)} %copy.597, pred[2,256,256]{2,1,0:T(8,128)(4,1)S(1)} %copy-done.124, ...), kind=kOutput, calls=%fused_computation.47 | convolution fusion | flops 3283959808 | bytes 9895936 | tf_op jit(solution)/shard_map/transpose(jvp(rcijh,rcjhp->rcihp))/dot_general | solution.py:79
  1029.7 7.4 fusion.170
  1042.9 15.8 convolution_bitcast_fusion
  1058.7 102.1 %all-gather.13.cloned.1.call-done = f32[512,64,128]{2,1,0:T(8,128)} async-done(((f32[32,64,128]{2,1,0:T(8,128)}), f32[512,64,128]{2,1,0:T(8,128)}) %all-gather.13.cloned.1.call-update) | async-done | bytes 16777232 | tf_op jit(solution)/shard_map/all_gather | solution.py:28
  1160.8 34.5 %while.63 = (s32[]{:T(128)}, f32[1,32,64,128]{3,2,1,0:T(8,128)S(1)}, s32[]{:T(128)}, f32[16,1,32]{2,1,0:T(1,128)}, f32[16,1,32,64,128]{4,3,2,1,0:T(8,128)}, /*index=5*/s32[]{:T(128)}, s32[]{:T(128)}, s32[]{:T(128)}, s32[]{:T(128)}) while((s32[]{:T(128)}, f32[1,32,64,128]{3,2,1,0:T(8,128)S(1)}, s32[]{:T(128)}, ...), condition=%wide.region_34.36_spmd.clone, body=%wide.region_33.35_spmd.clone.sunk | while | flops 1048584 | bytes 3146287 | solution.py:41
  1206.9 16.4 bitcast_add_fusion.4
  1229.1 6.0 fusion.209
  1240.4 6.5 reshape.1800
  1252.0 13.3 multiply_reduce_fusion.8
  1270.2 6.8 pad_add_fusion
  1287.0 10.2 fusion.131
  1297.2 15.0 convolution_bitcast_fusion.1
  1313.3 27.7 %pad_maximum_fusion = f32[2,1024,4384]{1,2,0:T(8,128)} fusion(f32[1,1024,4384]{1,2,0:T(8,128)} %convolution_bitcast_fusion, f32[1,1024,4384]{1,2,0:T(8,128)} %convolution_bitcast_fusion.1), kind=kLoop, calls=%fused_computation.12 | loop fusion | flops 8978432 | bytes 71827456 | tf_op jit(solution)/shard_map/stack | solution.py:265
  1341.0 53.2 %copy.684 = f32[2,1024,4384]{2,0,1:T(2,128)} copy(f32[2,1024,4384]{1,2,0:T(8,128)} %pad_maximum_fusion) | data formatting | bytes 71827456 | tf_op jit(solution)/shard_map/stack | solution.py:265
  1394.9 5.4 convolution_bitcast_fusion.2
  1402.7 6.8 pad_maximum_fusion.1
  1410.4 7.9 bitcast_add_fusion.8
  1420.1 41.7 %all-reduce.47 = (f32[2,2304]{1,0:T(2,128)S(1)}, f32[2,32]{1,0:T(2,128)}, f32[2,32]{1,0:T(2,128)}, f32[2,32]{1,0:T(2,128)}) all-reduce(f32[2,2304]{1,0:T(2,128)S(1)} %pad_maximum_fusion.11, f32[2,32]{1,0:T(2,128)S(1)} %pad_maximum_fusion.14, ...), channel_id=7, replica_groups=mesh['seq'=16,'rows'=2] {'seq','rows'}, use_global_device_ids=true, to_apply=%region_63.65.clone | all-reduce | flops 4800 | bytes 38400
  1467.8 82.9 %reduce-scatter.12.cloned.1.call-done = f32[32,2]{1,0:T(8,128)} async-done(((f32[1024,2]{1,0:T(8,128)}), f32[32,2]{1,0:T(8,128)}) %reduce-scatter.12.cloned.1.call-update) | async-done | bytes 272
  1552.0 541.4 %all-reduce.51.cloned.1.call-done = f32[2,1024,4384]{2,0,1:T(2,128)} async-done(((f32[2,1024,4384]{2,0,1:T(2,128)}), f32[2,1024,4384]{2,0,1:T(2,128)}) %all-reduce.51.cloned.1.call-update) | async-done | bytes 35913744
  2095.8 184.9 %reduce-scatter.10.cloned.1.call-done = f32[2,64,1024]{2,1,0:T(8,128)} async-done(((f32[2,2048,1024]{2,1,0:T(8,128)}), f32[2,64,1024]{2,1,0:T(8,128)}) %reduce-scatter.10.cloned.1.call-update) | async-done | bytes 524304 | tf_op jit(solution)/shard_map/reduce_scatter | solution.py:273
  (922 shorter events, 348.6 us)
Async XLA Ops:
  7.2 260.1 %all-gather.7.cloned.1.call-start = ((), (), s32[]{:S(2)}) async-start(), calls=%async_computation.3 | async-start | bytes 17825792 | tf_op jit(solution)/shard_map/all_gather | solution.py:28
  10.4 18.5 copy-start.236
  10.4 18.5 copy-start.247
  23.1 19.2 collective-permute-start
  29.0 311.4 %copy-start.142 = (f32[1,512]{1,0:T(1,128)}, f32[1,512]{1,0:T(1,128)S(1)}, u32[]{:S(2)}) copy-start(f32[1,512]{1,0:T(1,128)S(1)} %get-tuple-element.852) | copy-start | bytes 6148
  29.0 311.4 %copy-start.144 = (f32[1,512]{1,0:T(1,128)}, f32[1,512]{1,0:T(1,128)S(1)}, u32[]{:S(2)}) copy-start(f32[1,512]{1,0:T(1,128)S(1)} %get-tuple-element.853) | copy-start | bytes 6148
  30.5 44.8 %copy-start.81 = (f32[1,512,32]{1,2,0:T(8,128)}, f32[1,512,32]{1,2,0:T(8,128)S(1)}, u32[]{:S(2)}) copy-start(f32[1,512,32]{1,2,0:T(8,128)S(1)} %get-tuple-element.815) | copy-start | bytes 196612
  35.6 298.4 %copy-start.113 = (f32[2,256]{1,0:T(2,128)}, f32[2,256]{1,0:T(2,128)S(1)}, u32[]{:S(2)}) copy-start(f32[2,256]{1,0:T(2,128)S(1)} %get-tuple-element.855) | copy-start | bytes 6148
  35.6 298.5 %copy-start.116 = (f32[2,256]{1,0:T(2,128)}, f32[2,256]{1,0:T(2,128)S(1)}, u32[]{:S(2)}) copy-start(f32[2,256]{1,0:T(2,128)S(1)} %get-tuple-element.856) | copy-start | bytes 6148
  35.6 79.5 %copy-start.91 = (f32[2,256,32]{1,2,0:T(8,128)}, f32[2,256,32]{1,2,0:T(8,128)S(1)}, u32[]{:S(2)}) copy-start(f32[2,256,32]{1,2,0:T(8,128)S(1)} %get-tuple-element.812) | copy-start | bytes 196612
  35.9 36.9 %copy-start.217 = (f32[32]{0:T(128)}, f32[32]{0:T(128)S(1)}, u32[]{:S(2)}) copy-start(f32[32]{0:T(128)S(1)} %get-tuple-element.874) | copy-start | bytes 388
  35.9 36.9 %copy-start.219 = (f32[32]{0:T(128)}, f32[32]{0:T(128)S(1)}, u32[]{:S(2)}) copy-start(f32[32]{0:T(128)S(1)} %get-tuple-element.875) | copy-start | bytes 388
  36.6 30.1 %copy-start.89 = (f32[2,256,32]{1,2,0:T(8,128)}, f32[2,256,32]{1,2,0:T(8,128)S(1)}, u32[]{:S(2)}) copy-start(f32[2,256,32]{1,2,0:T(8,128)S(1)} %get-tuple-element.845) | copy-start | bytes 196612
  72.7 36.8 %copy-start.246 = (f32[2,32]{1,0:T(2,128)S(1)}, f32[2,32]{1,0:T(2,128)}, u32[]{:S(2)}) copy-start(f32[2,32]{1,0:T(2,128)} %param.29) | copy-start | bytes 772
  72.7 37.6 %copy-start.194 = (f32[2,2048]{1,0:T(2,128)S(1)}, f32[2,2048]{1,0:T(2,128)}, u32[]{:S(2)}) copy-start(f32[2,2048]{1,0:T(2,128)} %param.30) | copy-start | bytes 49156
  75.3 39.9 %copy-start.44 = (f32[1,1,32,64,128]{4,3,2,1,0:T(8,128)}, f32[1,1,32,64,128]{4,3,2,1,0:T(8,128)S(1)}, u32[]{:S(2)}) copy-start(f32[1,1,32,64,128]{4,3,2,1,0:T(8,128)S(1)} %get-tuple-element.811) | copy-start | bytes 3145732
  75.3 487.6 %all-gather.9.cloned.1.call-start = ((), (), s32[]{:S(2)}) async-start(), calls=%async_computation.4 | async-start | bytes 17825792 | tf_op jit(solution)/shard_map/all_gather | solution.py:28
  75.4 35.0 %copy-start.79 = (f32[2,256,32]{1,0,2:T(2,128)}, f32[2,256,32]{1,0,2:T(2,128)S(1)}, u32[]{:S(2)}) copy-start(f32[2,256,32]{1,0,2:T(2,128)S(1)} %mul.1465) | copy-start | bytes 196612
  76.3 219.9 %copy-start.87 = (f32[4,8,2,256]{3,1,2,0:T(8,128)}, f32[4,8,2,256]{3,1,2,0:T(8,128)S(1)}, u32[]{:S(2)}) copy-start(f32[4,8,2,256]{3,1,2,0:T(8,128)S(1)} %copy.762) | copy-start | bytes 196612
  110.2 186.1 %copy-start.213 = (f32[32]{0:T(128)}, f32[32]{0:T(128)S(1)}, u32[]{:S(2)}) copy-start(f32[32]{0:T(128)S(1)} %get-tuple-element.868) | copy-start | bytes 388
  110.4 197.1 %copy-start.109 = (f32[1,2048]{1,0:T(1,128)}, f32[1,2048]{1,0:T(1,128)S(1)}, u32[]{:S(2)}) copy-start(f32[1,2048]{1,0:T(1,128)S(1)} %get-tuple-element.847) | copy-start | bytes 24580
  110.4 499.2 %copy-start.107 = (f32[1,2048]{1,0:T(1,128)}, f32[1,2048]{1,0:T(1,128)S(1)}, u32[]{:S(2)}) copy-start(f32[1,2048]{1,0:T(1,128)S(1)} %get-tuple-element.846) | copy-start | bytes 24580
  110.6 25.9 %copy-start.54 = (f32[2,256,128]{2,1,0:T(8,128)}, f32[2,256,128]{2,1,0:T(8,128)S(1)}, u32[]{:S(2)}) copy-start(f32[2,256,128]{2,1,0:T(8,128)S(1)} %copy.591) | copy-start | bytes 786436
  110.9 25.6 %copy-start.60 = (f32[2,256,128]{2,1,0:T(8,128)}, f32[2,256,128]{2,1,0:T(8,128)S(1)}, u32[]{:S(2)}) copy-start(f32[2,256,128]{2,1,0:T(8,128)S(1)} %copy.590) | copy-start | bytes 786436
  111.0 25.5 %copy-start.64 = (f32[2,256,128,1]{2,1,3,0:T(8,128)}, f32[2,256,128,1]{2,1,3,0:T(8,128)S(1)}, u32[]{:S(2)}) copy-start(f32[2,256,128,1]{2,1,3,0:T(8,128)S(1)} %copy.689) | copy-start | bytes 786436
  325.4 47.2 %copy-start.83 = (f32[1,512,32]{1,2,0:T(8,128)}, f32[1,512,32]{1,2,0:T(8,128)S(1)}, u32[]{:S(2)}) copy-start(f32[1,512,32]{1,2,0:T(8,128)S(1)} %get-tuple-element.805) | copy-start | bytes 196612
  330.5 39.5 %copy-start.220 = (f32[32]{0:T(128)}, f32[32]{0:T(128)S(1)}, u32[]{:S(2)}) copy-start(f32[32]{0:T(128)S(1)} %get-tuple-element.864) | copy-start | bytes 388
  330.5 39.5 %copy-start.222 = (f32[32]{0:T(128)}, f32[32]{0:T(128)S(1)}, u32[]{:S(2)}) copy-start(f32[32]{0:T(128)S(1)} %get-tuple-element.865) | copy-start | bytes 388
  330.9 9.0 collective-permute-start.1
  334.7 29.2 %copy-start.93 = (f32[2,256,32]{1,2,0:T(8,128)}, f32[2,256,32]{1,2,0:T(8,128)S(1)}, u32[]{:S(2)}) copy-start(f32[2,256,32]{1,2,0:T(8,128)S(1)} %get-tuple-element.843) | copy-start | bytes 196612
  370.0 33.3 %copy-start.99 = (f32[1,2,32,2,128]{4,3,0,2,1:T(2,128)S(1)}, f32[1,2,32,2,128]{4,3,0,2,1:T(2,128)}, u32[]{:S(2)}) copy-start(f32[1,2,32,2,128]{4,3,0,2,1:T(2,128)} %copy-done.98) | copy-start | bytes 196612
  370.0 33.3 %copy-start.101 = (f32[1,2,32,256]{3,2,1,0:T(8,128)S(1)}, f32[1,2,32,256]{3,2,1,0:T(8,128)}, u32[]{:S(2)}) copy-start(f32[1,2,32,256]{3,2,1,0:T(8,128)} %copy-done.100) | copy-start | bytes 196612
  372.5 442.4 %all-gather.11.cloned.1.call-start = ((), (), s32[]{:S(2)}) async-start(), calls=%async_computation.6 | async-start | bytes 17825792 | tf_op jit(solution)/shard_map/all_gather | solution.py:28
  404.1 26.2 %copy-start.56 = (f32[2,256,128]{2,1,0:T(8,128)}, f32[2,256,128]{2,1,0:T(8,128)S(1)}, u32[]{:S(2)}) copy-start(f32[2,256,128]{2,1,0:T(8,128)S(1)} %copy.609) | copy-start | bytes 786436
  404.4 25.8 %copy-start.62 = (f32[2,256,128]{2,1,0:T(8,128)}, f32[2,256,128]{2,1,0:T(8,128)S(1)}, u32[]{:S(2)}) copy-start(f32[2,256,128]{2,1,0:T(8,128)S(1)} %copy.608) | copy-start | bytes 786436
  404.6 25.7 %copy-start.66 = (f32[2,256,128,1]{2,1,3,0:T(8,128)}, f32[2,256,128,1]{2,1,3,0:T(8,128)S(1)}, u32[]{:S(2)}) copy-start(f32[2,256,128,1]{2,1,3,0:T(8,128)S(1)} %copy.692) | copy-start | bytes 786436
  624.9 535.9 %all-gather.13.cloned.1.call-start = ((), (), s32[]{:S(2)}) async-start(), calls=%async_computation.7 | async-start | bytes 17825792 | tf_op jit(solution)/shard_map/all_gather | solution.py:28
  653.5 29.9 %copy-start.57 = (f32[2,256,128]{2,1,0:T(8,128)S(1)}, f32[2,256,128]{2,1,0:T(8,128)}, u32[]{:S(2)}) copy-start(f32[2,256,128]{2,1,0:T(8,128)} %copy-done.56) | copy-start | bytes 786436
  653.5 30.8 %copy-start.63 = (f32[2,256,128]{2,1,0:T(8,128)S(1)}, f32[2,256,128]{2,1,0:T(8,128)}, u32[]{:S(2)}) copy-start(f32[2,256,128]{2,1,0:T(8,128)} %copy-done.62) | copy-start | bytes 786436
  653.5 33.4 %copy-start.67 = (f32[2,256,128,1]{2,1,3,0:T(8,128)S(1)}, f32[2,256,128,1]{2,1,3,0:T(8,128)}, u32[]{:S(2)}) copy-start(f32[2,256,128,1]{2,1,3,0:T(8,128)} %copy-done.66) | copy-start | bytes 786436
  814.9 24.5 %copy-start.221 = (f32[32]{0:T(128)S(1)}, f32[32]{0:T(128)}, u32[]{:S(2)}) copy-start(f32[32]{0:T(128)} %copy-done.220) | copy-start | bytes 388
  814.9 24.5 %copy-start.223 = (f32[32]{0:T(128)S(1)}, f32[32]{0:T(128)}, u32[]{:S(2)}) copy-start(f32[32]{0:T(128)} %copy-done.222) | copy-start | bytes 388
  850.9 23.1 %copy-start.86 = (f32[1,2,256,128]{2,3,1,0:T(8,128)S(1)}, f32[1,2,256,128]{2,3,1,0:T(8,128)}, u32[]{:S(2)}) copy-start(f32[1,2,256,128]{2,3,1,0:T(8,128)} %convolution_bitcast_fusion.8) | copy-start | bytes 786436
  923.4 4.6 collective-permute-start.2
  928.4 18.7 slice-start.11
  967.9 450.6 %reduce-scatter.14.cloned.1.call-start = ((), (), s32[]{:S(2)}) async-start(), calls=%async_computation.9 | async-start | bytes 1081344
  996.9 29.9 %copy-start.55 = (f32[2,256,128]{2,1,0:T(8,128)S(1)}, f32[2,256,128]{2,1,0:T(8,128)}, u32[]{:S(2)}) copy-start(f32[2,256,128]{2,1,0:T(8,128)} %copy-done.54) | copy-start | bytes 786436
  996.9 31.4 %copy-start.61 = (f32[2,256,128]{2,1,0:T(8,128)S(1)}, f32[2,256,128]{2,1,0:T(8,128)}, u32[]{:S(2)}) copy-start(f32[2,256,128]{2,1,0:T(8,128)} %copy-done.60) | copy-start | bytes 786436
  997.0 32.7 %copy-start.65 = (f32[2,256,128,1]{2,1,3,0:T(8,128)S(1)}, f32[2,256,128,1]{2,1,3,0:T(8,128)}, u32[]{:S(2)}) copy-start(f32[2,256,128,1]{2,1,3,0:T(8,128)} %copy-done.64) | copy-start | bytes 786436
  1058.7 407.7 %all-reduce.53.cloned.1.call-start = ((), (), s32[]{:S(2)}) async-start(), calls=%async_computation.11 | async-start | bytes 147456
  1160.8 34.5 %copy-start.218 = (f32[32]{0:T(128)S(1)}, f32[32]{0:T(128)}, u32[]{:S(2)}) copy-start(f32[32]{0:T(128)} %copy-done.217) | copy-start | bytes 388
  1206.8 16.8 copy-start.198
  1206.8 16.8 copy-start.204
  1206.8 16.8 copy-start.239
  1206.8 17.0 copy-start.161
  1206.8 17.0 copy-start.162
  1206.8 17.0 copy-start.163
  1206.8 17.0 copy-start.233
  1206.8 22.3 copy-start.85
  1277.8 4.6 collective-permute-start.3
  1279.9 270.8 %reduce-scatter.12.cloned.1.call-start = ((), (), s32[]{:S(2)}) async-start(), calls=%async_computation.8 | async-start | bytes 540672
  1313.3 780.1 %all-reduce.51.cloned.1.call-start = ((), (), s32[]{:S(2)}) async-start(), calls=%async_computation.10 | async-start | bytes 73400320
  1394.2 886.5 %reduce-scatter.10.cloned.1.call-start = ((), (), s32[]{:S(2)}) async-start(), calls=%async_computation.5 | async-start | bytes 17301504 | tf_op jit(solution)/shard_map/reduce_scatter | solution.py:273
  1410.4 51.9 %copy-start.182 = (f32[512]{0:T(512)S(1)}, f32[512]{0:T(512)}, u32[]{:S(2)}) copy-start(f32[512]{0:T(512)} %copy-done.181) | copy-start | bytes 6148
  (211 other events, 1599.4 us)
Sparse Core Ops, SparseCore 0:
  75.4 191.8 all-gather.6
  372.7 190.1 all-gather.8
  625.1 189.7 all-gather.10
  968.0 192.7 all-gather.12
  1162.9 128.2 reduce-scatter.13
  1297.6 120.9 all-reduce.52
  1421.5 129.1 reduce-scatter.11
  1557.1 536.2 all-reduce.50
  2096.3 184.3 reduce-scatter.9
where the time goes:
time: 2300 us; the launch traced here: 2290 us
  waiting for transfers between devices  1270 us (55%)
  matrix products  340 us (15%)
  other arithmetic  320 us (14%)
  local copies, waits for them, and re-layouts  223 us (10%)
  blocking collectives  104 us (5%)
    unnamed x13, waiting for transfers between devices  624 us
    all_gather x4, waiting for transfers between devices, entering_2(): everything = jax.tree.map(lambda part: lax.all_gather(part, axis), value)  458 us
    reduce_scatter x1, waiting for transfers between devices, local(): lax.psum_scatter(stacked[5], ('seq', 'rows'), scatter_dimension=1, tiled=...  185 us
    dot_general x6, matrix products, local_scan(): jnp.einsum('rcijh,rcjhp->rcihp', mixing, values_c, precision=HIGHEST)  131 us
    select_n x64, other arithmetic, lap(): return jax.tree.map(lambda a, b: jnp.where(reached, a, b), new, before)  93.6 us
    all_gather x2, blocking collectives, entering_2(): everything = jax.tree.map(lambda part: lax.all_gather(part, axis), value)  62.5 us
    another operation x3, local copies, waits for them, and re-layouts, local(): jnp.stack([collected[level][member] for level in range(LAYERS)])  53.2 us
  transfers between devices with their start and end apart: 13, of which 9 were waited for; matrix products, arithmetic and copies ran while one was open for 23% of the time, Pallas kernels for 0%

commit v1 on v0

--- a/solution.py
+++ b/solution.py
@@ -17,28 +17,52 @@
 HIGHEST = lax.Precision.HIGHEST
 
 
+AXES = ("seq", "rows")
+
+
+def scattered(total):
+    return lax.psum_scatter(total, AXES, scatter_dimension=0, tiled=True)
+
+
 def shifted(value, axis, steps):
     count = lax.axis_size(axis)
     leading, last = (max(0, -steps), min(count, count - steps))
     return lax.ppermute(value, axis, [(source, source + steps) for source in range(leading, last)])
 
 
-def entering_2(value, axis, combine, identity, reverse):
-    peers, mine = (lax.axis_size(axis), lax.axis_index(axis))
-    everything = jax.tree.map(lambda part: lax.all_gather(part, axis), value)
-    start = jax.tree.map(
-        lambda part, zero: jnp.broadcast_to(jnp.asarray(zero, part.dtype), part.shape),
-        value,
-        identity,
-    )
-
-    def lap(k, before):
-        at = peers - 1 - k if reverse else k
-        reached = at > mine if reverse else at < mine
-        new = combine(before, jax.tree.map(lambda part: part[at], everything))
-        return jax.tree.map(lambda a, b: jnp.where(reached, a, b), new, before)
-
-    return lax.fori_loop(0, peers, lap, start)
+def exchange(parts):
+    return lax.all_to_all(parts, "seq", split_axis=0, concat_axis=0, tiled=True)
+
+
+def entering_states(keep, state):
+    peers = lax.axis_size("seq")
+    row_count, heads = keep.shape
+    share = heads // peers
+    lead = jnp.moveaxis(state, 0, 1)
+    tag = jnp.broadcast_to(jnp.moveaxis(keep, 0, 1)[..., None, None], lead.shape[:2] + (8, STATE))
+    mine = exchange(jnp.concatenate([lead, tag], 2))
+    mine = mine.reshape((peers, share, row_count, HEAD_DIM + 8, STATE))
+    keeps = mine[:, :, :, HEAD_DIM, 0]
+    carried = jnp.zeros(mine.shape[1:3] + (HEAD_DIM, STATE), jnp.float32)
+    before = []
+    for peer in range(peers):
+        before.append(carried)
+        carried = keeps[peer][..., None, None] * carried + mine[peer, :, :, :HEAD_DIM]
+    back = exchange(jnp.stack(before).reshape(lead.shape))
+    return jnp.moveaxis(back, 0, 1), keeps
+
+
+def entering_grads(keeps, grad):
+    peers, share, row_count = keeps.shape
+    lead = jnp.moveaxis(grad, 0, 1)
+    mine = exchange(lead).reshape((peers, share, row_count, HEAD_DIM, STATE))
+    carried = jnp.zeros(mine.shape[1:], jnp.float32)
+    after = [None] * peers
+    for peer in reversed(range(peers)):
+        after[peer] = carried
+        carried = keeps[peer][..., None, None] * carried + mine[peer]
+    back = exchange(jnp.stack(after).reshape(lead.shape))
+    return jnp.moveaxis(back, 0, 1)
 
 
 def norm_rows(values, gain):
@@ -49,10 +73,6 @@
     starts = jnp.cumsum(lengths, -1) - lengths
     places = first + jnp.arange(count, dtype=jnp.int32)
     return jnp.sum((starts[:, None, :] <= places[None, :, None]).astype(jnp.int32), -1) - 1
-
-
-def combine(earlier, later):
-    return (earlier[0] * later[0], later[0][..., None, None] * earlier[1] + later[1])
 
 
 def local_scan(values, in_map, out_map, step_size, log_rate, docs, before_doc):
@@ -177,8 +197,7 @@
             log_decay[depth],
         )
         values, out_map, scanned, final_state, total_keep, entering = mixer_out
-        identity = (jnp.ones_like(total_keep), jnp.zeros_like(final_state))
-        _, state_in = entering_2((total_keep, final_state), "seq", combine, identity, False)
+        state_in, keeps = entering_states(total_keep, final_state)
         normed_out, finish_pull = jax.vjp(
             finish,
             values,
@@ -199,18 +218,19 @@
                 norm_pull,
                 normed_low,
                 mixer_pull,
-                total_keep,
+                keeps,
                 state_in,
                 finish_pull,
                 out_low,
-                identity,
             )
         )
         hidden = hidden + branch
     gradient = cotangent
     collected = [None] * LAYERS
+    big_in = [None] * LAYERS
+    big_out = [None] * LAYERS
     for depth in reversed(range(LAYERS)):
-        norm_pull, normed_low, mixer_pull, total_keep, state_in, finish_pull, out_low, identity = (
+        norm_pull, normed_low, mixer_pull, keeps, state_in, finish_pull, out_low = (
             saved[depth]
         )
         grad_low = gradient.astype(jnp.bfloat16).reshape(row_count * span, width)
@@ -230,7 +250,7 @@
             grad_skip,
             grad_gain,
         ) = finish_pull(grad_normed)
-        _, grad_final = entering_2((total_keep, grad_state), "seq", combine, identity, True)
+        grad_final = entering_grads(keeps, grad_state)
         grad_total = jnp.sum(grad_final * state_in, axis=(2, 3))
         grad_ext, grad_conv_w, grad_conv_b, grad_rate, grad_bias, grad_decay = mixer_pull(
             (grad_values, grad_map, grad_scanned, grad_final, grad_total, grad_entering)
@@ -252,39 +272,39 @@
         ).reshape(row_count, span, width)
         grad_hidden, grad_norm_gain = norm_pull(grad_normed_in)
         gradient = gradient + grad_hidden
-        members = (
-            grad_norm_gain,
-            in_weight_grad,
-            grad_conv_w,
-            grad_conv_b,
-            grad_gain,
-            out_weight_grad,
-        )
-        collected[depth] = members + (grad_decay, grad_bias, grad_skip)
-    stacked = [
-        jnp.stack([collected[level][member] for level in range(LAYERS)]) for member in range(9)
-    ]
-    summed = (
-        lax.psum_scatter(stacked[0], ("seq", "rows"), scatter_dimension=1, tiled=True),
-        lax.psum_scatter(stacked[1], ("seq", "rows"), scatter_dimension=1, tiled=True),
-        lax.psum_scatter(stacked[2], ("seq", "rows"), scatter_dimension=1, tiled=True),
-        lax.psum_scatter(stacked[3], ("seq", "rows"), scatter_dimension=1, tiled=True),
-        lax.psum_scatter(stacked[4], ("seq", "rows"), scatter_dimension=1, tiled=True),
-        lax.psum_scatter(stacked[5], ("seq", "rows"), scatter_dimension=1, tiled=True),
-    )
-    head_sums = lax.psum((stacked[6], stacked[7], stacked[8]), ("seq", "rows"))
+        sums = (grad_norm_gain, grad_conv_w, grad_conv_b, grad_gain, grad_decay, grad_bias, grad_skip)
+        collected[depth] = sums
+        big_in[depth] = scattered(in_weight_grad)
+        big_out[depth] = scattered(out_weight_grad)
+    flat = jnp.concatenate([part.reshape(-1) for sums in collected for part in sums])
+    flat = lax.psum(flat, AXES)
+    index = position * lax.axis_size("rows") + lax.axis_index("rows")
+    small = []
+    at = 0
+    for sums in collected:
+        row = []
+        for member, part in enumerate(sums):
+            total = flat[at : at + part.size].reshape(part.shape)
+            at += part.size
+            if member < 4:
+                size = part.shape[0] // lax.axis_size(AXES)
+                total = lax.dynamic_slice_in_dim(total, index * size, size)
+            row.append(total)
+        small.append(row)
+    stacked = [jnp.stack([small[level][member] for level in range(LAYERS)]) for member in range(7)]
+    norm_gain_grad, conv_w_grad, conv_b_grad, gain_grad, decay_grad, bias_grad, skip_grad = stacked
     return (
         hidden,
         gradient,
-        summed[0],
-        summed[1],
-        summed[2],
-        summed[3],
-        head_sums[0],
-        head_sums[1],
-        head_sums[2],
-        summed[4],
-        summed[5],
+        norm_gain_grad,
+        jnp.stack(big_in),
+        conv_w_grad,
+        conv_b_grad,
+        decay_grad,
+        bias_grad,
+        skip_grad,
+        gain_grad,
+        jnp.stack(big_out),
     )
 
 

time: 2300 us -> 1720 us (0.75)
  waiting for transfers between devices: 1270 us -> 789 us
  blocking collectives: 104 us -> 0 us
  starting transfers between devices: 9.98 us -> 63.5 us
  other arithmetic: 320 us -> 269 us
  matrix products: 340 us -> 363 us
    unnamed x13 -> x5, waiting for transfers between devices: 624 us -> 0.08 us
    reduce_scatter x1 -> x4, waiting for transfers between devices: 185 us -> 686 us  [scattered(): return lax.psum_scatter(total, AXES, scatter_dimension=0, tiled=True)]
    all_gather x4 -> x0, waiting for transfers between devices: 458 us -> none  [entering_2(): everything = jax.tree.map(lambda part: lax.all_gather(part, axis), value)]
    select_n x64 -> x0, other arithmetic: 93.6 us -> none  [lap(): return jax.tree.map(lambda a, b: jnp.where(reached, a, b), new, before)]
    psum x0 -> x1, waiting for transfers between devices: none -> 72.1 us  [local(): flat = lax.psum(flat, AXES)]
    all_gather x2 -> x0, blocking collectives: 62.5 us -> none  [entering_2(): everything = jax.tree.map(lambda part: lax.all_gather(part, axis), value)]
    all_to_all x0 -> x8, starting transfers between devices: none -> 53.1 us  [exchange(): return lax.all_to_all(parts, 'seq', split_axis=0, concat_axis=0, tiled=True)]
    unnamed x14 -> x54, other arithmetic: 10 us -> 61.6 us
  transfers between devices with their start and end apart: 13 -> 17, of which waited for: 9 -> 8; matrix products, arithmetic and copies ran while one was open for 23% -> 20% of each run, Pallas kernels for 0% -> 0%
where the time goes in v1:
time: 1720 us; the launch traced here: 1710 us
  waiting for transfers between devices  789 us (46%)
  matrix products  363 us (21%)
  other arithmetic  269 us (16%)
  local copies, waits for them, and re-layouts  207 us (12%)
  starting transfers between devices  63.5 us (4%)
  between operations  18.2 us (1%)
    reduce_scatter x4, waiting for transfers between devices, scattered(): return lax.psum_scatter(total, AXES, scatter_dimension=0, tiled=True)  686 us
    dot_general x6, matrix products, local_scan(): jnp.einsum('rcijh,rcjhp->rcihp', mixing, values_c, precision=HIGHEST)  132 us
    psum x1, waiting for transfers between devices, local(): flat = lax.psum(flat, AXES)  72.1 us
    unnamed x54, other arithmetic  61.6 us
    unnamed x606, local copies, waits for them, and re-layouts  55.2 us
    all_to_all x8, starting transfers between devices, exchange(): return lax.all_to_all(parts, 'seq', split_axis=0, concat_axis=0, tiled=True)  53.1 us
    dot_general x6, matrix products, local_scan(): jnp.einsum('rcin,rchpn->rcihp', out_c, before_blocks, precision=HIGHEST)  42 us
    reshape x6, local copies, waits for them, and re-layouts, local_scan(): scanned = (inner + outer).reshape(values.shape)  36.5 us
  transfers between devices with their start and end apart: 17, of which 8 were waited for; matrix products, arithmetic and copies ran while one was open for 20% of the time, Pallas kernels for 0%

profile of v1, /device:TPU:1, one launch (start us, length us, event | category | flops | bytes accessed | tf_op | source)
XLA Modules:
  0.0 1710.0 jit_solution(6132950933074509493)
XLA Ops:
  10.4 8.5 fusion.44
  45.6 14.2 fusion.65
  63.7 6.0 reshape.2597
  69.8 6.0 fusion.170
  77.5 6.0 all-to-all-start
  95.6 12.5 all-to-all-done
  148.5 7.2 all-to-all-start.1
  168.2 19.3 %bitcast_add_fusion.3 = f32[1,2,256,32,64]{2,4,3,1,0:T(8,128)S(1)} fusion(f32[2,256,32,64]{1,3,2,0:T(8,128)S(1)} %fusion.140, f32[2,256,32]{1,2,0:T(8,128)S(1)} %copy-done.91, f32[2,256,32]{1,2,0:T(8,128)S(1)} %copy-done.159, f32[2,256,32]{1,2,0:T(8,128)S(1)} %copy-done.154, f32[2,256,256]{2,1,0:T(8,128)S(1)} %copy-done.104, ...), kind=kOutput, calls=%fused_computation.123 | convolution fusion | flops 3244294144 | bytes 13434880 | tf_op jit(solution)/shard_map/jvp(rcijh,rcjhp->rcihp)/dot_general | solution.py:99
  192.8 6.6 reshape.2610
  204.3 5.5 multiply_add_fusion.5
  215.0 6.3 multiply_reduce_fusion.20
  222.1 8.0 fusion.47
  249.3 14.7 fusion.64
  267.8 5.9 reshape.2621
  273.7 6.0 fusion.173
  294.2 17.0 all-to-all-done.2
  337.6 7.7 all-to-all-start.3
  356.6 19.5 %bitcast_add_fusion.2 = f32[1,2,256,32,64]{2,4,3,1,0:T(8,128)S(1)} fusion(f32[2,256,32,64]{1,3,2,0:T(8,128)S(1)} %fusion.135, f32[2,256,32]{1,2,0:T(8,128)S(1)} %copy-done.95, f32[2,256,32]{1,2,0:T(8,128)S(1)} %copy-done.162, f32[2,256,32]{1,2,0:T(8,128)S(1)} %copy-done.157, f32[2,256,256]{2,1,0:T(8,128)S(1)} %copy-done.107, ...), kind=kOutput, calls=%fused_computation.122 | convolution fusion | flops 3244294144 | bytes 13434880 | tf_op jit(solution)/shard_map/jvp(rcijh,rcjhp->rcihp)/dot_general | solution.py:99
  381.3 6.4 reshape.2633
  397.0 5.4 multiply_add_fusion.4
  404.0 9.6 fusion.72
  413.7 6.9 multiply_reduce_fusion.12
  425.0 5.9 reshape.2644
  430.9 6.6 convolution_bitcast_fusion.3
  437.5 6.4 all-to-all-start.4
  444.0 30.5 %fusion.17 = (f32[2,256,32]{1,2,0:T(8,128)}, f32[2,256,32]{1,2,0:T(8,128)}, f32[2,256,32]{1,2,0:T(8,128)}, f32[2,256,256]{2,1,0:T(8,128)}) fusion(f32[2,256,256]{2,1,0:T(8,128)} %fusion.347, f32[2,256,32]{1,2,0:T(8,128)} %fusion.282, f32[2,256,32]{1,2,0:T(8,128)} %copy.1123, pred[2,256,256]{2,1,0:T(8,128)(4,1)} %compare_and_fusion, ...), kind=kOutput, calls=%fused_computation.29 | convolution fusion | flops 3283959808 | bytes 9895936 | tf_op jit(solution)/shard_map/transpose(jvp(rcijh,rcjhp->rcihp))/dot_general | solution.py:99
  480.2 6.3 all-to-all-start.5
  491.7 5.9 reshape.2643
  501.2 9.1 fusion.179
  516.0 7.5 fusion.169
  540.1 16.3 bitcast_add_fusion.1
  563.1 5.4 reduce-window.34
  568.6 6.3 fusion.197
  575.0 5.4 copy.1196
  580.4 6.5 reshape.2651
  591.9 13.9 multiply_reduce_fusion.4
  610.7 6.8 pad_add_fusion.1
  628.4 12.2 fusion.126
  648.6 6.5 multiply_reduce_fusion.13
  659.6 5.9 reshape.2663
  665.5 6.7 convolution_bitcast_fusion.2
  672.2 7.7 all-to-all-start.6
  680.0 29.9 %fusion.19 = (f32[2,256,32]{1,2,0:T(8,128)}, f32[2,256,32]{1,2,0:T(8,128)}, f32[2,256,32]{1,2,0:T(8,128)}, f32[2,256,256]{2,1,0:T(8,128)S(1)}) fusion(f32[2,256,256]{2,1,0:T(8,128)S(1)} %copy-done.105, f32[2,256,32]{1,2,0:T(8,128)S(1)} %copy-done.155, f32[2,256,32]{1,2,0:T(8,128)S(1)} %copy-done.160, pred[2,256,256]{2,1,0:T(8,128)(4,1)S(1)} %copy-done.118, ...), kind=kOutput, calls=%fused_computation.31 | convolution fusion | flops 3283959808 | bytes 9895936 | tf_op jit(solution)/shard_map/transpose(jvp(rcijh,rcjhp->rcihp))/dot_general | solution.py:99
  720.8 6.4 all-to-all-start.7
  731.9 5.9 reshape.2662
  739.2 8.8 fusion.176
  751.9 7.4 fusion.168
  773.2 16.2 bitcast_add_fusion
  796.8 5.4 reduce-window.36
  802.4 6.3 fusion.207
  814.0 6.5 reshape.2670
  825.5 13.2 multiply_reduce_fusion.8
  843.6 6.8 pad_add_fusion
  860.5 11.0 fusion.127
  872.7 8.5 fusion.233
  881.8 8.6 fusion.225
  891.2 14.6 fusion.163
  906.1 13.9 fusion.162
  920.1 8.0 bitcast_add_fusion.4
  930.0 72.1 %all-reduce.46.cloned.1.call-done = f32[29376]{0:T(1024)} async-done(((f32[29376]{0:T(1024)}), f32[29376]{0:T(1024)}) %all-reduce.46.cloned.1.call-update) | async-done | bytes 117520 | tf_op jit(solution)/shard_map/psum | solution.py:280
  1012.5 134.9 %reduce-scatter.11.cloned.1.call-done = f32[64,1024]{1,0:T(8,128)} async-done(((f32[2048,1024]{1,0:T(8,128)}), f32[64,1024]{1,0:T(8,128)}) %reduce-scatter.11.cloned.1.call-update) | async-done | bytes 262160 | tf_op jit(solution)/shard_map/reduce_scatter | solution.py:24
  1147.4 147.0 %reduce-scatter.9.cloned.1.call-done = f32[64,1024]{1,0:T(8,128)} async-done(((f32[2048,1024]{1,0:T(8,128)}), f32[64,1024]{1,0:T(8,128)}) %reduce-scatter.9.cloned.1.call-update) | async-done | bytes 262160 | tf_op jit(solution)/shard_map/reduce_scatter | solution.py:24
  1296.3 201.3 %reduce-scatter.7.cloned.1.call-done = f32[32,4384]{1,0:T(8,128)} async-done(((f32[1024,4384]{1,0:T(8,128)}), f32[32,4384]{1,0:T(8,128)}) %reduce-scatter.7.cloned.1.call-update) | async-done | bytes 561168 | tf_op jit(solution)/shard_map/reduce_scatter | solution.py:24
  1497.6 203.0 %reduce-scatter.5.cloned.1.call-done = f32[32,4384]{1,0:T(8,128)} async-done(((f32[1024,4384]{1,0:T(8,128)}), f32[32,4384]{1,0:T(8,128)}) %reduce-scatter.5.cloned.1.call-update) | async-done | bytes 561168 | tf_op jit(solution)/shard_map/reduce_scatter | solution.py:24
  (938 shorter events, 373.4 us)
Async XLA Ops:
  10.4 16.8 copy-start.264
  10.4 18.6 %copy-start.262 = (f32[2,32]{1,0:T(2,128)S(1)}, f32[2,32]{1,0:T(2,128)}, u32[]{:S(2)}) copy-start(f32[2,32]{1,0:T(2,128)} %param.20) | copy-start | bytes 772
  10.4 19.2 %copy-start.247 = (f32[2,32]{1,0:T(2,128)S(1)}, f32[2,32]{1,0:T(2,128)}, u32[]{:S(2)}) copy-start(f32[2,32]{1,0:T(2,128)} %param.19) | copy-start | bytes 772
  22.5 17.1 copy-start.175
  23.2 21.9 %collective-permute-start = (f32[1,3,2304]{2,0,1:T(1,128)S(1)}, f32[1,3,2304]{2,0,1:T(1,128)S(1)}, u32[]{:S(2)}, u32[]{:S(2)}) collective-permute-start(f32[1,3,2304]{2,0,1:T(1,128)S(1)} %copy.1065), channel_id=1, source_target_pairs={{0,2},{2,4},{4,6},{6,8},{8,10},{10,12},{12,14},{14,16},{16,18},{18... | collective-permute-start | bytes 82952 | tf_op jit(solution)/shard_map/ppermute | solution.py:30
  29.0 16.5 copy-start.141
  31.1 52.3 %copy-start.74 = (f32[1,512,32]{1,2,0:T(8,128)}, f32[1,512,32]{1,2,0:T(8,128)S(1)}, u32[]{:S(2)}) copy-start(f32[1,512,32]{1,2,0:T(8,128)S(1)} %get-tuple-element.136) | copy-start | bytes 196612
  37.5 38.3 %copy-start.194 = (f32[32]{0:T(128)}, f32[32]{0:T(128)S(1)}, u32[]{:S(2)}) copy-start(f32[32]{0:T(128)S(1)} %get-tuple-element.241) | copy-start | bytes 388
  37.5 38.3 %copy-start.203 = (f32[32]{0:T(128)}, f32[32]{0:T(128)S(1)}, u32[]{:S(2)}) copy-start(f32[32]{0:T(128)S(1)} %get-tuple-element.239) | copy-start | bytes 388
  39.5 30.2 %copy-start.89 = (f32[2,256,32]{1,2,0:T(8,128)}, f32[2,256,32]{1,2,0:T(8,128)S(1)}, u32[]{:S(2)}) copy-start(f32[2,256,32]{1,2,0:T(8,128)S(1)} %get-tuple-element.210) | copy-start | bytes 196612
  75.8 84.1 %copy-start.22 = (f32[1,2,32,64,128]{4,3,2,1,0:T(8,128)}, f32[1,2,32,64,128]{4,3,2,1,0:T(8,128)S(1)}, u32[]{:S(2)}) copy-start(f32[1,2,32,64,128]{4,3,2,1,0:T(8,128)S(1)} %fusion.170) | copy-start | bytes 6291460
  77.5 30.7 %all-to-all-start = ((f32[32,1,72,128]{3,2,1,0:T(8,128)}), f32[32,1,72,128]{3,2,1,0:T(8,128)S(1)}, u32[]{:S(2)}, u32[]{:S(2)}) async-start(f32[32,1,72,128]{3,2,1,0:T(8,128)} %maximum_bitcast_fusion), calls=%async_computation | async-start | bytes 2359296 | tf_op jit(solution)/shard_map/all_to_all | solution.py:34
  90.8 124.2 %copy-start.83 = (f32[1,2048]{1,0:T(1,128)}, f32[1,2048]{1,0:T(1,128)S(1)}, u32[]{:S(2)}) copy-start(f32[1,2048]{1,0:T(1,128)S(1)} %get-tuple-element.212) | copy-start | bytes 24580
  90.8 322.8 %copy-start.81 = (f32[1,2048]{1,0:T(1,128)}, f32[1,2048]{1,0:T(1,128)S(1)}, u32[]{:S(2)}) copy-start(f32[1,2048]{1,0:T(1,128)S(1)} %get-tuple-element.211) | copy-start | bytes 24580
  91.9 67.9 %copy-start.54 = (f32[2,256,128]{2,1,0:T(8,128)}, f32[2,256,128]{2,1,0:T(8,128)S(1)}, u32[]{:S(2)}) copy-start(f32[2,256,128]{2,1,0:T(8,128)S(1)} %copy.1068) | copy-start | bytes 786436
  148.5 50.9 %all-to-all-start.1 = ((f32[32,1,64,128]{3,2,1,0:T(8,128)}), f32[32,1,64,128]{3,2,1,0:T(8,128)S(1)}, u32[]{:S(2)}, u32[]{:S(2)}) async-start(f32[32,1,64,128]{3,2,1,0:T(8,128)} %bitcast.1037), calls=%async_computation.1 | async-start | bytes 2097152 | tf_op jit(solution)/shard_map/all_to_all | solution.py:34
  239.1 9.7 collective-permute-start.1
  243.1 30.6 %copy-start.93 = (f32[2,256,32]{1,2,0:T(8,128)}, f32[2,256,32]{1,2,0:T(8,128)S(1)}, u32[]{:S(2)}) copy-start(f32[2,256,32]{1,2,0:T(8,128)S(1)} %get-tuple-element.208) | copy-start | bytes 196612
  281.2 30.0 %all-to-all-start.2 = ((f32[32,1,72,128]{3,2,1,0:T(8,128)}), f32[32,1,72,128]{3,2,1,0:T(8,128)}, u32[]{:S(2)}, u32[]{:S(2)}) async-start(f32[32,1,72,128]{3,2,1,0:T(8,128)} %maximum_bitcast_fusion.1), calls=%async_computation.2 | async-start | bytes 2359296 | tf_op jit(solution)/shard_map/all_to_all | solution.py:34
  292.3 45.2 %copy-start.57 = (f32[2,256,128]{1,0,2:T(2,128)}, f32[2,256,128]{1,0,2:T(2,128)S(1)}, u32[]{:S(2)}) copy-start(f32[2,256,128]{1,0,2:T(2,128)S(1)} %reshape.2622) | copy-start | bytes 786436
  312.8 24.7 %copy-start.254 = (f32[1,2,1,1,1]{1,4,3,2,0:T(1,128)}, f32[1,2,1,1,1]{1,4,3,2,0:T(1,128)S(1)}, u32[]{:S(2)}) copy-start(f32[1,2,1,1,1]{1,4,3,2,0:T(1,128)S(1)} %copy.1350) | copy-start | bytes 28
  312.9 24.6 %copy-start.222 = (f32[1,2,1,1,1]{1,4,3,2,0:T(1,128)}, f32[1,2,1,1,1]{1,4,3,2,0:T(1,128)S(1)}, u32[]{:S(2)}) copy-start(f32[1,2,1,1,1]{1,4,3,2,0:T(1,128)S(1)} %copy.1349) | copy-start | bytes 28
  312.9 24.5 %copy-start.229 = (f32[1,2,1,1,1]{1,4,3,2,0:T(1,128)}, f32[1,2,1,1,1]{1,4,3,2,0:T(1,128)S(1)}, u32[]{:S(2)}) copy-start(f32[1,2,1,1,1]{1,4,3,2,0:T(1,128)S(1)} %copy.1348) | copy-start | bytes 28
  313.0 24.5 %copy-start.224 = (f32[1,2,1,1,1]{1,4,3,2,0:T(1,128)}, f32[1,2,1,1,1]{1,4,3,2,0:T(1,128)S(1)}, u32[]{:S(2)}) copy-start(f32[1,2,1,1,1]{1,4,3,2,0:T(1,128)S(1)} %copy.1347) | copy-start | bytes 28
  313.1 24.4 %copy-start.230 = (f32[1,2,1,1,1]{1,4,3,2,0:T(1,128)}, f32[1,2,1,1,1]{1,4,3,2,0:T(1,128)S(1)}, u32[]{:S(2)}) copy-start(f32[1,2,1,1,1]{1,4,3,2,0:T(1,128)S(1)} %copy.1346) | copy-start | bytes 28
  313.2 24.3 %copy-start.226 = (f32[1,2,1,1,1]{1,4,3,2,0:T(1,128)}, f32[1,2,1,1,1]{1,4,3,2,0:T(1,128)S(1)}, u32[]{:S(2)}) copy-start(f32[1,2,1,1,1]{1,4,3,2,0:T(1,128)S(1)} %copy.1345) | copy-start | bytes 28
  313.3 24.2 %copy-start.231 = (f32[1,2,1,1,1]{1,4,3,2,0:T(1,128)}, f32[1,2,1,1,1]{1,4,3,2,0:T(1,128)S(1)}, u32[]{:S(2)}) copy-start(f32[1,2,1,1,1]{1,4,3,2,0:T(1,128)S(1)} %copy.1344) | copy-start | bytes 28
  313.4 24.1 %copy-start.227 = (f32[1,2,1,1,1]{1,4,3,2,0:T(1,128)}, f32[1,2,1,1,1]{1,4,3,2,0:T(1,128)S(1)}, u32[]{:S(2)}) copy-start(f32[1,2,1,1,1]{1,4,3,2,0:T(1,128)S(1)} %copy.1343) | copy-start | bytes 28
  313.5 24.0 %copy-start.233 = (f32[1,2,1,1,1]{1,4,3,2,0:T(1,128)}, f32[1,2,1,1,1]{1,4,3,2,0:T(1,128)S(1)}, u32[]{:S(2)}) copy-start(f32[1,2,1,1,1]{1,4,3,2,0:T(1,128)S(1)} %copy.1342) | copy-start | bytes 28
  313.6 23.9 %copy-start.228 = (f32[1,2,1,1,1]{1,4,3,2,0:T(1,128)}, f32[1,2,1,1,1]{1,4,3,2,0:T(1,128)S(1)}, u32[]{:S(2)}) copy-start(f32[1,2,1,1,1]{1,4,3,2,0:T(1,128)S(1)} %copy.1341) | copy-start | bytes 28
  313.7 23.9 %copy-start.234 = (f32[1,2,1,1,1]{1,4,3,2,0:T(1,128)}, f32[1,2,1,1,1]{1,4,3,2,0:T(1,128)S(1)}, u32[]{:S(2)}) copy-start(f32[1,2,1,1,1]{1,4,3,2,0:T(1,128)S(1)} %copy.1340) | copy-start | bytes 28
  313.8 23.8 %copy-start.232 = (f32[1,2,1,1,1]{1,4,3,2,0:T(1,128)}, f32[1,2,1,1,1]{1,4,3,2,0:T(1,128)S(1)}, u32[]{:S(2)}) copy-start(f32[1,2,1,1,1]{1,4,3,2,0:T(1,128)S(1)} %copy.1339) | copy-start | bytes 28
  313.9 23.7 %copy-start.235 = (f32[1,2,1,1,1]{1,4,3,2,0:T(1,128)}, f32[1,2,1,1,1]{1,4,3,2,0:T(1,128)S(1)}, u32[]{:S(2)}) copy-start(f32[1,2,1,1,1]{1,4,3,2,0:T(1,128)S(1)} %copy.1338) | copy-start | bytes 28
  337.6 52.5 %all-to-all-start.3 = ((f32[32,1,64,128]{3,2,1,0:T(8,128)}), f32[32,1,64,128]{3,2,1,0:T(8,128)S(1)}, u32[]{:S(2)}, u32[]{:S(2)}) async-start(f32[32,1,64,128]{3,2,1,0:T(8,128)} %bitcast.1038), calls=%async_computation.3 | async-start | bytes 2097152 | tf_op jit(solution)/shard_map/all_to_all | solution.py:34
  437.5 37.0 %all-to-all-start.4 = ((f32[32,1,64,128]{3,2,1,0:T(8,128)}), f32[32,1,64,128]{3,2,1,0:T(8,128)S(1)}, u32[]{:S(2)}, u32[]{:S(2)}) async-start(f32[32,1,64,128]{3,2,1,0:T(8,128)} %convolution_bitcast_fusion.3), calls=%async_computation.4 | async-start | bytes 2097152 | tf_op jit(solution)/shard_map/all_to_all | solution.py:34
  444.0 30.5 %copy-start.223 = (f32[1,2,1,1,1]{1,4,3,2,0:T(1,128)S(1)}, f32[1,2,1,1,1]{1,4,3,2,0:T(1,128)}, u32[]{:S(2)}) copy-start(f32[1,2,1,1,1]{1,4,3,2,0:T(1,128)} %copy-done.222) | copy-start | bytes 28
  444.0 30.5 %copy-start.225 = (f32[1,2,1,1,1]{1,4,3,2,0:T(1,128)S(1)}, f32[1,2,1,1,1]{1,4,3,2,0:T(1,128)}, u32[]{:S(2)}) copy-start(f32[1,2,1,1,1]{1,4,3,2,0:T(1,128)} %copy-done.224) | copy-start | bytes 28
  480.2 49.8 %all-to-all-start.5 = ((f32[32,1,64,128]{3,2,1,0:T(8,128)}), f32[32,1,64,128]{3,2,1,0:T(8,128)S(1)}, u32[]{:S(2)}, u32[]{:S(2)}) async-start(f32[32,1,64,128]{3,2,1,0:T(8,128)} %bitcast.1039), calls=%async_computation.5 | async-start | bytes 2097152 | tf_op jit(solution)/shard_map/all_to_all | solution.py:34
  618.4 5.3 collective-permute-start.2
  624.2 18.7 %slice-start.11 = ((s8[8388608]{0:T(1024)(128)(4,1)}), s8[4194304]{0:T(1024)(128)(4,1)S(1)}, s32[]{:S(2)}) async-start(s8[8388608]{0:T(1024)(128)(4,1)} %bitcast.995), calls=%async_computation.28 | async-start | bytes 8388608
  672.2 37.7 %all-to-all-start.6 = ((f32[32,1,64,128]{3,2,1,0:T(8,128)}), f32[32,1,64,128]{3,2,1,0:T(8,128)S(1)}, u32[]{:S(2)}, u32[]{:S(2)}) async-start(f32[32,1,64,128]{3,2,1,0:T(8,128)} %convolution_bitcast_fusion.2), calls=%async_computation.6 | async-start | bytes 2097152 | tf_op jit(solution)/shard_map/all_to_all | solution.py:34
  679.9 30.0 %copy-start.210 = (f32[1,2,1,1,1]{1,4,3,2,0:T(1,128)S(1)}, f32[1,2,1,1,1]{1,4,3,2,0:T(1,128)}, u32[]{:S(2)}) copy-start(f32[1,2,1,1,1]{1,4,3,2,0:T(1,128)} %copy.1334) | copy-start | bytes 28
  679.9 30.0 %copy-start.211 = (f32[1,2,1,1,1]{1,4,3,2,0:T(1,128)S(1)}, f32[1,2,1,1,1]{1,4,3,2,0:T(1,128)}, u32[]{:S(2)}) copy-start(f32[1,2,1,1,1]{1,4,3,2,0:T(1,128)} %copy.1332) | copy-start | bytes 28
  679.9 30.0 %copy-start.212 = (f32[1,2,1,1,1]{1,4,3,2,0:T(1,128)S(1)}, f32[1,2,1,1,1]{1,4,3,2,0:T(1,128)}, u32[]{:S(2)}) copy-start(f32[1,2,1,1,1]{1,4,3,2,0:T(1,128)} %copy.1330) | copy-start | bytes 28
  679.9 30.0 %copy-start.213 = (f32[1,2,1,1,1]{1,4,3,2,0:T(1,128)S(1)}, f32[1,2,1,1,1]{1,4,3,2,0:T(1,128)}, u32[]{:S(2)}) copy-start(f32[1,2,1,1,1]{1,4,3,2,0:T(1,128)} %copy.1328) | copy-start | bytes 28
  679.9 30.0 %copy-start.214 = (f32[1,2,1,1,1]{1,4,3,2,0:T(1,128)S(1)}, f32[1,2,1,1,1]{1,4,3,2,0:T(1,128)}, u32[]{:S(2)}) copy-start(f32[1,2,1,1,1]{1,4,3,2,0:T(1,128)} %copy.1326) | copy-start | bytes 28
  679.9 30.0 %copy-start.215 = (f32[1,2,1,1,1]{1,4,3,2,0:T(1,128)S(1)}, f32[1,2,1,1,1]{1,4,3,2,0:T(1,128)}, u32[]{:S(2)}) copy-start(f32[1,2,1,1,1]{1,4,3,2,0:T(1,128)} %copy.1333) | copy-start | bytes 28
  680.0 30.0 %copy-start.216 = (f32[1,2,1,1,1]{1,4,3,2,0:T(1,128)S(1)}, f32[1,2,1,1,1]{1,4,3,2,0:T(1,128)}, u32[]{:S(2)}) copy-start(f32[1,2,1,1,1]{1,4,3,2,0:T(1,128)} %copy.1331) | copy-start | bytes 28
  680.0 30.0 %copy-start.217 = (f32[1,2,1,1,1]{1,4,3,2,0:T(1,128)S(1)}, f32[1,2,1,1,1]{1,4,3,2,0:T(1,128)}, u32[]{:S(2)}) copy-start(f32[1,2,1,1,1]{1,4,3,2,0:T(1,128)} %copy.1329) | copy-start | bytes 28
  680.0 30.0 %copy-start.218 = (f32[1,2,1,1,1]{1,4,3,2,0:T(1,128)S(1)}, f32[1,2,1,1,1]{1,4,3,2,0:T(1,128)}, u32[]{:S(2)}) copy-start(f32[1,2,1,1,1]{1,4,3,2,0:T(1,128)} %copy.1324) | copy-start | bytes 28
  680.0 30.0 %copy-start.219 = (f32[1,2,1,1,1]{1,4,3,2,0:T(1,128)S(1)}, f32[1,2,1,1,1]{1,4,3,2,0:T(1,128)}, u32[]{:S(2)}) copy-start(f32[1,2,1,1,1]{1,4,3,2,0:T(1,128)} %copy.1327) | copy-start | bytes 28
  680.0 30.0 %copy-start.220 = (f32[1,2,1,1,1]{1,4,3,2,0:T(1,128)S(1)}, f32[1,2,1,1,1]{1,4,3,2,0:T(1,128)}, u32[]{:S(2)}) copy-start(f32[1,2,1,1,1]{1,4,3,2,0:T(1,128)} %copy.1325) | copy-start | bytes 28
  680.0 30.0 %copy-start.221 = (f32[1,2,1,1,1]{1,4,3,2,0:T(1,128)S(1)}, f32[1,2,1,1,1]{1,4,3,2,0:T(1,128)}, u32[]{:S(2)}) copy-start(f32[1,2,1,1,1]{1,4,3,2,0:T(1,128)} %copy.1323) | copy-start | bytes 28
  680.0 30.0 %copy-start.251 = (f32[1,2,1,1,1]{1,4,3,2,0:T(1,128)S(1)}, f32[1,2,1,1,1]{1,4,3,2,0:T(1,128)}, u32[]{:S(2)}) copy-start(f32[1,2,1,1,1]{1,4,3,2,0:T(1,128)} %copy.1335) | copy-start | bytes 28
  680.0 30.0 %copy-start.252 = (f32[1,2,1,1,1]{1,4,3,2,0:T(1,128)S(1)}, f32[1,2,1,1,1]{1,4,3,2,0:T(1,128)}, u32[]{:S(2)}) copy-start(f32[1,2,1,1,1]{1,4,3,2,0:T(1,128)} %copy.1322) | copy-start | bytes 28
  680.0 30.0 %copy-start.253 = (f32[2]{0:T(128)S(1)}, f32[2]{0:T(128)}, u32[]{:S(2)}) copy-start(f32[2]{0:T(128)} %multiply_bitcast_fusion) | copy-start | bytes 28
  720.8 43.5 %all-to-all-start.7 = ((f32[32,1,64,128]{3,2,1,0:T(8,128)}), f32[32,1,64,128]{3,2,1,0:T(8,128)S(1)}, u32[]{:S(2)}, u32[]{:S(2)}) async-start(f32[32,1,64,128]{3,2,1,0:T(8,128)} %bitcast.296), calls=%async_computation.7 | async-start | bytes 2097152 | tf_op jit(solution)/shard_map/all_to_all | solution.py:34
  727.3 274.8 %all-reduce.46.cloned.1.call-start = ((), (), s32[]{:S(2)}) async-start(), calls=%async_computation.12 | async-start | bytes 237568 | tf_op jit(solution)/shard_map/psum | solution.py:280
  773.2 18.4 %copy-start.23 = (f32[1,2,32,64,128]{4,3,2,1,0:T(8,128)S(1)}, f32[1,2,32,64,128]{4,3,2,1,0:T(8,128)}, u32[]{:S(2)}) copy-start(f32[1,2,32,64,128]{4,3,2,1,0:T(8,128)} %copy-done.22) | copy-start | bytes 6291460
  851.3 4.6 collective-permute-start.3
  872.4 275.1 %reduce-scatter.11.cloned.1.call-start = ((), (), s32[]{:S(2)}) async-start(), calls=%async_computation.16 | async-start | bytes 8650752 | tf_op jit(solution)/shard_map/reduce_scatter | solution.py:24
  881.2 413.3 %reduce-scatter.9.cloned.1.call-start = ((), (), s32[]{:S(2)}) async-start(), calls=%async_computation.15 | async-start | bytes 8650752 | tf_op jit(solution)/shard_map/reduce_scatter | solution.py:24
  890.5 607.2 %reduce-scatter.7.cloned.1.call-start = ((), (), s32[]{:S(2)}) async-start(), calls=%async_computation.14 | async-start | bytes 18923520 | tf_op jit(solution)/shard_map/reduce_scatter | solution.py:24
  905.8 794.9 %reduce-scatter.5.cloned.1.call-start = ((), (), s32[]{:S(2)}) async-start(), calls=%async_computation.13 | async-start | bytes 18923520 | tf_op jit(solution)/shard_map/reduce_scatter | solution.py:24
  (231 other events, 1776.8 us)
Sparse Core Ops, SparseCore 0:
  872.5 129.5 all-reduce.45
  1004.3 143.0 reduce-scatter.10
  1149.7 144.6 reduce-scatter.8
  1296.6 200.9 reduce-scatter.6
  1499.9 200.7 reduce-scatter.4

commit v2 on v1

v2 whole, which is shorter than its diff:
```python
from functools import partial

import jax
import jax.numpy as jnp
from jax import lax
from jax.experimental import pallas as pl
from jax.experimental.pallas import tpu as pltpu
from jax.sharding import PartitionSpec as P

DI = 2048
STATE = 128
HEAD_DIM = 64
HEADS = DI // HEAD_DIM
KW = 4
GROUP = 256
LAYERS = 2
CHANNELS = DI + 2 * STATE
TILE = 256
HALO = 8
ROWS_AT = 64
VMEM_BYTES = 48 * 1024 * 1024

EPS = 1e-05
HIGHEST = lax.Precision.HIGHEST
AXES = ("seq", "rows")


def pcall(body, grid, in_specs, out_specs, out_shape, scratch, args, flops=0, nbytes=0):
    return pl.pallas_call(
        body,
        grid=grid,
        in_specs=in_specs,
        out_specs=out_specs,
        out_shape=out_shape,
        scratch_shapes=scratch,
        compiler_params=pltpu.CompilerParams(vmem_limit_bytes=VMEM_BYTES),
        cost_estimate=pl.CostEstimate(flops=flops, bytes_accessed=nbytes, transcendentals=0),
    )(*args)


def dot(a, b, dims=(((1,), (0,)), ((), ()))):
    return lax.dot_general(
        a.astype(jnp.bfloat16), b.astype(jnp.bfloat16), dims, preferred_element_type=jnp.float32
    )


def dot_nt(a, b):
    return dot(a, b, (((1,), (1,)), ((), ())))


def dot_exact(a, b):
    return jnp.dot(a, b, precision=HIGHEST, preferred_element_type=jnp.float32)


def sigmoid(v):
    return 1.0 / (1.0 + jnp.exp(-v))


def lane_iota(shape):
    return lax.broadcasted_iota(jnp.int32, shape, 1)


def low_half(rows):
    return lane_iota((rows, 128)) < HEAD_DIM


def to_heads(cols, first, pairs):
    rows = cols.shape[0]
    low = low_half(rows)
    parts = []
    for pair in range(pairs):
        at = first + 2 * pair
        parts.append(
            jnp.where(
                low,
                jnp.broadcast_to(cols[:, at : at + 1], (rows, 128)),
                jnp.broadcast_to(cols[:, at + 1 : at + 2], (rows, 128)),
            )
        )
    return jnp.concatenate(parts, 1) if pairs > 1 else parts[0]


def group_lanes(cols, group):
    return pltpu.roll(cols, (128 - 4 * group) % 128, 1)


def head_sums(group):
    channel = lax.broadcasted_iota(jnp.int32, (TILE, 128), 0)
    return (channel // HEAD_DIM + 4 * group == lane_iota((TILE, 128))).astype(jnp.float32)


def conv_rows(x_ref, w_ref, aux_ref, first, count):
    total = jnp.broadcast_to(w_ref[4:5, :], (count, w_ref.shape[1]))
    for tap in range(KW - 1):
        match = aux_ref[first : first + count, tap : tap + 1]
        total = total + w_ref[tap : tap + 1, :] * x_ref[first + 5 + tap : first + 5 + tap + count, :] * match
    return total + w_ref[3:4, :] * x_ref[first + 8 : first + 8 + count, :]


def states_kernel(
    x_ref, xbc_ref, rate_ref, aux_ref, w_ref, wbc_ref, hp_ref,
    v_ref, bc_ref, col_ref, cumr_ref, made_ref, kx_ref, pay_ref,
    bt_ref,
):
    group = pl.program_id(0)
    span = rate_ref.shape[0]
    count = span // GROUP

    @pl.when(group == 0)
    def _():
        for first in range(0, span, ROWS_AT):
            conv = conv_rows(xbc_ref, wbc_ref, aux_ref, first, ROWS_AT)
            bc_ref[first : first + ROWS_AT, :] = conv * sigmoid(conv)
        tri = (
            lax.broadcasted_iota(jnp.int32, (GROUP, GROUP), 0) >= lane_iota((GROUP, GROUP))
        ).astype(jnp.float32)
        for block in range(count):
            rows = slice(block * GROUP, (block + 1) * GROUP)
            bt_ref[block] = bc_ref[rows, :STATE].T.astype(jnp.bfloat16)
            raw = rate_ref[rows, :] + hp_ref[0:1, :]
            step = jnp.maximum(raw, 0.0) + jnp.log1p(jnp.exp(-jnp.abs(raw)))
            cum = dot_exact(tri, hp_ref[1:2, :] * step)
            last = cum[GROUP - 1 :, :]
            col_ref[0, rows, :] = cum
            col_ref[1, rows, :] = step
            col_ref[2, rows, :] = jnp.exp(cum) * aux_ref[rows, 3:4]
            col_ref[3, rows, :] = jnp.exp(last - cum) * aux_ref[rows, 4:5]
            cumr_ref[:, rows] = cum.T

    for first in range(0, span, ROWS_AT):
        conv = conv_rows(x_ref, w_ref, aux_ref, first, ROWS_AT)
        v_ref[first : first + ROWS_AT, :] = conv * sigmoid(conv)
    made = []
    keep = []
    for block in range(count):
        rows = slice(block * GROUP, (block + 1) * GROUP)
        weight = to_heads(group_lanes(col_ref[3, rows, :] * col_ref[1, rows, :], group), 0, 2)
        made.append(dot(bt_ref[block], weight * v_ref[rows, :]))
        ends = group_lanes(col_ref[2, (block + 1) * GROUP - 8 : (block + 1) * GROUP, :], group)
        keep.append(to_heads(ends, 0, 2)[7:8, :])
    made_ref[...] = made[0]
    kx_ref[...] = jnp.concatenate([keep[0], keep[1], jnp.zeros((6, TILE), jnp.float32)], 0)
    final = keep[1] * made[0] + made[1]
    total = jnp.broadcast_to(keep[0] * keep[1], (8, TILE))
    chunks = pay_ref.shape[0] // 2
    size = STATE // chunks
    for pair in range(2):
        lanes = slice(pair * 128, (pair + 1) * 128)
        for chunk in range(chunks):
            pay_ref[pair * chunks + chunk, :size, :] = final[chunk * size : (chunk + 1) * size, lanes]
            pay_ref[pair * chunks + chunk, size:, :] = total[:, lanes]


def inner_kernel(bc_ref, v_ref, col_ref, cumr_ref, aux_ref, auxr_ref, y_ref, g_ref):
    group = pl.program_id(1)

    @pl.when(group == 0)
    def _():
        scores = dot_nt(bc_ref[:, STATE:], bc_ref[:, :STATE])
        allowed = (aux_ref[:, 5:6] == auxr_ref[0:1, :]) & (
            lax.broadcasted_iota(jnp.int32, (GROUP, GROUP), 0) >= lane_iota((GROUP, GROUP))
        )
        g_ref[...] = jnp.where(allowed, scores, 0.0)

    cum = group_lanes(col_ref[0], group)
    step = group_lanes(col_ref[1], group)
    low = low_half(GROUP)
    for pair in range(2):
        lanes = slice(pair * 128, (pair + 1) * 128)
        scaled = to_heads(step, 2 * pair, 1) * v_ref[:, lanes]
        result = None
        for half in range(2):
            head = 2 * pair + half
            row = cumr_ref[pl.ds(4 * group + head, 1), :]
            parts = []
            for first in range(0, GROUP, 64):
                spread = cum[first : first + 64, head : head + 1] - row
                decay = jnp.exp(jnp.minimum(spread, 0.0))
                parts.append((g_ref[first : first + 64, :] * decay).astype(jnp.bfloat16))
            mixing = jnp.concatenate(parts, 0)
            picked = jnp.where(low if half == 0 else ~low, scaled, 0.0)
            part = dot(mixing, picked)
            result = part if result is None else result + part
        y_ref[:, lanes] = result


def finish_kernel(
    yi_ref, v_ref, gate_ref, bc_ref, col_ref, sin_ref, made_ref, kx_ref, ch_ref,
    y_ref, out_ref,
    gated_ref,
):
    block = pl.program_id(0)
    out_map = bc_ref[:, STATE:].astype(jnp.bfloat16)
    total = jnp.zeros((GROUP, 128), jnp.float32)
    pairs = v_ref.shape[1] // 128
    for pair in range(pairs):
        lanes = slice(pair * 128, (pair + 1) * 128)
        state = sin_ref[pair]
        state = jnp.where(block == 0, state, kx_ref[0:1, lanes] * state + made_ref[:, lanes])
        outer = to_heads(col_ref[2], 2 * pair, 1) * dot(out_map, state)
        result = yi_ref[:, lanes] + outer + ch_ref[0:1, lanes] * v_ref[:, lanes]
        y_ref[:, lanes] = result
        gate = gate_ref[:, lanes]
        gated = result * gate * sigmoid(gate)
        gated_ref[:, lanes] = gated
        total = total + gated * gated
    scale = lax.rsqrt(jnp.sum(total, 1, keepdims=True) / (pairs * 128) + EPS)
    for pair in range(pairs):
        lanes = slice(pair * 128, (pair + 1) * 128)
        out_ref[:, lanes] = (gated_ref[:, lanes] * scale * ch_ref[1:2, lanes]).astype(jnp.bfloat16)


def gate_back_kernel(
    dno_ref, y_ref, gate_ref, v_ref, bc_ref, col_ref, kx_ref, ch_ref,
    dy_ref, dgate_ref, sum_ref, d1_ref, pay_ref,
    gated_ref,
):
    block = pl.program_id(0)
    pairs = v_ref.shape[1] // 128
    square = jnp.zeros((GROUP, 128), jnp.float32)
    cross = jnp.zeros((GROUP, 128), jnp.float32)
    for pair in range(pairs):
        lanes = slice(pair * 128, (pair + 1) * 128)
        gate = gate_ref[:, lanes]
        gated = y_ref[:, lanes] * gate * sigmoid(gate)
        gated_ref[:, lanes] = gated
        square = square + gated * gated
        cross = cross + gated * dno_ref[:, lanes] * ch_ref[1:2, lanes]
    width = pairs * 128
    scale = lax.rsqrt(jnp.sum(square, 1, keepdims=True) / width + EPS)
    pull = scale * scale * scale * (jnp.sum(cross, 1, keepdims=True) / width)
    out_t = bc_ref[:, STATE:].T.astype(jnp.bfloat16)
    chunks = pay_ref.shape[0] // pairs
    size = STATE // chunks
    for pair in range(pairs):
        lanes = slice(pair * 128, (pair + 1) * 128)
        gate = gate_ref[:, lanes]
        gated = gated_ref[:, lanes]
        dno = dno_ref[:, lanes]
        sig = sigmoid(gate)
        dgated = scale * dno * ch_ref[1:2, lanes] - gated * pull
        dy = dgated * gate * sig
        dy_ref[:, lanes] = dy
        dgate_ref[:, lanes] = (dgated * y_ref[:, lanes] * sig * (1.0 + gate * (1.0 - sig))).astype(
            jnp.bfloat16
        )
        sums = jnp.concatenate(
            [
                jnp.sum(dno * gated * scale, 0, keepdims=True),
                jnp.sum(dy * v_ref[:, lanes], 0, keepdims=True),
                jnp.zeros((6, 128), jnp.float32),
            ],
            0,
        )
        fresh = dot(out_t, to_heads(col_ref[2], 2 * pair, 1) * dy)
        d1_ref[:, lanes] = fresh

        @pl.when(block == 0)
        def _():
            sum_ref[:, lanes] = sums
            for chunk in range(chunks):
                pay_ref[pair * chunks + chunk] = fresh[chunk * size : (chunk + 1) * size]

        @pl.when(block > 0)
        def _():
            sum_ref[:, lanes] += sums
            more = kx_ref[0:1, lanes] * fresh
            for chunk in range(chunks):
                pay_ref[pair * chunks + chunk] += more[chunk * size : (chunk + 1) * size]


def inner_back_kernel(
    bc_ref, v_ref, dy_ref, col_ref, cumr_ref, aux_ref, auxr_ref,
    x_ref, dbc_ref, dcum_ref,
    g_ref, dg_ref, cols_ref, rows_ref,
):
    group = pl.program_id(1)
    groups = pl.num_programs(1)

    def allowed():
        return (aux_ref[:, 5:6] == auxr_ref[0:1, :]) & (
            lax.broadcasted_iota(jnp.int32, (GROUP, GROUP), 0) <= lane_iota((GROUP, GROUP))
        )

    @pl.when(group == 0)
    def _():
        scores = dot_nt(bc_ref[:, :STATE], bc_ref[:, STATE:])
        g_ref[...] = jnp.where(allowed(), scores, 0.0)
        dg_ref[...] = jnp.zeros_like(dg_ref)
        cols_ref[...] = jnp.zeros_like(cols_ref)
        rows_ref[...] = jnp.zeros_like(rows_ref)

    cum = group_lanes(col_ref[0], group)
    step = group_lanes(col_ref[1], group)
    low = low_half(GROUP)
    lane = lane_iota((GROUP, 128))
    for pair in range(2):
        lanes = slice(pair * 128, (pair + 1) * 128)
        scaled = to_heads(step, 2 * pair, 1) * v_ref[:, lanes]
        dy = dy_ref[:, lanes]
        dy_low = dy.astype(jnp.bfloat16)
        result = None
        for half in range(2):
            head = 2 * pair + half
            row = cumr_ref[pl.ds(4 * group + head, 1), :]
            mine = low if half == 0 else ~low
            picked = jnp.where(mine, scaled, 0.0).astype(jnp.bfloat16)
            products = dot_nt(picked, dy_low)
            parts = []
            row_sum = jnp.zeros((8, GROUP), jnp.float32)
            col_sums = []
            for first in range(0, GROUP, 64):
                rows = slice(first, first + 64)
                spread = row - cum[rows, head : head + 1]
                decay = jnp.exp(jnp.minimum(spread, 0.0))
                scores = g_ref[rows, :]
                parts.append((scores * decay).astype(jnp.bfloat16))
                part = products[rows, :] * decay
                dg_ref[rows, :] += part
                both = part * scores
                row_sum = row_sum + jnp.sum(both.reshape(8, 8, GROUP), 0)
                col_sums.append(jnp.sum(both, 1, keepdims=True))
            mixing = jnp.concatenate(parts, 0)
            part = dot(mixing, jnp.where(mine, dy, 0.0))
            result = part if result is None else result + part
            rows_ref[pl.ds(4 * group + head, 1), :] = jnp.sum(row_sum, 0, keepdims=True)
            col_sum = jnp.concatenate(col_sums, 0)
            cols_ref[...] += jnp.where(lane == 4 * group + head, col_sum, 0.0)
        x_ref[:, lanes] = result

    @pl.when(group == groups - 1)
    def _():
        dg = jnp.where(allowed(), dg_ref[...], 0.0)
        dbc_ref[:, :STATE] = dot(dg, bc_ref[:, STATE:])
        dbc_ref[:, STATE:] = dot(dg.T, bc_ref[:, :STATE])
        dcum_ref[...] = rows_ref[...].T - cols_ref[...]


def states_back_kernel(
    xi_ref, v_ref, dy_ref, x_ref, xbc_ref, bc_ref, col_ref, dso_ref, sin_ref, made_ref, d1_ref,
    kx_ref, dbc_ref, dcum_ref, aux_ref, w_ref, wbc_ref, ch_ref, hp_ref, rate_ref,
    dconv_ref, dconv_bc_ref, drate_ref, sum_ref,
    ds_ref, dc_ref, z_ref, kd_ref, dmap_ref,
):
    group = pl.program_id(0)
    groups = pl.num_programs(0)
    span = v_ref.shape[0]
    count = span // GROUP

    @pl.when(group == 0)
    def _():
        ds_ref[...] = jnp.zeros_like(ds_ref)
        dc_ref[...] = dcum_ref[...]
        z_ref[...] = jnp.zeros_like(z_ref)
        kd_ref[...] = jnp.zeros_like(kd_ref)
        dmap_ref[...] = dbc_ref[...]

    sums = head_sums(group)
    end_grad = jnp.concatenate([dso_ref[0], dso_ref[1]], 1)
    state = jnp.concatenate([sin_ref[0], sin_ref[1]], 1)
    ends = [d1_ref[...] + kx_ref[1:2, :] * end_grad, end_grad]
    starts = [state, kx_ref[0:1, :] * state + made_ref[...]]
    for block in range(count):
        rows = slice(block * GROUP, (block + 1) * GROUP)
        step = to_heads(group_lanes(col_ref[1, rows, :], group), 0, 2)
        entering = to_heads(group_lanes(col_ref[2, rows, :], group), 0, 2)
        tail = to_heads(group_lanes(col_ref[3, rows, :], group), 0, 2)
        values = v_ref[rows, :]
        dy = dy_ref[rows, :]
        from_end = tail * dot(bc_ref[rows, :STATE], ends[block])
        outer = entering * dot(bc_ref[rows, STATE:], starts[block])
        pulled = xi_ref[rows, :] + from_end
        ds_ref[rows, :] += dot(values * pulled, sums)
        z_ref[rows, :] += dot(step * values * from_end, sums)
        dc_ref[rows, :] += dot(dy * outer, sums)
        dmap_ref[rows, :STATE] += dot_nt(tail * step * values, ends[block])
        dmap_ref[rows, STATE:] += dot_nt(entering * dy, starts[block])
        kept = kx_ref[block : block + 1, :] * jnp.sum(ends[block] * starts[block], 0, keepdims=True)
        kd_ref[block] += dot_exact(jnp.broadcast_to(kept, (8, TILE)), sums)
        grad = step * pulled + ch_ref[0:1, :] * dy
        conv = conv_rows(x_ref, w_ref, aux_ref, block * GROUP, GROUP)
        sig = sigmoid(conv)
        dconv_ref[rows, :] = grad * sig * (1.0 + conv * (1.0 - sig))

    @pl.when(group == groups - 1)
    def _():
        after = (
            lax.broadcasted_iota(jnp.int32, (GROUP, GROUP), 0) <= lane_iota((GROUP, GROUP))
        ).astype(jnp.float32)
        before = (
            lax.broadcasted_iota(jnp.int32, (GROUP, GROUP), 0) > lane_iota((GROUP, GROUP))
        ).astype(jnp.float32)
        bias_sum = jnp.zeros((1, 128), jnp.float32)
        decay_sum = jnp.zeros((1, 128), jnp.float32)
        for block in range(count):
            rows = slice(block * GROUP, (block + 1) * GROUP)
            conv = conv_rows(xbc_ref, wbc_ref, aux_ref, block * GROUP, GROUP)
            sig = sigmoid(conv)
            dconv_bc_ref[rows, :] = dmap_ref[rows, :] * sig * (1.0 + conv * (1.0 - sig))
            z = z_ref[rows, :]
            da = dot_exact(after, dc_ref[rows, :]) + kd_ref[block, 0:1, :]
            da = da + dot_exact(before, z)
            ds = ds_ref[rows, :] + hp_ref[1:2, :] * da
            drate = ds * sigmoid(rate_ref[rows, :] + hp_ref[0:1, :])
            drate_ref[rows, :] = drate.astype(jnp.bfloat16)
            bias_sum = bias_sum + jnp.sum(drate, 0, keepdims=True)
            decay_sum = decay_sum + jnp.sum(da * hp_ref[1:2, :] * col_ref[1, rows, :], 0, keepdims=True)
        sum_ref[...] = jnp.concatenate([bias_sum, decay_sum, jnp.zeros((6, 128), jnp.float32)], 0)


def conv_back_kernel(dconv_ref, dconv_bc_ref, next_ref, x_ref, aux_ref, w_ref, dx_ref, sum_ref, ext_ref):
    tile = pl.program_id(0)
    span = dconv_ref.shape[0]

    @pl.when(tile < pl.num_programs(0) - 1)
    def _():
        ext_ref[:span, :] = dconv_ref[...]

    @pl.when(tile == pl.num_programs(0) - 1)
    def _():
        ext_ref[:span, :] = dconv_bc_ref[...]

    ext_ref[span:, :] = next_ref[...]
    sums = [jnp.zeros((1, TILE), jnp.float32) for _ in range(KW + 1)]
    for first in range(0, span, ROWS_AT):
        here = ext_ref[first : first + ROWS_AT, :]
        grad = w_ref[3:4, :] * here
        for ahead in range(1, KW):
            match = aux_ref[first : first + ROWS_AT, 5 + ahead : 6 + ahead]
            grad = grad + w_ref[3 - ahead : 4 - ahead, :] * ext_ref[first + ahead : first + ahead + ROWS_AT, :] * match
        dx_ref[first : first + ROWS_AT, :] = grad.astype(jnp.bfloat16)
        for tap in range(KW):
            term = here * x_ref[first + 5 + tap : first + 5 + tap + ROWS_AT, :]
            if tap < KW - 1:
                term = term * aux_ref[first : first + ROWS_AT, tap : tap + 1]
            sums[tap] = sums[tap] + jnp.sum(term, 0, keepdims=True)
        sums[KW] = sums[KW] + jnp.sum(here, 0, keepdims=True)
    sum_ref[...] = jnp.concatenate(sums + [jnp.zeros((3, TILE), jnp.float32)], 0)


def scan_kernel(reverse, rows, in_ref, keep_ref, out_ref):
    peers = out_ref.shape[0]
    carried = jnp.zeros((rows, 128), jnp.float32)
    for at in range(peers):
        peer = peers - 1 - at if reverse else at
        out_ref[peer] = carried
        carried = keep_ref[peer, 0:1, :] * carried + in_ref[peer, :rows, :]


def full(shape):
    return pl.BlockSpec(shape, lambda *at: (0,) * len(shape))


def shape_of(dims, dtype=jnp.float32):
    return jax.ShapeDtypeStruct(dims, dtype)


def vmem(dims, dtype=jnp.float32):
    return pltpu.VMEM(dims, dtype)


def make_states(peers, mixed_ext, rate, aux, conv, hp):
    span = rate.shape[0]
    groups = DI // TILE
    chunks = peers * 128 // DI
    tile = lambda rows: pl.BlockSpec((rows, TILE), lambda g: (0, g))
    maps = lambda rows: pl.BlockSpec((rows, TILE), lambda g: (0, groups))
    pay = (2 * chunks, STATE // chunks + 8, 128)
    return pcall(
        states_kernel,
        (groups,),
        [tile(span + HALO), maps(span + HALO), full((span, 128)), full((span, 128)), tile(8), maps(8), full((8, 128))],
        [
            tile(span),
            full((span, TILE)),
            full((4, span, 128)),
            full((128, span)),
            tile(STATE),
            tile(8),
            pl.BlockSpec(pay, lambda g: (g, 0, 0)),
        ],
        [
            shape_of((span, DI)),
            shape_of((span, TILE)),
            shape_of((4, span, 128)),
            shape_of((128, span)),
            shape_of((STATE, DI)),
            shape_of((8, DI)),
            shape_of((peers,) + pay[1:]),
        ],
        [vmem((span // GROUP, STATE, GROUP), jnp.bfloat16)],
        (mixed_ext, mixed_ext, rate, aux, conv, conv, hp),
        flops=2 * span * DI * STATE,
        nbytes=12 * span * DI,
    )


def block_specs(span):
    blocks = span // GROUP
    tile = pl.BlockSpec((GROUP, TILE), lambda b, g: (b, g))
    maps = pl.BlockSpec((GROUP, TILE), lambda b, g: (b, 0))
    col = pl.BlockSpec((4, GROUP, 128), lambda b, g: (0, b, 0))
    row = pl.BlockSpec((128, GROUP), lambda b, g: (0, b))
    aux = pl.BlockSpec((GROUP, 128), lambda b, g: (b, 0))
    auxr = pl.BlockSpec((8, GROUP), lambda b, g: (0, b))
    return (blocks, DI // TILE), tile, maps, col, row, aux, auxr


def inner(bc, values, col, cumr, aux, auxr):
    span = values.shape[0]
    grid, tile, maps, cols, row, auxs, auxrs = block_specs(span)
    return pcall(
        inner_kernel,
        grid,
        [maps, tile, cols, row, auxs, auxrs],
        tile,
        shape_of((span, DI)),
        [vmem((GROUP, GROUP))],
        (bc, values, col, cumr, aux, auxr),
        flops=2 * span * GROUP * DI * 4,
        nbytes=8 * span * DI,
    )


def finish(yi, values, gate, bc, col, state_in, made, kx, ch):
    span = values.shape[0]
    wide = pl.BlockSpec((GROUP, DI), lambda b: (b, 0))
    maps = pl.BlockSpec((GROUP, TILE), lambda b: (b, 0))
    cols = pl.BlockSpec((4, GROUP, 128), lambda b: (0, b, 0))
    return pcall(
        finish_kernel,
        (span // GROUP,),
        [wide, wide, wide, maps, cols, full((DI // 128, STATE, 128)), full((STATE, DI)), full((8, DI)), full((8, DI))],
        [wide, wide],
        [shape_of((span, DI)), shape_of((span, DI), jnp.bfloat16)],
        [vmem((GROUP, DI))],
        (yi, values, gate, bc, col, state_in, made, kx, ch),
        flops=2 * span * DI * STATE,
        nbytes=18 * span * DI,
    )


def gate_back(peers, dno, y, gate, values, bc, col, kx, ch):
    span = values.shape[0]
    chunks = peers * 128 // DI
    wide = pl.BlockSpec((GROUP, DI), lambda b: (b, 0))
    maps = pl.BlockSpec((GROUP, TILE), lambda b: (b, 0))
    cols = pl.BlockSpec((4, GROUP, 128), lambda b: (0, b, 0))
    pay = (peers, STATE // chunks, 128)
    return pcall(
        gate_back_kernel,
        (span // GROUP,),
        [wide, wide, wide, wide, maps, cols, full((8, DI)), full((8, DI))],
        [wide, wide, full((8, DI)), full((STATE, DI)), full(pay)],
        [
            shape_of((span, DI)),
            shape_of((span, DI), jnp.bfloat16),
            shape_of((8, DI)),
            shape_of((STATE, DI)),
            shape_of(pay),
        ],
        [vmem((GROUP, DI))],
        (dno, y, gate, values, bc, col, kx, ch),
        flops=2 * span * DI * STATE,
        nbytes=22 * span * DI,
    )


def inner_back(bc, values, dy, col, cumr, aux, auxr):
    span = values.shape[0]
    grid, tile, maps, cols, row, auxs, auxrs = block_specs(span)
    return pcall(
        inner_back_kernel,
        grid,
        [maps, tile, tile, cols, row, auxs, auxrs],
        [tile, maps, auxs],
        [shape_of((span, DI)), shape_of((span, TILE)), shape_of((span, 128))],
        [vmem((GROUP, GROUP)), vmem((GROUP, GROUP)), vmem((GROUP, 128)), vmem((128, GROUP))],
        (bc, values, dy, col, cumr, aux, auxr),
        flops=2 * span * GROUP * DI * 8,
        nbytes=12 * span * DI,
    )


def states_back(xi, values, dy, mixed_ext, bc, col, dso, state_in, made, d1, kx, dbc, dcum, aux, conv, ch, hp, rate):
    span = values.shape[0]
    groups = DI // TILE
    tile = lambda rows: pl.BlockSpec((rows, TILE), lambda g: (0, g))
    maps = lambda rows: pl.BlockSpec((rows, TILE), lambda g: (0, groups))
    state = pl.BlockSpec((2, STATE, 128), lambda g: (g, 0, 0))
    small = full((span, 128))
    return pcall(
        states_back_kernel,
        (groups,),
        [
            tile(span), tile(span), tile(span), tile(span + HALO), maps(span + HALO), full((span, TILE)),
            full((4, span, 128)), state, state, tile(STATE), tile(STATE), tile(8), full((span, TILE)), small,
            small, tile(8), maps(8), tile(8), full((8, 128)), small,
        ],
        [tile(span), full((span, TILE)), small, full((8, 128))],
        [shape_of((span, DI)), shape_of((span, TILE)), shape_of((span, 128), jnp.bfloat16), shape_of((8, 128))],
        [vmem((span, 128)), vmem((span, 128)), vmem((span, 128)), vmem((span // GROUP, 8, 128)), vmem((span, TILE))],
        (xi, values, dy, mixed_ext, mixed_ext, bc, col, dso, state_in, made, d1, kx, dbc, dcum, aux, conv, conv, ch, hp, rate),
        flops=8 * span * DI * STATE,
        nbytes=20 * span * DI,
    )


def conv_back(dconv, dconv_bc, following, mixed_ext, aux, conv):
    span = dconv.shape[0]
    groups = DI // TILE
    tile = lambda rows: pl.BlockSpec((rows, TILE), lambda g: (0, g))
    return pcall(
        conv_back_kernel,
        (groups + 1,),
        [
            pl.BlockSpec((span, TILE), lambda g: (0, jnp.minimum(g, groups - 1))),
            full((span, TILE)), tile(HALO), tile(span + HALO), full((span, 128)), tile(8),
        ],
        [tile(span), tile(8)],
        [shape_of((span, CHANNELS), jnp.bfloat16), shape_of((8, CHANNELS))],
        [vmem((span + HALO, TILE))],
        (dconv, dconv_bc, following, mixed_ext, aux, conv),
        flops=8 * span * DI,
        nbytes=10 * span * DI,
    )


def scan_states(received, keeps, reverse):
    peers = received.shape[0]
    rows = STATE * DI // 128 // peers
    return pcall(
        partial(scan_kernel, reverse, rows),
        (1,),
        [full(received.shape), full(keeps.shape)],
        full((peers, rows, 128)),
        shape_of((peers, rows, 128)),
        [],
        (received, keeps),
        nbytes=8 * peers * rows * 128,
    )


def exchange(parts):
    return lax.all_to_all(parts, "seq", split_axis=0, concat_axis=0, tiled=True)


def shifted(value, steps):
    count = lax.axis_size("seq")
    first, last = max(0, -steps), min(count, count - steps)
    return lax.ppermute(value, "seq", [(source, source + steps) for source in range(first, last)])


def doc_table(lengths, first, count):
    starts = jnp.cumsum(lengths, -1) - lengths
    places = first + jnp.arange(count, dtype=jnp.int32)
    return jnp.sum((starts[None, :] <= places[:, None]).astype(jnp.int32), -1) - 1


def token_marks(lengths, span):
    docs_all = doc_table(lengths, lax.axis_index("seq") * span - HALO, span + 2 * HALO)
    docs = docs_all[HALO : HALO + span]
    ends = docs_all[HALO - 1 : HALO + span : GROUP]
    prior, final = jnp.repeat(ends[:-1], GROUP), jnp.repeat(ends[1:], GROUP)
    near = lambda step: docs_all[HALO + step : HALO + step + span] == docs
    marks = [near(-3), near(-2), near(-1), docs == prior, docs == final, docs, near(1), near(2), near(3)]
    marks = jnp.stack([mark.astype(jnp.float32) for mark in marks], 1)
    aux = jnp.pad(marks, ((0, 0), (0, 128 - marks.shape[1])))
    auxr = jnp.broadcast_to(docs.astype(jnp.float32)[None, :], (8, span))
    return aux, auxr


def scattered(total):
    return lax.psum_scatter(total, AXES, scatter_dimension=0, tiled=True)


def matmul(a, b):
    return jnp.dot(a, b, preferred_element_type=jnp.float32)


def matmul_tn(a, b):
    return jnp.einsum("tn,tm->nm", a, b, preferred_element_type=jnp.float32)


def matmul_nt(a, b):
    return jnp.einsum("tn,mn->tm", a, b, preferred_element_type=jnp.float32)


def normalise(values, gain):
    scale = lax.rsqrt(jnp.mean(values * values, -1, keepdims=True) + EPS)
    return (values * scale * gain).astype(jnp.bfloat16)


def normalise_back(values, gain, grad):
    scale = lax.rsqrt(jnp.mean(values * values, -1, keepdims=True) + EPS)
    gain_grad = jnp.sum(grad * values * scale, 0)
    pulled = grad * gain
    return scale * pulled - values * (scale**3 * jnp.mean(pulled * values, -1, keepdims=True)), gain_grad


def padded(rows, width):
    table = jnp.stack([jnp.pad(row, (0, width - row.shape[0])) for row in rows])
    return jnp.pad(table, ((0, 8 - len(rows)), (0, 0)))


def local(
    inputs,
    lengths,
    norm_gain,
    in_weight,
    conv_weight,
    conv_bias,
    log_decay,
    dt_bias,
    skip,
    gate_gain,
    out_weight,
    cotangent,
):
    _, span, width = inputs.shape
    peers = lax.axis_size("seq")
    aux, auxr = token_marks(lengths[0], span)
    hidden = inputs[0]
    saved = []
    for depth in range(LAYERS):
        conv = jnp.concatenate([conv_weight[depth].T, conv_bias[depth][None], jnp.zeros((3, CHANNELS), jnp.float32)])
        hp = padded([dt_bias[depth], -jnp.exp(log_decay[depth])], 128)
        ch = padded([jnp.repeat(skip[depth], HEAD_DIM), gate_gain[depth]], DI)
        gate_weight = in_weight[depth][:, :DI]
        mixed_weight = in_weight[depth][:, DI : DI + CHANNELS]
        rate_weight = jnp.pad(in_weight[depth][:, DI + CHANNELS :], ((0, 0), (0, 128 - HEADS)))
        before = shifted(hidden[span - HALO :], 1)
        normed = normalise(hidden, norm_gain[depth])
        normed_ext = jnp.concatenate([normalise(before, norm_gain[depth]), normed])
        mixed_ext = matmul(normed_ext, mixed_weight)
        rate = matmul(normed, rate_weight)
        gate = matmul(normed, gate_weight)
        values, bc, col, cumr, made, kx, pay = make_states(peers, mixed_ext, rate, aux, conv, hp)
        received = exchange(pay)
        yi = inner(bc, values, col, cumr, aux, auxr)
        keeps = received[:, -8:]
        state_in = exchange(scan_states(received, keeps, False)).reshape(DI // 128, STATE, 128)
        y, out_low = finish(yi, values, gate, bc, col, state_in, made, kx, ch)
        saved.append(
            (hidden, normed, mixed_ext, rate, gate, values, bc, col, cumr, made, kx, keeps, state_in, y, out_low)
            + (conv, hp, ch, gate_weight, mixed_weight, rate_weight)
        )
        hidden = hidden + matmul(out_low, out_weight[depth])
    gradient = cotangent[0]
    collected = [None] * LAYERS
    big_in = [None] * LAYERS
    big_out = [None] * LAYERS
    for depth in reversed(range(LAYERS)):
        entry, normed, mixed_ext, rate, gate, values, bc, col, cumr, made, kx, keeps, state_in, y, out_low = saved[depth][:15]
        conv, hp, ch, gate_weight, mixed_weight, rate_weight = saved[depth][15:]
        grad_low = gradient.astype(jnp.bfloat16)
        big_out[depth] = scattered(matmul_tn(out_low, grad_low))
        dno = matmul_nt(grad_low, out_weight[depth])
        dy, dgate, gate_sums, d1, pay = gate_back(peers, dno, y, gate, values, bc, col, kx, ch)
        received = exchange(pay)
        xi, dbc, dcum = inner_back(bc, values, dy, col, cumr, aux, auxr)
        dso = exchange(scan_states(received, keeps, True)).reshape(DI // 128, STATE, 128)
        dconv, dconv_bc, drate, head_rows = states_back(
            xi, values, dy, mixed_ext, bc, col, dso, state_in, made, d1, kx, dbc, dcum, aux, conv, ch, hp, rate
        )
        following = shifted(jnp.concatenate([dconv[:HALO], dconv_bc[:HALO]], 1), -1)
        dmixed, conv_sums = conv_back(dconv, dconv_bc, following, mixed_ext, aux, conv)
        dprojected = jnp.concatenate([dgate, dmixed, drate[:, :HEADS]], 1)
        big_in[depth] = scattered(matmul_tn(normed, dprojected))
        grad_normed = matmul_nt(dprojected, in_weight[depth])
        grad_hidden, gain_grad = normalise_back(entry, norm_gain[depth], grad_normed)
        gradient = gradient + grad_hidden
        collected[depth] = (
            gain_grad,
            conv_sums[:KW].T,
            conv_sums[KW],
            gate_sums[0],
            head_rows[1, :HEADS],
            head_rows[0, :HEADS],
            jnp.sum(gate_sums[1].reshape(HEADS, HEAD_DIM), 1),
        )
    flat = jnp.concatenate([part.reshape(-1) for sums in collected for part in sums])
    flat = lax.psum(flat, AXES)
    index = lax.axis_index("seq") * lax.axis_size("rows") + lax.axis_index("rows")
    small = []
    at = 0
    for sums in collected:
        row = []
        for member, part in enumerate(sums):
            total = flat[at : at + part.size].reshape(part.shape)
            at += part.size
            if member < 4:
                size = part.shape[0] // lax.axis_size(AXES)
                total = lax.dynamic_slice_in_dim(total, index * size, size)
            row.append(total)
        small.append(row)
    stacked = [jnp.stack([small[level][member] for level in range(LAYERS)]) for member in range(7)]
    norm_gain_grad, conv_w_grad, conv_b_grad, gain_grad, decay_grad, bias_grad, skip_grad = stacked
    return (
        hidden[None],
        gradient[None],
        norm_gain_grad,
        jnp.stack(big_in),
        conv_w_grad,
        conv_b_grad,
        decay_grad,
        bias_grad,
        skip_grad,
        gain_grad,
        jnp.stack(big_out),
    )


def solution(mesh):
    in_specs = (
        P("rows", "seq", None),
        P("rows", None),
        P(),
        P(),
        P(),
        P(),
        P(),
        P(),
        P(),
        P(),
        P(),
        P("rows", "seq", None),
    )
    out_specs = (
        P("rows", "seq", None),
        P("rows", "seq", None),
        P(None, ("seq", "rows")),
        P(None, ("seq", "rows"), None),
        P(None, ("seq", "rows"), None),
        P(None, ("seq", "rows")),
        P(),
        P(),
        P(),
        P(None, ("seq", "rows")),
        P(None, ("seq", "rows"), None),
    )
    return jax.shard_map(local, mesh=mesh, in_specs=in_specs, out_specs=out_specs, check_vma=False)
```

time: 1720 us -> 1440 us (0.84)
  Pallas kernels: 0 us -> 271 us
  other arithmetic: 269 us -> 18.2 us
  matrix products: 363 us -> 116 us
  blocking collectives: 0 us -> 127 us
  local copies, waits for them, and re-layouts: 207 us -> 81.2 us
  waiting for transfers between devices: 789 us -> 764 us
  starting transfers between devices: 63.5 us -> 42.4 us
    pallas_call x0 -> x18, Pallas kernels: none -> 271 us  [pcall(): pl.pallas_call(body, grid=grid, in_specs=in_specs, out_specs=out_specs, o...]
    dot_general x42 -> x16, matrix products: 363 us -> 116 us  [the longest x4 41.8 us: matmul_tn(): return jnp.einsum('tn,tm->nm', a, b, preferred_element_type=jnp.float32)]
    all_to_all x0 -> x4, blocking collectives: none -> 127 us  [exchange(): return lax.all_to_all(parts, 'seq', split_axis=0, concat_axis=0, tiled=True)]
    reduce_sum x20 -> x6, other arithmetic: 73.5 us -> 3.39 us  [the longest x3 2.05 us: normalise(): scale = lax.rsqrt(jnp.mean(values * values, -1, keepdims=True) + EPS)]
    unnamed x54 -> x1, other arithmetic: 61.6 us -> 0.01 us
    reshape x24 -> x0, local copies, waits for them, and re-layouts: 55.6 us -> none  [the longest x6 36.5 us: local_scan(): scanned = (inner + outer).reshape(values.shape)]
    mul x25 -> x2, other arithmetic: 51.3 us -> 0.02 us  [normalise_back(): scale ** 3 * jnp.mean(pulled * values, -1, keepdims=True)]
    all_to_all x8 -> x4, waiting for transfers between devices: 29.5 us -> 0.01 us  [exchange(): return lax.all_to_all(parts, 'seq', split_axis=0, concat_axis=0, tiled=True)]
  transfers between devices with their start and end apart: 17 -> 13, of which waited for: 8 -> 8; matrix products, arithmetic and copies ran while one was open for 20% -> 8% of each run, Pallas kernels for 0% -> 8%
where the time goes in v2:
time: 1440 us; the launch traced here: 1430 us
  waiting for transfers between devices  764 us (53%)
  Pallas kernels  271 us (19%)
  blocking collectives  127 us (9%)
  matrix products  116 us (8%)
  local copies, waits for them, and re-layouts  81.2 us (6%)
  starting transfers between devices  42.4 us (3%)
  other arithmetic  18.2 us (1%)
  between operations  15.4 us (1%)
    reduce_scatter x4, waiting for transfers between devices, scattered(): return lax.psum_scatter(total, AXES, scatter_dimension=0, tiled=True)  685 us
    pallas_call x18, Pallas kernels, pcall(): pl.pallas_call(body, grid=grid, in_specs=in_specs, out_specs=out_specs, o...  271 us
    all_to_all x4, blocking collectives, exchange(): return lax.all_to_all(parts, 'seq', split_axis=0, concat_axis=0, tiled=True)  127 us
    psum x1, waiting for transfers between devices, local(): flat = lax.psum(flat, AXES)  71.1 us
    unnamed x223, local copies, waits for them, and re-layouts  43.5 us
    dot_general x4, matrix products, matmul_tn(): return jnp.einsum('tn,tm->nm', a, b, preferred_element_type=jnp.float32)  41.8 us
    dot_general x8, matrix products, matmul(): return jnp.dot(a, b, preferred_element_type=jnp.float32)  38.5 us
    dot_general x4, matrix products, matmul_nt(): return jnp.einsum('tn,mn->tm', a, b, preferred_element_type=jnp.float32)  35.7 us
  transfers between devices with their start and end apart: 13, of which 8 were waited for; matrix products, arithmetic and copies ran while one was open for 8% of the time, Pallas kernels for 8%

profile of v2, /device:TPU:1, one launch (start us, length us, event | category | flops | bytes accessed | tf_op | source)
XLA Modules:
  0.0 1434.5 jit_solution(71926201716657673)
XLA Ops:
  7.9 3.9 collective-permute-start
  13.6 1.8 fusion.20
  15.6 1.4 fusion.76
  17.1 10.3 slice_bitcast_fusion
  28.4 2.4 copy-done.79
  31.3 7.2 fusion.2.x_ref.xbc_ref
  38.5 15.3 %shard_map.203 = (f32[512,2048]{1,0:T(8,128)}, f32[512,256]{1,0:T(8,128)S(1)}, f32[4,512,128]{2,1,0:T(8,128)S(1)}, f32[128,512]{1,0:T(8,128)S(1)}, f32[128,2048]...) custom-call(f32[520,2304]{1,0:T(8,128)} %fusion.2.x_ref.xbc_ref, f32[520,2304]{1,0:T(8,128)} %fusion.2.x_ref.xbc_ref, ...), custom_call_target="tpu_custom_call" | custom-call | flops 268435456 | bytes 12582912 | tf_op jit(solution)/shard_map/pallas_call | solution.py:29
  55.6 33.2 %all_to_all.40.in_ref = f32[16,136,128]{2,1,0:T(8,128)S(1)} all-to-all(f32[16,136,128]{2,1,0:T(8,128)S(1)} %get-tuple-element.61), channel_id=1, replica_groups=mesh['seq'=16,'rows'=2] {'seq'}, dimensions={0} | all-to-all | bytes 2228224 | tf_op jit(solution)/shard_map/all_to_all | solution.py:645
  89.8 3.9 all-to-all-start.1
  94.4 1.5 slice.318
  97.2 6.9 fusion.6.gate_ref
  104.1 15.8 %shard_map.204.yi_ref = f32[512,2048]{1,0:T(8,128)} custom-call(f32[512,256]{1,0:T(8,128)S(1)} %get-tuple-element.57.bc_ref, f32[512,2048]{1,0:T(8,128)} %get-tuple-element.58.v_ref, f32[4,512,128]{2,1,0:T(8,128)S(1)} %get-tuple-element.59.col_ref, f32[128,512]{1,0:T(8,128)S(1)} %copy-done.54, f32[512,128]{1,0:T(8,128)S(1)} %pad.39.aux_ref, ...), custom_call_target="tpu_custom_call" | custom-call | flops 2147483648 | bytes 8388608 | tf_op jit(solution)/shard_map/pallas_call | solution.py:29
  121.1 7.6 shard_map.206
  128.7 5.4 multiply_reduce_fusion.2
  134.7 3.3 collective-permute-start.1
  139.3 5.0 fusion.x_ref.xbc_ref
  144.2 15.4 %shard_map.207 = (f32[512,2048]{1,0:T(8,128)}, f32[512,256]{1,0:T(8,128)S(1)}, f32[4,512,128]{2,1,0:T(8,128)S(1)}, f32[128,512]{1,0:T(8,128)S(1)}, f32[128,2048]...) custom-call(f32[520,2304]{1,0:T(8,128)} %fusion.x_ref.xbc_ref, f32[520,2304]{1,0:T(8,128)} %fusion.x_ref.xbc_ref, ...), custom_call_target="tpu_custom_call" | custom-call | flops 268435456 | bytes 12582912 | tf_op jit(solution)/shard_map/pallas_call | solution.py:29
  161.4 33.6 %all_to_all.41.in_ref = f32[16,136,128]{2,1,0:T(8,128)S(1)} all-to-all(f32[16,136,128]{2,1,0:T(8,128)S(1)} %get-tuple-element.69), channel_id=1, replica_groups=mesh['seq'=16,'rows'=2] {'seq'}, dimensions={0} | all-to-all | bytes 2228224 | tf_op jit(solution)/shard_map/all_to_all | solution.py:645
  196.7 16.8 %all-to-all-start.3 = ((f32[16,128,128]{2,1,0:T(8,128)}), f32[16,128,128]{2,1,0:T(8,128)}, u32[]{:S(2)}, u32[]{:S(2)}) async-start(f32[16,128,128]{2,1,0:T(8,128)} %copy-done.13), calls=%async_computation.3 | async-start | bytes 2097152 | tf_op jit(solution)/shard_map/all_to_all | solution.py:645
  214.9 1.4 stack.193
  216.3 1.3 select_maximum_fusion.ch_ref
  217.6 7.2 fusion.8.dno_ref
  224.9 6.6 fusion.4.gate_ref
  231.4 15.7 %shard_map.208.yi_ref = f32[512,2048]{1,0:T(8,128)} custom-call(f32[512,256]{1,0:T(8,128)S(1)} %copy-done.3, f32[512,2048]{1,0:T(8,128)} %get-tuple-element.66.v_ref, f32[4,512,128]{2,1,0:T(8,128)S(1)} %get-tuple-element.67.col_ref, f32[128,512]{1,0:T(8,128)S(1)} %copy-done.57, f32[512,128]{1,0:T(8,128)S(1)} %pad.39.aux_ref, f32[8,512]{1,0:T(8,128)S(1)} %copy-done.60), custom_call_target="tpu_custom_call" | custom-call | flops 2147483648 | bytes 8388608 | tf_op jit(solution)/shard_map/pallas_call | solution.py:29
  251.1 7.9 shard_map.210
  260.3 17.0 %shard_map.211 = (f32[512,2048]{1,0:T(8,128)}, bf16[512,2048]{1,0:T(8,128)(2,1)S(1)}, f32[8,2048]{1,0:T(8,128)S(1)}, f32[128,2048]{1,0:T(8,128)S(1)}, f32[16,128,128]{2,1,0:T(8,128)S(1)}) custom-call(f32[512,2048]{1,0:T(8,128)} %fusion.8.dno_ref, f32[512,2048]{1,0:T(8,128)} %get-tuple-element.73.y_ref, f32[512,2048]{1,0:T(8,128)} %fusion.4.gate_ref, ...), custom_call_target="tpu_custom_call" | custom-call | flops 268435456 | bytes 23068672 | tf_op jit(solution)/shard_map/pallas_call | solution.py:29
  279.7 29.9 %all_to_all.42.in_ref = f32[16,128,128]{2,1,0:T(8,128)S(1)} all-to-all(f32[16,128,128]{2,1,0:T(8,128)S(1)} %get-tuple-element.77), channel_id=1, replica_groups=mesh['seq'=16,'rows'=2] {'seq'}, dimensions={0} | all-to-all | bytes 2097152 | tf_op jit(solution)/shard_map/all_to_all | solution.py:645
  310.6 5.0 all-to-all-start.5
  318.3 41.3 %shard_map.212 = (f32[512,2048]{1,0:T(8,128)}, f32[512,256]{1,0:T(8,128)S(1)}, f32[512,128]{1,0:T(8,128)S(1)}) custom-call(f32[512,256]{1,0:T(8,128)S(1)} %copy-done.5, f32[512,2048]{1,0:T(8,128)} %get-tuple-element.66.v_ref, f32[512,2048]{1,0:T(8,128)} %get-tuple-element.75.dy_ref, f32[4,512,128]{2,1,0:T(8,128)S(1)} %get-tuple-element.67.col_ref, ...), custom_call_target="tpu_custom_call" | custom-call | flops 4294967296 | bytes 12582912 | tf_op jit(solution)/shard_map/pallas_call | solution.py:29
  367.5 27.4 %shard_map.214 = (f32[512,2048]{1,0:T(8,128)}, f32[512,256]{1,0:T(8,128)S(1)}, bf16[512,128]{1,0:T(8,128)(2,1)S(1)}, f32[8,128]{1,0:T(8,128)S(1)}) custom-call(f32[512,2048]{1,0:T(8,128)} %get-tuple-element.76.xi_ref, f32[512,2048]{1,0:T(8,128)} %get-tuple-element.66.v_ref, f32[512,2048]{1,0:T(8,128)} %get-tuple-element.75.dy_ref, ...), custom_call_target="tpu_custom_call" | custom-call | flops 1073741824 | bytes 20971520 | tf_op jit(solution)/shard_map/pallas_call | solution.py:29
  395.9 2.0 collective-permute-start.2
  397.8 3.4 collective-permute-done.2.next_ref
  401.2 10.7 shard_map.215
  412.0 9.7 multiply_reduce_fusion
  422.3 7.4 fusion.12.dno_ref
  429.7 17.0 %shard_map.216 = (f32[512,2048]{1,0:T(8,128)}, bf16[512,2048]{1,0:T(8,128)(2,1)S(1)}, f32[8,2048]{1,0:T(8,128)S(1)}, f32[128,2048]{1,0:T(8,128)S(1)}, f32[16,128,128]{2,1,0:T(8,128)S(1)}) custom-call(f32[512,2048]{1,0:T(8,128)} %fusion.12.dno_ref, f32[512,2048]{1,0:T(8,128)} %get-tuple-element.85.y_ref, f32[512,2048]{1,0:T(8,128)} %fusion.6.gate_ref, ...), custom_call_target="tpu_custom_call" | custom-call | flops 268435456 | bytes 23068672 | tf_op jit(solution)/shard_map/pallas_call | solution.py:29
  449.0 29.9 %all_to_all.43.in_ref = f32[16,128,128]{2,1,0:T(8,128)S(1)} all-to-all(f32[16,128,128]{2,1,0:T(8,128)S(1)} %get-tuple-element.89), channel_id=1, replica_groups=mesh['seq'=16,'rows'=2] {'seq'}, dimensions={0} | all-to-all | bytes 2097152 | tf_op jit(solution)/shard_map/all_to_all | solution.py:645
  480.0 5.6 all-to-all-start.7
  489.3 1.5 copy.54
  490.8 2.0 reshape.136
  493.8 41.3 %shard_map.217 = (f32[512,2048]{1,0:T(8,128)}, f32[512,256]{1,0:T(8,128)S(1)}, f32[512,128]{1,0:T(8,128)S(1)}) custom-call(f32[512,256]{1,0:T(8,128)S(1)} %copy-done.1, f32[512,2048]{1,0:T(8,128)} %get-tuple-element.58.v_ref, f32[512,2048]{1,0:T(8,128)} %get-tuple-element.87.dy_ref, f32[4,512,128]{2,1,0:T(8,128)S(1)} %get-tuple-element.59.col_ref, ...), custom_call_target="tpu_custom_call" | custom-call | flops 4294967296 | bytes 12582912 | tf_op jit(solution)/shard_map/pallas_call | solution.py:29
  538.6 27.4 %shard_map.219 = (f32[512,2048]{1,0:T(8,128)}, f32[512,256]{1,0:T(8,128)S(1)}, bf16[512,128]{1,0:T(8,128)(2,1)S(1)}, f32[8,128]{1,0:T(8,128)S(1)}) custom-call(f32[512,2048]{1,0:T(8,128)} %get-tuple-element.88.xi_ref, f32[512,2048]{1,0:T(8,128)} %get-tuple-element.58.v_ref, f32[512,2048]{1,0:T(8,128)} %get-tuple-element.87.dy_ref, ...), custom_call_target="tpu_custom_call" | custom-call | flops 1073741824 | bytes 20971520 | tf_op jit(solution)/shard_map/pallas_call | solution.py:29
  566.8 1.5 collective-permute-start.3
  568.4 3.6 collective-permute-done.3.next_ref
  571.9 10.7 shard_map.220
  582.7 1.7 copy.53
  584.5 2.0 reshape.135
  586.5 11.3 fusion.28
  598.7 7.9 fusion.78
  606.6 1.5 copy-done.29
  608.1 7.3 fusion.46
  617.1 13.3 fusion.31
  630.5 1.6 copy-done.22
  632.1 13.4 fusion.29
  645.5 1.6 copy-done.27
  647.1 6.7 add_bitcast_fusion
  653.8 1.8 fusion.26
  655.6 71.1 %all-reduce.13.cloned.1.call-done = f32[29376]{0:T(1024)} async-done(((f32[29376]{0:T(1024)}), f32[29376]{0:T(1024)}) %all-reduce.13.cloned.1.call-update) | async-done | bytes 117520 | tf_op jit(solution)/shard_map/psum | solution.py:783
  737.9 134.2 %reduce-scatter.11.cloned.1.call-done = f32[64,1024]{1,0:T(8,128)} async-done(((f32[2048,1024]{1,0:T(8,128)}), f32[64,1024]{1,0:T(8,128)}) %reduce-scatter.11.cloned.1.call-update) | async-done | bytes 262160 | tf_op jit(solution)/shard_map/reduce_scatter | solution.py:674
  872.0 146.9 %reduce-scatter.9.cloned.1.call-done = f32[64,1024]{1,0:T(8,128)} async-done(((f32[2048,1024]{1,0:T(8,128)}), f32[64,1024]{1,0:T(8,128)}) %reduce-scatter.9.cloned.1.call-update) | async-done | bytes 262160 | tf_op jit(solution)/shard_map/reduce_scatter | solution.py:674
  1019.0 1.9 pad_maximum_fusion.7
  1020.8 201.3 %reduce-scatter.7.cloned.1.call-done = f32[32,4384]{1,0:T(8,128)} async-done(((f32[1024,4384]{1,0:T(8,128)}), f32[32,4384]{1,0:T(8,128)}) %reduce-scatter.7.cloned.1.call-update) | async-done | bytes 561168 | tf_op jit(solution)/shard_map/reduce_scatter | solution.py:674
  1222.1 203.0 %reduce-scatter.5.cloned.1.call-done = f32[32,4384]{1,0:T(8,128)} async-done(((f32[1024,4384]{1,0:T(8,128)}), f32[32,4384]{1,0:T(8,128)}) %reduce-scatter.5.cloned.1.call-update) | async-done | bytes 561168 | tf_op jit(solution)/shard_map/reduce_scatter | solution.py:674
  1425.2 2.3 pad_maximum_fusion.6
  (333 shorter events, 63.4 us)
Async XLA Ops:
  7.9 23.1 %collective-permute-start = (f32[8,1024]{1,0:T(8,128)S(1)}, f32[8,1024]{1,0:T(8,128)S(1)}, u32[]{:S(2)}, u32[]{:S(2)}) collective-permute-start(f32[8,1024]{1,0:T(8,128)S(1)} %slice_bitcast_fusion.6), channel_id=1, source_target_pairs={{0,2},{2,4},{4,6},{6,8},{8,10},{10,12},{12,14},{14,16},{16,18},{18... | collective-permute-start | bytes 98312 | tf_op jit(solution)/shard_map/ppermute | solution.py:651
  15.5 11.9 copy-start.90
  17.0 14.2 copy-start.86
  17.0 10.5 copy-start.93
  17.0 10.3 copy-start.85
  17.0 10.4 copy-start.92
  17.0 10.4 copy-start.104
  17.0 10.4 copy-start.105
  17.0 10.5 copy-start.71
  27.8 10.7 copy-start.76
  28.2 10.3 copy-start.15
  30.9 7.6 copy-start.65
  55.5 64.3 %copy-start = (f32[512,256]{1,0:T(8,128)}, f32[512,256]{1,0:T(8,128)S(1)}, u32[]{:S(2)}) copy-start(f32[512,256]{1,0:T(8,128)S(1)} %get-tuple-element.57.bc_ref) | copy-start | bytes 1572868
  55.5 64.3 %copy-start.36 = (f32[8,2048]{1,0:T(8,128)}, f32[8,2048]{1,0:T(8,128)S(1)}, u32[]{:S(2)}) copy-start(f32[8,2048]{1,0:T(8,128)S(1)} %get-tuple-element.63.kx_ref) | copy-start | bytes 196612
  88.8 7.8 copy-start.97
  88.8 15.3 %copy-start.41 = (f32[16,8,128]{2,1,0:T(8,128)}, f32[16,8,128]{2,1,0:T(8,128)S(1)}, u32[]{:S(2)}) copy-start(f32[16,8,128]{2,1,0:T(8,128)S(1)} %slice.315.keep_ref) | copy-start | bytes 196612
  89.8 30.0 %all-to-all-start.1 = ((f32[16,128,128]{2,1,0:T(8,128)}), f32[16,128,128]{2,1,0:T(8,128)S(1)}, u32[]{:S(2)}, u32[]{:S(2)}) async-start(f32[16,128,128]{2,1,0:T(8,128)} %copy-done.12), calls=%async_computation.1 | async-start | bytes 2097152 | tf_op jit(solution)/shard_map/all_to_all | solution.py:645
  97.2 22.7 %copy-start.30 = (f32[8,2048]{1,0:T(8,128)}, f32[8,2048]{1,0:T(8,128)S(1)}, u32[]{:S(2)}) copy-start(f32[8,2048]{1,0:T(8,128)S(1)} %select_maximum_fusion.1.ch_ref) | copy-start | bytes 196612
  97.2 6.9 copy-start.54
  104.1 15.8 %copy-start.59 = (f32[8,512]{1,0:T(8,128)}, f32[8,512]{1,0:T(8,128)S(1)}, u32[]{:S(2)}) copy-start(f32[8,512]{1,0:T(8,128)S(1)} %broadcast_in_dim.16.auxr_ref) | copy-start | bytes 49156
  121.1 7.6 copy-start.72
  128.7 10.5 slice-start
  128.7 9.3 copy-start.88
  128.7 10.5 slice-start.1
  128.7 10.5 slice-start.2
  134.2 10.1 copy-start.95
  134.7 4.3 collective-permute-start.1
  161.4 33.6 %copy-start.38 = (f32[8,2048]{1,0:T(8,128)}, f32[8,2048]{1,0:T(8,128)S(1)}, u32[]{:S(2)}) copy-start(f32[8,2048]{1,0:T(8,128)S(1)} %get-tuple-element.71.kx_ref) | copy-start | bytes 196612
  161.4 33.6 %copy-start.56 = (f32[128,512]{1,0:T(8,128)}, f32[128,512]{1,0:T(8,128)S(1)}, u32[]{:S(2)}) copy-start(f32[128,512]{1,0:T(8,128)S(1)} %get-tuple-element.68.cumr_ref) | copy-start | bytes 786436
  196.7 50.5 %all-to-all-start.3 = ((f32[16,128,128]{2,1,0:T(8,128)}), f32[16,128,128]{2,1,0:T(8,128)}, u32[]{:S(2)}, u32[]{:S(2)}) async-start(f32[16,128,128]{2,1,0:T(8,128)} %copy-done.13), calls=%async_computation.3 | async-start | bytes 2097152 | tf_op jit(solution)/shard_map/all_to_all | solution.py:645
  217.6 7.2 copy-start.78
  260.3 49.2 %copy-start.44 = (f32[16,8,128]{2,1,0:T(8,128)S(1)}, f32[16,8,128]{2,1,0:T(8,128)}, u32[]{:S(2)}) copy-start(f32[16,8,128]{2,1,0:T(8,128)} %copy-done.43) | copy-start | bytes 196612
  279.6 29.9 %copy-start.69 = (f32[8,2048]{1,0:T(8,128)}, f32[8,2048]{1,0:T(8,128)S(1)}, u32[]{:S(2)}) copy-start(f32[8,2048]{1,0:T(8,128)S(1)} %get-tuple-element.101) | copy-start | bytes 196612
  310.6 50.5 %all-to-all-start.5 = ((f32[16,128,128]{2,1,0:T(8,128)}), f32[16,128,128]{2,1,0:T(8,128)}, u32[]{:S(2)}, u32[]{:S(2)}) async-start(f32[16,128,128]{2,1,0:T(8,128)} %copy-done.14), calls=%async_computation.5 | async-start | bytes 2097152 | tf_op jit(solution)/shard_map/all_to_all | solution.py:645
  394.9 17.1 %copy-start.63 = (bf16[512,128]{1,0:T(8,128)(2,1)}, bf16[512,128]{1,0:T(8,128)(2,1)S(1)}, u32[]{:S(2)}) copy-start(bf16[512,128]{1,0:T(8,128)(2,1)S(1)} %get-tuple-element.84) | copy-start | bytes 393220
  395.8 16.1 %copy-start.24 = (bf16[512,2048]{1,0:T(8,128)(2,1)S(1)}, bf16[512,2048]{1,0:T(8,128)(2,1)}, u32[]{:S(2)}) copy-start(bf16[512,2048]{1,0:T(8,128)(2,1)} %copy-done.23) | copy-start | bytes 6291460
  395.8 16.1 %copy-start.81 = (f32[512,1024]{1,0:T(8,128)S(1)}, f32[512,1024]{1,0:T(8,128)}, u32[]{:S(2)}) copy-start(f32[512,1024]{1,0:T(8,128)} %copy-done.80) | copy-start | bytes 6291460
  395.8 16.1 %copy-start.89 = (f32[1,1024]{1,0:T(1,128)S(1)}, f32[1,1024]{1,0:T(1,128)}, u32[]{:S(2)}) copy-start(f32[1,1024]{1,0:T(1,128)} %get-tuple-element.133) | copy-start | bytes 12292
  395.9 16.1 %copy-start.96 = (f32[512]{0:T(512)S(1)}, f32[512]{0:T(512)}, u32[]{:S(2)}) copy-start(f32[512]{0:T(512)} %copy-done.95) | copy-start | bytes 6148
  395.9 5.4 collective-permute-start.2
  411.9 9.8 copy-start.19
  412.0 9.8 copy-start.99
  412.0 9.8 copy-start.82
  422.2 7.4 copy-start.74
  422.2 7.4 copy-start.1
  422.3 7.4 copy-start.31
  422.3 7.4 copy-start.37
  429.7 49.3 %copy-start.42 = (f32[16,8,128]{2,1,0:T(8,128)S(1)}, f32[16,8,128]{2,1,0:T(8,128)}, u32[]{:S(2)}) copy-start(f32[16,8,128]{2,1,0:T(8,128)} %copy-done.41) | copy-start | bytes 196612
  480.0 12.8 copy-start.62
  480.0 56.6 %all-to-all-start.7 = ((f32[16,128,128]{2,1,0:T(8,128)}), f32[16,128,128]{2,1,0:T(8,128)}, u32[]{:S(2)}, u32[]{:S(2)}) async-start(f32[16,128,128]{2,1,0:T(8,128)} %copy-done.11), calls=%async_computation.7 | async-start | bytes 2097152 | tf_op jit(solution)/shard_map/all_to_all | solution.py:645
  485.6 241.0 %all-reduce.13.cloned.1.call-start = ((), (), s32[]{:S(2)}) async-start(), calls=%async_computation.12 | async-start | bytes 237568 | tf_op jit(solution)/shard_map/psum | solution.py:783
  493.8 42.8 %copy-start.16 = (f32[512,128]{1,0:T(8,128)S(1)}, f32[512,128]{1,0:T(8,128)}, u32[]{:S(2)}) copy-start(f32[512,128]{1,0:T(8,128)} %copy-done.15) | copy-start | bytes 786436
  493.8 42.8 %copy-start.66 = (f32[8,128]{1,0:T(8,128)S(1)}, f32[8,128]{1,0:T(8,128)}, u32[]{:S(2)}) copy-start(f32[8,128]{1,0:T(8,128)} %copy-done.65) | copy-start | bytes 12292
  566.8 5.1 collective-permute-start.3
  582.7 15.2 %copy-start.21 = (bf16[512,2304]{1,0:T(8,128)(2,1)}, bf16[512,2304]{1,0:T(8,128)(2,1)S(1)}, u32[]{:S(2)}) copy-start(bf16[512,2304]{1,0:T(8,128)(2,1)S(1)} %get-tuple-element.95) | copy-start | bytes 7077892
  586.5 11.4 copy-start.100
  586.5 11.4 copy-start.101
  586.5 11.4 copy-start.102
  586.5 11.4 copy-start.103
  598.7 273.4 %reduce-scatter.11.cloned.1.call-start = ((), (), s32[]{:S(2)}) async-start(), calls=%async_computation.16 | async-start | bytes 8650752 | tf_op jit(solution)/shard_map/reduce_scatter | solution.py:674
  606.6 412.4 %reduce-scatter.9.cloned.1.call-start = ((), (), s32[]{:S(2)}) async-start(), calls=%async_computation.15 | async-start | bytes 8650752 | tf_op jit(solution)/shard_map/reduce_scatter | solution.py:674
  615.5 606.7 %reduce-scatter.7.cloned.1.call-start = ((), (), s32[]{:S(2)}) async-start(), calls=%async_computation.14 | async-start | bytes 18923520 | tf_op jit(solution)/shard_map/reduce_scatter | solution.py:674
  630.5 794.7 %reduce-scatter.5.cloned.1.call-start = ((), (), s32[]{:S(2)}) async-start(), calls=%async_computation.13 | async-start | bytes 18923520 | tf_op jit(solution)/shard_map/reduce_scatter | solution.py:674
  647.1 6.7 copy-start.83
  (59 other events, 130.9 us)
Sparse Core Ops, SparseCore 0:
  598.8 127.8 all-reduce.12
  728.9 143.0 reduce-scatter.10
  874.3 144.5 reduce-scatter.8
  1021.1 200.9 reduce-scatter.6
  1224.4 200.7 reduce-scatter.4

commit v3 on v2

--- a/solution.py
+++ b/solution.py
@@ -670,8 +670,51 @@
     return aux, auxr
 
 
-def scattered(total):
-    return lax.psum_scatter(total, AXES, scatter_dimension=0, tiled=True)
+def halving(count, rows):
+    def seq_masks(odd):
+        masks = [rows << bit for bit in range(count.bit_length() - 1)]
+        return masks[1::-1] + masks[2:] if odd else masks
+
+    return [1 << bit for bit in range(rows.bit_length() - 1)], seq_masks(False), seq_masks(True)
+
+
+def slab_order():
+    count, rows = lax.axis_size("seq"), lax.axis_size("rows")
+    row_masks, even, odd = halving(count, rows)
+    stages = len(row_masks) + len(even)
+    place = jnp.arange(count * rows, dtype=jnp.int32)
+    bit = lambda stage: (place >> (stages - 1 - stage)) & 1
+    slab = lax.axis_index("seq") * rows + lax.axis_index("rows") + 0 * place
+    for stage, mask in enumerate(row_masks):
+        slab = slab ^ (bit(stage) * mask)
+    swapped = slab & 1
+    for at, (one, two) in enumerate(zip(even, odd)):
+        slab = slab ^ (bit(len(row_masks) + at) * jnp.where(swapped == 1, two, one))
+    return slab
+
+
+def in_order(values, order):
+    width = values.shape[1]
+    size = width // order.shape[0]
+    source = (order[:, None] * size + jnp.arange(size, dtype=jnp.int32)[None, :]).reshape(-1)
+    pick = (jnp.arange(width, dtype=jnp.int32)[:, None] == source[None, :]).astype(jnp.bfloat16)
+    return jnp.dot(values, pick, preferred_element_type=jnp.float32).astype(jnp.bfloat16)
+
+
+def scattered(left, right):
+    count, rows = lax.axis_size("seq"), lax.axis_size("rows")
+    row_masks, even, odd = halving(count, rows)
+    half = left.shape[1] // 2
+    send = matmul_tn(left[:, half:], right)
+    keep = matmul_tn(left[:, :half], right)
+    pairs = [(mask, mask) for mask in row_masks] + list(zip(even, odd))
+    for stage, masks in enumerate(pairs):
+        got = lax.ppermute(send, AXES, [(at, at ^ masks[at & 1]) for at in range(count * rows)])
+        half = keep.shape[0] // 2
+        if stage == len(pairs) - 1:
+            return keep + got
+        send = keep[half:] + got[half:]
+        keep = keep[:half] + got[:half]
 
 
 def matmul(a, b):
@@ -720,6 +763,7 @@
     _, span, width = inputs.shape
     peers = lax.axis_size("seq")
     aux, auxr = token_marks(lengths[0], span)
+    order = slab_order()
     hidden = inputs[0]
     saved = []
     for depth in range(LAYERS):
@@ -754,7 +798,7 @@
         entry, normed, mixed_ext, rate, gate, values, bc, col, cumr, made, kx, keeps, state_in, y, out_low = saved[depth][:15]
         conv, hp, ch, gate_weight, mixed_weight, rate_weight = saved[depth][15:]
         grad_low = gradient.astype(jnp.bfloat16)
-        big_out[depth] = scattered(matmul_tn(out_low, grad_low))
+        big_out[depth] = scattered(in_order(out_low, order), grad_low)
         dno = matmul_nt(grad_low, out_weight[depth])
         dy, dgate, gate_sums, d1, pay = gate_back(peers, dno, y, gate, values, bc, col, kx, ch)
         received = exchange(pay)
@@ -766,7 +810,7 @@
         following = shifted(jnp.concatenate([dconv[:HALO], dconv_bc[:HALO]], 1), -1)
         dmixed, conv_sums = conv_back(dconv, dconv_bc, following, mixed_ext, aux, conv)
         dprojected = jnp.concatenate([dgate, dmixed, drate[:, :HEADS]], 1)
-        big_in[depth] = scattered(matmul_tn(normed, dprojected))
+        big_in[depth] = scattered(in_order(normed, order), dprojected)
         grad_normed = matmul_nt(dprojected, in_weight[depth])
         grad_hidden, gain_grad = normalise_back(entry, norm_gain[depth], grad_normed)
         gradient = gradient + grad_hidden
@@ -779,21 +823,25 @@
             head_rows[0, :HEADS],
             jnp.sum(gate_sums[1].reshape(HEADS, HEAD_DIM), 1),
         )
-    flat = jnp.concatenate([part.reshape(-1) for sums in collected for part in sums])
-    flat = lax.psum(flat, AXES)
-    index = lax.axis_index("seq") * lax.axis_size("rows") + lax.axis_index("rows")
+    devices = lax.axis_size(AXES)
+    shares = [part.reshape(devices, -1) for sums in collected for part in sums[:4]]
+    heads = jnp.concatenate([part for sums in collected for part in sums[4:]])
+    table = jnp.concatenate(shares + [jnp.broadcast_to(heads, (devices,) + heads.shape)], 1)
+    table = jnp.pad(table, ((0, 0), (0, -table.shape[1] % 128)))
+    table = jnp.sum(lax.all_to_all(table, AXES, split_axis=0, concat_axis=0, tiled=True), 0)
     small = []
     at = 0
     for sums in collected:
         row = []
-        for member, part in enumerate(sums):
-            total = flat[at : at + part.size].reshape(part.shape)
-            at += part.size
-            if member < 4:
-                size = part.shape[0] // lax.axis_size(AXES)
-                total = lax.dynamic_slice_in_dim(total, index * size, size)
-            row.append(total)
+        for part in sums[:4]:
+            size = part.size // devices
+            row.append(table[at : at + size].reshape((part.shape[0] // devices,) + part.shape[1:]))
+            at += size
         small.append(row)
+    for row in small:
+        for _ in range(3):
+            row.append(table[at : at + HEADS])
+            at += HEADS
     stacked = [jnp.stack([small[level][member] for level in range(LAYERS)]) for member in range(7)]
     norm_gain_grad, conv_w_grad, conv_b_grad, gain_grad, decay_grad, bias_grad, skip_grad = stacked
     return (

time: 1440 us -> 970 us (0.67)
  waiting for transfers between devices: 764 us -> 193 us
  other arithmetic: 18.2 us -> 108 us
  blocking collectives: 127 us -> 66.9 us
  starting transfers between devices: 42.4 us -> 80.6 us
  matrix products: 116 us -> 136 us
  local copies, waits for them, and re-layouts: 81.2 us -> 98 us
    reduce_scatter x4 -> x0, waiting for transfers between devices: 685 us -> none  [scattered(): return lax.psum_scatter(total, AXES, scatter_dimension=0, tiled=True)]
    ppermute x0 -> x20, waiting for transfers between devices: none -> 89.2 us  [scattered(): lax.ppermute(send, AXES, [(at, at ^ masks[at & 1]) for at in range(count...]
    all_to_all x0 -> x1, waiting for transfers between devices: none -> 78.7 us  [local(): lax.all_to_all(table, AXES, split_axis=0, concat_axis=0, tiled=True)]
    add x0 -> x18, other arithmetic: none -> 78 us  [the longest x12 66.7 us: scattered(): keep = keep[:half] + got[:half]]
    psum x1 -> x0, waiting for transfers between devices: 71.1 us -> none  [local(): flat = lax.psum(flat, AXES)]
    all_to_all x4 -> x2, blocking collectives: 127 us -> 66.9 us  [exchange(): return lax.all_to_all(parts, 'seq', split_axis=0, concat_axis=0, tiled=True)]
    ppermute x0 -> x20, starting transfers between devices: none -> 27.4 us  [scattered(): lax.ppermute(send, AXES, [(at, at ^ masks[at & 1]) for at in range(count...]
    all_to_all x4 -> x6, waiting for transfers between devices: 0.01 us -> 21.1 us  [exchange(): return lax.all_to_all(parts, 'seq', split_axis=0, concat_axis=0, tiled=True)]
  transfers between devices with their start and end apart: 13 -> 31, of which waited for: 8 -> 11; matrix products, arithmetic and copies ran while one was open for 8% -> 27% of each run, Pallas kernels for 8% -> 19%
where the time goes in v3:
time: 970 us; the launch traced here: 959 us
  Pallas kernels  274 us (28%)
  waiting for transfers between devices  193 us (20%)
  matrix products  136 us (14%)
  other arithmetic  108 us (11%)
  local copies, waits for them, and re-layouts  98 us (10%)
  starting transfers between devices  80.6 us (8%)
  blocking collectives  66.9 us (7%)
    pallas_call x18, Pallas kernels, pcall(): pl.pallas_call(body, grid=grid, in_specs=in_specs, out_specs=out_specs, o...  274 us
    ppermute x20, waiting for transfers between devices, scattered(): lax.ppermute(send, AXES, [(at, at ^ masks[at & 1]) for at in range(count...  89.2 us
    all_to_all x1, waiting for transfers between devices, local(): lax.all_to_all(table, AXES, split_axis=0, concat_axis=0, tiled=True)  78.7 us
    all_to_all x2, blocking collectives, exchange(): return lax.all_to_all(parts, 'seq', split_axis=0, concat_axis=0, tiled=True)  66.9 us
    add x12, other arithmetic, scattered(): keep = keep[:half] + got[:half]  66.7 us
    unnamed x275, local copies, waits for them, and re-layouts  44.8 us
    dot_general x8, matrix products, matmul_tn(): return jnp.einsum('tn,tm->nm', a, b, preferred_element_type=jnp.float32)  43 us
    dot_general x8, matrix products, matmul(): return jnp.dot(a, b, preferred_element_type=jnp.float32)  40.1 us
  transfers between devices with their start and end apart: 31, of which 11 were waited for; matrix products, arithmetic and copies ran while one was open for 27% of the time, Pallas kernels for 19%

profile of v3, /device:TPU:1, one launch (start us, length us, event | category | flops | bytes accessed | tf_op | source)
XLA Modules:
  0.0 959.1 jit_solution(975962520685480544)
XLA Ops:
  1.4 3.9 collective-permute-start
  10.0 10.2 %slice_bitcast_fusion = (bf16[1024,4384]{0,1:T(8,128)(2,1)}, bf16[1024,4384]{0,1:T(8,128)(2,1)S(1)}) fusion(bf16[2,1024,4384]{1,2,0:T(8,128)(2,1)} %param.15), kind=kLoop, calls=%fused_computation.3 | loop fusion | bytes 35913728 | tf_op jit(solution)/shard_map/squeeze | solution.py:774
  24.1 7.2 fusion.6.x_ref.xbc_ref
  31.3 15.3 %shard_map.203 = (f32[512,2048]{1,0:T(8,128)}, f32[512,256]{1,0:T(8,128)S(1)}, f32[4,512,128]{2,1,0:T(8,128)S(1)}, f32[128,512]{1,0:T(8,128)S(1)}, f32[128,2048]...) custom-call(f32[520,2304]{1,0:T(8,128)} %fusion.6.x_ref.xbc_ref, f32[520,2304]{1,0:T(8,128)} %fusion.6.x_ref.xbc_ref, ...), custom_call_target="tpu_custom_call" | custom-call | flops 268435456 | bytes 12582912 | tf_op jit(solution)/shard_map/pallas_call | solution.py:29
  48.4 33.2 %all_to_all.49.in_ref = f32[16,136,128]{2,1,0:T(8,128)S(1)} all-to-all(f32[16,136,128]{2,1,0:T(8,128)S(1)} %get-tuple-element.61), channel_id=1, replica_groups=mesh['seq'=16,'rows'=2] {'seq'}, dimensions={0} | all-to-all | bytes 2228224 | tf_op jit(solution)/shard_map/all_to_all | solution.py:645
  82.7 4.1 all-to-all-start.1
  89.7 6.9 fusion.10.gate_ref
  96.6 15.7 %shard_map.204.yi_ref = f32[512,2048]{1,0:T(8,128)} custom-call(f32[512,256]{1,0:T(8,128)S(1)} %get-tuple-element.57.bc_ref, f32[512,2048]{1,0:T(8,128)} %get-tuple-element.58.v_ref, f32[4,512,128]{2,1,0:T(8,128)S(1)} %get-tuple-element.59.col_ref, f32[128,512]{1,0:T(8,128)S(1)} %copy-done.47, f32[512,128]{1,0:T(8,128)S(1)} %pad.43.aux_ref, ...), custom_call_target="tpu_custom_call" | custom-call | flops 2147483648 | bytes 8388608 | tf_op jit(solution)/shard_map/pallas_call | solution.py:29
  113.6 7.7 shard_map.206
  121.3 5.4 multiply_reduce_fusion.2
  131.8 7.2 fusion.4.x_ref.xbc_ref
  138.9 15.3 %shard_map.207 = (f32[512,2048]{1,0:T(8,128)}, f32[512,256]{1,0:T(8,128)S(1)}, f32[4,512,128]{2,1,0:T(8,128)S(1)}, f32[128,512]{1,0:T(8,128)S(1)}, f32[128,2048]...) custom-call(f32[520,2304]{1,0:T(8,128)} %fusion.4.x_ref.xbc_ref, f32[520,2304]{1,0:T(8,128)} %fusion.4.x_ref.xbc_ref, ...), custom_call_target="tpu_custom_call" | custom-call | flops 268435456 | bytes 12582912 | tf_op jit(solution)/shard_map/pallas_call | solution.py:29
  156.0 33.6 %all_to_all.50.in_ref = f32[16,136,128]{2,1,0:T(8,128)S(1)} all-to-all(f32[16,136,128]{2,1,0:T(8,128)S(1)} %get-tuple-element.69), channel_id=1, replica_groups=mesh['seq'=16,'rows'=2] {'seq'}, dimensions={0} | all-to-all | bytes 2228224 | tf_op jit(solution)/shard_map/all_to_all | solution.py:645
  191.4 4.5 all-to-all-start.3
  199.3 7.2 fusion.12.dno_ref
  206.6 6.7 fusion.8.gate_ref
  213.2 15.7 %shard_map.208.yi_ref = f32[512,2048]{1,0:T(8,128)} custom-call(f32[512,256]{1,0:T(8,128)S(1)} %copy-done.3, f32[512,2048]{1,0:T(8,128)} %get-tuple-element.66.v_ref, f32[4,512,128]{2,1,0:T(8,128)S(1)} %get-tuple-element.67.col_ref, f32[128,512]{1,0:T(8,128)S(1)} %copy-done.50, f32[512,128]{1,0:T(8,128)S(1)} %pad.43.aux_ref, f32[8,512]{1,0:T(8,128)S(1)} %copy-done.53), custom_call_target="tpu_custom_call" | custom-call | flops 2147483648 | bytes 8388608 | tf_op jit(solution)/shard_map/pallas_call | solution.py:29
  232.9 7.8 shard_map.210
  242.0 16.9 %shard_map.211 = (f32[512,2048]{1,0:T(8,128)}, bf16[512,2048]{1,0:T(8,128)(2,1)S(1)}, f32[8,2048]{1,0:T(8,128)S(1)}, f32[128,2048]{1,0:T(8,128)S(1)}, f32[16,128,128]{2,1,0:T(8,128)S(1)}) custom-call(f32[512,2048]{1,0:T(8,128)} %fusion.12.dno_ref, f32[512,2048]{1,0:T(8,128)} %get-tuple-element.73.y_ref, f32[512,2048]{1,0:T(8,128)} %fusion.8.gate_ref, ...), custom_call_target="tpu_custom_call" | custom-call | flops 268435456 | bytes 23068672 | tf_op jit(solution)/shard_map/pallas_call | solution.py:29
  262.8 6.3 all-to-all-start.4
  269.8 20.9 %all-to-all-done.4.in_ref = f32[16,128,128]{2,1,0:T(8,128)} async-done(((f32[16,128,128]{2,1,0:T(8,128)}), f32[16,128,128]{2,1,0:T(8,128)}, u32[]{:S(2)}, u32[]{:S(2)}) %all-to-all-start.4) | async-done | bytes 1048608 | tf_op jit(solution)/shard_map/all_to_all | solution.py:645
  293.9 7.6 all-to-all-start.5
  310.3 41.4 %shard_map.212 = (f32[512,2048]{1,0:T(8,128)}, f32[512,256]{1,0:T(8,128)S(1)}, f32[512,128]{1,0:T(8,128)S(1)}) custom-call(f32[512,256]{1,0:T(8,128)S(1)} %copy-done.5, f32[512,2048]{1,0:T(8,128)} %get-tuple-element.66.v_ref, f32[512,2048]{1,0:T(8,128)} %get-tuple-element.75.dy_ref, f32[4,512,128]{2,1,0:T(8,128)S(1)} %get-tuple-element.67.col_ref, ...), custom_call_target="tpu_custom_call" | custom-call | flops 4294967296 | bytes 12582912 | tf_op jit(solution)/shard_map/pallas_call | solution.py:29
  353.2 5.8 fusion.27
  364.7 27.7 %shard_map.214 = (f32[512,2048]{1,0:T(8,128)}, f32[512,256]{1,0:T(8,128)S(1)}, bf16[512,128]{1,0:T(8,128)(2,1)S(1)}, f32[8,128]{1,0:T(8,128)S(1)}) custom-call(f32[512,2048]{1,0:T(8,128)} %get-tuple-element.76.xi_ref, f32[512,2048]{1,0:T(8,128)} %get-tuple-element.66.v_ref, f32[512,2048]{1,0:T(8,128)} %get-tuple-element.75.dy_ref, ...), custom_call_target="tpu_custom_call" | custom-call | flops 1073741824 | bytes 20971520 | tf_op jit(solution)/shard_map/pallas_call | solution.py:29
  400.5 11.1 %shard_map.215 = (bf16[512,2304]{1,0:T(8,128)(2,1)S(1)}, f32[8,2304]{1,0:T(8,128)S(1)}) custom-call(f32[512,2048]{1,0:T(8,128)} %get-tuple-element.81.dconv_ref, f32[512,256]{1,0:T(8,128)S(1)} %get-tuple-element.82.dconv_bc_ref, f32[8,2304]{1,0:T(8,128)S(1)} %collective-permute-done.2.next_ref, f32[520,2304]{1,0:T(8,128)} %fusion.4.x_ref.xbc_ref, ...), custom_call_target="tpu_custom_call" | custom-call | flops 8388608 | bytes 10485760 | tf_op jit(solution)/shard_map/pallas_call | solution.py:29
  411.7 9.7 %multiply_reduce_fusion = (f32[1024]{0:T(1024)S(1)}, f32[512]{0:T(512)S(1)}, f32[512,1024]{1,0:T(8,128)S(1)}) fusion(f32[512,1024]{1,0:T(8,128)S(1)} %copy-done.92, f32[512]{0:T(512)S(1)} %copy-done.118, f32[1024]{0:T(1024)S(1)} %bitcast.200, bf16[2,1024,4384]{1,2,0:T(8,128)(2,1)} %param.15, bf16[512,32]{1,0:T(8,128)(2,1)S(1)} %bitcast.188, ...), kind=kOutput, calls=%fused_computation.77 | convolution fusion | flops 4613569024 | bytes 17674240 | tf_op jit(solution)/shard_map/tn,mn->tm/dot_general | solution.py:729
  421.9 7.3 fusion.16.dno_ref
  429.2 17.1 %shard_map.216 = (f32[512,2048]{1,0:T(8,128)}, bf16[512,2048]{1,0:T(8,128)(2,1)S(1)}, f32[8,2048]{1,0:T(8,128)S(1)}, f32[128,2048]{1,0:T(8,128)S(1)}, f32[16,128,128]{2,1,0:T(8,128)S(1)}) custom-call(f32[512,2048]{1,0:T(8,128)} %fusion.16.dno_ref, f32[512,2048]{1,0:T(8,128)} %get-tuple-element.85.y_ref, f32[512,2048]{1,0:T(8,128)} %fusion.10.gate_ref, ...), custom_call_target="tpu_custom_call" | custom-call | flops 268435456 | bytes 23068672 | tf_op jit(solution)/shard_map/pallas_call | solution.py:29
  449.6 8.1 all-to-all-start.6
  457.7 8.6 fusion.65
  467.9 5.8 fusion.26
  473.8 5.9 add_bitcast_fusion
  482.2 6.9 all-to-all-start.7
  501.1 41.3 %shard_map.217 = (f32[512,2048]{1,0:T(8,128)}, f32[512,256]{1,0:T(8,128)S(1)}, f32[512,128]{1,0:T(8,128)S(1)}) custom-call(f32[512,256]{1,0:T(8,128)S(1)} %copy-done.1, f32[512,2048]{1,0:T(8,128)} %get-tuple-element.58.v_ref, f32[512,2048]{1,0:T(8,128)} %get-tuple-element.87.dy_ref, f32[4,512,128]{2,1,0:T(8,128)S(1)} %get-tuple-element.59.col_ref, ...), custom_call_target="tpu_custom_call" | custom-call | flops 4294967296 | bytes 12582912 | tf_op jit(solution)/shard_map/pallas_call | solution.py:29
  542.4 6.0 slice_add_fusion.17
  552.1 27.4 %shard_map.219 = (f32[512,2048]{1,0:T(8,128)}, f32[512,256]{1,0:T(8,128)S(1)}, bf16[512,128]{1,0:T(8,128)(2,1)S(1)}, f32[8,128]{1,0:T(8,128)S(1)}) custom-call(f32[512,2048]{1,0:T(8,128)} %get-tuple-element.88.xi_ref, f32[512,2048]{1,0:T(8,128)} %get-tuple-element.58.v_ref, f32[512,2048]{1,0:T(8,128)} %get-tuple-element.87.dy_ref, ...), custom_call_target="tpu_custom_call" | custom-call | flops 1073741824 | bytes 20971520 | tf_op jit(solution)/shard_map/pallas_call | solution.py:29
  582.8 3.8 collective-permute-done.3.next_ref
  587.7 11.1 %shard_map.220 = (bf16[512,2304]{1,0:T(8,128)(2,1)S(1)}, f32[8,2304]{1,0:T(8,128)S(1)}) custom-call(f32[512,2048]{1,0:T(8,128)} %get-tuple-element.93.dconv_ref, f32[512,256]{1,0:T(8,128)S(1)} %copy-done.37, f32[8,2304]{1,0:T(8,128)S(1)} %collective-permute-done.3.next_ref, f32[520,2304]{1,0:T(8,128)} %fusion.6.x_ref.xbc_ref, f32[512,128]{1,0:T(8,128)S(1)} %pad.43.aux_ref, ...), custom_call_target="tpu_custom_call" | custom-call | flops 8388608 | bytes 10485760 | tf_op jit(solution)/shard_map/pallas_call | solution.py:29
  598.8 5.8 fusion.69
  610.4 6.1 fusion.67
  616.6 6.8 collective-permute-done.21
  626.2 4.6 fusion.61
  630.8 6.8 collective-permute-done.22
  641.4 11.0 %slice_add_fusion.1 = (f32[256,4384]{0,1:T(8,128)}, f32[256,4384]{0,1:T(8,128)}) fusion(f32[512,4384]{0,1:T(8,128)} %collective-permute-done.9, f32[512,4384]{0,1:T(8,128)} %fusion.67), kind=kLoop, calls=%fused_computation.14 | loop fusion | flops 2244608 | bytes 26935296 | tf_op jit(solution)/shard_map/add | solution.py:717
  653.8 11.3 %fusion.40 = (f32[1024]{0:T(1024)S(1)}, f32[512]{0:T(512)S(1)}, f32[512,1024]{1,0:T(8,128)}) fusion(f32[1,512,1024]{2,1,0:T(8,128)} %param.12, f32[512]{0:T(512)S(1)} %copy-done.116, f32[1024]{0:T(1024)S(1)} %bitcast.196, bf16[2,1024,4384]{1,2,0:T(8,128)(2,1)} %param.15, bf16[512,32]{1,0:T(8,128)(2,1)S(1)} %bitcast.192, ...), kind=kOutput, calls=%fused_computation.74 | convolution fusion | flops 4613569024 | bytes 17674240 | tf_op jit(solution)/shard_map/tn,mn->tm/dot_general | solution.py:729
  668.6 7.9 fusion.71
  676.5 5.2 slice_add_fusion.19
  681.7 10.9 %slice_add_fusion.3 = (f32[256,4384]{0,1:T(8,128)}, f32[256,4384]{0,1:T(8,128)}) fusion(f32[512,4384]{0,1:T(8,128)} %collective-permute-done.4, f32[512,4384]{0,1:T(8,128)} %fusion.71), kind=kLoop, calls=%fused_computation.16 | loop fusion | flops 2244608 | bytes 26935296 | tf_op jit(solution)/shard_map/add | solution.py:717
  694.1 9.4 collective-permute-done.10
  703.5 6.4 slice_add_fusion.9
  711.8 5.9 all-to-all-start.8
  717.8 4.0 fusion.38
  723.6 78.7 %all-to-all-done.8 = f32[32,1,1152]{2,1,0:T(1,128)S(1)} async-done(((f32[32,1,1152]{2,1,0:T(1,128)}), f32[32,1,1152]{2,1,0:T(1,128)S(1)}, u32[]{:S(2)}, u32[]{:S(2)}) %all-to-all-start.8) | async-done | bytes 147488 | tf_op jit(solution)/shard_map/all_to_all | solution.py:831
  804.2 3.9 slice_add_fusion.23
  810.0 5.0 slice_add_fusion.7
  817.9 6.2 slice_add_fusion.15
  828.7 27.6 %collective-permute-done.17 = f32[128,1024]{1,0:T(8,128)S(1)} collective-permute-done((f32[128,1024]{1,0:T(8,128)S(1)}, f32[128,1024]{1,0:T(8,128)S(1)}, u32[]{:S(2)}, u32[]{:S(2)}) %collective-permute-start.17) | collective-permute-done | bytes 524320 | tf_op jit(solution)/shard_map/ppermute | solution.py:712
  859.5 7.0 slice_add_fusion.13
  884.4 22.6 %collective-permute-done.13 = f32[32,4384]{1,0:T(8,128)} collective-permute-done((f32[32,4384]{1,0:T(8,128)}, f32[32,4384]{1,0:T(8,128)}, u32[]{:S(2)}, u32[]{:S(2)}) %collective-permute-start.13) | collective-permute-done | bytes 561184 | tf_op jit(solution)/shard_map/ppermute | solution.py:712
  913.5 4.4 slice_add_fusion.10
  924.1 4.0 fusion.29
  932.5 16.0 %collective-permute-done.8 = f32[32,4384]{1,0:T(8,128)} collective-permute-done((f32[32,4384]{1,0:T(8,128)}, f32[32,4384]{1,0:T(8,128)}, u32[]{:S(2)}, u32[]{:S(2)}) %collective-permute-start.8) | collective-permute-done | bytes 561184 | tf_op jit(solution)/shard_map/ppermute | solution.py:712
  951.5 4.0 fusion.31
  (458 shorter events, 170.9 us)
Async XLA Ops:
  1.4 22.4 %collective-permute-start = (f32[8,1024]{1,0:T(8,128)S(1)}, f32[8,1024]{1,0:T(8,128)S(1)}, u32[]{:S(2)}, u32[]{:S(2)}) collective-permute-start(f32[8,1024]{1,0:T(8,128)S(1)} %slice_bitcast_fusion.6), channel_id=1, source_target_pairs={{0,2},{2,4},{4,6},{6,8},{8,10},{10,12},{12,14},{14,16},{16,18},{18... | collective-permute-start | bytes 98312 | tf_op jit(solution)/shard_map/ppermute | solution.py:651
  8.9 11.2 %copy-start.112 = (f32[512]{0:T(512)}, f32[512]{0:T(512)S(1)}, u32[]{:S(2)}) copy-start(f32[512]{0:T(512)S(1)} %fusion.32) | copy-start | bytes 6148
  9.9 14.1 %copy-start.107 = (f32[1,1024]{1,0:T(1,128)}, f32[1,1024]{1,0:T(1,128)S(1)}, u32[]{:S(2)}) copy-start(f32[1,1024]{1,0:T(1,128)S(1)} %get-tuple-element.184) | copy-start | bytes 12292
  9.9 121.8 %copy-start.109 = (f32[1,1024]{1,0:T(1,128)}, f32[1,1024]{1,0:T(1,128)S(1)}, u32[]{:S(2)}) copy-start(f32[1,1024]{1,0:T(1,128)S(1)} %get-tuple-element.183) | copy-start | bytes 12292
  9.9 11.1 %copy-start.115 = (f32[512]{0:T(512)}, f32[512]{0:T(512)S(1)}, u32[]{:S(2)}) copy-start(f32[512]{0:T(512)S(1)} %add_rsqrt_fusion.1) | copy-start | bytes 6148
  48.4 64.0 %copy-start = (f32[512,256]{1,0:T(8,128)}, f32[512,256]{1,0:T(8,128)S(1)}, u32[]{:S(2)}) copy-start(f32[512,256]{1,0:T(8,128)S(1)} %get-tuple-element.57.bc_ref) | copy-start | bytes 1572868
  48.4 64.0 %copy-start.27 = (f32[8,2048]{1,0:T(8,128)}, f32[8,2048]{1,0:T(8,128)S(1)}, u32[]{:S(2)}) copy-start(f32[8,2048]{1,0:T(8,128)S(1)} %get-tuple-element.63.kx_ref) | copy-start | bytes 196612
  82.7 29.7 %all-to-all-start.1 = ((f32[16,128,128]{2,1,0:T(8,128)}), f32[16,128,128]{2,1,0:T(8,128)S(1)}, u32[]{:S(2)}, u32[]{:S(2)}) async-start(f32[16,128,128]{2,1,0:T(8,128)} %copy-done.12), calls=%async_computation.1 | async-start | bytes 2097152 | tf_op jit(solution)/shard_map/all_to_all | solution.py:645
  96.6 15.7 %copy-start.52 = (f32[8,512]{1,0:T(8,128)}, f32[8,512]{1,0:T(8,128)S(1)}, u32[]{:S(2)}) copy-start(f32[8,512]{1,0:T(8,128)S(1)} %broadcast_in_dim.34.auxr_ref) | copy-start | bytes 49156
  127.3 4.3 collective-permute-start.1
  156.0 33.6 %copy-start.29 = (f32[8,2048]{1,0:T(8,128)}, f32[8,2048]{1,0:T(8,128)S(1)}, u32[]{:S(2)}) copy-start(f32[8,2048]{1,0:T(8,128)S(1)} %get-tuple-element.71.kx_ref) | copy-start | bytes 196612
  156.0 33.7 %copy-start.49 = (f32[128,512]{1,0:T(8,128)}, f32[128,512]{1,0:T(8,128)S(1)}, u32[]{:S(2)}) copy-start(f32[128,512]{1,0:T(8,128)S(1)} %get-tuple-element.68.cumr_ref) | copy-start | bytes 786436
  191.4 37.6 %all-to-all-start.3 = ((f32[16,128,128]{2,1,0:T(8,128)}), f32[16,128,128]{2,1,0:T(8,128)}, u32[]{:S(2)}, u32[]{:S(2)}) async-start(f32[16,128,128]{2,1,0:T(8,128)} %copy-done.14), calls=%async_computation.3 | async-start | bytes 2097152 | tf_op jit(solution)/shard_map/all_to_all | solution.py:645
  262.8 27.9 %all-to-all-start.4 = ((f32[16,128,128]{2,1,0:T(8,128)}), f32[16,128,128]{2,1,0:T(8,128)}, u32[]{:S(2)}, u32[]{:S(2)}) async-start(f32[16,128,128]{2,1,0:T(8,128)} %copy-done.25), calls=%async_computation.4 | async-start | bytes 2097152 | tf_op jit(solution)/shard_map/all_to_all | solution.py:645
  293.9 65.2 %all-to-all-start.5 = ((f32[16,128,128]{2,1,0:T(8,128)}), f32[16,128,128]{2,1,0:T(8,128)}, u32[]{:S(2)}, u32[]{:S(2)}) async-start(f32[16,128,128]{2,1,0:T(8,128)} %copy-done.13), calls=%async_computation.5 | async-start | bytes 2097152 | tf_op jit(solution)/shard_map/all_to_all | solution.py:645
  310.3 42.9 %copy-start.73 = (bf16[512,2048]{1,0:T(8,128)(2,1)S(1)}, bf16[512,2048]{1,0:T(8,128)(2,1)}, u32[]{:S(2)}) copy-start(bf16[512,2048]{1,0:T(8,128)(2,1)} %copy-done.72) | copy-start | bytes 6291460
  310.3 42.9 %copy-start.120 = (s32[2048]{0:T(1024)S(1)}, s32[2048]{0:T(1024)}, u32[]{:S(2)}) copy-start(s32[2048]{0:T(1024)} %add.293) | copy-start | bytes 24580
  364.7 29.9 %copy-start.89 = (f32[1,512,1024]{2,1,0:T(8,128)S(1)}, f32[1,512,1024]{2,1,0:T(8,128)}, u32[]{:S(2)}) copy-start(f32[1,512,1024]{2,1,0:T(8,128)} %param.23) | copy-start | bytes 6291460
  364.7 29.9 %copy-start.95 = (bf16[512,2048]{1,0:T(8,128)(2,1)S(1)}, bf16[512,2048]{1,0:T(8,128)(2,1)}, u32[]{:S(2)}) copy-start(bf16[512,2048]{1,0:T(8,128)(2,1)} %fusion.27) | copy-start | bytes 6291460
  392.4 19.2 %copy-start.75 = (bf16[512,128]{1,0:T(8,128)(2,1)}, bf16[512,128]{1,0:T(8,128)(2,1)S(1)}, u32[]{:S(2)}) copy-start(bf16[512,128]{1,0:T(8,128)(2,1)S(1)} %get-tuple-element.84) | copy-start | bytes 393220
  393.3 7.2 collective-permute-start.2
  397.9 13.7 %copy-start.66 = (bf16[512,2048]{1,0:T(8,128)(2,1)S(1)}, bf16[512,2048]{1,0:T(8,128)(2,1)}, u32[]{:S(2)}) copy-start(bf16[512,2048]{1,0:T(8,128)(2,1)} %copy-done.65) | copy-start | bytes 6291460
  397.9 13.7 %copy-start.92 = (f32[512,1024]{1,0:T(8,128)S(1)}, f32[512,1024]{1,0:T(8,128)}, u32[]{:S(2)}) copy-start(f32[512,1024]{1,0:T(8,128)} %copy-done.91) | copy-start | bytes 6291460
  397.9 13.7 %copy-start.110 = (f32[1,1024]{1,0:T(1,128)S(1)}, f32[1,1024]{1,0:T(1,128)}, u32[]{:S(2)}) copy-start(f32[1,1024]{1,0:T(1,128)} %copy-done.109) | copy-start | bytes 12292
  397.9 13.7 %copy-start.118 = (f32[512]{0:T(512)S(1)}, f32[512]{0:T(512)}, u32[]{:S(2)}) copy-start(f32[512]{0:T(512)} %copy-done.117) | copy-start | bytes 6148
  398.0 144.4 %collective-permute-start.19 = (f32[1024,1024]{1,0:T(8,128)}, f32[1024,1024]{1,0:T(8,128)}, u32[]{:S(2)}, u32[]{:S(2)}) collective-permute-start(f32[1024,1024]{1,0:T(8,128)} %fusion.55), channel_id=1, source_target_pairs={{0,1},{1,0},{2,3},{3,2},{4,5},{5,4},{6,7},{7,6},{8,9},{9,8},{10,11... | collective-permute-start | bytes 12582920 | tf_op jit(solution)/shard_map/ppermute | solution.py:712
  429.2 28.5 %copy-start.76 = (bf16[512,128]{1,0:T(8,128)(2,1)S(1)}, bf16[512,128]{1,0:T(8,128)(2,1)}, u32[]{:S(2)}) copy-start(bf16[512,128]{1,0:T(8,128)(2,1)} %copy-done.75) | copy-start | bytes 393220
  449.6 30.4 %all-to-all-start.6 = ((f32[16,128,128]{2,1,0:T(8,128)}), f32[16,128,128]{2,1,0:T(8,128)}, u32[]{:S(2)}, u32[]{:S(2)}) async-start(f32[16,128,128]{2,1,0:T(8,128)} %copy-done.26), calls=%async_computation.6 | async-start | bytes 2097152 | tf_op jit(solution)/shard_map/all_to_all | solution.py:645
  466.4 175.0 %collective-permute-start.9 = (f32[512,4384]{0,1:T(8,128)}, f32[512,4384]{0,1:T(8,128)}, u32[]{:S(2)}, u32[]{:S(2)}) collective-permute-start(f32[512,4384]{0,1:T(8,128)} %fusion.65), channel_id=1, source_target_pairs={{0,1},{1,0},{2,3},{3,2},{4,5},{5,4},{6,7},{7,6},{8,9},{9,8},{10,11... | collective-permute-start | bytes 26935304 | tf_op jit(solution)/shard_map/ppermute | solution.py:712
  482.2 67.9 %all-to-all-start.7 = ((f32[16,128,128]{2,1,0:T(8,128)}), f32[16,128,128]{2,1,0:T(8,128)}, u32[]{:S(2)}, u32[]{:S(2)}) async-start(f32[16,128,128]{2,1,0:T(8,128)} %copy-done.11), calls=%async_computation.7 | async-start | bytes 2097152 | tf_op jit(solution)/shard_map/all_to_all | solution.py:645
  498.6 177.8 %collective-permute-start.14 = (f32[1024,1024]{1,0:T(8,128)}, f32[1024,1024]{1,0:T(8,128)}, u32[]{:S(2)}, u32[]{:S(2)}) collective-permute-start(f32[1024,1024]{1,0:T(8,128)} %fusion.59), channel_id=1, source_target_pairs={{0,1},{1,0},{2,3},{3,2},{4,5},{5,4},{6,7},{7,6},{8,9},{9,8},{10,11... | collective-permute-start | bytes 12582920 | tf_op jit(solution)/shard_map/ppermute | solution.py:712
  548.3 58.2 %collective-permute-start.20 = (f32[512,1024]{1,0:T(8,128)}, f32[512,1024]{1,0:T(8,128)}, u32[]{:S(2)}, u32[]{:S(2)}) collective-permute-start(f32[512,1024]{1,0:T(8,128)} %get-tuple-element.146), channel_id=1, source_target_pairs={{0,2},{1,5},{2,0},{3,7},{4,6},{5,1},{6,4},{7,3},{8,10},{9,13},{10,... | collective-permute-start | bytes 6291464 | tf_op jit(solution)/shard_map/ppermute | solution.py:712
  581.2 5.4 collective-permute-start.3
  587.6 11.1 %copy-start.69 = (bf16[512,2048]{1,0:T(8,128)(2,1)S(1)}, bf16[512,2048]{1,0:T(8,128)(2,1)}, u32[]{:S(2)}) copy-start(bf16[512,2048]{1,0:T(8,128)(2,1)} %copy-done.68) | copy-start | bytes 6291460
  587.7 11.2 %copy-start.79 = (bf16[512,128]{1,0:T(8,128)(2,1)S(1)}, bf16[512,128]{1,0:T(8,128)(2,1)}, u32[]{:S(2)}) copy-start(bf16[512,128]{1,0:T(8,128)(2,1)} %copy-done.78) | copy-start | bytes 393220
  587.7 11.2 %copy-start.132 = (bf16[512,1024]{1,0:T(8,128)(2,1)S(1)}, bf16[512,1024]{1,0:T(8,128)(2,1)}, u32[]{:S(2)}) copy-start(bf16[512,1024]{1,0:T(8,128)(2,1)} %fusion.47) | copy-start | bytes 3145732
  604.6 77.1 %collective-permute-start.4 = (f32[512,4384]{0,1:T(8,128)}, f32[512,4384]{0,1:T(8,128)}, u32[]{:S(2)}, u32[]{:S(2)}) collective-permute-start(f32[512,4384]{0,1:T(8,128)} %fusion.69), channel_id=1, source_target_pairs={{0,1},{1,0},{2,3},{3,2},{4,5},{5,4},{6,7},{7,6},{8,9},{9,8},{10,11... | collective-permute-start | bytes 26935304 | tf_op jit(solution)/shard_map/ppermute | solution.py:712
  609.4 14.0 %collective-permute-start.21 = (f32[256,1024]{1,0:T(8,128)S(1)}, f32[256,1024]{1,0:T(8,128)S(1)}, u32[]{:S(2)}, u32[]{:S(2)}) collective-permute-start(f32[256,1024]{1,0:T(8,128)S(1)} %get-tuple-element.154), channel_id=1, source_target_pairs={{0,4},{1,3},{2,6},{3,1},{4,0},{5,7},{6,2},{7,5},{8,12},{9,11},{10,... | collective-permute-start | bytes 3145736 | tf_op jit(solution)/shard_map/ppermute | solution.py:712
  624.5 13.0 %collective-permute-start.22 = (f32[128,1024]{1,0:T(8,128)}, f32[128,1024]{1,0:T(8,128)}, u32[]{:S(2)}, u32[]{:S(2)}) collective-permute-start(f32[128,1024]{1,0:T(8,128)} %get-tuple-element.158), channel_id=1, source_target_pairs={{0,8},{1,9},{2,10},{3,11},{4,12},{5,13},{6,14},{7,15},{8,0},{9,1},... | collective-permute-start | bytes 1572872 | tf_op jit(solution)/shard_map/ppermute | solution.py:712
  626.2 11.4 %copy-start.100 = (f32[128,1024]{1,0:T(8,128)S(1)}, f32[128,1024]{1,0:T(8,128)}, u32[]{:S(2)}) copy-start(f32[128,1024]{1,0:T(8,128)} %get-tuple-element.157) | copy-start | bytes 1572868
  626.2 15.1 %copy-start.125 = (f32[32]{0:T(128)S(1)}, f32[32]{0:T(128)}, u32[]{:S(2)}) copy-start(f32[32]{0:T(128)} %reduce_sum.126) | copy-start | bytes 388
  626.2 15.1 %copy-start.127 = (f32[32]{0:T(128)S(1)}, f32[32]{0:T(128)}, u32[]{:S(2)}) copy-start(f32[32]{0:T(128)} %get-tuple-element.185) | copy-start | bytes 388
  626.2 15.1 %copy-start.128 = (f32[32]{0:T(128)S(1)}, f32[32]{0:T(128)}, u32[]{:S(2)}) copy-start(f32[32]{0:T(128)} %get-tuple-element.186) | copy-start | bytes 388
  638.6 83.2 %collective-permute-start.23 = (f32[64,1024]{1,0:T(8,128)S(1)}, f32[64,1024]{1,0:T(8,128)}, u32[]{:S(2)}, u32[]{:S(2)}) collective-permute-start(f32[64,1024]{1,0:T(8,128)S(1)} %slice_add_fusion.28), channel_id=1, source_target_pairs={{0,16},{1,17},{2,18},{3,19},{4,20},{5,21},{6,22},{7,23},{8,24},{9,... | collective-permute-start | bytes 786440 | tf_op jit(solution)/shard_map/ppermute | solution.py:712
  641.4 12.4 %copy-start.64 = (bf16[512,2304]{1,0:T(8,128)(2,1)S(1)}, bf16[512,2304]{1,0:T(8,128)(2,1)}, u32[]{:S(2)}) copy-start(bf16[512,2304]{1,0:T(8,128)(2,1)} %copy-done.63) | copy-start | bytes 7077892
  641.4 12.4 %copy-start.108 = (f32[1,1024]{1,0:T(1,128)S(1)}, f32[1,1024]{1,0:T(1,128)}, u32[]{:S(2)}) copy-start(f32[1,1024]{1,0:T(1,128)} %copy-done.107) | copy-start | bytes 12292
  641.4 12.4 %copy-start.116 = (f32[512]{0:T(512)S(1)}, f32[512]{0:T(512)}, u32[]{:S(2)}) copy-start(f32[512]{0:T(512)} %copy-done.115) | copy-start | bytes 6148
  652.4 51.1 %collective-permute-start.10 = (f32[256,4384]{0,1:T(8,128)}, f32[256,4384]{0,1:T(8,128)}, u32[]{:S(2)}, u32[]{:S(2)}) collective-permute-start(f32[256,4384]{0,1:T(8,128)} %get-tuple-element.136), channel_id=1, source_target_pairs={{0,2},{1,5},{2,0},{3,7},{4,6},{5,1},{6,4},{7,3},{8,10},{9,13},{10,... | collective-permute-start | bytes 13467656 | tf_op jit(solution)/shard_map/ppermute | solution.py:712
  681.7 122.5 %collective-permute-start.15 = (f32[512,1024]{1,0:T(8,128)}, f32[512,1024]{1,0:T(8,128)}, u32[]{:S(2)}, u32[]{:S(2)}) collective-permute-start(f32[512,1024]{1,0:T(8,128)} %get-tuple-element.144), channel_id=1, source_target_pairs={{0,2},{1,5},{2,0},{3,7},{4,6},{5,1},{6,4},{7,3},{8,10},{9,13},{10,... | collective-permute-start | bytes 6291464 | tf_op jit(solution)/shard_map/ppermute | solution.py:712
  692.7 125.3 %collective-permute-start.5 = (f32[256,4384]{0,1:T(8,128)}, f32[256,4384]{0,1:T(8,128)}, u32[]{:S(2)}, u32[]{:S(2)}) collective-permute-start(f32[256,4384]{0,1:T(8,128)} %get-tuple-element.134), channel_id=1, source_target_pairs={{0,2},{1,5},{2,0},{3,7},{4,6},{5,1},{6,4},{7,3},{8,10},{9,13},{10,... | collective-permute-start | bytes 13467656 | tf_op jit(solution)/shard_map/ppermute | solution.py:712
  703.5 14.2 %copy-start.113 = (f32[512]{0:T(512)S(1)}, f32[512]{0:T(512)}, u32[]{:S(2)}) copy-start(f32[512]{0:T(512)} %copy-done.112) | copy-start | bytes 6148
  703.5 14.2 %copy-start.83 = (f32[512,1024]{1,0:T(8,128)S(1)}, f32[512,1024]{1,0:T(8,128)}, u32[]{:S(2)}) copy-start(f32[512,1024]{1,0:T(8,128)} %copy-done.80) | copy-start | bytes 6291460
  709.9 100.1 %collective-permute-start.11 = (f32[128,4384]{0,1:T(8,128)}, f32[128,4384]{0,1:T(8,128)}, u32[]{:S(2)}, u32[]{:S(2)}) collective-permute-start(f32[128,4384]{0,1:T(8,128)} %get-tuple-element.142), channel_id=1, source_target_pairs={{0,4},{1,3},{2,6},{3,1},{4,0},{5,7},{6,2},{7,5},{8,12},{9,11},{10,... | collective-permute-start | bytes 6733832 | tf_op jit(solution)/shard_map/ppermute | solution.py:712
  711.8 90.5 %all-to-all-start.8 = ((f32[32,1,1152]{2,1,0:T(1,128)}), f32[32,1,1152]{2,1,0:T(1,128)S(1)}, u32[]{:S(2)}, u32[]{:S(2)}) async-start(f32[32,1,1152]{2,1,0:T(1,128)} %copy.58), calls=%async_computation.8 | async-start | bytes 294912 | tf_op jit(solution)/shard_map/all_to_all | solution.py:831
  808.0 16.2 %collective-permute-start.16 = (f32[256,1024]{1,0:T(8,128)}, f32[256,1024]{1,0:T(8,128)}, u32[]{:S(2)}, u32[]{:S(2)}) collective-permute-start(f32[256,1024]{1,0:T(8,128)} %get-tuple-element.152), channel_id=1, source_target_pairs={{0,4},{1,3},{2,6},{3,1},{4,0},{5,7},{6,2},{7,5},{8,12},{9,11},{10,... | collective-permute-start | bytes 3145736 | tf_op jit(solution)/shard_map/ppermute | solution.py:712
  817.8 39.5 %collective-permute-start.12 = (f32[64,4384]{1,0:T(8,128)}, f32[64,4384]{1,0:T(8,128)S(1)}, u32[]{:S(2)}, u32[]{:S(2)}) collective-permute-start(f32[64,4384]{1,0:T(8,128)} %copy.64), channel_id=1, source_target_pairs={{0,8},{1,9},{2,10},{3,11},{4,12},{5,13},{6,14},{7,15},{8,0},{9,1},... | collective-permute-start | bytes 3366920 | tf_op jit(solution)/shard_map/ppermute | solution.py:712
  824.1 35.4 %collective-permute-start.6 = (f32[128,4384]{0,1:T(8,128)}, f32[128,4384]{0,1:T(8,128)}, u32[]{:S(2)}, u32[]{:S(2)}) collective-permute-start(f32[128,4384]{0,1:T(8,128)} %get-tuple-element.140), channel_id=1, source_target_pairs={{0,4},{1,3},{2,6},{3,1},{4,0},{5,7},{6,2},{7,5},{8,12},{9,11},{10,... | collective-permute-start | bytes 6733832 | tf_op jit(solution)/shard_map/ppermute | solution.py:712
  825.6 31.8 %copy-start.102 = (f32[128,1024]{1,0:T(8,128)}, f32[128,1024]{1,0:T(8,128)S(1)}, u32[]{:S(2)}) copy-start(f32[128,1024]{1,0:T(8,128)S(1)} %get-tuple-element.155) | copy-start | bytes 1572868
  825.6 30.6 %collective-permute-start.17 = (f32[128,1024]{1,0:T(8,128)S(1)}, f32[128,1024]{1,0:T(8,128)S(1)}, u32[]{:S(2)}, u32[]{:S(2)}) collective-permute-start(f32[128,1024]{1,0:T(8,128)S(1)} %get-tuple-element.156), channel_id=1, source_target_pairs={{0,8},{1,9},{2,10},{3,11},{4,12},{5,13},{6,14},{7,15},{8,0},{9,1},... | collective-permute-start | bytes 1572872 | tf_op jit(solution)/shard_map/ppermute | solution.py:712
  857.0 22.4 %collective-permute-start.18 = (f32[64,1024]{1,0:T(8,128)}, f32[64,1024]{1,0:T(8,128)}, u32[]{:S(2)}, u32[]{:S(2)}) collective-permute-start(f32[64,1024]{1,0:T(8,128)} %slice_add_fusion.30), channel_id=1, source_target_pairs={{0,16},{1,17},{2,18},{3,19},{4,20},{5,21},{6,22},{7,23},{8,24},{9,... | collective-permute-start | bytes 786440 | tf_op jit(solution)/shard_map/ppermute | solution.py:712
  869.3 40.8 %collective-permute-start.7 = (f32[64,4384]{1,0:T(8,128)}, f32[64,4384]{1,0:T(8,128)}, u32[]{:S(2)}, u32[]{:S(2)}) collective-permute-start(f32[64,4384]{1,0:T(8,128)} %copy.59), channel_id=1, source_target_pairs={{0,8},{1,9},{2,10},{3,11},{4,12},{5,13},{6,14},{7,15},{8,0},{9,1},... | collective-permute-start | bytes 3366920 | tf_op jit(solution)/shard_map/ppermute | solution.py:712
  877.3 29.7 %collective-permute-start.13 = (f32[32,4384]{1,0:T(8,128)}, f32[32,4384]{1,0:T(8,128)}, u32[]{:S(2)}, u32[]{:S(2)}) collective-permute-start(f32[32,4384]{1,0:T(8,128)} %copy.67), channel_id=1, source_target_pairs={{0,16},{1,17},{2,18},{3,19},{4,20},{5,21},{6,22},{7,23},{8,24},{9,... | collective-permute-start | bytes 1683464 | tf_op jit(solution)/shard_map/ppermute | solution.py:712
  921.0 27.4 %collective-permute-start.8 = (f32[32,4384]{1,0:T(8,128)}, f32[32,4384]{1,0:T(8,128)}, u32[]{:S(2)}, u32[]{:S(2)}) collective-permute-start(f32[32,4384]{1,0:T(8,128)} %copy.62), channel_id=1, source_target_pairs={{0,16},{1,17},{2,18},{3,19},{4,20},{5,21},{6,22},{7,23},{8,24},{9,... | collective-permute-start | bytes 1683464 | tf_op jit(solution)/shard_map/ppermute | solution.py:712
  930.3 21.2 %copy-start.86 = (f32[64,4384]{0,1:T(8,128)S(1)}, f32[64,4384]{0,1:T(8,128)}, u32[]{:S(2)}) copy-start(f32[64,4384]{0,1:T(8,128)} %get-tuple-element.147) | copy-start | bytes 3366916
  (101 other events, 461.8 us)

commit v4 on v3

v4 whole, which is shorter than its diff:
```python
from functools import partial

import jax
import jax.numpy as jnp
from jax import lax
from jax.experimental import pallas as pl
from jax.experimental.pallas import tpu as pltpu
from jax.sharding import PartitionSpec as P

DI = 2048
STATE = 128
HEAD_DIM = 64
HEADS = DI // HEAD_DIM
KW = 4
GROUP = 256
LAYERS = 2
CHANNELS = DI + 2 * STATE
TILE = 512
HEADS_AT = TILE // HEAD_DIM
MAPS = 2 * STATE
ROWS_STEP = 128
HALO = 8
HALF = 128
LOG2E = 1.4426950408889634
ROWS_AT = 64
VMEM_BYTES = 48 * 1024 * 1024

EPS = 1e-05
HIGHEST = lax.Precision.HIGHEST
AXES = ("seq", "rows")


def pcall(body, grid, in_specs, out_specs, out_shape, scratch, args, flops=0, nbytes=0, after=()):
    taken = len(args)

    def run(*refs):
        body(*refs[:taken], *refs[taken + len(after) :])

    return pl.pallas_call(
        run,
        grid=grid,
        in_specs=list(in_specs) + [pl.BlockSpec(memory_space=pltpu.HBM)] * len(after),
        out_specs=out_specs,
        out_shape=out_shape,
        scratch_shapes=scratch,
        compiler_params=pltpu.CompilerParams(vmem_limit_bytes=VMEM_BYTES),
        cost_estimate=pl.CostEstimate(flops=flops, bytes_accessed=nbytes, transcendentals=0),
    )(*args, *after)


def dot(a, b, dims=(((1,), (0,)), ((), ()))):
    return lax.dot_general(
        a.astype(jnp.bfloat16), b.astype(jnp.bfloat16), dims, preferred_element_type=jnp.float32
    )


def dot_nt(a, b):
    return dot(a, b, (((1,), (1,)), ((), ())))


def dot_exact(a, b):
    return jnp.dot(a, b, precision=HIGHEST, preferred_element_type=jnp.float32)


def sigmoid(v):
    return 0.5 * jnp.tanh(0.5 * v) + 0.5


def lane_iota(shape):
    return lax.broadcasted_iota(jnp.int32, shape, 1)


def low_half(rows):
    return lane_iota((rows, 128)) < HEAD_DIM


def to_heads(cols, first, pairs):
    rows = cols.shape[0]
    low = low_half(rows)
    parts = []
    for pair in range(pairs):
        at = first + 2 * pair
        parts.append(
            jnp.where(
                low,
                jnp.broadcast_to(cols[:, at : at + 1], (rows, 128)),
                jnp.broadcast_to(cols[:, at + 1 : at + 2], (rows, 128)),
            )
        )
    return jnp.concatenate(parts, 1) if pairs > 1 else parts[0]


def spread_heads(cols, pairs):
    pick = (
        lax.broadcasted_iota(jnp.int32, (128, 128 * pairs), 0) == lane_iota((128, 128 * pairs)) // HEAD_DIM
    ).astype(jnp.bfloat16)
    high = cols.astype(jnp.bfloat16)
    return dot(high, pick) + dot(cols - high.astype(jnp.float32), pick)


def head_pick(first, heads):
    shape = (128, HEAD_DIM * heads)
    return (lax.broadcasted_iota(jnp.int32, shape, 0) == first + lane_iota(shape) // HEAD_DIM).astype(jnp.bfloat16)


def picked_heads(cols, pick):
    high = cols.astype(jnp.bfloat16)
    return dot(high, pick) + dot(cols - high.astype(jnp.float32), pick)


def head_sums(first):
    channel = lax.broadcasted_iota(jnp.int32, (TILE, 128), 0)
    return (channel // HEAD_DIM + first == lane_iota((TILE, 128))).astype(jnp.bfloat16)


def keep_marks(marks_ref, aux_ref, lanes):
    for at, lane in enumerate(lanes):
        marks_ref[at] = jnp.broadcast_to(aux_ref[:, lane : lane + 1], marks_ref.shape[1:])


def conv_rows(x_ref, w_ref, marks_ref, first, count, lanes):
    total = w_ref[4:5, lanes] + w_ref[3:4, lanes] * x_ref[first + 8 : first + 8 + count, lanes]
    for tap in range(KW - 1):
        match = marks_ref[tap, first : first + count, :]
        total = total + w_ref[tap : tap + 1, lanes] * (x_ref[first + 5 + tap : first + 5 + tap + count, lanes] * match)
    return total


def chunks_of(rows, width):
    for pair in range(width // 128):
        for first in range(0, rows, ROWS_AT):
            yield first, slice(first, first + ROWS_AT), slice(pair * 128, (pair + 1) * 128)


def states_kernel(
    x_ref, xbc_ref, rate_ref, aux_ref, w_ref, wbc_ref, hp_ref,
    v_ref, bc_ref, col_ref, cumr_ref, made_ref, kx_ref, pay_ref,
    bt_ref, marks_ref,
):
    turn = pl.program_id(0)
    span = rate_ref.shape[0]
    count = span // GROUP

    @pl.when(turn == 0)
    def _():
        keep_marks(marks_ref, aux_ref, range(KW - 1))
        for first, rows, lanes in chunks_of(span, MAPS):
            conv = conv_rows(xbc_ref, wbc_ref, marks_ref, first, ROWS_AT, lanes)
            bc_ref[rows, lanes] = conv * sigmoid(conv)
        tri = (
            lax.broadcasted_iota(jnp.int32, (GROUP, GROUP), 0) >= lane_iota((GROUP, GROUP))
        ).astype(jnp.float32)
        for block in range(count):
            rows = slice(block * GROUP, (block + 1) * GROUP)
            bt_ref[block] = bc_ref[rows, :STATE].T.astype(jnp.bfloat16)
            raw = rate_ref[rows, :] + hp_ref[0:1, :]
            step = jnp.maximum(raw, 0.0) + jnp.log1p(jnp.exp(-jnp.abs(raw)))
            cum = dot_exact(tri, hp_ref[1:2, :] * step)
            last = cum[GROUP - 1 :, :]
            col_ref[0, rows, :] = cum
            col_ref[1, rows, :] = step
            col_ref[2, rows, :] = jnp.exp(cum) * aux_ref[rows, 3:4]
            col_ref[3, rows, :] = jnp.exp(last - cum) * aux_ref[rows, 4:5]
            cumr_ref[:, rows] = cum.T

    for first, rows, lanes in chunks_of(span, TILE):
        conv = conv_rows(x_ref, w_ref, marks_ref, first, ROWS_AT, lanes)
        v_ref[rows, lanes] = conv * sigmoid(conv)
    pick = head_pick(turn * HEADS_AT, HEADS_AT)
    made = []
    keep = []
    for block in range(count):
        rows = slice(block * GROUP, (block + 1) * GROUP)
        weight = picked_heads(col_ref[3, rows, :] * col_ref[1, rows, :], pick)
        made.append(dot(bt_ref[block], weight * v_ref[rows, :]))
        ends = col_ref[2, (block + 1) * GROUP - 8 : (block + 1) * GROUP, :]
        keep.append(picked_heads(ends, pick)[7:8, :])
    made_ref[...] = made[0]
    kx_ref[...] = jnp.concatenate([keep[0], keep[1], jnp.zeros((6, TILE), jnp.float32)], 0)
    final = keep[1] * made[0] + made[1]
    total = jnp.broadcast_to(keep[0] * keep[1], (8, TILE))
    pairs = TILE // 128
    chunks = pay_ref.shape[0] // pairs
    size = STATE // chunks
    for pair in range(pairs):
        lanes = slice(pair * 128, (pair + 1) * 128)
        for chunk in range(chunks):
            pay_ref[pair * chunks + chunk, :size, :] = final[chunk * size : (chunk + 1) * size, lanes]
            pay_ref[pair * chunks + chunk, size:, :] = total[:, lanes]


def inner_kernel(bc_ref, v_ref, col_ref, cumr_ref, aux_ref, auxr_ref, y_ref, g_ref):
    scores = dot_nt(bc_ref[:, STATE:], bc_ref[:, :STATE])
    allowed = (aux_ref[:, 5:6] == auxr_ref[0:1, :]) & (
        lax.broadcasted_iota(jnp.int32, (GROUP, GROUP), 0) >= lane_iota((GROUP, GROUP))
    )
    g_ref[...] = jnp.where(allowed, scores, 0.0)
    low = low_half(GROUP)
    cum = LOG2E * col_ref[0]
    cum_row = LOG2E * cumr_ref[:HEADS, :]
    steps = picked_heads(col_ref[1], head_pick(0, HEADS))
    for pair in range(HEADS // 2):
        lanes = slice(pair * 128, (pair + 1) * 128)
        scaled = steps[:, lanes] * v_ref[:, lanes]
        result = None
        for half in range(2):
            head = 2 * pair + half
            row = cum_row[head : head + 1, :]
            tops, bottoms = [], []
            for first in range(0, GROUP, 64):
                width = HALF if first < HALF else GROUP
                spread = cum[first : first + 64, head : head + 1] - row[:, :width]
                decay = jnp.exp2(jnp.minimum(spread, 0.0))
                mixing = (g_ref[first : first + 64, :width] * decay).astype(jnp.bfloat16)
                (tops if first < HALF else bottoms).append(mixing)
            picked = jnp.where(low if half == 0 else ~low, scaled, 0.0).astype(jnp.bfloat16)
            top = dot(jnp.concatenate(tops, 0), picked[:HALF])
            bottom = dot(jnp.concatenate(bottoms, 0), picked)
            result = (top, bottom) if result is None else (result[0] + top, result[1] + bottom)
        y_ref[:HALF, lanes] = result[0]
        y_ref[HALF:, lanes] = result[1]


def finish_kernel(
    yi_ref, v_ref, gate_ref, bc_ref, col_ref, sin_ref, made_ref, kx_ref, ch_ref,
    y_ref, out_ref,
    gated_ref,
):
    later = pl.program_id(0) * ROWS_STEP >= GROUP
    out_map = bc_ref[:, STATE:].astype(jnp.bfloat16)
    entering = picked_heads(col_ref[2], head_pick(0, HEADS))
    total = [jnp.zeros((ROWS_AT, 128), jnp.float32) for _ in range(ROWS_STEP // ROWS_AT)]
    for pair in range(HEADS // 2):
        lanes = slice(pair * 128, (pair + 1) * 128)
        state = sin_ref[pair]
        state = jnp.where(later, kx_ref[0:1, lanes] * state + made_ref[:, lanes], state)
        outer = entering[:, lanes] * dot(out_map, state)
        for at in range(ROWS_STEP // ROWS_AT):
            rows = slice(at * ROWS_AT, (at + 1) * ROWS_AT)
            result = yi_ref[rows, lanes] + outer[rows] + ch_ref[0:1, lanes] * v_ref[rows, lanes]
            y_ref[rows, lanes] = result
            gate = gate_ref[rows, lanes]
            gated = result * (gate * sigmoid(gate))
            gated_ref[rows, lanes] = gated
            total[at] = total[at] + gated * gated
    for at in range(ROWS_STEP // ROWS_AT):
        rows = slice(at * ROWS_AT, (at + 1) * ROWS_AT)
        scale = lax.rsqrt(jnp.sum(total[at], 1, keepdims=True) / DI + EPS)
        out_ref[rows, :] = (gated_ref[rows, :] * scale * ch_ref[1:2, :]).astype(jnp.bfloat16)


def gate_back_kernel(
    dno_ref, y_ref, gate_ref, v_ref, bc_ref, col_ref, kx_ref, ch_ref,
    dy_ref, dgate_ref, sum_ref, d1_ref, pay_ref,
    gated_ref, silu_ref,
):
    at_step = pl.program_id(0)
    later = at_step * ROWS_STEP >= GROUP
    parts = ROWS_STEP // ROWS_AT
    square = [jnp.zeros((ROWS_AT, 128), jnp.float32) for _ in range(parts)]
    cross = [jnp.zeros((ROWS_AT, 128), jnp.float32) for _ in range(parts)]
    for first, rows, lanes in chunks_of(ROWS_STEP, DI):
        gate = gate_ref[rows, lanes]
        sig = sigmoid(gate)
        silu = gate * sig
        y = y_ref[rows, lanes]
        gated = y * silu
        gated_ref[rows, lanes] = gated
        silu_ref[0, rows, lanes] = silu
        silu_ref[1, rows, lanes] = y * (sig * (1.0 + gate * (1.0 - sig)))
        at = first // ROWS_AT
        square[at] = square[at] + gated * gated
        cross[at] = cross[at] + gated * (dno_ref[rows, lanes] * ch_ref[1:2, lanes])
    scales = [lax.rsqrt(jnp.sum(part, 1, keepdims=True) / DI + EPS) for part in square]
    pulls = [scale * scale * scale * (jnp.sum(part, 1, keepdims=True) / DI) for scale, part in zip(scales, cross)]
    out_t = bc_ref[:, STATE:].T.astype(jnp.bfloat16)
    entering = picked_heads(col_ref[2], head_pick(0, HEADS))
    pairs = DI // 128
    chunks = pay_ref.shape[0] // pairs
    size = STATE // chunks

    @pl.when(at_step == 0)
    def _():
        sum_ref[...] = jnp.zeros_like(sum_ref)
        pay_ref[...] = jnp.zeros_like(pay_ref)

    @pl.when((at_step == 0) | (at_step * ROWS_STEP == GROUP))
    def _():
        d1_ref[...] = jnp.zeros_like(d1_ref)

    for pair in range(pairs):
        lanes = slice(pair * 128, (pair + 1) * 128)
        gain_sum = jnp.zeros((8, 128), jnp.float32)
        skip_sum = jnp.zeros((8, 128), jnp.float32)
        weighted = []
        for at in range(parts):
            rows = slice(at * ROWS_AT, (at + 1) * ROWS_AT)
            gated = gated_ref[rows, lanes]
            dno = dno_ref[rows, lanes] * scales[at]
            dgated = dno * ch_ref[1:2, lanes] - gated * pulls[at]
            dy = dgated * silu_ref[0, rows, lanes]
            dy_ref[rows, lanes] = dy
            dgate_ref[rows, lanes] = (dgated * silu_ref[1, rows, lanes]).astype(jnp.bfloat16)
            gain_sum = gain_sum + jnp.sum((dno * gated).reshape(-1, 8, 128), 0)
            skip_sum = skip_sum + jnp.sum((dy * v_ref[rows, lanes]).reshape(-1, 8, 128), 0)
            weighted.append((entering[rows, lanes] * dy).astype(jnp.bfloat16))
        sum_ref[0:1, lanes] += jnp.sum(gain_sum, 0, keepdims=True)
        sum_ref[1:2, lanes] += jnp.sum(skip_sum, 0, keepdims=True)
        fresh = dot(out_t, jnp.concatenate(weighted, 0))
        d1_ref[:, lanes] += fresh
        more = jnp.where(later, kx_ref[0:1, lanes], 1.0) * fresh
        for chunk in range(chunks):
            pay_ref[pair * chunks + chunk] += more[chunk * size : (chunk + 1) * size]


def inner_back_kernel(
    bc_ref, v_ref, dy_ref, col_ref, cumr_ref, aux_ref, auxr_ref,
    x_ref, dbc_ref,
    g_ref, dg_ref,
):
    allowed = (aux_ref[:, 5:6] == auxr_ref[0:1, :]) & (
        lax.broadcasted_iota(jnp.int32, (GROUP, GROUP), 0) <= lane_iota((GROUP, GROUP))
    )
    g_ref[...] = jnp.where(allowed, dot_nt(bc_ref[:, :STATE], bc_ref[:, STATE:]), 0.0)
    dg_ref[...] = jnp.zeros_like(dg_ref)
    low = low_half(GROUP)
    cum = LOG2E * col_ref[0]
    cum_row = LOG2E * cumr_ref[:HEADS, :]
    steps = picked_heads(col_ref[1], head_pick(0, HEADS))
    for pair in range(HEADS // 2):
        lanes = slice(pair * 128, (pair + 1) * 128)
        scaled = steps[:, lanes] * v_ref[:, lanes]
        dy = dy_ref[:, lanes]
        dy_low = dy.astype(jnp.bfloat16)
        result = None
        grads = {}
        for half in range(2):
            head = 2 * pair + half
            row = cum_row[head : head + 1, :]
            mine = low if half == 0 else ~low
            picked = jnp.where(mine, scaled, 0.0).astype(jnp.bfloat16)
            top_grad = dot_nt(picked[:HALF], dy_low)
            bottom_grad = dot_nt(picked[HALF:], dy_low[HALF:])
            tops, bottoms = [], []
            for first in range(0, GROUP, 64):
                rows = slice(first, first + 64)
                top = first < HALF
                across = slice(0 if top else HALF, GROUP)
                spread = row[:, across] - cum[rows, head : head + 1]
                decay = jnp.exp2(jnp.minimum(spread, 0.0))
                (tops if top else bottoms).append((g_ref[rows, across] * decay).astype(jnp.bfloat16))
                part = (top_grad[rows] if top else bottom_grad[first - HALF : first - HALF + 64]) * decay
                if half == 0:
                    grads[first] = part
                else:
                    dg_ref[rows, across] += grads[first] + part
            dy_mine = jnp.where(mine, dy, 0.0).astype(jnp.bfloat16)
            top = dot(jnp.concatenate(tops, 0), dy_mine)
            bottom = dot(jnp.concatenate(bottoms, 0), dy_mine[HALF:])
            result = (top, bottom) if result is None else (result[0] + top, result[1] + bottom)
        x_ref[:HALF, lanes] = result[0]
        x_ref[HALF:, lanes] = result[1]
    dg = jnp.where(allowed, dg_ref[...], 0.0)
    dbc_ref[:, :STATE] = dot(dg, bc_ref[:, STATE:])
    dbc_ref[:, STATE:] = dot(dg.T, bc_ref[:, :STATE])


def states_back_kernel(
    xi_ref, v_ref, dy_ref, yi_ref, x_ref, xbc_ref, bc_ref, col_ref, dso_ref, sin_ref, made_ref, d1_ref,
    kx_ref, dbc_ref, aux_ref, w_ref, wbc_ref, ch_ref, hp_ref, rate_ref,
    dconv_ref, dconv_bc_ref, drate_ref, sum_ref,
    ds_ref, dc_ref, z_ref, kd_ref, dmap_ref, marks_ref,
):
    turn = pl.program_id(0)
    span = v_ref.shape[0]
    count = span // GROUP

    @pl.when(turn == 0)
    def _():
        keep_marks(marks_ref, aux_ref, range(KW - 1))
        ds_ref[...] = jnp.zeros_like(ds_ref)
        dc_ref[...] = jnp.zeros_like(dc_ref)
        z_ref[...] = jnp.zeros_like(z_ref)
        kd_ref[...] = jnp.zeros_like(kd_ref)
        dmap_ref[...] = dbc_ref[...]

    sums = head_sums(turn * HEADS_AT)
    pick = head_pick(turn * HEADS_AT, HEADS_AT)
    end_grad = jnp.concatenate([dso_ref[pair] for pair in range(TILE // 128)], 1)
    state = jnp.concatenate([sin_ref[pair] for pair in range(TILE // 128)], 1)
    ends = [d1_ref[...] + kx_ref[1:2, :] * end_grad, end_grad]
    starts = [state, kx_ref[0:1, :] * state + made_ref[...]]
    for block in range(count):
        at = slice(block * GROUP, (block + 1) * GROUP)
        step = picked_heads(col_ref[1, at, :], pick)
        entering = picked_heads(col_ref[2, at, :], pick)
        tail = picked_heads(col_ref[3, at, :], pick)
        from_end = dot(bc_ref[at, :STATE], ends[block])
        outer = dot(bc_ref[at, STATE:], starts[block])
        kinds = {name: [] for name in ("ds", "z", "dc", "low", "values", "dy")}
        for first in range(0, GROUP, ROWS_AT):
            local = slice(first, first + ROWS_AT)
            rows = slice(block * GROUP + first, block * GROUP + first + ROWS_AT)
            pieces = {name: [] for name in kinds}
            for pair in range(TILE // 128):
                lanes = slice(pair * 128, (pair + 1) * 128)
                v = v_ref[rows, lanes]
                dy = dy_ref[rows, lanes]
                xi = xi_ref[rows, lanes]
                scaled = step[local, lanes] * v
                low = dy.astype(jnp.bfloat16).astype(jnp.float32)
                inside = low * yi_ref[rows, lanes] - scaled.astype(jnp.bfloat16).astype(jnp.float32) * xi
                ended = tail[local, lanes] * from_end[local, lanes]
                inside = inside + dy * (entering[local, lanes] * outer[local, lanes])
                pulled = xi + ended
                high = inside.astype(jnp.bfloat16)
                pieces["dc"].append(high)
                pieces["low"].append((inside - high.astype(jnp.float32)).astype(jnp.bfloat16))
                pieces["ds"].append((v * pulled).astype(jnp.bfloat16))
                pieces["z"].append((scaled * ended).astype(jnp.bfloat16))
                pieces["values"].append((tail[local, lanes] * scaled).astype(jnp.bfloat16))
                pieces["dy"].append((entering[local, lanes] * dy).astype(jnp.bfloat16))
                grad = step[local, lanes] * pulled + ch_ref[0:1, lanes] * dy
                conv = conv_rows(x_ref, w_ref, marks_ref, block * GROUP + first, ROWS_AT, lanes)
                sig = sigmoid(conv)
                dconv_ref[rows, lanes] = grad * (sig * (1.0 + conv * (1.0 - sig)))
            for name in kinds:
                kinds[name].append(jnp.concatenate(pieces[name], 1))
        whole = {name: jnp.concatenate(parts, 0) for name, parts in kinds.items()}
        ds_ref[at, :] += dot(whole["ds"], sums)
        z_ref[at, :] += dot(whole["z"], sums)
        dc_ref[at, :] += dot(whole["dc"], sums) + dot(whole["low"], sums)
        dmap_ref[at, :STATE] += dot_nt(whole["values"], ends[block])
        dmap_ref[at, STATE:] += dot_nt(whole["dy"], starts[block])
        kept = kx_ref[block : block + 1, :] * jnp.sum(ends[block] * starts[block], 0, keepdims=True)
        kd_ref[block] += dot_exact(jnp.broadcast_to(kept, (8, TILE)), sums.astype(jnp.float32))

    @pl.when(turn == pl.num_programs(0) - 1)
    def _():
        here = lax.broadcasted_iota(jnp.int32, (GROUP, GROUP), 0)
        after = (here <= lane_iota((GROUP, GROUP))).astype(jnp.float32)
        before = (here > lane_iota((GROUP, GROUP))).astype(jnp.float32)
        bias_sum = jnp.zeros((1, 128), jnp.float32)
        decay_sum = jnp.zeros((1, 128), jnp.float32)
        for first, rows, lanes in chunks_of(span, MAPS):
            conv = conv_rows(xbc_ref, wbc_ref, marks_ref, first, ROWS_AT, lanes)
            sig = sigmoid(conv)
            dconv_bc_ref[rows, lanes] = dmap_ref[rows, lanes] * (sig * (1.0 + conv * (1.0 - sig)))
        for block in range(count):
            rows = slice(block * GROUP, (block + 1) * GROUP)
            z = z_ref[rows, :]
            da = dot_exact(after, dc_ref[rows, :]) + kd_ref[block, 0:1, :]
            da = da + dot_exact(before, z)
            ds = ds_ref[rows, :] + hp_ref[1:2, :] * da
            drate = ds * sigmoid(rate_ref[rows, :] + hp_ref[0:1, :])
            drate_ref[rows, :] = drate.astype(jnp.bfloat16)
            bias_sum = bias_sum + jnp.sum(drate, 0, keepdims=True)
            decay_sum = decay_sum + jnp.sum(da * hp_ref[1:2, :] * col_ref[1, rows, :], 0, keepdims=True)
        sum_ref[...] = jnp.concatenate([bias_sum, decay_sum, jnp.zeros((6, 128), jnp.float32)], 0)


def conv_back_kernel(
    dconv_ref, dconv_bc_ref, next_ref, x_ref, aux_ref, w_ref, dx_ref, sum_ref, ext_ref, marks_ref
):
    turn = pl.program_id(0)
    last = pl.num_programs(0) - 1
    span = dconv_ref.shape[0]

    @pl.when(turn == 0)
    def _():
        keep_marks(marks_ref, aux_ref, (0, 1, 2, 6, 7, 8))

    @pl.when(turn < last)
    def _():
        ext_ref[:span, :] = dconv_ref[...]

    @pl.when(turn == last)
    def _():
        ext_ref[:span, :MAPS] = dconv_bc_ref[...]

    ext_ref[span:, :] = next_ref[...]
    for pair in range(TILE // 128):
        lanes = slice(pair * 128, (pair + 1) * 128)
        sums = [jnp.zeros((8, 128), jnp.float32) for _ in range(KW + 1)]
        for first in range(0, span, ROWS_AT):
            rows = slice(first, first + ROWS_AT)
            here = ext_ref[rows, lanes]
            grad = w_ref[3:4, lanes] * here
            for ahead in range(1, KW):
                shifted_grad = ext_ref[first + ahead : first + ahead + ROWS_AT, lanes]
                grad = grad + w_ref[3 - ahead : 4 - ahead, lanes] * (shifted_grad * marks_ref[2 + ahead, rows, :])
            dx_ref[rows, lanes] = grad.astype(jnp.bfloat16)
            for tap in range(KW):
                term = here * x_ref[first + 5 + tap : first + 5 + tap + ROWS_AT, lanes]
                if tap < KW - 1:
                    term = term * marks_ref[tap, rows, :]
                sums[tap] = sums[tap] + jnp.sum(term.reshape(-1, 8, 128), 0)
            sums[KW] = sums[KW] + jnp.sum(here.reshape(-1, 8, 128), 0)
        sums = [jnp.sum(part, 0, keepdims=True) for part in sums]
        sum_ref[:, lanes] = jnp.concatenate(sums + [jnp.zeros((3, 128), jnp.float32)], 0)


def scan_kernel(reverse, rows, in_ref, keep_ref, out_ref):
    peers = out_ref.shape[0]
    carried = jnp.zeros((rows, 128), jnp.float32)
    for at in range(peers):
        peer = peers - 1 - at if reverse else at
        out_ref[peer] = carried
        carried = keep_ref[peer, 0:1, :] * carried + in_ref[peer, :rows, :]


def total_kernel(in_ref, out_ref):
    out_ref[...] = jnp.sum(in_ref[...], 0)


def full(shape):
    return pl.BlockSpec(shape, lambda *at: (0,) * len(shape))


def shape_of(dims, dtype=jnp.float32):
    return jax.ShapeDtypeStruct(dims, dtype)


def vmem(dims, dtype=jnp.float32):
    return pltpu.VMEM(dims, dtype)


def make_states(peers, mixed_ext, rate, aux, conv, hp):
    span = rate.shape[0]
    groups = DI // TILE
    chunks = peers * 128 // DI
    tile = lambda rows: pl.BlockSpec((rows, TILE), lambda g: (0, g))
    maps = lambda rows: pl.BlockSpec((rows, MAPS), lambda g: (0, DI // MAPS))
    pay = (TILE // 128 * chunks, STATE // chunks + 8, 128)
    return pcall(
        states_kernel,
        (groups,),
        [tile(span + HALO), maps(span + HALO), full((span, 128)), full((span, 128)), tile(8), maps(8), full((8, 128))],
        [
            tile(span),
            full((span, MAPS)),
            full((4, span, 128)),
            full((128, span)),
            tile(STATE),
            tile(8),
            pl.BlockSpec(pay, lambda g: (g, 0, 0)),
        ],
        [
            shape_of((span, DI)),
            shape_of((span, MAPS)),
            shape_of((4, span, 128)),
            shape_of((128, span)),
            shape_of((STATE, DI)),
            shape_of((8, DI)),
            shape_of((peers,) + pay[1:]),
        ],
        [vmem((span // GROUP, STATE, GROUP), jnp.bfloat16), vmem((KW - 1, span, 128))],
        (mixed_ext, mixed_ext, rate, aux, conv, conv, hp),
        flops=2 * span * DI * STATE,
        nbytes=12 * span * DI,
    )


def block_rows(span):
    wide = pl.BlockSpec((GROUP, DI), lambda b: (b, 0))
    maps = pl.BlockSpec((GROUP, MAPS), lambda b: (b, 0))
    col = pl.BlockSpec((4, GROUP, 128), lambda b: (0, b, 0))
    row = pl.BlockSpec((128, GROUP), lambda b: (0, b))
    aux = pl.BlockSpec((GROUP, 128), lambda b: (b, 0))
    auxr = pl.BlockSpec((8, GROUP), lambda b: (0, b))
    return wide, maps, col, row, aux, auxr


def inner(bc, values, col, cumr, aux, auxr):
    span = values.shape[0]
    wide, maps, cols, row, auxs, auxrs = block_rows(span)
    return pcall(
        inner_kernel,
        (span // GROUP,),
        [maps, wide, cols, row, auxs, auxrs],
        wide,
        shape_of((span, DI)),
        [vmem((GROUP, GROUP))],
        (bc, values, col, cumr, aux, auxr),
        flops=2 * span * GROUP * DI * 4,
        nbytes=8 * span * DI,
    )


def finish(yi, values, gate, bc, col, state_in, made, kx, ch):
    span = values.shape[0]
    wide = pl.BlockSpec((ROWS_STEP, DI), lambda b: (b, 0))
    maps = pl.BlockSpec((ROWS_STEP, MAPS), lambda b: (b, 0))
    cols = pl.BlockSpec((4, ROWS_STEP, 128), lambda b: (0, b, 0))
    return pcall(
        finish_kernel,
        (span // ROWS_STEP,),
        [wide, wide, wide, maps, cols, full((DI // 128, STATE, 128)), full((STATE, DI)), full((8, DI)), full((8, DI))],
        [wide, wide],
        [shape_of((span, DI)), shape_of((span, DI), jnp.bfloat16)],
        [vmem((ROWS_STEP, DI))],
        (yi, values, gate, bc, col, state_in, made, kx, ch),
        flops=2 * span * DI * STATE,
        nbytes=18 * span * DI,
    )


def gate_back(peers, dno, y, gate, values, bc, col, kx, ch, after=()):
    span = values.shape[0]
    chunks = peers * 128 // DI
    wide = pl.BlockSpec((ROWS_STEP, DI), lambda b: (b, 0))
    maps = pl.BlockSpec((ROWS_STEP, MAPS), lambda b: (b, 0))
    cols = pl.BlockSpec((4, ROWS_STEP, 128), lambda b: (0, b, 0))
    pay = (peers, STATE // chunks, 128)
    return pcall(
        gate_back_kernel,
        (span // ROWS_STEP,),
        [wide, wide, wide, wide, maps, cols, full((8, DI)), full((8, DI))],
        [wide, wide, full((8, DI)), full((STATE, DI)), full(pay)],
        [
            shape_of((span, DI)),
            shape_of((span, DI), jnp.bfloat16),
            shape_of((8, DI)),
            shape_of((STATE, DI)),
            shape_of(pay),
        ],
        [vmem((ROWS_STEP, DI)), vmem((2, ROWS_STEP, DI))],
        (dno, y, gate, values, bc, col, kx, ch),
        flops=2 * span * DI * STATE,
        nbytes=22 * span * DI,
        after=after,
    )


def inner_back(bc, values, dy, col, cumr, aux, auxr, after=()):
    span = values.shape[0]
    wide, maps, cols, row, auxs, auxrs = block_rows(span)
    return pcall(
        inner_back_kernel,
        (span // GROUP,),
        [maps, wide, wide, cols, row, auxs, auxrs],
        [wide, maps],
        [shape_of((span, DI)), shape_of((span, MAPS))],
        [vmem((GROUP, GROUP)), vmem((GROUP, GROUP))],
        (bc, values, dy, col, cumr, aux, auxr),
        flops=2 * span * GROUP * DI * 8,
        nbytes=12 * span * DI,
        after=after,
    )


def states_back(xi, values, dy, yi, mixed_ext, bc, col, dso, state_in, made, d1, kx, dbc, aux, conv, ch, hp, rate, after=()):
    span = values.shape[0]
    groups = DI // TILE
    tile = lambda rows: pl.BlockSpec((rows, TILE), lambda g: (0, g))
    maps = lambda rows: pl.BlockSpec((rows, MAPS), lambda g: (0, DI // MAPS))
    state = pl.BlockSpec((TILE // 128, STATE, 128), lambda g: (g, 0, 0))
    small = full((span, 128))
    return pcall(
        states_back_kernel,
        (groups,),
        [
            tile(span), tile(span), tile(span), tile(span), tile(span + HALO), maps(span + HALO), full((span, MAPS)),
            full((4, span, 128)), state, state, tile(STATE), tile(STATE), tile(8), full((span, MAPS)),
            small, tile(8), maps(8), tile(8), full((8, 128)), small,
        ],
        [tile(span), full((span, MAPS)), small, full((8, 128))],
        [shape_of((span, DI)), shape_of((span, MAPS)), shape_of((span, 128), jnp.bfloat16), shape_of((8, 128))],
        [vmem((span, 128)), vmem((span, 128)), vmem((span, 128)), vmem((span // GROUP, 8, 128)), vmem((span, MAPS)), vmem((KW - 1, span, 128))],
        (xi, values, dy, yi, mixed_ext, mixed_ext, bc, col, dso, state_in, made, d1, kx, dbc, aux, conv, conv, ch, hp, rate),
        flops=8 * span * DI * STATE,
        nbytes=20 * span * DI,
        after=after,
    )


def conv_back(dconv, dconv_bc, following, mixed_ext, aux, conv, after=()):
    span = dconv.shape[0]
    groups = DI // TILE
    tile = lambda rows: pl.BlockSpec((rows, TILE), lambda g: (0, g))
    return pcall(
        conv_back_kernel,
        (groups + 1,),
        [
            pl.BlockSpec((span, TILE), lambda g: (0, jnp.minimum(g, groups - 1))),
            full((span, MAPS)), tile(HALO), tile(span + HALO), full((span, 128)), tile(8),
        ],
        [tile(span), tile(8)],
        [shape_of((span, CHANNELS), jnp.bfloat16), shape_of((8, CHANNELS))],
        [vmem((span + HALO, TILE)), vmem((2 * (KW - 1), span, 128))],
        (dconv, dconv_bc, following, mixed_ext, aux, conv),
        flops=8 * span * DI,
        nbytes=10 * span * DI,
        after=after,
    )


def scan_states(received, keeps, reverse, after=()):
    peers = received.shape[0]
    rows = STATE * DI // 128 // peers
    return pcall(
        partial(scan_kernel, reverse, rows),
        (1,),
        [full(received.shape), full(keeps.shape)],
        full((peers, rows, 128)),
        shape_of((peers, rows, 128)),
        [],
        (received, keeps),
        nbytes=8 * peers * rows * 128,
        after=after,
    )


def exchange(parts):
    return lax.all_to_all(parts, "seq", split_axis=0, concat_axis=0, tiled=True)


def shifted(value, steps):
    count = lax.axis_size("seq")
    first, last = max(0, -steps), min(count, count - steps)
    return lax.ppermute(value, "seq", [(source, source + steps) for source in range(first, last)])


def doc_table(lengths, first, count):
    starts = jnp.cumsum(lengths, -1) - lengths
    places = first + jnp.arange(count, dtype=jnp.int32)
    return jnp.sum((starts[None, :] <= places[:, None]).astype(jnp.int32), -1) - 1


def token_marks(lengths, span):
    docs_all = doc_table(lengths, lax.axis_index("seq") * span - HALO, span + 2 * HALO)
    docs = docs_all[HALO : HALO + span]
    ends = docs_all[HALO - 1 : HALO + span : GROUP]
    prior, final = jnp.repeat(ends[:-1], GROUP), jnp.repeat(ends[1:], GROUP)
    near = lambda step: docs_all[HALO + step : HALO + step + span] == docs
    marks = [near(-3), near(-2), near(-1), docs == prior, docs == final, docs, near(1), near(2), near(3)]
    marks = jnp.stack([mark.astype(jnp.float32) for mark in marks], 1)
    aux = jnp.pad(marks, ((0, 0), (0, 128 - marks.shape[1])))
    auxr = jnp.broadcast_to(docs.astype(jnp.float32)[None, :], (8, span))
    return aux, auxr


def halving(count, rows):
    def seq_masks(odd):
        masks = [rows << bit for bit in range(count.bit_length() - 1)]
        return masks[1::-1] + masks[2:] if odd else masks

    return [1 << bit for bit in range(rows.bit_length() - 1)], seq_masks(False), seq_masks(True)


def slab_order():
    count, rows = lax.axis_size("seq"), lax.axis_size("rows")
    row_masks, even, odd = halving(count, rows)
    stages = len(row_masks) + len(even)
    place = jnp.arange(count * rows, dtype=jnp.int32)
    bit = lambda stage: (place >> (stages - 1 - stage)) & 1
    slab = lax.axis_index("seq") * rows + lax.axis_index("rows") + 0 * place
    for stage, mask in enumerate(row_masks):
        slab = slab ^ (bit(stage) * mask)
    swapped = slab & 1
    for at, (one, two) in enumerate(zip(even, odd)):
        slab = slab ^ (bit(len(row_masks) + at) * jnp.where(swapped == 1, two, one))
    return slab


def in_order(values, order):
    width = values.shape[1]
    size = width // order.shape[0]
    source = (order[:, None] * size + jnp.arange(size, dtype=jnp.int32)[None, :]).reshape(-1)
    pick = (jnp.arange(width, dtype=jnp.int32)[:, None] == source[None, :]).astype(jnp.bfloat16)
    return jnp.dot(values, pick, preferred_element_type=jnp.float32).astype(jnp.bfloat16)


class Scatter:

    def __init__(self, left, right):
        half = left.shape[1] // 2
        self.send = matmul_tn(left[:, half:], right)
        self.keep = matmul_tn(left[:, :half], right)
        count, rows = lax.axis_size("seq"), lax.axis_size("rows")
        row_masks, even, odd = halving(count, rows)
        self.devices = count * rows
        self.stages = [(mask, mask) for mask in row_masks] + list(zip(even, odd))
        self.share()

    def share(self):
        masks = self.stages.pop(0)
        self.got = lax.ppermute(self.send, AXES, [(at, at ^ masks[at & 1]) for at in range(self.devices)])

    def step(self):
        if not self.stages:
            if self.got is not None:
                self.keep = self.keep + self.got
            self.got = None
            return (self.keep,)
        half = self.keep.shape[0] // 2
        self.send = self.keep[half:] + self.got[half:]
        self.keep = self.keep[:half] + self.got[:half]
        self.share()
        return (self.send, self.keep)

    def result(self):
        while self.got is not None:
            self.step()
        return self.keep


def steps(*scatters):
    return sum((scatter.step() for scatter in scatters), ())


def matmul(a, b):
    return jnp.dot(a, b, preferred_element_type=jnp.float32)


def matmul_tn(a, b):
    return jnp.einsum("tn,tm->nm", a, b, preferred_element_type=jnp.float32)


def matmul_nt(a, b):
    return jnp.einsum("tn,mn->tm", a, b, preferred_element_type=jnp.float32)


def normalise(values, gain):
    scale = lax.rsqrt(jnp.mean(values * values, -1, keepdims=True) + EPS)
    return (values * scale * gain).astype(jnp.bfloat16)


def normalise_back(values, gain, grad):
    scale = lax.rsqrt(jnp.mean(values * values, -1, keepdims=True) + EPS)
    gain_grad = jnp.sum(grad * values * scale, 0)
    pulled = grad * gain
    return scale * pulled - values * (scale**3 * jnp.mean(pulled * values, -1, keepdims=True)), gain_grad


def padded(rows, width):
    table = jnp.stack([jnp.pad(row, (0, width - row.shape[0])) for row in rows])
    return jnp.pad(table, ((0, 8 - len(rows)), (0, 0)))


def local(
    inputs,
    lengths,
    norm_gain,
    in_weight,
    conv_weight,
    conv_bias,
    log_decay,
    dt_bias,
    skip,
    gate_gain,
    out_weight,
    cotangent,
):
    _, span, width = inputs.shape
    peers = lax.axis_size("seq")
    aux, auxr = token_marks(lengths[0], span)
    order = slab_order()
    hidden = inputs[0]
    saved = []
    for depth in range(LAYERS):
        conv = jnp.concatenate([conv_weight[depth].T, conv_bias[depth][None], jnp.zeros((3, CHANNELS), jnp.float32)])
        hp = padded([dt_bias[depth], -jnp.exp(log_decay[depth])], 128)
        ch = padded([jnp.repeat(skip[depth], HEAD_DIM), gate_gain[depth]], DI)
        gate_weight = in_weight[depth][:, :DI]
        mixed_weight = in_weight[depth][:, DI : DI + CHANNELS]
        rate_weight = jnp.pad(in_weight[depth][:, DI + CHANNELS :], ((0, 0), (0, 128 - HEADS)))
        before = shifted(hidden[span - HALO :], 1)
        normed = normalise(hidden, norm_gain[depth])
        normed_ext = jnp.concatenate([normalise(before, norm_gain[depth]), normed])
        mixed_ext = matmul(normed_ext, mixed_weight)
        rate = matmul(normed, rate_weight)
        gate = matmul(normed, gate_weight)
        values, bc, col, cumr, made, kx, pay = make_states(peers, mixed_ext, rate, aux, conv, hp)
        received = exchange(pay)
        yi = inner(bc, values, col, cumr, aux, auxr)
        keeps = received[:, -8:]
        state_in = exchange(scan_states(received, keeps, False)).reshape(DI // 128, STATE, 128)
        y, out_low = finish(yi, values, gate, bc, col, state_in, made, kx, ch)
        saved.append(
            (hidden, normed, mixed_ext, rate, gate, values, bc, col, cumr, made, kx, keeps, state_in, y, out_low, yi)
            + (conv, hp, ch, gate_weight, mixed_weight, rate_weight)
        )
        hidden = hidden + matmul(out_low, out_weight[depth])
    gradient = cotangent[0]
    collected = [None] * LAYERS
    parts = [None] * LAYERS
    earlier = None
    for depth in reversed(range(LAYERS)):
        entry, normed, mixed_ext, rate, gate, values, bc, col, cumr, made, kx, keeps, state_in, y, out_low, yi = saved[depth][:16]
        conv, hp, ch, gate_weight, mixed_weight, rate_weight = saved[depth][16:]
        grad_low = gradient.astype(jnp.bfloat16)
        dno = matmul_nt(grad_low, out_weight[depth])
        waits = () if earlier is None else steps(*earlier[:2])
        dy, dgate, gate_sums, d1, pay = gate_back(peers, dno, y, gate, values, bc, col, kx, ch, after=waits)
        received = exchange(pay)
        normed_sorted = in_order(normed, order)
        if earlier is not None:
            parts[depth + 1] = earlier = earlier[:2] + (Scatter(normed_sorted_before, dmixed),)
        out_part = Scatter(in_order(out_low, order), grad_low)
        gate_part = Scatter(normed_sorted, dgate)
        waits = (out_part.send, out_part.keep, gate_part.send, gate_part.keep)
        if earlier is not None:
            waits += (earlier[2].send, earlier[2].keep) + steps(*earlier[:2])
        scanned = scan_states(received, keeps, True, after=waits)
        dso = exchange(scanned).reshape(DI // 128, STATE, 128)
        waits = steps(out_part, gate_part)
        if earlier is not None:
            waits += steps(earlier[2])
        xi, dbc = inner_back(bc, values, dy, col, cumr, aux, auxr, after=waits)
        waits = () if earlier is None else steps(*earlier)
        dconv, dconv_bc, drate, head_rows = states_back(
            xi, values, dy, yi, mixed_ext, bc, col, dso, state_in, made, d1, kx, dbc, aux, conv, ch, hp, rate,
            after=waits,
        )
        following = shifted(jnp.concatenate([dconv[:HALO], dconv_bc[:HALO]], 1), -1)
        waits = steps(out_part, gate_part) + (() if earlier is None else steps(earlier[2]))
        dmixed, conv_sums = conv_back(dconv, dconv_bc, following, mixed_ext, aux, conv, after=waits)
        dmixed = jnp.concatenate([dmixed, drate[:, :HEADS]], 1)
        normed_sorted_before = normed_sorted
        earlier = (out_part, gate_part)
        parts[depth] = earlier
        if depth == 0:
            parts[depth] = earlier + (Scatter(normed_sorted, dmixed),)
        grad_normed = matmul_nt(dgate, gate_weight) + matmul_nt(dmixed, in_weight[depth][:, DI:])
        grad_hidden, gain_grad = normalise_back(entry, norm_gain[depth], grad_normed)
        gradient = gradient + grad_hidden
        collected[depth] = (
            gain_grad,
            conv_sums[:KW].T,
            conv_sums[KW],
            gate_sums[0],
            head_rows[1, :HEADS],
            head_rows[0, :HEADS],
            jnp.sum(gate_sums[1].reshape(HEADS, HEAD_DIM), 1),
        )
    big_out = [trio[0].result() for trio in parts]
    big_in = [jnp.concatenate([trio[1].result(), trio[2].result()], 1) for trio in parts]
    devices = lax.axis_size(AXES)
    shares = [part.reshape(devices, -1) for sums in collected for part in sums[:4]]
    heads = jnp.concatenate([part for sums in collected for part in sums[4:]])
    table = jnp.concatenate(shares + [jnp.broadcast_to(heads, (devices,) + heads.shape)], 1)
    table = jnp.pad(table, ((0, 0), (0, -table.shape[1] % 128)))
    table = lax.all_to_all(table, AXES, split_axis=0, concat_axis=0, tiled=True).reshape(devices, -1, 128)
    table = pcall(
        total_kernel,
        (1,),
        [full(table.shape)],
        full(table.shape[1:]),
        shape_of(table.shape[1:]),
        [],
        (table,),
        after=tuple(big_in + big_out),
    ).reshape(-1)
    small = []
    at = 0
    for sums in collected:
        row = []
        for part in sums[:4]:
            size = part.size // devices
            row.append(table[at : at + size].reshape((part.shape[0] // devices,) + part.shape[1:]))
            at += size
        small.append(row)
    for row in small:
        for _ in range(3):
            row.append(table[at : at + HEADS])
            at += HEADS
    stacked = [jnp.stack([small[level][member] for level in range(LAYERS)]) for member in range(7)]
    norm_gain_grad, conv_w_grad, conv_b_grad, gain_grad, decay_grad, bias_grad, skip_grad = stacked
    return (
        hidden[None],
        gradient[None],
        norm_gain_grad,
        jnp.stack(big_in),
        conv_w_grad,
        conv_b_grad,
        decay_grad,
        bias_grad,
        skip_grad,
        gain_grad,
        jnp.stack(big_out),
    )


def solution(mesh):
    in_specs = (
        P("rows", "seq", None),
        P("rows", None),
        P(),
        P(),
        P(),
        P(),
        P(),
        P(),
        P(),
        P(),
        P(),
        P("rows", "seq", None),
    )
    out_specs = (
        P("rows", "seq", None),
        P("rows", "seq", None),
        P(None, ("seq", "rows")),
        P(None, ("seq", "rows"), None),
        P(None, ("seq", "rows"), None),
        P(None, ("seq", "rows")),
        P(),
        P(),
        P(),
        P(None, ("seq", "rows")),
        P(None, ("seq", "rows"), None),
    )
    return jax.shard_map(local, mesh=mesh, in_specs=in_specs, out_specs=out_specs, check_vma=False)
```

time: 970 us -> 806 us (0.83)
  Pallas kernels: 274 us -> 164 us
  waiting for transfers between devices: 193 us -> 127 us
  blocking collectives: 66.9 us -> 33.2 us
  local copies, waits for them, and re-layouts: 98 us -> 118 us
  starting transfers between devices: 80.6 us -> 99.7 us
  matrix products: 136 us -> 146 us
    pallas_call x18 -> x19, Pallas kernels: 274 us -> 164 us  [pcall(): pl.pallas_call(run, grid=grid, in_specs=list(in_specs) + [pl.BlockSpec(me...]
    all_to_all x1, waiting for transfers between devices: 78.7 us -> 6.76 us  [local(): lax.all_to_all(table, AXES, split_axis=0, concat_axis=0, tiled=True)]
    all_to_all x2 -> x1, blocking collectives: 66.9 us -> 33.2 us  [exchange(): return lax.all_to_all(parts, 'seq', split_axis=0, concat_axis=0, tiled=True)]
    all_to_all x6 -> x7, waiting for transfers between devices: 21.1 us -> 39.1 us  [exchange(): return lax.all_to_all(parts, 'seq', split_axis=0, concat_axis=0, tiled=True)]
    slice x2 -> x5, local copies, waits for them, and re-layouts: 1.38 us -> 15.2 us  [step(): self.keep = self.keep[:half] + self.got[:half]]
    unnamed x275 -> x279, local copies, waits for them, and re-layouts: 44.8 us -> 57.4 us
    ppermute x20 -> x30, starting transfers between devices: 27.4 us -> 39 us  [share(): lax.ppermute(self.send, AXES, [(at, at ^ masks[at & 1]) for at in range(s...]
    all_to_all x6 -> x7, starting transfers between devices: 37.6 us -> 46.8 us  [exchange(): return lax.all_to_all(parts, 'seq', split_axis=0, concat_axis=0, tiled=True)]
  transfers between devices with their start and end apart: 31 -> 42, of which waited for: 11 -> 13; matrix products, arithmetic and copies ran while one was open for 27% -> 38% of each run, Pallas kernels for 19% -> 13%
where the time goes in v4:
time: 806 us; the launch traced here: 797 us
  Pallas kernels  164 us (20%)
  matrix products  146 us (18%)
  waiting for transfers between devices  127 us (16%)
  local copies, waits for them, and re-layouts  118 us (15%)
  other arithmetic  107 us (13%)
  starting transfers between devices  99.7 us (12%)
  blocking collectives  33.2 us (4%)
    pallas_call x19, Pallas kernels, pcall(): pl.pallas_call(run, grid=grid, in_specs=list(in_specs) + [pl.BlockSpec(me...  164 us
    ppermute x30, waiting for transfers between devices, share(): lax.ppermute(self.send, AXES, [(at, at ^ masks[at & 1]) for at in range(s...  80.9 us
    add x18, other arithmetic, step(): self.keep = self.keep[:half] + self.got[:half]  68 us
    unnamed x279, local copies, waits for them, and re-layouts  57.4 us
    dot_general x12, matrix products, matmul_tn(): return jnp.einsum('tn,tm->nm', a, b, preferred_element_type=jnp.float32)  49.9 us
    all_to_all x7, starting transfers between devices, exchange(): return lax.all_to_all(parts, 'seq', split_axis=0, concat_axis=0, tiled=True)  46.8 us
    dot_general x8, matrix products, matmul(): return jnp.dot(a, b, preferred_element_type=jnp.float32)  41.4 us
    all_to_all x7, waiting for transfers between devices, exchange(): return lax.all_to_all(parts, 'seq', split_axis=0, concat_axis=0, tiled=True)  39.1 us
  transfers between devices with their start and end apart: 42, of which 13 were waited for; matrix products, arithmetic and copies ran while one was open for 38% of the time, Pallas kernels for 13%

profile of v4, /device:TPU:1, one launch (start us, length us, event | category | flops | bytes accessed | tf_op | source)
XLA Modules:
  0.0 796.6 jit_solution(1298825946543141217)
XLA Ops:
  8.1 10.2 %slice_bitcast_fusion = (bf16[1024,4384]{0,1:T(8,128)(2,1)}, bf16[1024,4384]{0,1:T(8,128)(2,1)S(1)}) fusion(bf16[2,1024,4384]{1,2,0:T(8,128)(2,1)} %param.15), kind=kLoop, calls=%fused_computation.3 | loop fusion | bytes 35913728 | tf_op jit(solution)/shard_map/squeeze | solution.py:866
  22.2 7.2 fusion.10.refs_0_.refs_1_.refs_4_.refs_5_.refs_3_
  29.5 9.8 %shard_map.203 = (f32[512,2048]{1,0:T(8,128)}, f32[512,256]{1,0:T(8,128)S(1)}, f32[4,512,128]{2,1,0:T(8,128)S(1)}, f32[128,512]{1,0:T(8,128)S(1)}, f32[128,2048]...) custom-call(f32[520,2304]{1,0:T(8,128)} %fusion.10.refs_0_.refs_1_.refs_4_.refs_5_.refs_3_, ...), custom_call_target="tpu_custom_call" | custom-call | flops 268435456 | bytes 12582912 | tf_op jit(solution)/shard_map/pallas_call | solution.py:39
  40.2 33.2 %all_to_all.49.refs_0_ = f32[16,136,128]{2,1,0:T(8,128)S(1)} all-to-all(f32[16,136,128]{2,1,0:T(8,128)S(1)} %get-tuple-element.59), channel_id=1, replica_groups=mesh['seq'=16,'rows'=2] {'seq'}, dimensions={0} | all-to-all | bytes 2228224 | tf_op jit(solution)/shard_map/all_to_all | solution.py:715
  80.9 7.0 fusion.28.refs_2_
  87.9 6.8 shard_map.204.refs_0_.refs_3_
  94.7 6.1 all-to-all-done.1.refs_5_.refs_9_
  102.4 8.3 %shard_map.206 = (f32[512,2048]{1,0:T(8,128)}, bf16[512,2048]{1,0:T(8,128)(2,1)S(1)}) custom-call(f32[512,2048]{1,0:T(8,128)} %shard_map.204.refs_0_.refs_3_, f32[512,2048]{1,0:T(8,128)} %get-tuple-element.56.refs_1_.refs_3_, f32[512,2048]{1,0:T(8,128)} %fusion.28.refs_2_, f32[512,256]{1,0:T(8,128)S(1)} %get-tuple-element.55.refs_0_.refs_3_.refs_4_.refs_6_, ...), custom_call_target="tpu_custom_call" | custom-call | flops 268435456 | bytes 18874368 | tf_op jit(solution)/shard_map/pallas_call | solution.py:39
  110.7 5.4 multiply_reduce_fusion.2
  119.2 7.3 fusion.8.refs_0_.refs_1_.refs_4_.refs_5_.refs_3_
  126.5 9.8 %shard_map.207 = (f32[512,2048]{1,0:T(8,128)}, f32[512,256]{1,0:T(8,128)S(1)}, f32[4,512,128]{2,1,0:T(8,128)S(1)}, f32[128,512]{1,0:T(8,128)S(1)}, f32[128,2048]...) custom-call(f32[520,2304]{1,0:T(8,128)} %fusion.8.refs_0_.refs_1_.refs_4_.refs_5_.refs_3_, ...), custom_call_target="tpu_custom_call" | custom-call | flops 268435456 | bytes 12582912 | tf_op jit(solution)/shard_map/pallas_call | solution.py:39
  139.5 9.3 %all-to-all-start.2 = ((f32[16,136,128]{2,1,0:T(8,128)}), f32[16,136,128]{2,1,0:T(8,128)}, u32[]{:S(2)}, u32[]{:S(2)}) async-start(f32[16,136,128]{2,1,0:T(8,128)} %copy-done.27), calls=%async_computation.2 | async-start | bytes 2228224 | tf_op jit(solution)/shard_map/all_to_all | solution.py:715
  150.0 21.5 %all-to-all-done.2.refs_0_ = f32[16,136,128]{2,1,0:T(8,128)} async-done(((f32[16,136,128]{2,1,0:T(8,128)}), f32[16,136,128]{2,1,0:T(8,128)}, u32[]{:S(2)}, u32[]{:S(2)}) %all-to-all-start.2) | async-done | bytes 1114144 | tf_op jit(solution)/shard_map/all_to_all | solution.py:715
  175.3 9.1 %all-to-all-start.3 = ((f32[16,128,128]{2,1,0:T(8,128)}), f32[16,128,128]{2,1,0:T(8,128)}, u32[]{:S(2)}, u32[]{:S(2)}) async-start(f32[16,128,128]{2,1,0:T(8,128)} %copy-done.18), calls=%async_computation.3 | async-start | bytes 2097152 | tf_op jit(solution)/shard_map/all_to_all | solution.py:715
  191.3 7.4 fusion.12.refs_0_
  200.9 6.6 fusion.24.refs_2_
  207.5 6.7 shard_map.208.refs_0_.refs_3_
  217.2 8.5 %shard_map.210 = (f32[512,2048]{1,0:T(8,128)}, bf16[512,2048]{1,0:T(8,128)(2,1)S(1)}) custom-call(f32[512,2048]{1,0:T(8,128)} %shard_map.208.refs_0_.refs_3_, f32[512,2048]{1,0:T(8,128)} %get-tuple-element.64.refs_1_.refs_3_, f32[512,2048]{1,0:T(8,128)} %fusion.24.refs_2_, f32[512,256]{1,0:T(8,128)S(1)} %get-tuple-element.63.refs_0_.refs_3_.refs_4_.refs_6_, ...), custom_call_target="tpu_custom_call" | custom-call | flops 268435456 | bytes 18874368 | tf_op jit(solution)/shard_map/pallas_call | solution.py:39
  225.7 11.5 %shard_map.211 = (f32[512,2048]{1,0:T(8,128)}, bf16[512,2048]{1,0:T(8,128)(2,1)S(1)}, f32[8,2048]{1,0:T(8,128)S(1)}, f32[128,2048]{1,0:T(8,128)S(1)}, f32[16,128,128]{2,1,0:T(8,128)S(1)}) custom-call(f32[512,2048]{1,0:T(8,128)} %fusion.12.refs_0_, f32[512,2048]{1,0:T(8,128)} %get-tuple-element.71.refs_1_, f32[512,2048]{1,0:T(8,128)} %fusion.24.refs_2_, ...), custom_call_target="tpu_custom_call" | custom-call | flops 268435456 | bytes 23068672 | tf_op jit(solution)/shard_map/pallas_call | solution.py:39
  242.7 5.1 fusion.34
  251.1 6.8 all-to-all-start.4
  268.4 11.5 %all-to-all-done.4.refs_0_ = f32[16,128,128]{2,1,0:T(8,128)} async-done(((f32[16,128,128]{2,1,0:T(8,128)}), f32[16,128,128]{2,1,0:T(8,128)}, u32[]{:S(2)}, u32[]{:S(2)}) %all-to-all-start.4) | async-done | bytes 1048608 | tf_op jit(solution)/shard_map/all_to_all | solution.py:715
  283.0 7.6 all-to-all-start.5
  290.7 6.7 slice_add_fusion.7
  298.8 5.3 slice_add_fusion.9
  304.3 5.8 fusion.35
  310.1 5.9 fusion.22
  316.1 9.8 %shard_map.212 = (f32[512,2048]{1,0:T(8,128)}, f32[512,256]{1,0:T(8,128)S(1)}) custom-call(f32[512,256]{1,0:T(8,128)S(1)} %get-tuple-element.63.refs_0_.refs_3_.refs_4_.refs_6_, f32[512,2048]{1,0:T(8,128)} %get-tuple-element.64.refs_1_.refs_3_, f32[512,2048]{1,0:T(8,128)} %get-tuple-element.73.refs_2_, ...), custom_call_target="tpu_custom_call" | custom-call | flops 4294967296 | bytes 12582912 | tf_op jit(solution)/shard_map/pallas_call | solution.py:39
  330.3 22.2 %shard_map.214 = (f32[512,2048]{1,0:T(8,128)}, f32[512,256]{1,0:T(8,128)S(1)}, bf16[512,128]{1,0:T(8,128)(2,1)S(1)}, f32[8,128]{1,0:T(8,128)S(1)}) custom-call(f32[512,2048]{1,0:T(8,128)} %get-tuple-element.74.refs_0_, f32[512,2048]{1,0:T(8,128)} %get-tuple-element.64.refs_1_.refs_3_, f32[512,2048]{1,0:T(8,128)} %get-tuple-element.73.refs_2_, ...), custom_call_target="tpu_custom_call" | custom-call | flops 1073741824 | bytes 20971520 | tf_op jit(solution)/shard_map/pallas_call | solution.py:39
  362.8 11.5 %shard_map.215 = (bf16[512,2304]{1,0:T(8,128)(2,1)}, f32[8,2304]{1,0:T(8,128)S(1)}) custom-call(f32[512,2048]{1,0:T(8,128)} %get-tuple-element.78.refs_0_, f32[512,256]{1,0:T(8,128)S(1)} %get-tuple-element.79.refs_1_, f32[8,2304]{1,0:T(8,128)S(1)} %collective-permute-done.4.refs_2_, f32[520,2304]{1,0:T(8,128)} %fusion.8.refs_0_.refs_1_.refs_4_.refs_5_.refs_3_, ...), custom_call_target="tpu_custom_call" | custom-call | flops 8388608 | bytes 10485760 | tf_op jit(solution)/shard_map/pallas_call | solution.py:39
  374.4 5.4 fusion.77
  379.9 4.6 collective-permute-start.11
  384.5 6.2 multiply_reduce_fusion
  399.4 6.0 copy.81.refs_6_
  405.6 5.3 fusion.67.refs_3_
  410.9 6.7 fusion.16.refs_0_
  423.5 11.5 %shard_map.216 = (f32[512,2048]{1,0:T(8,128)}, bf16[512,2048]{1,0:T(8,128)(2,1)}, f32[8,2048]{1,0:T(8,128)S(1)}, f32[128,2048]{1,0:T(8,128)S(1)}, f32[16,128,128]{2,1,0:T(8,128)S(1)}) custom-call(f32[512,2048]{1,0:T(8,128)} %fusion.16.refs_0_, f32[512,2048]{1,0:T(8,128)} %get-tuple-element.82.refs_1_, f32[512,2048]{1,0:T(8,128)} %fusion.28.refs_2_, ...), custom_call_target="tpu_custom_call" | custom-call | flops 268435456 | bytes 23068672 | tf_op jit(solution)/shard_map/pallas_call | solution.py:39
  437.5 4.7 all-to-all-start.6
  442.3 5.0 fusion.80.refs_4_
  453.8 4.9 fusion.131
  465.0 6.6 slice_add_fusion
  476.2 5.1 fusion.83.refs_5_
  481.3 8.2 %collective-permute-done.14 = f32[64,1024]{1,0:T(8,128)} collective-permute-done((f32[64,1024]{1,0:T(8,128)S(1)}, f32[64,1024]{1,0:T(8,128)}, u32[]{:S(2)}, u32[]{:S(2)}) %collective-permute-start.14) | collective-permute-done | bytes 262176 | tf_op jit(solution)/shard_map/ppermute | solution.py:788
  495.4 5.1 all-to-all-start.7
  500.5 7.0 slice_add_fusion.5
  509.1 5.4 slice_add_fusion.3
  514.5 9.8 %shard_map.217 = (f32[512,2048]{1,0:T(8,128)}, f32[512,256]{1,0:T(8,128)S(1)}) custom-call(f32[512,256]{1,0:T(8,128)S(1)} %get-tuple-element.55.refs_0_.refs_3_.refs_4_.refs_6_, f32[512,2048]{1,0:T(8,128)} %get-tuple-element.56.refs_1_.refs_3_, f32[512,2048]{1,0:T(8,128)} %get-tuple-element.84.refs_2_, ...), custom_call_target="tpu_custom_call" | custom-call | flops 4294967296 | bytes 12582912 | tf_op jit(solution)/shard_map/pallas_call | solution.py:39
  546.1 22.1 %shard_map.219 = (f32[512,2048]{1,0:T(8,128)}, f32[512,256]{1,0:T(8,128)S(1)}, bf16[512,128]{1,0:T(8,128)(2,1)S(1)}, f32[8,128]{1,0:T(8,128)S(1)}) custom-call(f32[512,2048]{1,0:T(8,128)} %get-tuple-element.85.refs_0_, f32[512,2048]{1,0:T(8,128)} %get-tuple-element.56.refs_1_.refs_3_, f32[512,2048]{1,0:T(8,128)} %get-tuple-element.84.refs_2_, ...), custom_call_target="tpu_custom_call" | custom-call | flops 1073741824 | bytes 20971520 | tf_op jit(solution)/shard_map/pallas_call | solution.py:39
  586.6 11.2 %shard_map.220 = (bf16[512,2304]{1,0:T(8,128)(2,1)}, f32[8,2304]{1,0:T(8,128)S(1)}) custom-call(f32[512,2048]{1,0:T(8,128)} %get-tuple-element.89.refs_0_, f32[512,256]{1,0:T(8,128)S(1)} %copy-done.51, f32[8,2304]{1,0:T(8,128)S(1)} %collective-permute-done.17.refs_2_, f32[520,2304]{1,0:T(8,128)} %fusion.10.refs_0_.refs_1_.refs_4_.refs_5_.refs_3_, ...), custom_call_target="tpu_custom_call" | custom-call | flops 8388608 | bytes 10485760 | tf_op jit(solution)/shard_map/pallas_call | solution.py:39
  597.8 5.3 fusion.75
  603.0 5.3 collective-permute-start.24
  610.2 7.1 add_bitcast_fusion
  617.5 6.4 collective-permute-done.31
  630.8 8.5 %collective-permute-done.32 = f32[128,1024]{1,0:T(8,128)} collective-permute-done((f32[128,1024]{1,0:T(8,128)}, f32[128,1024]{1,0:T(8,128)}, u32[]{:S(2)}, u32[]{:S(2)}) %collective-permute-start.32) | collective-permute-done | bytes 524320 | tf_op jit(solution)/shard_map/ppermute | solution.py:788
  646.2 9.0 %collective-permute-done.33 = f32[64,1024]{1,0:T(8,128)} collective-permute-done((f32[64,1024]{1,0:T(8,128)S(1)}, f32[64,1024]{1,0:T(8,128)}, u32[]{:S(2)}, u32[]{:S(2)}) %collective-permute-start.33) | collective-permute-done | bytes 262176 | tf_op jit(solution)/shard_map/ppermute | solution.py:788
  660.5 5.0 fusion.4
  665.5 5.9 fusion.130
  672.3 6.2 fusion.44
  682.7 5.3 all-to-all-start.8
  688.1 4.7 fusion.42
  696.4 6.8 all-to-all-done.8
  734.7 16.5 %collective-permute-done.23 = f32[32,2048]{1,0:T(8,128)S(1)} collective-permute-done((f32[32,2048]{1,0:T(8,128)S(1)}, f32[32,2048]{1,0:T(8,128)S(1)}, u32[]{:S(2)}, u32[]{:S(2)}) %collective-permute-start.23) | collective-permute-done | bytes 262176 | tf_op jit(solution)/shard_map/ppermute | solution.py:788
  761.1 12.3 %collective-permute-done.27 = f32[64,2336]{1,0:T(8,128)S(1)} collective-permute-done((f32[64,2336]{1,0:T(8,128)S(1)}, f32[64,2336]{1,0:T(8,128)S(1)}, u32[]{:S(2)}, u32[]{:S(2)}) %collective-permute-start.27) | collective-permute-done | bytes 598048 | tf_op jit(solution)/shard_map/ppermute | solution.py:788
  773.7 16.7 %collective-permute-done.28 = f32[32,2336]{1,0:T(8,128)S(1)} collective-permute-done((f32[32,2336]{1,0:T(8,128)S(1)}, f32[32,2336]{1,0:T(8,128)S(1)}, u32[]{:S(2)}, u32[]{:S(2)}) %collective-permute-start.28) | collective-permute-done | bytes 299040 | tf_op jit(solution)/shard_map/ppermute | solution.py:788
  (503 shorter events, 242.7 us)
Async XLA Ops:
  1.5 20.5 %collective-permute-start = (f32[8,1024]{1,0:T(8,128)S(1)}, f32[8,1024]{1,0:T(8,128)S(1)}, u32[]{:S(2)}, u32[]{:S(2)}) collective-permute-start(f32[8,1024]{1,0:T(8,128)S(1)} %slice_bitcast_fusion.6), channel_id=1, source_target_pairs={{0,2},{2,4},{4,6},{6,8},{8,10},{10,12},{12,14},{14,16},{16,18},{18... | collective-permute-start | bytes 98312 | tf_op jit(solution)/shard_map/ppermute | solution.py:721
  7.3 11.0 %copy-start.112 = (f32[512]{0:T(512)}, f32[512]{0:T(512)S(1)}, u32[]{:S(2)}) copy-start(f32[512]{0:T(512)S(1)} %fusion.36) | copy-start | bytes 6148
  8.0 14.2 %copy-start.108 = (f32[1,1024]{1,0:T(1,128)}, f32[1,1024]{1,0:T(1,128)S(1)}, u32[]{:S(2)}) copy-start(f32[1,1024]{1,0:T(1,128)S(1)} %get-tuple-element.196) | copy-start | bytes 12292
  8.0 111.1 %copy-start.110 = (f32[1,1024]{1,0:T(1,128)}, f32[1,1024]{1,0:T(1,128)S(1)}, u32[]{:S(2)}) copy-start(f32[1,1024]{1,0:T(1,128)S(1)} %get-tuple-element.195) | copy-start | bytes 12292
  18.7 10.8 %copy-start.96 = (bf16[512,1024]{1,0:T(8,128)(2,1)}, bf16[512,1024]{1,0:T(8,128)(2,1)S(1)}, u32[]{:S(2)}) copy-start(bf16[512,1024]{1,0:T(8,128)(2,1)S(1)} %fusion.38) | copy-start | bytes 3145732
  40.2 33.2 %copy-start.30 = (f32[128,512]{1,0:T(8,128)}, f32[128,512]{1,0:T(8,128)S(1)}, u32[]{:S(2)}) copy-start(f32[128,512]{1,0:T(8,128)S(1)} %get-tuple-element.58.refs_3_.refs_4_) | copy-start | bytes 786436
  40.2 60.6 %copy-start.40 = (f32[8,2048]{1,0:T(8,128)}, f32[8,2048]{1,0:T(8,128)S(1)}, u32[]{:S(2)}) copy-start(f32[8,2048]{1,0:T(8,128)S(1)} %get-tuple-element.61.refs_7_.refs_6_.refs_12_) | copy-start | bytes 196612
  74.5 26.3 %all-to-all-start.1 = ((f32[16,128,128]{2,1,0:T(8,128)}), f32[16,128,128]{2,1,0:T(8,128)S(1)}, u32[]{:S(2)}, u32[]{:S(2)}) async-start(f32[16,128,128]{2,1,0:T(8,128)} %copy-done.17), calls=%async_computation.1 | async-start | bytes 2097152 | tf_op jit(solution)/shard_map/all_to_all | solution.py:715
  116.1 2.8 collective-permute-start.1
  139.5 31.9 %all-to-all-start.2 = ((f32[16,136,128]{2,1,0:T(8,128)}), f32[16,136,128]{2,1,0:T(8,128)}, u32[]{:S(2)}, u32[]{:S(2)}) async-start(f32[16,136,128]{2,1,0:T(8,128)} %copy-done.27), calls=%async_computation.2 | async-start | bytes 2228224 | tf_op jit(solution)/shard_map/all_to_all | solution.py:715
  172.3 13.4 %copy-start.126 = (f32[32]{0:T(128)S(1)}, f32[32]{0:T(128)}, u32[]{:S(2)}) copy-start(f32[32]{0:T(128)} %get-tuple-element.209) | copy-start | bytes 388
  175.3 39.0 %all-to-all-start.3 = ((f32[16,128,128]{2,1,0:T(8,128)}), f32[16,128,128]{2,1,0:T(8,128)}, u32[]{:S(2)}, u32[]{:S(2)}) async-start(f32[16,128,128]{2,1,0:T(8,128)} %copy-done.18), calls=%async_computation.3 | async-start | bytes 2097152 | tf_op jit(solution)/shard_map/all_to_all | solution.py:715
  225.7 17.0 %copy-start.69 = (bf16[512,2048]{1,0:T(8,128)(2,1)}, bf16[512,2048]{1,0:T(8,128)(2,1)S(1)}, u32[]{:S(2)}) copy-start(bf16[512,2048]{1,0:T(8,128)(2,1)S(1)} %get-tuple-element.70) | copy-start | bytes 6291460
  225.7 11.5 %copy-start.101 = (bf16[512,1024]{1,0:T(8,128)(2,1)S(1)}, bf16[512,1024]{1,0:T(8,128)(2,1)}, u32[]{:S(2)}) copy-start(bf16[512,1024]{1,0:T(8,128)(2,1)} %fusion.57) | copy-start | bytes 3145732
  240.5 50.1 %collective-permute-start.3 = (f32[512,2048]{1,0:T(8,128)}, f32[512,2048]{1,0:T(8,128)}, u32[]{:S(2)}, u32[]{:S(2)}) collective-permute-start(f32[512,2048]{1,0:T(8,128)} %fusion.86.refs_4_), channel_id=1, source_target_pairs={{0,1},{1,0},{2,3},{3,2},{4,5},{5,4},{6,7},{7,6},{8,9},{9,8},{10,11... | collective-permute-start | bytes 12582920 | tf_op jit(solution)/shard_map/ppermute | solution.py:788
  251.0 47.8 %collective-permute-start.2 = (f32[1024,1024]{1,0:T(8,128)}, f32[1024,1024]{1,0:T(8,128)}, u32[]{:S(2)}, u32[]{:S(2)}) collective-permute-start(f32[1024,1024]{1,0:T(8,128)} %fusion.69.refs_2_), channel_id=1, source_target_pairs={{0,1},{1,0},{2,3},{3,2},{4,5},{5,4},{6,7},{7,6},{8,9},{9,8},{10,11... | collective-permute-start | bytes 12582920 | tf_op jit(solution)/shard_map/ppermute | solution.py:788
  251.1 28.8 %all-to-all-start.4 = ((f32[16,128,128]{2,1,0:T(8,128)}), f32[16,128,128]{2,1,0:T(8,128)}, u32[]{:S(2)}, u32[]{:S(2)}) async-start(f32[16,128,128]{2,1,0:T(8,128)} %copy-done.39), calls=%async_computation.4 | async-start | bytes 2097152 | tf_op jit(solution)/shard_map/all_to_all | solution.py:715
  283.0 43.6 %all-to-all-start.5 = ((f32[16,128,128]{2,1,0:T(8,128)}), f32[16,128,128]{2,1,0:T(8,128)}, u32[]{:S(2)}, u32[]{:S(2)}) async-start(f32[16,128,128]{2,1,0:T(8,128)} %copy-done.13), calls=%async_computation.5 | async-start | bytes 2097152 | tf_op jit(solution)/shard_map/all_to_all | solution.py:715
  297.4 57.5 %collective-permute-start.6 = (f32[256,2048]{1,0:T(8,128)}, f32[256,2048]{1,0:T(8,128)}, u32[]{:S(2)}, u32[]{:S(2)}) collective-permute-start(f32[256,2048]{1,0:T(8,128)} %get-tuple-element.129.refs_9_), channel_id=1, source_target_pairs={{0,2},{1,5},{2,0},{3,7},{4,6},{5,1},{6,4},{7,3},{8,10},{9,13},{10,... | collective-permute-start | bytes 6291464 | tf_op jit(solution)/shard_map/ppermute | solution.py:788
  304.1 55.6 %collective-permute-start.5 = (f32[512,1024]{1,0:T(8,128)}, f32[512,1024]{1,0:T(8,128)}, u32[]{:S(2)}, u32[]{:S(2)}) collective-permute-start(f32[512,1024]{1,0:T(8,128)} %get-tuple-element.131.refs_7_), channel_id=1, source_target_pairs={{0,2},{1,5},{2,0},{3,7},{4,6},{5,1},{6,4},{7,3},{8,10},{9,13},{10,... | collective-permute-start | bytes 6291464 | tf_op jit(solution)/shard_map/ppermute | solution.py:788
  330.3 24.6 %copy-start.83 = (f32[256,2048]{1,0:T(8,128)S(1)}, f32[256,2048]{1,0:T(8,128)}, u32[]{:S(2)}) copy-start(f32[256,2048]{1,0:T(8,128)} %get-tuple-element.128.refs_10_) | copy-start | bytes 6291460
  353.4 9.4 %collective-permute-start.4 = (f32[8,2304]{1,0:T(8,128)S(1)}, f32[8,2304]{1,0:T(8,128)S(1)}, u32[]{:S(2)}, u32[]{:S(2)}) collective-permute-start(f32[8,2304]{1,0:T(8,128)S(1)} %pad_maximum_fusion.12), channel_id=1, source_target_pairs={{2,0},{4,2},{6,4},{8,6},{10,8},{12,10},{14,12},{16,14},{18,16},{20... | collective-permute-start | bytes 221192 | tf_op jit(solution)/shard_map/ppermute | solution.py:721
  357.6 59.9 %collective-permute-start.8 = (f32[128,2048]{1,0:T(8,128)}, f32[128,2048]{1,0:T(8,128)}, u32[]{:S(2)}, u32[]{:S(2)}) collective-permute-start(f32[128,2048]{1,0:T(8,128)} %get-tuple-element.144.refs_8_), channel_id=1, source_target_pairs={{0,4},{1,3},{2,6},{3,1},{4,0},{5,7},{6,2},{7,5},{8,12},{9,11},{10,... | collective-permute-start | bytes 3145736 | tf_op jit(solution)/shard_map/ppermute | solution.py:788
  362.8 11.6 %copy-start.3 = (f32[256,1024]{1,0:T(8,128)}, f32[256,1024]{1,0:T(8,128)S(1)}, u32[]{:S(2)}) copy-start(f32[256,1024]{1,0:T(8,128)S(1)} %get-tuple-element.145.refs_7_) | copy-start | bytes 3145732
  362.8 59.2 %collective-permute-start.7 = (f32[256,1024]{1,0:T(8,128)}, f32[256,1024]{1,0:T(8,128)}, u32[]{:S(2)}, u32[]{:S(2)}) collective-permute-start(f32[256,1024]{1,0:T(8,128)} %get-tuple-element.146.refs_6_), channel_id=1, source_target_pairs={{0,4},{1,3},{2,6},{3,1},{4,0},{5,7},{6,2},{7,5},{8,12},{9,11},{10,... | collective-permute-start | bytes 3145736 | tf_op jit(solution)/shard_map/ppermute | solution.py:788
  362.8 11.6 %copy-start.103 = (bf16[512,1024]{1,0:T(8,128)(2,1)S(1)}, bf16[512,1024]{1,0:T(8,128)(2,1)}, u32[]{:S(2)}) copy-start(bf16[512,1024]{1,0:T(8,128)(2,1)} %fusion.57) | copy-start | bytes 3145732
  379.8 10.8 %copy-start.123 = (f32[512]{0:T(512)S(1)}, f32[512]{0:T(512)}, u32[]{:S(2)}) copy-start(f32[512]{0:T(512)} %copy-done.122) | copy-start | bytes 6148
  379.9 10.9 %copy-start.81 = (f32[1,512,1024]{2,1,0:T(8,128)S(1)}, f32[1,512,1024]{2,1,0:T(8,128)}, u32[]{:S(2)}) copy-start(f32[1,512,1024]{2,1,0:T(8,128)} %param.23) | copy-start | bytes 6291460
  379.9 73.9 %collective-permute-start.11 = (f32[512,2336]{0,1:T(8,128)}, f32[512,2336]{0,1:T(8,128)}, u32[]{:S(2)}, u32[]{:S(2)}) collective-permute-start(f32[512,2336]{0,1:T(8,128)} %fusion.77), channel_id=1, source_target_pairs={{0,1},{1,0},{2,3},{3,2},{4,5},{5,4},{6,7},{7,6},{8,9},{9,8},{10,11... | collective-permute-start | bytes 14352392 | tf_op jit(solution)/shard_map/ppermute | solution.py:788
  405.3 95.2 %collective-permute-start.9 = (f32[1024,1024]{1,0:T(8,128)}, f32[1024,1024]{1,0:T(8,128)}, u32[]{:S(2)}, u32[]{:S(2)}) collective-permute-start(f32[1024,1024]{1,0:T(8,128)} %fusion.65.refs_2_), channel_id=1, source_target_pairs={{0,1},{1,0},{2,3},{3,2},{4,5},{5,4},{6,7},{7,6},{8,9},{9,8},{10,11... | collective-permute-start | bytes 12582920 | tf_op jit(solution)/shard_map/ppermute | solution.py:788
  419.8 28.8 %collective-permute-start.13 = (f32[64,2048]{1,0:T(8,128)}, f32[64,2048]{1,0:T(8,128)}, u32[]{:S(2)}, u32[]{:S(2)}) collective-permute-start(f32[64,2048]{1,0:T(8,128)} %get-tuple-element.160.refs_10_), channel_id=1, source_target_pairs={{0,8},{1,9},{2,10},{3,11},{4,12},{5,13},{6,14},{7,15},{8,0},{9,1},... | collective-permute-start | bytes 1572872 | tf_op jit(solution)/shard_map/ppermute | solution.py:788
  423.4 29.4 %collective-permute-start.12 = (f32[128,1024]{1,0:T(8,128)S(1)}, f32[128,1024]{1,0:T(8,128)}, u32[]{:S(2)}, u32[]{:S(2)}) collective-permute-start(f32[128,1024]{1,0:T(8,128)S(1)} %get-tuple-element.162.refs_8_), channel_id=1, source_target_pairs={{0,8},{1,9},{2,10},{3,11},{4,12},{5,13},{6,14},{7,15},{8,0},{9,1},... | collective-permute-start | bytes 1572872 | tf_op jit(solution)/shard_map/ppermute | solution.py:788
  437.5 55.6 %all-to-all-start.6 = ((f32[16,128,128]{2,1,0:T(8,128)}), f32[16,128,128]{2,1,0:T(8,128)}, u32[]{:S(2)}, u32[]{:S(2)}) async-start(f32[16,128,128]{2,1,0:T(8,128)} %copy-done.38), calls=%async_computation.6 | async-start | bytes 2097152 | tf_op jit(solution)/shard_map/all_to_all | solution.py:715
  447.3 61.8 %collective-permute-start.10 = (f32[512,2048]{1,0:T(8,128)}, f32[512,2048]{1,0:T(8,128)}, u32[]{:S(2)}, u32[]{:S(2)}) collective-permute-start(f32[512,2048]{1,0:T(8,128)} %fusion.80.refs_4_), channel_id=1, source_target_pairs={{0,1},{1,0},{2,3},{3,2},{4,5},{5,4},{6,7},{7,6},{8,9},{9,8},{10,11... | collective-permute-start | bytes 12582920 | tf_op jit(solution)/shard_map/ppermute | solution.py:788
  450.2 41.1 %collective-permute-start.15 = (f32[32,2048]{1,0:T(8,128)}, f32[32,2048]{1,0:T(8,128)}, u32[]{:S(2)}, u32[]{:S(2)}) collective-permute-start(f32[32,2048]{1,0:T(8,128)} %slice_add_fusion.44.refs_10_), channel_id=1, source_target_pairs={{0,16},{1,17},{2,18},{3,19},{4,20},{5,21},{6,22},{7,23},{8,24},{9,... | collective-permute-start | bytes 786440 | tf_op jit(solution)/shard_map/ppermute | solution.py:788
  453.7 35.8 %collective-permute-start.14 = (f32[64,1024]{1,0:T(8,128)S(1)}, f32[64,1024]{1,0:T(8,128)}, u32[]{:S(2)}, u32[]{:S(2)}) collective-permute-start(f32[64,1024]{1,0:T(8,128)S(1)} %slice_add_fusion.46.refs_8_), channel_id=1, source_target_pairs={{0,16},{1,17},{2,18},{3,19},{4,20},{5,21},{6,22},{7,23},{8,24},{9,... | collective-permute-start | bytes 786440 | tf_op jit(solution)/shard_map/ppermute | solution.py:788
  474.7 49.6 %collective-permute-start.16 = (f32[256,2336]{0,1:T(8,128)}, f32[256,2336]{0,1:T(8,128)}, u32[]{:S(2)}, u32[]{:S(2)}) collective-permute-start(f32[256,2336]{0,1:T(8,128)} %copy.83), channel_id=1, source_target_pairs={{0,2},{1,5},{2,0},{3,7},{4,6},{5,1},{6,4},{7,3},{8,10},{9,13},{10,... | collective-permute-start | bytes 7176200 | tf_op jit(solution)/shard_map/ppermute | solution.py:788
  481.3 11.8 %copy-start.47 = (f32[16,8,128]{2,1,0:T(8,128)S(1)}, f32[16,8,128]{2,1,0:T(8,128)}, u32[]{:S(2)}) copy-start(f32[16,8,128]{2,1,0:T(8,128)} %copy-done.46) | copy-start | bytes 196612
  495.4 47.9 %all-to-all-start.7 = ((f32[16,128,128]{2,1,0:T(8,128)}), f32[16,128,128]{2,1,0:T(8,128)}, u32[]{:S(2)}, u32[]{:S(2)}) async-start(f32[16,128,128]{2,1,0:T(8,128)} %shard_map.218), calls=%async_computation.7 | async-start | bytes 2097152 | tf_op jit(solution)/shard_map/all_to_all | solution.py:715
  507.6 31.6 %collective-permute-start.18 = (f32[512,1024]{1,0:T(8,128)}, f32[512,1024]{1,0:T(8,128)}, u32[]{:S(2)}, u32[]{:S(2)}) collective-permute-start(f32[512,1024]{1,0:T(8,128)} %get-tuple-element.127.refs_7_), channel_id=1, source_target_pairs={{0,2},{1,5},{2,0},{3,7},{4,6},{5,1},{6,4},{7,3},{8,10},{9,13},{10,... | collective-permute-start | bytes 6291464 | tf_op jit(solution)/shard_map/ppermute | solution.py:788
  514.4 59.4 %collective-permute-start.19 = (f32[256,2048]{1,0:T(8,128)}, f32[256,2048]{1,0:T(8,128)}, u32[]{:S(2)}, u32[]{:S(2)}) collective-permute-start(f32[256,2048]{1,0:T(8,128)} %get-tuple-element.125.refs_9_), channel_id=1, source_target_pairs={{0,2},{1,5},{2,0},{3,7},{4,6},{5,1},{6,4},{7,3},{8,10},{9,13},{10,... | collective-permute-start | bytes 6291464 | tf_op jit(solution)/shard_map/ppermute | solution.py:788
  537.7 39.3 %collective-permute-start.20 = (f32[128,2336]{0,1:T(8,128)}, f32[128,2336]{0,1:T(8,128)}, u32[]{:S(2)}, u32[]{:S(2)}) collective-permute-start(f32[128,2336]{0,1:T(8,128)} %copy.86), channel_id=1, source_target_pairs={{0,4},{1,3},{2,6},{3,1},{4,0},{5,7},{6,2},{7,5},{8,12},{9,11},{10,... | collective-permute-start | bytes 3588104 | tf_op jit(solution)/shard_map/ppermute | solution.py:788
  546.1 27.7 %copy-start.82 = (f32[256,2048]{1,0:T(8,128)S(1)}, f32[256,2048]{1,0:T(8,128)}, u32[]{:S(2)}) copy-start(f32[256,2048]{1,0:T(8,128)} %get-tuple-element.124.refs_10_) | copy-start | bytes 6291460
  569.2 16.5 %collective-permute-start.17 = (f32[8,2304]{1,0:T(8,128)S(1)}, f32[8,2304]{1,0:T(8,128)S(1)}, u32[]{:S(2)}, u32[]{:S(2)}) collective-permute-start(f32[8,2304]{1,0:T(8,128)S(1)} %pad_maximum_fusion.13), channel_id=1, source_target_pairs={{2,0},{4,2},{6,4},{8,6},{10,8},{12,10},{14,12},{16,14},{18,16},{20... | collective-permute-start | bytes 221192 | tf_op jit(solution)/shard_map/ppermute | solution.py:721
  586.6 11.2 %copy-start.57 = (bf16[512,128]{1,0:T(8,128)(2,1)S(1)}, bf16[512,128]{1,0:T(8,128)(2,1)}, u32[]{:S(2)}) copy-start(bf16[512,128]{1,0:T(8,128)(2,1)} %copy-done.56) | copy-start | bytes 393220
  586.6 11.2 %copy-start.99 = (bf16[512,1024]{1,0:T(8,128)(2,1)S(1)}, bf16[512,1024]{1,0:T(8,128)(2,1)}, u32[]{:S(2)}) copy-start(bf16[512,1024]{1,0:T(8,128)(2,1)} %fusion.58) | copy-start | bytes 3145732
  603.0 62.5 %collective-permute-start.24 = (f32[512,2336]{0,1:T(8,128)}, f32[512,2336]{0,1:T(8,128)}, u32[]{:S(2)}, u32[]{:S(2)}) collective-permute-start(f32[512,2336]{0,1:T(8,128)} %fusion.75), channel_id=1, source_target_pairs={{0,1},{1,0},{2,3},{3,2},{4,5},{5,4},{6,7},{7,6},{8,9},{9,8},{10,11... | collective-permute-start | bytes 14352392 | tf_op jit(solution)/shard_map/ppermute | solution.py:788
  609.6 14.3 %collective-permute-start.31 = (f32[256,1024]{1,0:T(8,128)}, f32[256,1024]{1,0:T(8,128)}, u32[]{:S(2)}, u32[]{:S(2)}) collective-permute-start(f32[256,1024]{1,0:T(8,128)} %get-tuple-element.142.refs_6_), channel_id=1, source_target_pairs={{0,4},{1,3},{2,6},{3,1},{4,0},{5,7},{6,2},{7,5},{8,12},{9,11},{10,... | collective-permute-start | bytes 3145736 | tf_op jit(solution)/shard_map/ppermute | solution.py:788
  626.2 19.2 %copy-start.15 = (f32[128,2048]{1,0:T(8,128)S(1)}, f32[128,2048]{1,0:T(8,128)}, u32[]{:S(2)}) copy-start(f32[128,2048]{1,0:T(8,128)} %get-tuple-element.140.refs_8_) | copy-start | bytes 3145732
  626.2 13.1 %collective-permute-start.32 = (f32[128,1024]{1,0:T(8,128)}, f32[128,1024]{1,0:T(8,128)}, u32[]{:S(2)}, u32[]{:S(2)}) collective-permute-start(f32[128,1024]{1,0:T(8,128)} %get-tuple-element.156), channel_id=1, source_target_pairs={{0,8},{1,9},{2,10},{3,11},{4,12},{5,13},{6,14},{7,15},{8,0},{9,1},... | collective-permute-start | bytes 1572872 | tf_op jit(solution)/shard_map/ppermute | solution.py:788
  640.3 14.8 %collective-permute-start.33 = (f32[64,1024]{1,0:T(8,128)S(1)}, f32[64,1024]{1,0:T(8,128)}, u32[]{:S(2)}, u32[]{:S(2)}) collective-permute-start(f32[64,1024]{1,0:T(8,128)S(1)} %slice_add_fusion.39), channel_id=1, source_target_pairs={{0,16},{1,17},{2,18},{3,19},{4,20},{5,21},{6,22},{7,23},{8,24},{9,... | collective-permute-start | bytes 786440 | tf_op jit(solution)/shard_map/ppermute | solution.py:788
  645.4 11.8 %copy-start.100 = (bf16[512,1024]{1,0:T(8,128)(2,1)S(1)}, bf16[512,1024]{1,0:T(8,128)(2,1)}, u32[]{:S(2)}) copy-start(bf16[512,1024]{1,0:T(8,128)(2,1)} %fusion.58) | copy-start | bytes 3145732
  645.4 47.4 %collective-permute-start.21 = (f32[128,2048]{1,0:T(8,128)S(1)}, f32[128,2048]{1,0:T(8,128)}, u32[]{:S(2)}, u32[]{:S(2)}) collective-permute-start(f32[128,2048]{1,0:T(8,128)S(1)} %copy-done.15), channel_id=1, source_target_pairs={{0,4},{1,3},{2,6},{3,1},{4,0},{5,7},{6,2},{7,5},{8,12},{9,11},{10,... | collective-permute-start | bytes 3145736 | tf_op jit(solution)/shard_map/ppermute | solution.py:788
  657.2 75.8 %collective-permute-start.29 = (f32[64,2336]{1,0:T(8,128)S(1)}, f32[64,2336]{1,0:T(8,128)}, u32[]{:S(2)}, u32[]{:S(2)}) collective-permute-start(f32[64,2336]{1,0:T(8,128)S(1)} %get-tuple-element.166.refs_10_), channel_id=1, source_target_pairs={{0,8},{1,9},{2,10},{3,11},{4,12},{5,13},{6,14},{7,15},{8,0},{9,1},... | collective-permute-start | bytes 1794056 | tf_op jit(solution)/shard_map/ppermute | solution.py:788
  671.5 42.6 %collective-permute-start.25 = (f32[256,2336]{0,1:T(8,128)}, f32[256,2336]{0,1:T(8,128)}, u32[]{:S(2)}, u32[]{:S(2)}) collective-permute-start(f32[256,2336]{0,1:T(8,128)} %get-tuple-element.135), channel_id=1, source_target_pairs={{0,2},{1,5},{2,0},{3,7},{4,6},{5,1},{6,4},{7,3},{8,10},{9,13},{10,... | collective-permute-start | bytes 7176200 | tf_op jit(solution)/shard_map/ppermute | solution.py:788
  682.7 20.5 %all-to-all-start.8 = ((f32[32,1,1152]{2,1,0:T(1,128)}), f32[32,1,1152]{2,1,0:T(1,128)S(1)}, u32[]{:S(2)}, u32[]{:S(2)}) async-start(f32[32,1,1152]{2,1,0:T(1,128)} %copy.91), calls=%async_computation.8 | async-start | bytes 294912 | tf_op jit(solution)/shard_map/all_to_all | solution.py:944
  695.1 34.0 %collective-permute-start.22 = (f32[64,2048]{1,0:T(8,128)}, f32[64,2048]{1,0:T(8,128)}, u32[]{:S(2)}, u32[]{:S(2)}) collective-permute-start(f32[64,2048]{1,0:T(8,128)} %get-tuple-element.158), channel_id=1, source_target_pairs={{0,8},{1,9},{2,10},{3,11},{4,12},{5,13},{6,14},{7,15},{8,0},{9,1},... | collective-permute-start | bytes 1572872 | tf_op jit(solution)/shard_map/ppermute | solution.py:788
  728.0 25.0 %collective-permute-start.26 = (f32[128,2336]{0,1:T(8,128)}, f32[128,2336]{0,1:T(8,128)S(1)}, u32[]{:S(2)}, u32[]{:S(2)}) collective-permute-start(f32[128,2336]{0,1:T(8,128)} %copy.96), channel_id=1, source_target_pairs={{0,4},{1,3},{2,6},{3,1},{4,0},{5,7},{6,2},{7,5},{8,12},{9,11},{10,... | collective-permute-start | bytes 3588104 | tf_op jit(solution)/shard_map/ppermute | solution.py:788
  730.1 21.2 %collective-permute-start.23 = (f32[32,2048]{1,0:T(8,128)S(1)}, f32[32,2048]{1,0:T(8,128)S(1)}, u32[]{:S(2)}, u32[]{:S(2)}) collective-permute-start(f32[32,2048]{1,0:T(8,128)S(1)} %slice_add_fusion.41), channel_id=1, source_target_pairs={{0,16},{1,17},{2,18},{3,19},{4,20},{5,21},{6,22},{7,23},{8,24},{9,... | collective-permute-start | bytes 786440 | tf_op jit(solution)/shard_map/ppermute | solution.py:788
  734.7 25.3 %collective-permute-start.30 = (f32[32,2336]{1,0:T(8,128)}, f32[32,2336]{1,0:T(8,128)}, u32[]{:S(2)}, u32[]{:S(2)}) collective-permute-start(f32[32,2336]{1,0:T(8,128)} %slice_add_fusion.35), channel_id=1, source_target_pairs={{0,16},{1,17},{2,18},{3,19},{4,20},{5,21},{6,22},{7,23},{8,24},{9,... | collective-permute-start | bytes 897032 | tf_op jit(solution)/shard_map/ppermute | solution.py:788
  758.1 15.5 %copy-start.24 = (f32[32,2048]{1,0:T(8,128)S(1)}, f32[32,2048]{1,0:T(8,128)}, u32[]{:S(2)}) copy-start(f32[32,2048]{1,0:T(8,128)} %get-tuple-element.118.refs_21_) | copy-start | bytes 786436
  759.9 13.5 %collective-permute-start.27 = (f32[64,2336]{1,0:T(8,128)S(1)}, f32[64,2336]{1,0:T(8,128)S(1)}, u32[]{:S(2)}, u32[]{:S(2)}) collective-permute-start(f32[64,2336]{1,0:T(8,128)S(1)} %get-tuple-element.164), channel_id=1, source_target_pairs={{0,8},{1,9},{2,10},{3,11},{4,12},{5,13},{6,14},{7,15},{8,0},{9,1},... | collective-permute-start | bytes 1794056 | tf_op jit(solution)/shard_map/ppermute | solution.py:788
  761.1 29.3 %copy-start.106 = (f32[32,2048]{1,0:T(8,128)S(1)}, f32[32,2048]{1,0:T(8,128)}, u32[]{:S(2)}) copy-start(f32[32,2048]{1,0:T(8,128)} %fusion.94) | copy-start | bytes 786436
  773.4 16.9 %collective-permute-start.28 = (f32[32,2336]{1,0:T(8,128)S(1)}, f32[32,2336]{1,0:T(8,128)S(1)}, u32[]{:S(2)}, u32[]{:S(2)}) collective-permute-start(f32[32,2336]{1,0:T(8,128)S(1)} %slice_add_fusion.37), channel_id=1, source_target_pairs={{0,16},{1,17},{2,18},{3,19},{4,20},{5,21},{6,22},{7,23},{8,24},{9,... | collective-permute-start | bytes 897032 | tf_op jit(solution)/shard_map/ppermute | solution.py:788
  (110 other events, 533.3 us)

commit v5 on v4

--- a/solution.py
+++ b/solution.py
@@ -19,6 +19,9 @@
 HEADS_AT = TILE // HEAD_DIM
 MAPS = 2 * STATE
 ROWS_STEP = 128
+SUM_ROWS = 512
+LAG = 2
+AHEAD = 4
 HALO = 8
 HALF = 128
 LOG2E = 1.4426950408889634
@@ -460,7 +463,7 @@
 
 
 def conv_back_kernel(
-    dconv_ref, dconv_bc_ref, next_ref, x_ref, aux_ref, w_ref, dx_ref, sum_ref, ext_ref, marks_ref
+    dconv_ref, dconv_bc_ref, drate_ref, next_ref, x_ref, aux_ref, w_ref, dx_ref, sum_ref, ext_ref, marks_ref
 ):
     turn = pl.program_id(0)
     last = pl.num_programs(0) - 1
@@ -499,6 +502,11 @@
         sums = [jnp.sum(part, 0, keepdims=True) for part in sums]
         sum_ref[:, lanes] = jnp.concatenate(sums + [jnp.zeros((3, 128), jnp.float32)], 0)
 
+    @pl.when(turn == last)
+    def _():
+        dx_ref[:, MAPS : MAPS + 128] = drate_ref[...]
+        dx_ref[:, MAPS + 128 :] = jnp.zeros_like(drate_ref)
+
 
 def scan_kernel(reverse, rows, in_ref, keep_ref, out_ref):
     peers = out_ref.shape[0]
@@ -511,6 +519,108 @@
 
 def total_kernel(in_ref, out_ref):
     out_ref[...] = jnp.sum(in_ref[...], 0)
+
+
+def weight_kernel(each, left_ref, right_ref, send_ref, keep_ref):
+    slabs, size = send_ref.shape[0], SUM_ROWS
+    total = dot(left_ref[...], right_ref[...])
+    half = total.shape[0] // 2
+    for out_ref, rows in ((keep_ref, total[:half]), (send_ref, total[half:])):
+        if slabs == 1:
+            out_ref[0] = rows
+        else:
+            split = rows.reshape(-1, slabs, each // slabs, rows.shape[1])
+            for part in range(slabs):
+                out_ref[part] = split[:, part].reshape(size, rows.shape[1])
+
+
+def sums_kernel(counts, masks, *refs):
+    pieces = len(counts)
+    sends, keeps, out_ref, kept_ref = refs[:pieces], refs[pieces : 2 * pieces], refs[2 * pieces], refs[2 * pieces + 1]
+    stages = len(masks)
+    got = refs[2 * pieces + 2 : 2 * pieces + 2 + stages]
+    load_sem, send_sem, recv_sem = refs[2 * pieces + 2 + stages :]
+    chunks = sum(counts)
+    seq, row = lax.axis_index("seq"), lax.axis_index("rows")
+    odd = lax.rem(row, 2)
+
+    def over(at, mask):
+        return at + mask * (1 - 2 * lax.rem(at // mask, 2))
+
+    partners = []
+    for axis, even_mask, odd_mask in masks:
+        if axis == "rows":
+            partners.append({"seq": seq, "rows": over(row, even_mask)})
+        else:
+            one, two = over(seq, even_mask), over(seq, odd_mask)
+            partners.append({"seq": one + odd * (two - one), "rows": row})
+
+    barrier = pltpu.get_barrier_semaphore()
+    for partner in partners:
+        pl.semaphore_signal(barrier, inc=1, device_id=partner, device_id_type=pl.DeviceIdType.MESH)
+    pl.semaphore_wait(barrier, stages)
+
+    def copy(stage, chunk, source=None):
+        size = SUM_ROWS >> stage
+        if source is None:
+            source = kept_ref.at[chunk] if stage == 0 else kept_ref.at[chunk, pl.ds(size, size)]
+        return pltpu.make_async_remote_copy(
+            src_ref=source,
+            dst_ref=got[stage].at[chunk],
+            send_sem=send_sem.at[stage, chunk],
+            recv_sem=recv_sem.at[stage, chunk],
+            device_id=partners[stage],
+            device_id_type=pl.DeviceIdType.MESH,
+        )
+
+    def load(chunk, source):
+        return pltpu.make_async_copy(source, kept_ref.at[chunk], load_sem.at[chunk])
+
+    def begin(chunk):
+        base = 0
+        for count, send_ref, keep_ref in zip(counts, sends, keeps):
+
+            @pl.when((chunk >= base) & (chunk < base + count))
+            def _(base=base, send_ref=send_ref, keep_ref=keep_ref):
+                copy(0, chunk, send_ref.at[chunk - base]).start()
+                load(chunk, keep_ref.at[chunk - base]).start()
+
+            base += count
+
+    def first(chunk, _):
+        begin(chunk)
+        return 0
+
+    lax.fori_loop(0, AHEAD, first, 0)
+
+    def turn(at, _):
+        begin(at + AHEAD)
+        for stage in range(stages):
+            chunk = at - LAG * stage
+
+            @pl.when((chunk >= 0) & (chunk < chunks))
+            def _():
+                size = SUM_ROWS >> stage
+                if stage == 0:
+                    load(chunk, keeps[0].at[0]).wait()
+                copy(stage, chunk, sends[0].at[0] if stage == 0 else None).wait_recv()
+                total = kept_ref[chunk, :size] + got[stage][chunk]
+                if stage + 1 < stages:
+                    kept_ref[chunk, :size] = total
+                    copy(stage + 1, chunk).start()
+                else:
+                    out_ref[chunk] = total
+
+        return 0
+
+    lax.fori_loop(0, chunks + LAG * (stages - 1), turn, 0)
+
+    def ended(chunk, _):
+        for stage in range(stages):
+            copy(stage, chunk, sends[0].at[0] if stage == 0 else None).wait_send()
+        return 0
+
+    lax.fori_loop(0, chunks, ended, 0)
 
 
 def full(shape):
@@ -674,7 +784,7 @@
     )
 
 
-def conv_back(dconv, dconv_bc, following, mixed_ext, aux, conv, after=()):
+def conv_back(dconv, dconv_bc, drate, following, mixed_ext, aux, conv, after=()):
     span = dconv.shape[0]
     groups = DI // TILE
     tile = lambda rows: pl.BlockSpec((rows, TILE), lambda g: (0, g))
@@ -683,12 +793,12 @@
         (groups + 1,),
         [
             pl.BlockSpec((span, TILE), lambda g: (0, jnp.minimum(g, groups - 1))),
-            full((span, MAPS)), tile(HALO), tile(span + HALO), full((span, 128)), tile(8),
+            full((span, MAPS)), full((span, 128)), tile(HALO), tile(span + HALO), full((span, 128)), tile(8),
         ],
         [tile(span), tile(8)],
-        [shape_of((span, CHANNELS), jnp.bfloat16), shape_of((8, CHANNELS))],
+        [shape_of((span, DI + TILE), jnp.bfloat16), shape_of((8, CHANNELS))],
         [vmem((span + HALO, TILE)), vmem((2 * (KW - 1), span, 128))],
-        (dconv, dconv_bc, following, mixed_ext, aux, conv),
+        (dconv, dconv_bc, drate, following, mixed_ext, aux, conv),
         flops=8 * span * DI,
         nbytes=10 * span * DI,
         after=after,
@@ -769,6 +879,66 @@
     source = (order[:, None] * size + jnp.arange(size, dtype=jnp.int32)[None, :]).reshape(-1)
     pick = (jnp.arange(width, dtype=jnp.int32)[:, None] == source[None, :]).astype(jnp.bfloat16)
     return jnp.dot(values, pick, preferred_element_type=jnp.float32).astype(jnp.bfloat16)
+
+
+def in_order_rows(values, order):
+    width = values.shape[1]
+    size = width // order.shape[0]
+    source = (order[:, None] * size + jnp.arange(size, dtype=jnp.int32)[None, :]).reshape(-1)
+    pick = (source[:, None] == jnp.arange(width, dtype=jnp.int32)[None, :]).astype(jnp.bfloat16)
+    return jnp.einsum("ns,ts->nt", pick, values, preferred_element_type=jnp.float32).astype(jnp.bfloat16)
+
+
+def weight_sums(devices, left, right, after=()):
+    width, span = left.shape
+    columns = right.shape[1]
+    slabs = width // 2 // SUM_ROWS
+    out = pl.BlockSpec((slabs, SUM_ROWS, 256), lambda g: (g, 0, 0))
+    return pcall(
+        partial(weight_kernel, width // devices),
+        (columns // 256,),
+        [full((width, span)), pl.BlockSpec((span, 256), lambda g: (0, g))],
+        [out, out],
+        [shape_of((columns // 256 * slabs, SUM_ROWS, 256))] * 2,
+        [],
+        (left, right),
+        flops=2 * span * width * columns,
+        nbytes=4 * width * columns,
+        after=after,
+    )
+
+
+def summed(parts, after=()):
+    count, rows = lax.axis_size("seq"), lax.axis_size("rows")
+    row_masks, even, odd = halving(count, rows)
+    masks = [("rows", mask, mask) for mask in row_masks] + [("seq", one, two) for one, two in zip(even, odd)]
+    masks = [(axis, one // rows, two // rows) if axis == "seq" else (axis, one, two) for axis, one, two in masks]
+    counts = [send.shape[0] for send, _ in parts]
+    chunks, stages = sum(counts), len(masks)
+    last = SUM_ROWS >> (stages - 1)
+    anywhere = pl.BlockSpec(memory_space=pltpu.HBM)
+
+    def run(*refs):
+        taken = 2 * len(parts)
+        sums_kernel(counts, masks, *refs[:taken], *refs[taken + len(after) :])
+
+    return pl.pallas_call(
+        run,
+        in_specs=[anywhere] * (2 * len(parts) + len(after)),
+        out_specs=pl.BlockSpec(memory_space=pltpu.VMEM),
+        out_shape=shape_of((chunks, last, 256)),
+        scratch_shapes=[vmem((chunks, SUM_ROWS, 256))]
+        + [vmem((chunks, SUM_ROWS >> stage, 256)) for stage in range(stages)]
+        + [
+            pltpu.SemaphoreType.DMA((chunks,)),
+            pltpu.SemaphoreType.DMA((stages, chunks)),
+            pltpu.SemaphoreType.DMA((stages, chunks)),
+        ],
+        compiler_params=pltpu.CompilerParams(
+            vmem_limit_bytes=56 * 1024 * 1024, collective_id=0, has_side_effects=True
+        ),
+        cost_estimate=pl.CostEstimate(flops=0, bytes_accessed=400 * 1024 * 1024, transcendentals=0),
+    )(*[send for send, _ in parts], *[keep for _, keep in parts], *after)
 
 
 class Scatter:
@@ -883,46 +1053,49 @@
         )
         hidden = hidden + matmul(out_low, out_weight[depth])
     gradient = cotangent[0]
+    devices = lax.axis_size(AXES)
     collected = [None] * LAYERS
-    parts = [None] * LAYERS
-    earlier = None
+    big_out = [None] * LAYERS
+    big_in = [None] * LAYERS
+    early, late = (), ()
     for depth in reversed(range(LAYERS)):
         entry, normed, mixed_ext, rate, gate, values, bc, col, cumr, made, kx, keeps, state_in, y, out_low, yi = saved[depth][:16]
         conv, hp, ch, gate_weight, mixed_weight, rate_weight = saved[depth][16:]
+        normed_sorted = in_order(normed, order) if depth else in_order_rows(normed, order)
+        out_sorted = in_order(out_low, order) if depth else in_order_rows(out_low, order)
         grad_low = gradient.astype(jnp.bfloat16)
         dno = matmul_nt(grad_low, out_weight[depth])
-        waits = () if earlier is None else steps(*earlier[:2])
+        waits = steps(*late)
         dy, dgate, gate_sums, d1, pay = gate_back(peers, dno, y, gate, values, bc, col, kx, ch, after=waits)
         received = exchange(pay)
-        normed_sorted = in_order(normed, order)
-        if earlier is not None:
-            parts[depth + 1] = earlier = earlier[:2] + (Scatter(normed_sorted_before, dmixed),)
-        out_part = Scatter(in_order(out_low, order), grad_low)
-        gate_part = Scatter(normed_sorted, dgate)
-        waits = (out_part.send, out_part.keep, gate_part.send, gate_part.keep)
-        if earlier is not None:
-            waits += (earlier[2].send, earlier[2].keep) + steps(*earlier[:2])
+        if depth:
+            early_now = Scatter(out_sorted, grad_low), Scatter(normed_sorted, dgate)
+            waits = sum(((part.send, part.keep) for part in early_now), ())
+        else:
+            out_chunks = weight_sums(devices, out_sorted, grad_low)
+            gate_chunks = weight_sums(devices, normed_sorted, dgate, after=out_chunks[:1])
+            waits = (gate_chunks[0],) + steps(*early)
         scanned = scan_states(received, keeps, True, after=waits)
         dso = exchange(scanned).reshape(DI // 128, STATE, 128)
-        waits = steps(out_part, gate_part)
-        if earlier is not None:
-            waits += steps(earlier[2])
+        if depth:
+            early = early_now
+        waits = steps(*early) if depth else steps(*late)
         xi, dbc = inner_back(bc, values, dy, col, cumr, aux, auxr, after=waits)
-        waits = () if earlier is None else steps(*earlier)
+        waits = () if depth else steps(*early, *late)
         dconv, dconv_bc, drate, head_rows = states_back(
             xi, values, dy, yi, mixed_ext, bc, col, dso, state_in, made, d1, kx, dbc, aux, conv, ch, hp, rate,
             after=waits,
         )
         following = shifted(jnp.concatenate([dconv[:HALO], dconv_bc[:HALO]], 1), -1)
-        waits = steps(out_part, gate_part) + (() if earlier is None else steps(earlier[2]))
-        dmixed, conv_sums = conv_back(dconv, dconv_bc, following, mixed_ext, aux, conv, after=waits)
-        dmixed = jnp.concatenate([dmixed, drate[:, :HEADS]], 1)
-        normed_sorted_before = normed_sorted
-        earlier = (out_part, gate_part)
-        parts[depth] = earlier
-        if depth == 0:
-            parts[depth] = earlier + (Scatter(normed_sorted, dmixed),)
-        grad_normed = matmul_nt(dgate, gate_weight) + matmul_nt(dmixed, in_weight[depth][:, DI:])
+        waits = steps(*early) if depth else steps(*late)
+        dmixed, conv_sums = conv_back(dconv, dconv_bc, drate, following, mixed_ext, aux, conv, after=waits)
+        if depth:
+            late = (Scatter(normed_sorted, dmixed),)
+        else:
+            rest_chunks = weight_sums(devices, normed_sorted, dmixed)
+        grad_normed = matmul_nt(dgate, gate_weight) + matmul_nt(
+            dmixed[:, : CHANNELS + HEADS], in_weight[depth][:, DI:]
+        )
         grad_hidden, gain_grad = normalise_back(entry, norm_gain[depth], grad_normed)
         gradient = gradient + grad_hidden
         collected[depth] = (
@@ -934,9 +1107,16 @@
             head_rows[0, :HEADS],
             jnp.sum(gate_sums[1].reshape(HEADS, HEAD_DIM), 1),
         )
-    big_out = [trio[0].result() for trio in parts]
-    big_in = [jnp.concatenate([trio[1].result(), trio[2].result()], 1) for trio in parts]
-    devices = lax.axis_size(AXES)
+        if depth:
+            trio = early + late
+    big_out[1] = trio[0].result()
+    big_in[1] = jnp.concatenate([trio[1].result(), trio[2].result()[:, : CHANNELS + HEADS]], 1)
+    total = summed([out_chunks, gate_chunks, rest_chunks], after=(gradient, big_out[1], big_in[1]))
+    wide = lambda part: jnp.moveaxis(part, 0, 1).reshape(part.shape[1], -1)
+    n_out, n_gate = out_chunks[0].shape[0], gate_chunks[0].shape[0]
+    slabs = n_out * 256 // out_weight.shape[2]
+    big_out[0] = jnp.concatenate([wide(total[part:n_out:slabs]) for part in range(slabs)], 0)
+    big_in[0] = wide(total[n_out:])[:, : DI + CHANNELS + HEADS]
     shares = [part.reshape(devices, -1) for sums in collected for part in sums[:4]]
     heads = jnp.concatenate([part for sums in collected for part in sums[4:]])
     table = jnp.concatenate(shares + [jnp.broadcast_to(heads, (devices,) + heads.shape)], 1)
@@ -950,7 +1130,7 @@
         shape_of(table.shape[1:]),
         [],
         (table,),
-        after=tuple(big_in + big_out),
+        after=(total,),
     ).reshape(-1)
     small = []
     at = 0

time: 806 us -> 755 us (0.937)
  Pallas kernels: 164 us -> 310 us
  local copies, waits for them, and re-layouts: 118 us -> 59.5 us
  waiting for transfers between devices: 127 us -> 72.9 us
  other arithmetic: 107 us -> 60.6 us
  matrix products: 146 us -> 113 us
    pallas_call x0 -> x1, Pallas kernels: none -> 130 us  [summed(): pl.pallas_call(run, in_specs=[anywhere] * (2 * len(parts) + len(after)),...]
    ppermute x30 -> x15, waiting for transfers between devices: 80.9 us -> 31.5 us  [share(): lax.ppermute(self.send, AXES, [(at, at ^ masks[at & 1]) for at in range(s...]
    add x18 -> x10, other arithmetic: 68 us -> 34.4 us  [step(): self.keep = self.keep[:half] + self.got[:half]]
    unnamed x279 -> x273, local copies, waits for them, and re-layouts: 57.4 us -> 28.9 us
    dot_general x12 -> x6, matrix products: 49.9 us -> 22.6 us  [matmul_tn(): return jnp.einsum('tn,tm->nm', a, b, preferred_element_type=jnp.float32)]
    slice x5 -> x0, local copies, waits for them, and re-layouts: 15.2 us -> none  [step(): self.keep = self.keep[:half] + self.got[:half]]
    pallas_call x19 -> x22, Pallas kernels: 164 us -> 179 us  [pcall(): pl.pallas_call(run, grid=grid, in_specs=list(in_specs) + [pl.BlockSpec(me...]
    ppermute x30 -> x15, starting transfers between devices: 39 us -> 27.4 us  [share(): lax.ppermute(self.send, AXES, [(at, at ^ masks[at & 1]) for at in range(s...]
  transfers between devices with their start and end apart: 42 -> 27, of which waited for: 13 -> 6; matrix products, arithmetic and copies ran while one was open for 38% -> 22% of each run, Pallas kernels for 13% -> 16%
where the time goes in v5:
time: 755 us; the launch traced here: 746 us
  Pallas kernels  310 us (41%)
  matrix products  113 us (15%)
  starting transfers between devices  95.4 us (13%)
  waiting for transfers between devices  72.9 us (10%)
  other arithmetic  60.6 us (8%)
  local copies, waits for them, and re-layouts  59.5 us (8%)
  blocking collectives  33.2 us (4%)
    pallas_call x22, Pallas kernels, pcall(): pl.pallas_call(run, grid=grid, in_specs=list(in_specs) + [pl.BlockSpec(me...  179 us
    pallas_call x1, Pallas kernels, summed(): pl.pallas_call(run, in_specs=[anywhere] * (2 * len(parts) + len(after)),...  130 us
    all_to_all x7, starting transfers between devices, exchange(): return lax.all_to_all(parts, 'seq', split_axis=0, concat_axis=0, tiled=True)  47.3 us
    all_to_all x7, waiting for transfers between devices, exchange(): return lax.all_to_all(parts, 'seq', split_axis=0, concat_axis=0, tiled=True)  41.4 us
    dot_general x8, matrix products, matmul(): return jnp.dot(a, b, preferred_element_type=jnp.float32)  40.2 us
    add x10, other arithmetic, step(): self.keep = self.keep[:half] + self.got[:half]  34.4 us
    dot_general x6, matrix products, matmul_nt(): return jnp.einsum('tn,mn->tm', a, b, preferred_element_type=jnp.float32)  34.3 us
    all_to_all x1, blocking collectives, exchange(): return lax.all_to_all(parts, 'seq', split_axis=0, concat_axis=0, tiled=True)  33.2 us
  transfers between devices with their start and end apart: 27, of which 6 were waited for; matrix products, arithmetic and copies ran while one was open for 22% of the time, Pallas kernels for 16%

profile of v5, /device:TPU:1, one launch (start us, length us, event | category | flops | bytes accessed | tf_op | source)
XLA Modules:
  0.0 746.4 jit_solution(6571020451930862699)
XLA Ops:
  1.5 3.9 collective-permute-start
  8.1 10.2 %slice_bitcast_fusion = (bf16[1024,4384]{0,1:T(8,128)(2,1)}, bf16[1024,4384]{0,1:T(8,128)(2,1)S(1)}) fusion(bf16[2,1024,4384]{1,2,0:T(8,128)(2,1)} %param.15), kind=kLoop, calls=%fused_computation.4 | loop fusion | bytes 35913728 | tf_op jit(solution)/shard_map/squeeze | solution.py:1036
  19.2 2.6 copy-done.87
  22.3 7.1 fusion.10.refs_0_.refs_1_.refs_4_.refs_5_
  29.4 9.8 %shard_map.203 = (f32[512,2048]{1,0:T(8,128)}, f32[512,256]{1,0:T(8,128)S(1)}, f32[4,512,128]{2,1,0:T(8,128)S(1)}, f32[128,512]{1,0:T(8,128)S(1)}, f32[128,2048]...) custom-call(f32[520,2304]{1,0:T(8,128)} %fusion.10.refs_0_.refs_1_.refs_4_.refs_5_, ...), custom_call_target="tpu_custom_call" | custom-call | flops 268435456 | bytes 12582912 | tf_op jit(solution)/shard_map/pallas_call | solution.py:42
  40.3 33.2 %all_to_all.49.refs_0_ = f32[16,136,128]{2,1,0:T(8,128)S(1)} all-to-all(f32[16,136,128]{2,1,0:T(8,128)S(1)} %get-tuple-element.65), channel_id=1, replica_groups=mesh['seq'=16,'rows'=2] {'seq'}, dimensions={0} | all-to-all | bytes 2228224 | tf_op jit(solution)/shard_map/all_to_all | solution.py:825
  74.6 3.9 all-to-all-start.1
  80.2 7.0 fusion.28.refs_2_
  87.2 6.8 shard_map.204.refs_0_.refs_3_
  94.0 6.6 all-to-all-done.1.refs_5_.refs_9_
  102.2 8.3 %shard_map.206 = (f32[512,2048]{1,0:T(8,128)}, bf16[512,2048]{1,0:T(8,128)(2,1)S(1)}) custom-call(f32[512,2048]{1,0:T(8,128)} %shard_map.204.refs_0_.refs_3_, f32[512,2048]{1,0:T(8,128)} %get-tuple-element.62.refs_1_.refs_3_, f32[512,2048]{1,0:T(8,128)} %fusion.28.refs_2_, f32[512,256]{1,0:T(8,128)S(1)} %get-tuple-element.61.refs_0_.refs_3_.refs_4_.refs_6_, ...), custom_call_target="tpu_custom_call" | custom-call | flops 268435456 | bytes 18874368 | tf_op jit(solution)/shard_map/pallas_call | solution.py:42
  110.5 5.4 multiply_reduce_fusion.2
  119.0 7.2 fusion.8.refs_0_.refs_1_.refs_4_.refs_5_
  126.2 9.8 %shard_map.207 = (f32[512,2048]{1,0:T(8,128)}, f32[512,256]{1,0:T(8,128)S(1)}, f32[4,512,128]{2,1,0:T(8,128)S(1)}, f32[128,512]{1,0:T(8,128)S(1)}, f32[128,2048]...) custom-call(f32[520,2304]{1,0:T(8,128)} %fusion.8.refs_0_.refs_1_.refs_4_.refs_5_, ...), custom_call_target="tpu_custom_call" | custom-call | flops 268435456 | bytes 12582912 | tf_op jit(solution)/shard_map/pallas_call | solution.py:42
  138.6 9.2 %all-to-all-start.2 = ((f32[16,136,128]{2,1,0:T(8,128)}), f32[16,136,128]{2,1,0:T(8,128)}, u32[]{:S(2)}, u32[]{:S(2)}) async-start(f32[16,136,128]{2,1,0:T(8,128)} %copy-done.22), calls=%async_computation.2 | async-start | bytes 2228224 | tf_op jit(solution)/shard_map/all_to_all | solution.py:825
  149.0 21.4 %all-to-all-done.2.refs_0_ = f32[16,136,128]{2,1,0:T(8,128)} async-done(((f32[16,136,128]{2,1,0:T(8,128)}), f32[16,136,128]{2,1,0:T(8,128)}, u32[]{:S(2)}, u32[]{:S(2)}) %all-to-all-start.2) | async-done | bytes 1114144 | tf_op jit(solution)/shard_map/all_to_all | solution.py:825
  174.2 9.4 %all-to-all-start.3 = ((f32[16,128,128]{2,1,0:T(8,128)}), f32[16,128,128]{2,1,0:T(8,128)}, u32[]{:S(2)}, u32[]{:S(2)}) async-start(f32[16,128,128]{2,1,0:T(8,128)} %copy-done.14), calls=%async_computation.3 | async-start | bytes 2097152 | tf_op jit(solution)/shard_map/all_to_all | solution.py:825
  186.1 7.4 fusion.12.refs_0_
  195.8 6.6 fusion.24.refs_2_
  202.4 6.7 shard_map.208.refs_0_.refs_3_
  210.3 8.5 %shard_map.210 = (f32[512,2048]{1,0:T(8,128)}, bf16[512,2048]{1,0:T(8,128)(2,1)S(1)}) custom-call(f32[512,2048]{1,0:T(8,128)} %shard_map.208.refs_0_.refs_3_, f32[512,2048]{1,0:T(8,128)} %get-tuple-element.70.refs_1_.refs_3_, f32[512,2048]{1,0:T(8,128)} %fusion.24.refs_2_, f32[512,256]{1,0:T(8,128)S(1)} %get-tuple-element.69.refs_0_.refs_3_.refs_4_.refs_6_, ...), custom_call_target="tpu_custom_call" | custom-call | flops 268435456 | bytes 18874368 | tf_op jit(solution)/shard_map/pallas_call | solution.py:42
  218.8 11.5 %shard_map.211 = (f32[512,2048]{1,0:T(8,128)}, bf16[512,2048]{1,0:T(8,128)(2,1)S(1)}, f32[8,2048]{1,0:T(8,128)S(1)}, f32[128,2048]{1,0:T(8,128)S(1)}, f32[16,128,128]{2,1,0:T(8,128)S(1)}) custom-call(f32[512,2048]{1,0:T(8,128)} %fusion.12.refs_0_, f32[512,2048]{1,0:T(8,128)} %get-tuple-element.77.refs_1_, f32[512,2048]{1,0:T(8,128)} %fusion.24.refs_2_, ...), custom_call_target="tpu_custom_call" | custom-call | flops 268435456 | bytes 23068672 | tf_op jit(solution)/shard_map/pallas_call | solution.py:42
  230.3 3.4 fusion.76.refs_4_
  235.8 5.0 fusion.35
  240.8 3.3 fusion.68.refs_2_
  244.2 6.8 all-to-all-start.4
  251.0 5.1 fusion.80.refs_5_
  256.1 3.4 fusion.70.refs_3_
  259.6 13.1 %all-to-all-done.4.refs_0_ = f32[16,128,128]{2,1,0:T(8,128)} async-done(((f32[16,128,128]{2,1,0:T(8,128)}), f32[16,128,128]{2,1,0:T(8,128)}, u32[]{:S(2)}, u32[]{:S(2)}) %all-to-all-start.4) | async-done | bytes 1048608 | tf_op jit(solution)/shard_map/all_to_all | solution.py:825
  274.9 7.5 %all-to-all-start.5 = ((f32[16,128,128]{2,1,0:T(8,128)}), f32[16,128,128]{2,1,0:T(8,128)}, u32[]{:S(2)}, u32[]{:S(2)}) async-start(f32[16,128,128]{2,1,0:T(8,128)} %copy-done.12), calls=%async_computation.5 | async-start | bytes 2097152 | tf_op jit(solution)/shard_map/all_to_all | solution.py:825
  282.5 6.7 slice_add_fusion.2
  290.5 5.6 slice_add_fusion.4
  296.2 9.7 %shard_map.212 = (f32[512,2048]{1,0:T(8,128)}, f32[512,256]{1,0:T(8,128)S(1)}) custom-call(f32[512,256]{1,0:T(8,128)S(1)} %get-tuple-element.69.refs_0_.refs_3_.refs_4_.refs_6_, f32[512,2048]{1,0:T(8,128)} %get-tuple-element.70.refs_1_.refs_3_, f32[512,2048]{1,0:T(8,128)} %get-tuple-element.79.refs_2_, ...), custom_call_target="tpu_custom_call" | custom-call | flops 4294967296 | bytes 12582912 | tf_op jit(solution)/shard_map/pallas_call | solution.py:42
  307.8 22.0 %shard_map.214 = (f32[512,2048]{1,0:T(8,128)}, f32[512,256]{1,0:T(8,128)S(1)}, bf16[512,128]{1,0:T(8,128)(2,1)S(1)}, f32[8,128]{1,0:T(8,128)S(1)}) custom-call(f32[512,2048]{1,0:T(8,128)} %get-tuple-element.80.refs_0_, f32[512,2048]{1,0:T(8,128)} %get-tuple-element.70.refs_1_.refs_3_, f32[512,2048]{1,0:T(8,128)} %get-tuple-element.79.refs_2_, ...), custom_call_target="tpu_custom_call" | custom-call | flops 1073741824 | bytes 20971520 | tf_op jit(solution)/shard_map/pallas_call | solution.py:42
  333.9 8.6 %collective-permute-done.5 = f32[512,1024]{1,0:T(8,128)} collective-permute-done((f32[512,1024]{1,0:T(8,128)}, f32[512,1024]{1,0:T(8,128)}, u32[]{:S(2)}, u32[]{:S(2)}) %collective-permute-start.5) | collective-permute-done | bytes 2097184 | tf_op jit(solution)/shard_map/ppermute | solution.py:958
  342.5 2.9 slice_add_fusion.10
  345.4 11.4 %shard_map.215 = (bf16[512,2560]{1,0:T(8,128)(2,1)}, f32[8,2304]{1,0:T(8,128)S(1)}) custom-call(f32[512,2048]{1,0:T(8,128)} %get-tuple-element.84.refs_0_, f32[512,256]{1,0:T(8,128)S(1)} %get-tuple-element.85.refs_1_, bf16[512,128]{1,0:T(8,128)(2,1)S(1)} %get-tuple-element.86.refs_2_, f32[8,2304]{1,0:T(8,128)S(1)} %collective-permute-done.4.refs_3_, ...), custom_call_target="tpu_custom_call" | custom-call | flops 8388608 | bytes 10485760 | tf_op jit(solution)/shard_map/pallas_call | solution.py:42
  356.8 5.8 fusion.74
  362.6 5.6 collective-permute-start.7
  370.6 5.9 fusion.34.refs_0_
  378.8 5.3 fusion.22
  384.2 6.1 add_bitcast_fusion
  392.3 3.3 multiply_reduce_fusion
  397.9 5.9 slice_add_fusion
  405.8 6.6 fusion.16.refs_0_
  415.5 4.4 shard_map.218
  419.9 10.9 %shard_map.216 = (f32[512,2048]{1,0:T(8,128)}, bf16[512,2048]{1,0:T(8,128)(2,1)S(1)}, f32[8,2048]{1,0:T(8,128)S(1)}, f32[128,2048]{1,0:T(8,128)S(1)}, f32[16,128,128]{2,1,0:T(8,128)S(1)}) custom-call(f32[512,2048]{1,0:T(8,128)} %fusion.16.refs_0_, f32[512,2048]{1,0:T(8,128)} %get-tuple-element.88.refs_1_, f32[512,2048]{1,0:T(8,128)} %fusion.28.refs_2_, ...), custom_call_target="tpu_custom_call" | custom-call | flops 268435456 | bytes 23068672 | tf_op jit(solution)/shard_map/pallas_call | solution.py:42
  434.8 5.9 all-to-all-start.6
  440.7 2.4 slice_add_fusion.16
  453.4 22.9 %collective-permute-done.11 = f32[128,1024]{1,0:T(8,128)} collective-permute-done((f32[128,1024]{1,0:T(8,128)}, f32[128,1024]{1,0:T(8,128)}, u32[]{:S(2)}, u32[]{:S(2)}) %collective-permute-start.11) | collective-permute-done | bytes 524320 | tf_op jit(solution)/shard_map/ppermute | solution.py:958
  477.4 4.5 slice_add_fusion.6
  483.3 5.9 shard_map.219
  491.5 4.7 all-to-all-start.7
  503.1 9.7 %shard_map.217 = (f32[512,2048]{1,0:T(8,128)}, f32[512,256]{1,0:T(8,128)S(1)}) custom-call(f32[512,256]{1,0:T(8,128)S(1)} %copy-done.2, f32[512,2048]{1,0:T(8,128)} %get-tuple-element.62.refs_1_.refs_3_, f32[512,2048]{1,0:T(8,128)} %get-tuple-element.90.refs_2_, f32[4,512,128]{2,1,0:T(8,128)S(1)} %get-tuple-element.63.refs_2_.refs_4_.refs_5_.refs_3_.refs_7_, ...), custom_call_target="tpu_custom_call" | custom-call | flops 4294967296 | bytes 12582912 | tf_op jit(solution)/shard_map/pallas_call | solution.py:42
  513.7 2.4 slice_add_fusion.12
  521.0 21.9 %shard_map.221 = (f32[512,2048]{1,0:T(8,128)}, f32[512,256]{1,0:T(8,128)S(1)}, bf16[512,128]{1,0:T(8,128)(2,1)S(1)}, f32[8,128]{1,0:T(8,128)S(1)}) custom-call(f32[512,2048]{1,0:T(8,128)} %get-tuple-element.91.refs_0_, f32[512,2048]{1,0:T(8,128)} %get-tuple-element.62.refs_1_.refs_3_, f32[512,2048]{1,0:T(8,128)} %get-tuple-element.90.refs_2_, ...), custom_call_target="tpu_custom_call" | custom-call | flops 1073741824 | bytes 20971520 | tf_op jit(solution)/shard_map/pallas_call | solution.py:42
  548.5 7.8 %collective-permute-start.18 = (f32[32,2560]{1,0:T(8,128)S(1)}, f32[32,2560]{1,0:T(8,128)S(1)}, u32[]{:S(2)}, u32[]{:S(2)}) collective-permute-start(f32[32,2560]{1,0:T(8,128)S(1)} %get-tuple-element.157.refs_7_), channel_id=1, source_target_pairs={{0,16},{1,17},{2,18},{3,19},{4,20},{5,21},{6,22},{7,23},{8,24},{9,... | collective-permute-start | bytes 983048 | tf_op jit(solution)/shard_map/ppermute | solution.py:958
  556.3 10.6 %shard_map.222 = (bf16[512,2560]{1,0:T(8,128)(2,1)S(1)}, f32[8,2304]{1,0:T(8,128)S(1)}) custom-call(f32[512,2048]{1,0:T(8,128)} %get-tuple-element.97.refs_0_, f32[512,256]{1,0:T(8,128)S(1)} %copy-done.46, bf16[512,128]{1,0:T(8,128)(2,1)S(1)} %copy-done.58, f32[8,2304]{1,0:T(8,128)S(1)} %collective-permute-done.14.refs_3_, ...), custom_call_target="tpu_custom_call" | custom-call | flops 8388608 | bytes 10485760 | tf_op jit(solution)/shard_map/pallas_call | solution.py:42
  569.3 5.6 fusion.4
  575.0 6.1 fusion.45
  582.3 11.9 %all-to-all-start.8 = ((f32[32,1,1152]{2,1,0:T(1,128)}), f32[32,1,1152]{2,1,0:T(1,128)S(1)}, u32[]{:S(2)}, u32[]{:S(2)}) async-start(f32[32,1,1152]{2,1,0:T(1,128)} %copy.53), calls=%async_computation.8 | async-start | bytes 294912 | tf_op jit(solution)/shard_map/all_to_all | solution.py:1124
  594.2 4.8 fusion.43.refs_6_
  599.0 7.2 shard_map.223
  607.5 130.4 %shard_map.224.refs_1_ = f32[26,32,256]{2,1,0:T(8,128)} custom-call(f32[8,512,256]{2,1,0:T(8,128)} %get-tuple-element.93.refs_2_.refs_0_, f32[8,512,256]{2,1,0:T(8,128)} %get-tuple-element.94.refs_2_.refs_1_, f32[10,512,256]{2,1,0:T(8,128)} %get-tuple-element.107.refs_2_, f32[8,512,256]{2,1,0:T(8,128)} %get-tuple-element.108.refs_3_, ...), custom_call_target="tpu_custom_call" | custom-call | bytes 419430400 | tf_op jit(solution)/shard_map/pallas_call | solution.py:925
  (445 shorter events, 102.4 us)
Async XLA Ops:
  1.5 20.5 %collective-permute-start = (f32[8,1024]{1,0:T(8,128)S(1)}, f32[8,1024]{1,0:T(8,128)S(1)}, u32[]{:S(2)}, u32[]{:S(2)}) collective-permute-start(f32[8,1024]{1,0:T(8,128)S(1)} %slice_bitcast_fusion.10), channel_id=1, source_target_pairs={{0,2},{2,4},{4,6},{6,8},{8,10},{10,12},{12,14},{14,16},{16,18},{18... | collective-permute-start | bytes 98312 | tf_op jit(solution)/shard_map/ppermute | solution.py:831
  7.8 10.6 %copy-start.114 = (f32[512]{0:T(512)}, f32[512]{0:T(512)S(1)}, u32[]{:S(2)}) copy-start(f32[512]{0:T(512)S(1)} %add_rsqrt_fusion.1) | copy-start | bytes 6148
  8.0 14.2 %copy-start.103 = (f32[1,1024]{1,0:T(1,128)}, f32[1,1024]{1,0:T(1,128)S(1)}, u32[]{:S(2)}) copy-start(f32[1,1024]{1,0:T(1,128)S(1)} %get-tuple-element.183) | copy-start | bytes 12292
  8.0 110.9 %copy-start.105 = (f32[1,1024]{1,0:T(1,128)}, f32[1,1024]{1,0:T(1,128)S(1)}, u32[]{:S(2)}) copy-start(f32[1,1024]{1,0:T(1,128)S(1)} %get-tuple-element.182) | copy-start | bytes 12292
  8.1 10.4 %copy-start.78 = (f32[1,512,1024]{2,1,0:T(8,128)S(1)}, f32[1,512,1024]{2,1,0:T(8,128)}, u32[]{:S(2)}) copy-start(f32[1,512,1024]{2,1,0:T(8,128)} %param.12) | copy-start | bytes 6291460
  18.7 10.7 %copy-start.92 = (bf16[512,1024]{1,0:T(8,128)(2,1)}, bf16[512,1024]{1,0:T(8,128)(2,1)S(1)}, u32[]{:S(2)}) copy-start(bf16[512,1024]{1,0:T(8,128)(2,1)S(1)} %fusion.40) | copy-start | bytes 3145732
  19.1 10.3 %copy-start.20 = (f32[512,128]{1,0:T(8,128)}, f32[512,128]{1,0:T(8,128)S(1)}, u32[]{:S(2)}) copy-start(f32[512,128]{1,0:T(8,128)S(1)} %fusion.84.refs_2_.refs_19_) | copy-start | bytes 786436
  19.2 10.2 %copy-start.18 = (f32[8,2304]{1,0:T(8,128)}, f32[8,2304]{1,0:T(8,128)S(1)}, u32[]{:S(2)}) copy-start(f32[8,2304]{1,0:T(8,128)S(1)} %get-tuple-element.203.refs_4_.refs_5_.refs_15_.refs_16_.refs_6_) | copy-start | bytes 221188
  40.3 33.2 %copy-start.51 = (f32[128,512]{1,0:T(8,128)}, f32[128,512]{1,0:T(8,128)S(1)}, u32[]{:S(2)}) copy-start(f32[128,512]{1,0:T(8,128)S(1)} %get-tuple-element.64.refs_3_.refs_4_) | copy-start | bytes 786436
  40.3 60.3 %copy-start.1 = (f32[512,256]{1,0:T(8,128)}, f32[512,256]{1,0:T(8,128)S(1)}, u32[]{:S(2)}) copy-start(f32[512,256]{1,0:T(8,128)S(1)} %get-tuple-element.61.refs_0_.refs_3_.refs_4_.refs_6_) | copy-start | bytes 1572868
  40.3 60.3 %copy-start.36 = (f32[8,2048]{1,0:T(8,128)}, f32[8,2048]{1,0:T(8,128)S(1)}, u32[]{:S(2)}) copy-start(f32[8,2048]{1,0:T(8,128)S(1)} %get-tuple-element.67.refs_7_.refs_6_.refs_12_) | copy-start | bytes 196612
  74.6 26.0 %all-to-all-start.1 = ((f32[16,128,128]{2,1,0:T(8,128)}), f32[16,128,128]{2,1,0:T(8,128)S(1)}, u32[]{:S(2)}, u32[]{:S(2)}) async-start(f32[16,128,128]{2,1,0:T(8,128)} %copy-done.13), calls=%async_computation.1 | async-start | bytes 2097152 | tf_op jit(solution)/shard_map/all_to_all | solution.py:825
  100.6 9.9 %copy-start = (f32[16,128,128]{2,1,0:T(8,128)}, f32[16,128,128]{2,1,0:T(8,128)S(1)}, u32[]{:S(2)}) copy-start(f32[16,128,128]{2,1,0:T(8,128)S(1)} %all-to-all-done.1.refs_5_.refs_9_) | copy-start | bytes 3145732
  102.2 8.3 %copy-start.79 = (f32[1,512,1024]{2,1,0:T(8,128)S(1)}, f32[1,512,1024]{2,1,0:T(8,128)}, u32[]{:S(2)}) copy-start(f32[1,512,1024]{2,1,0:T(8,128)} %param.12) | copy-start | bytes 6291460
  115.9 2.8 collective-permute-start.1
  138.6 34.1 %copy-start.23 = (f32[128,512]{1,0:T(8,128)}, f32[128,512]{1,0:T(8,128)S(1)}, u32[]{:S(2)}) copy-start(f32[128,512]{1,0:T(8,128)S(1)} %get-tuple-element.72.refs_3_.refs_4_) | copy-start | bytes 786436
  138.6 31.9 %all-to-all-start.2 = ((f32[16,136,128]{2,1,0:T(8,128)}), f32[16,136,128]{2,1,0:T(8,128)}, u32[]{:S(2)}, u32[]{:S(2)}) async-start(f32[16,136,128]{2,1,0:T(8,128)} %copy-done.22), calls=%async_computation.2 | async-start | bytes 2228224 | tf_op jit(solution)/shard_map/all_to_all | solution.py:825
  174.2 34.9 %all-to-all-start.3 = ((f32[16,128,128]{2,1,0:T(8,128)}), f32[16,128,128]{2,1,0:T(8,128)}, u32[]{:S(2)}, u32[]{:S(2)}) async-start(f32[16,128,128]{2,1,0:T(8,128)} %copy-done.14), calls=%async_computation.3 | async-start | bytes 2097152 | tf_op jit(solution)/shard_map/all_to_all | solution.py:825
  185.3 8.2 %copy-start.124 = (s32[1024]{0:T(1024)}, s32[1024]{0:T(1024)S(1)}, u32[]{:S(2)}) copy-start(s32[1024]{0:T(1024)S(1)} %add.262) | copy-start | bytes 12292
  185.4 50.4 %copy-start.119 = (s32[2048]{0:T(1024)}, s32[2048]{0:T(1024)S(1)}, u32[]{:S(2)}) copy-start(s32[2048]{0:T(1024)S(1)} %add.256) | copy-start | bytes 24580
  218.8 17.0 %copy-start.72 = (bf16[512,2048]{1,0:T(8,128)(2,1)}, bf16[512,2048]{1,0:T(8,128)(2,1)S(1)}, u32[]{:S(2)}) copy-start(bf16[512,2048]{1,0:T(8,128)(2,1)S(1)} %get-tuple-element.76) | copy-start | bytes 6291460
  218.8 11.5 %copy-start.96 = (bf16[512,1024]{1,0:T(8,128)(2,1)S(1)}, bf16[512,1024]{1,0:T(8,128)(2,1)}, u32[]{:S(2)}) copy-start(bf16[512,1024]{1,0:T(8,128)(2,1)} %fusion.61) | copy-start | bytes 3145732
  230.3 10.5 %copy-start.3 = (bf16[512,2048]{1,0:T(8,128)(2,1)}, bf16[512,2048]{1,0:T(8,128)(2,1)S(1)}, u32[]{:S(2)}) copy-start(bf16[512,2048]{1,0:T(8,128)(2,1)S(1)} %get-tuple-element.78) | copy-start | bytes 6291460
  233.7 48.8 %collective-permute-start.3 = (f32[512,2048]{1,0:T(8,128)}, f32[512,2048]{1,0:T(8,128)}, u32[]{:S(2)}, u32[]{:S(2)}) collective-permute-start(f32[512,2048]{1,0:T(8,128)} %fusion.76.refs_4_), channel_id=1, source_target_pairs={{0,1},{1,0},{2,3},{3,2},{4,5},{5,4},{6,7},{7,6},{8,9},{9,8},{10,11... | collective-permute-start | bytes 12582920 | tf_op jit(solution)/shard_map/ppermute | solution.py:958
  244.1 46.4 %collective-permute-start.2 = (f32[1024,1024]{1,0:T(8,128)}, f32[1024,1024]{1,0:T(8,128)}, u32[]{:S(2)}, u32[]{:S(2)}) collective-permute-start(f32[1024,1024]{1,0:T(8,128)} %fusion.68.refs_2_), channel_id=1, source_target_pairs={{0,1},{1,0},{2,3},{3,2},{4,5},{5,4},{6,7},{7,6},{8,9},{9,8},{10,11... | collective-permute-start | bytes 12582920 | tf_op jit(solution)/shard_map/ppermute | solution.py:958
  244.2 28.5 %all-to-all-start.4 = ((f32[16,128,128]{2,1,0:T(8,128)}), f32[16,128,128]{2,1,0:T(8,128)}, u32[]{:S(2)}, u32[]{:S(2)}) async-start(f32[16,128,128]{2,1,0:T(8,128)} %copy-done.35), calls=%async_computation.4 | async-start | bytes 2097152 | tf_op jit(solution)/shard_map/all_to_all | solution.py:825
  256.1 16.5 %copy-start.44 = (f32[16,8,128]{2,1,0:T(8,128)S(1)}, f32[16,8,128]{2,1,0:T(8,128)}, u32[]{:S(2)}) copy-start(f32[16,8,128]{2,1,0:T(8,128)} %copy-done.43) | copy-start | bytes 196612
  274.9 31.8 %all-to-all-start.5 = ((f32[16,128,128]{2,1,0:T(8,128)}), f32[16,128,128]{2,1,0:T(8,128)}, u32[]{:S(2)}, u32[]{:S(2)}) async-start(f32[16,128,128]{2,1,0:T(8,128)} %copy-done.12), calls=%async_computation.5 | async-start | bytes 2097152 | tf_op jit(solution)/shard_map/all_to_all | solution.py:825
  289.1 42.9 %collective-permute-start.6 = (f32[256,2048]{1,0:T(8,128)}, f32[256,2048]{1,0:T(8,128)}, u32[]{:S(2)}, u32[]{:S(2)}) collective-permute-start(f32[256,2048]{1,0:T(8,128)} %get-tuple-element.141.refs_9_), channel_id=1, source_target_pairs={{0,2},{1,5},{2,0},{3,7},{4,6},{5,1},{6,4},{7,3},{8,10},{9,13},{10,... | collective-permute-start | bytes 6291464 | tf_op jit(solution)/shard_map/ppermute | solution.py:958
  296.0 46.5 %collective-permute-start.5 = (f32[512,1024]{1,0:T(8,128)}, f32[512,1024]{1,0:T(8,128)}, u32[]{:S(2)}, u32[]{:S(2)}) collective-permute-start(f32[512,1024]{1,0:T(8,128)} %get-tuple-element.143.refs_7_), channel_id=1, source_target_pairs={{0,2},{1,5},{2,0},{3,7},{4,6},{5,1},{6,4},{7,3},{8,10},{9,13},{10,... | collective-permute-start | bytes 6291464 | tf_op jit(solution)/shard_map/ppermute | solution.py:958
  307.8 24.3 %copy-start.84 = (f32[256,2048]{1,0:T(8,128)S(1)}, f32[256,2048]{1,0:T(8,128)}, u32[]{:S(2)}) copy-start(f32[256,2048]{1,0:T(8,128)} %get-tuple-element.140.refs_10_) | copy-start | bytes 6291460
  330.6 11.9 %copy-start.85 = (f32[512,1024]{1,0:T(8,128)S(1)}, f32[512,1024]{1,0:T(8,128)}, u32[]{:S(2)}) copy-start(f32[512,1024]{1,0:T(8,128)} %get-tuple-element.142.refs_8_) | copy-start | bytes 6291460
  330.6 14.8 %collective-permute-start.4 = (f32[8,2304]{1,0:T(8,128)S(1)}, f32[8,2304]{1,0:T(8,128)S(1)}, u32[]{:S(2)}, u32[]{:S(2)}) collective-permute-start(f32[8,2304]{1,0:T(8,128)S(1)} %pad_maximum_fusion.3), channel_id=1, source_target_pairs={{2,0},{4,2},{6,4},{8,6},{10,8},{12,10},{14,12},{16,14},{18,16},{20... | collective-permute-start | bytes 221192 | tf_op jit(solution)/shard_map/ppermute | solution.py:831
  333.9 11.5 %copy-start.16 = (f32[128,2048]{1,0:T(8,128)}, f32[128,2048]{1,0:T(8,128)S(1)}, u32[]{:S(2)}) copy-start(f32[128,2048]{1,0:T(8,128)S(1)} %get-tuple-element.147.refs_9_) | copy-start | bytes 3145732
  345.4 11.4 %copy-start.97 = (bf16[512,1024]{1,0:T(8,128)(2,1)S(1)}, bf16[512,1024]{1,0:T(8,128)(2,1)}, u32[]{:S(2)}) copy-start(bf16[512,1024]{1,0:T(8,128)(2,1)} %fusion.61) | copy-start | bytes 3145732
  356.8 11.4 %copy-start.93 = (bf16[512,1024]{1,0:T(8,128)(2,1)S(1)}, bf16[512,1024]{1,0:T(8,128)(2,1)}, u32[]{:S(2)}) copy-start(bf16[512,1024]{1,0:T(8,128)(2,1)} %copy-done.92) | copy-start | bytes 3145732
  356.8 11.4 %copy-start.125 = (s32[1024]{0:T(1024)S(1)}, s32[1024]{0:T(1024)}, u32[]{:S(2)}) copy-start(s32[1024]{0:T(1024)} %copy-done.124) | copy-start | bytes 12292
  362.6 35.3 %collective-permute-start.7 = (f32[512,2560]{1,0:T(8,128)}, f32[512,2560]{1,0:T(8,128)}, u32[]{:S(2)}, u32[]{:S(2)}) collective-permute-start(f32[512,2560]{1,0:T(8,128)} %fusion.74), channel_id=1, source_target_pairs={{0,1},{1,0},{2,3},{3,2},{4,5},{5,4},{6,7},{7,6},{8,9},{9,8},{10,11... | collective-permute-start | bytes 15728648 | tf_op jit(solution)/shard_map/ppermute | solution.py:958
  378.8 13.5 %slice-start = ((s8[8978432]{0:T(1024)(128)(4,1)}), s8[4194304]{0:T(1024)(128)(4,1)S(1)}, s32[]{:S(2)}) async-start(s8[8978432]{0:T(1024)(128)(4,1)} %bitcast.201), calls=%async_computation.9 | async-start | bytes 8388608
  378.8 13.5 %slice-start.1 = ((s8[8978432]{0:T(1024)(128)(4,1)}), s8[4194304]{0:T(1024)(128)(4,1)S(1)}, s32[]{:S(2)}) async-start(s8[8978432]{0:T(1024)(128)(4,1)} %bitcast.201), calls=%async_computation.10 | async-start | bytes 8388608
  384.1 8.2 %copy-start.86 = (bf16[512,2560]{1,0:T(8,128)(2,1)S(1)}, bf16[512,2560]{1,0:T(8,128)(2,1)}, u32[]{:S(2)}) copy-start(bf16[512,2560]{1,0:T(8,128)(2,1)} %get-tuple-element.87) | copy-start | bytes 7864324
  384.1 8.2 %slice-start.2 = ((s8[8978432]{0:T(1024)(128)(4,1)}), s8[589824]{0:T(1024)(128)(4,1)S(1)}, s32[]{:S(2)}) async-start(s8[8978432]{0:T(1024)(128)(4,1)} %bitcast.201), calls=%async_computation.11 | async-start | bytes 1179648
  384.1 8.2 %copy-start.106 = (f32[1,1024]{1,0:T(1,128)S(1)}, f32[1,1024]{1,0:T(1,128)}, u32[]{:S(2)}) copy-start(f32[1,1024]{1,0:T(1,128)} %copy-done.105) | copy-start | bytes 12292
  390.8 21.6 %collective-permute-start.10 = (f32[128,2048]{1,0:T(8,128)S(1)}, f32[128,2048]{1,0:T(8,128)S(1)}, u32[]{:S(2)}, u32[]{:S(2)}) collective-permute-start(f32[128,2048]{1,0:T(8,128)S(1)} %copy-done.17), channel_id=1, source_target_pairs={{0,4},{1,3},{2,6},{3,1},{4,0},{5,7},{6,2},{7,5},{8,12},{9,11},{10,... | collective-permute-start | bytes 3145736 | tf_op jit(solution)/shard_map/ppermute | solution.py:958
  392.2 48.5 %collective-permute-start.9 = (f32[256,1024]{1,0:T(8,128)}, f32[256,1024]{1,0:T(8,128)}, u32[]{:S(2)}, u32[]{:S(2)}) collective-permute-start(f32[256,1024]{1,0:T(8,128)} %get-tuple-element.149.refs_7_), channel_id=1, source_target_pairs={{0,4},{1,3},{2,6},{3,1},{4,0},{5,7},{6,2},{7,5},{8,12},{9,11},{10,... | collective-permute-start | bytes 3145736 | tf_op jit(solution)/shard_map/ppermute | solution.py:958
  403.8 73.5 %collective-permute-start.8 = (f32[256,2560]{1,0:T(8,128)}, f32[256,2560]{1,0:T(8,128)}, u32[]{:S(2)}, u32[]{:S(2)}) collective-permute-start(f32[256,2560]{1,0:T(8,128)} %get-tuple-element.139.refs_8_), channel_id=1, source_target_pairs={{0,2},{1,5},{2,0},{3,7},{4,6},{5,1},{6,4},{7,3},{8,10},{9,13},{10,... | collective-permute-start | bytes 7864328 | tf_op jit(solution)/shard_map/ppermute | solution.py:958
  413.4 36.8 %collective-permute-start.12 = (f32[64,2048]{1,0:T(8,128)}, f32[64,2048]{1,0:T(8,128)}, u32[]{:S(2)}, u32[]{:S(2)}) collective-permute-start(f32[64,2048]{1,0:T(8,128)} %get-tuple-element.153.refs_5_), channel_id=1, source_target_pairs={{0,8},{1,9},{2,10},{3,11},{4,12},{5,13},{6,14},{7,15},{8,0},{9,1},... | collective-permute-start | bytes 1572872 | tf_op jit(solution)/shard_map/ppermute | solution.py:958
  434.8 54.4 %all-to-all-start.6 = ((f32[16,128,128]{2,1,0:T(8,128)}), f32[16,128,128]{2,1,0:T(8,128)}, u32[]{:S(2)}, u32[]{:S(2)}) async-start(f32[16,128,128]{2,1,0:T(8,128)} %copy-done.34), calls=%async_computation.6 | async-start | bytes 2097152 | tf_op jit(solution)/shard_map/all_to_all | solution.py:825
  440.7 9.6 %copy-start.6 = (f32[64,2048]{1,0:T(8,128)S(1)}, f32[64,2048]{1,0:T(8,128)}, u32[]{:S(2)}) copy-start(f32[64,2048]{1,0:T(8,128)} %get-tuple-element.152.refs_6_) | copy-start | bytes 1572868
  443.1 33.2 %copy-start.7 = (f32[128,1024]{1,0:T(8,128)S(1)}, f32[128,1024]{1,0:T(8,128)}, u32[]{:S(2)}) copy-start(f32[128,1024]{1,0:T(8,128)} %get-tuple-element.154.refs_4_) | copy-start | bytes 1572868
  443.1 33.2 %collective-permute-start.11 = (f32[128,1024]{1,0:T(8,128)}, f32[128,1024]{1,0:T(8,128)}, u32[]{:S(2)}, u32[]{:S(2)}) collective-permute-start(f32[128,1024]{1,0:T(8,128)} %get-tuple-element.155.refs_3_), channel_id=1, source_target_pairs={{0,8},{1,9},{2,10},{3,11},{4,12},{5,13},{6,14},{7,15},{8,0},{9,1},... | collective-permute-start | bytes 1572872 | tf_op jit(solution)/shard_map/ppermute | solution.py:958
  451.2 30.7 %copy-start.26 = (f32[32,2048]{1,0:T(8,128)}, f32[32,2048]{1,0:T(8,128)S(1)}, u32[]{:S(2)}) copy-start(f32[32,2048]{1,0:T(8,128)S(1)} %slice_add_fusion.22.refs_22_) | copy-start | bytes 786436
  451.2 46.9 %collective-permute-start.17 = (f32[32,2048]{1,0:T(8,128)S(1)}, f32[32,2048]{1,0:T(8,128)}, u32[]{:S(2)}, u32[]{:S(2)}) collective-permute-start(f32[32,2048]{1,0:T(8,128)S(1)} %slice_add_fusion.22.refs_22_), channel_id=1, source_target_pairs={{0,16},{1,17},{2,18},{3,19},{4,20},{5,21},{6,22},{7,23},{8,24},{9,... | collective-permute-start | bytes 786440 | tf_op jit(solution)/shard_map/ppermute | solution.py:958
  477.3 18.9 %collective-permute-start.16 = (f32[64,1024]{1,0:T(8,128)S(1)}, f32[64,1024]{1,0:T(8,128)}, u32[]{:S(2)}, u32[]{:S(2)}) collective-permute-start(f32[64,1024]{1,0:T(8,128)S(1)} %slice_add_fusion.24.refs_20_), channel_id=1, source_target_pairs={{0,16},{1,17},{2,18},{3,19},{4,20},{5,21},{6,22},{7,23},{8,24},{9,... | collective-permute-start | bytes 786440 | tf_op jit(solution)/shard_map/ppermute | solution.py:958
  481.9 31.8 %collective-permute-start.13 = (f32[128,2560]{1,0:T(8,128)}, f32[128,2560]{1,0:T(8,128)}, u32[]{:S(2)}, u32[]{:S(2)}) collective-permute-start(f32[128,2560]{1,0:T(8,128)} %get-tuple-element.145.refs_7_), channel_id=1, source_target_pairs={{0,4},{1,3},{2,6},{3,1},{4,0},{5,7},{6,2},{7,5},{8,12},{9,11},{10,... | collective-permute-start | bytes 3932168 | tf_op jit(solution)/shard_map/ppermute | solution.py:958
  491.5 10.3 %copy-start.56 = (f32[8,512]{1,0:T(8,128)S(1)}, f32[8,512]{1,0:T(8,128)}, u32[]{:S(2)}) copy-start(f32[8,512]{1,0:T(8,128)} %copy-done.54) | copy-start | bytes 49156
  491.5 26.5 %all-to-all-start.7 = ((f32[16,128,128]{2,1,0:T(8,128)}), f32[16,128,128]{2,1,0:T(8,128)}, u32[]{:S(2)}, u32[]{:S(2)}) async-start(f32[16,128,128]{2,1,0:T(8,128)} %copy-done.15), calls=%async_computation.7 | async-start | bytes 2097152 | tf_op jit(solution)/shard_map/all_to_all | solution.py:825
  516.1 31.3 %collective-permute-start.15 = (f32[64,2560]{1,0:T(8,128)}, f32[64,2560]{1,0:T(8,128)}, u32[]{:S(2)}, u32[]{:S(2)}) collective-permute-start(f32[64,2560]{1,0:T(8,128)} %get-tuple-element.151.refs_24_), channel_id=1, source_target_pairs={{0,8},{1,9},{2,10},{3,11},{4,12},{5,13},{6,14},{7,15},{8,0},{9,1},... | collective-permute-start | bytes 1966088 | tf_op jit(solution)/shard_map/ppermute | solution.py:958
  521.0 25.6 %copy-start.126 = (f32[32]{0:T(128)S(1)}, f32[32]{0:T(128)}, u32[]{:S(2)}) copy-start(f32[32]{0:T(128)} %reduce_sum.117) | copy-start | bytes 388
  543.5 12.7 %copy-start.58 = (bf16[512,128]{1,0:T(8,128)(2,1)S(1)}, bf16[512,128]{1,0:T(8,128)(2,1)}, u32[]{:S(2)}) copy-start(bf16[512,128]{1,0:T(8,128)(2,1)} %copy-done.57) | copy-start | bytes 393220
  544.3 11.9 %copy-start.46 = (f32[512,256]{1,0:T(8,128)S(1)}, f32[512,256]{1,0:T(8,128)}, u32[]{:S(2)}) copy-start(f32[512,256]{1,0:T(8,128)} %copy-done.45) | copy-start | bytes 1572868
  545.3 11.0 %collective-permute-start.14 = (f32[8,2304]{1,0:T(8,128)S(1)}, f32[8,2304]{1,0:T(8,128)S(1)}, u32[]{:S(2)}, u32[]{:S(2)}) collective-permute-start(f32[8,2304]{1,0:T(8,128)S(1)} %pad_maximum_fusion.4), channel_id=1, source_target_pairs={{2,0},{4,2},{6,4},{8,6},{10,8},{12,10},{14,12},{16,14},{18,16},{20... | collective-permute-start | bytes 221192 | tf_op jit(solution)/shard_map/ppermute | solution.py:831
  548.5 58.1 %collective-permute-start.18 = (f32[32,2560]{1,0:T(8,128)S(1)}, f32[32,2560]{1,0:T(8,128)S(1)}, u32[]{:S(2)}, u32[]{:S(2)}) collective-permute-start(f32[32,2560]{1,0:T(8,128)S(1)} %get-tuple-element.157.refs_7_), channel_id=1, source_target_pairs={{0,16},{1,17},{2,18},{3,19},{4,20},{5,21},{6,22},{7,23},{8,24},{9,... | collective-permute-start | bytes 983048 | tf_op jit(solution)/shard_map/ppermute | solution.py:958
  582.3 23.9 %all-to-all-start.8 = ((f32[32,1,1152]{2,1,0:T(1,128)}), f32[32,1,1152]{2,1,0:T(1,128)S(1)}, u32[]{:S(2)}, u32[]{:S(2)}) async-start(f32[32,1,1152]{2,1,0:T(1,128)} %copy.53), calls=%async_computation.8 | async-start | bytes 294912 | tf_op jit(solution)/shard_map/all_to_all | solution.py:1124
  (97 other events, 416.7 us)

commit v6 on v5

--- a/solution.py
+++ b/solution.py
@@ -18,22 +18,24 @@
 TILE = 512
 HEADS_AT = TILE // HEAD_DIM
 MAPS = 2 * STATE
-ROWS_STEP = 128
+ROWS_STEP = 256
 SUM_ROWS = 512
-LAG = 2
-AHEAD = 4
+LAG = 3
+AHEAD = 6
+EVERY = 5
 HALO = 8
 HALF = 128
 LOG2E = 1.4426950408889634
 ROWS_AT = 64
-VMEM_BYTES = 48 * 1024 * 1024
+ROWS_CONV = 64
+VMEM_BYTES = 60 * 1024 * 1024
 
 EPS = 1e-05
 HIGHEST = lax.Precision.HIGHEST
 AXES = ("seq", "rows")
 
 
-def pcall(body, grid, in_specs, out_specs, out_shape, scratch, args, flops=0, nbytes=0, after=()):
+def pcall(body, grid, in_specs, out_specs, out_shape, scratch, args, flops=0, nbytes=0, after=(), aliases={}):
     taken = len(args)
 
     def run(*refs):
@@ -46,6 +48,7 @@
         out_specs=out_specs,
         out_shape=out_shape,
         scratch_shapes=scratch,
+        input_output_aliases=aliases,
         compiler_params=pltpu.CompilerParams(vmem_limit_bytes=VMEM_BYTES),
         cost_estimate=pl.CostEstimate(flops=flops, bytes_accessed=nbytes, transcendentals=0),
     )(*args, *after)
@@ -137,11 +140,11 @@
 
 def states_kernel(
     x_ref, xbc_ref, rate_ref, aux_ref, w_ref, wbc_ref, hp_ref,
-    v_ref, bc_ref, col_ref, cumr_ref, made_ref, kx_ref, pay_ref,
+    v_ref, bc_ref, col_ref, cumr_ref, made_ref, kx_ref, pay_ref, slope_ref, slope_bc_ref,
     bt_ref, marks_ref,
 ):
     turn = pl.program_id(0)
-    span = rate_ref.shape[0]
+    span = v_ref.shape[0]
     count = span // GROUP
 
     @pl.when(turn == 0)
@@ -149,14 +152,16 @@
         keep_marks(marks_ref, aux_ref, range(KW - 1))
         for first, rows, lanes in chunks_of(span, MAPS):
             conv = conv_rows(xbc_ref, wbc_ref, marks_ref, first, ROWS_AT, lanes)
-            bc_ref[rows, lanes] = conv * sigmoid(conv)
+            sig = sigmoid(conv)
+            bc_ref[rows, lanes] = conv * sig
+            slope_bc_ref[rows, lanes] = sig * (1.0 + conv * (1.0 - sig))
         tri = (
             lax.broadcasted_iota(jnp.int32, (GROUP, GROUP), 0) >= lane_iota((GROUP, GROUP))
         ).astype(jnp.float32)
         for block in range(count):
             rows = slice(block * GROUP, (block + 1) * GROUP)
             bt_ref[block] = bc_ref[rows, :STATE].T.astype(jnp.bfloat16)
-            raw = rate_ref[rows, :] + hp_ref[0:1, :]
+            raw = rate_ref[HALO + block * GROUP : HALO + (block + 1) * GROUP, :] + hp_ref[0:1, :]
             step = jnp.maximum(raw, 0.0) + jnp.log1p(jnp.exp(-jnp.abs(raw)))
             cum = dot_exact(tri, hp_ref[1:2, :] * step)
             last = cum[GROUP - 1 :, :]
@@ -168,7 +173,9 @@
 
     for first, rows, lanes in chunks_of(span, TILE):
         conv = conv_rows(x_ref, w_ref, marks_ref, first, ROWS_AT, lanes)
-        v_ref[rows, lanes] = conv * sigmoid(conv)
+        sig = sigmoid(conv)
+        v_ref[rows, lanes] = conv * sig
+        slope_ref[rows, lanes] = sig * (1.0 + conv * (1.0 - sig))
     pick = head_pick(turn * HEADS_AT, HEADS_AT)
     made = []
     keep = []
@@ -368,39 +375,29 @@
     dbc_ref[:, STATE:] = dot(dg.T, bc_ref[:, :STATE])
 
 
-def states_back_kernel(
-    xi_ref, v_ref, dy_ref, yi_ref, x_ref, xbc_ref, bc_ref, col_ref, dso_ref, sin_ref, made_ref, d1_ref,
-    kx_ref, dbc_ref, aux_ref, w_ref, wbc_ref, ch_ref, hp_ref, rate_ref,
-    dconv_ref, dconv_bc_ref, drate_ref, sum_ref,
-    ds_ref, dc_ref, z_ref, kd_ref, dmap_ref, marks_ref,
+def states_pre_kernel(
+    xi_ref, v_ref, dy_ref, yi_ref, bc_ref, col_ref, sin_ref, made_ref, kx_ref, dbc_ref, ch_ref,
+    base_ref, ds_ref, dc_ref, dmap_ref,
 ):
     turn = pl.program_id(0)
-    span = v_ref.shape[0]
-    count = span // GROUP
+    count = v_ref.shape[0] // GROUP
 
     @pl.when(turn == 0)
     def _():
-        keep_marks(marks_ref, aux_ref, range(KW - 1))
         ds_ref[...] = jnp.zeros_like(ds_ref)
         dc_ref[...] = jnp.zeros_like(dc_ref)
-        z_ref[...] = jnp.zeros_like(z_ref)
-        kd_ref[...] = jnp.zeros_like(kd_ref)
         dmap_ref[...] = dbc_ref[...]
 
     sums = head_sums(turn * HEADS_AT)
     pick = head_pick(turn * HEADS_AT, HEADS_AT)
-    end_grad = jnp.concatenate([dso_ref[pair] for pair in range(TILE // 128)], 1)
     state = jnp.concatenate([sin_ref[pair] for pair in range(TILE // 128)], 1)
-    ends = [d1_ref[...] + kx_ref[1:2, :] * end_grad, end_grad]
     starts = [state, kx_ref[0:1, :] * state + made_ref[...]]
     for block in range(count):
         at = slice(block * GROUP, (block + 1) * GROUP)
         step = picked_heads(col_ref[1, at, :], pick)
         entering = picked_heads(col_ref[2, at, :], pick)
-        tail = picked_heads(col_ref[3, at, :], pick)
-        from_end = dot(bc_ref[at, :STATE], ends[block])
         outer = dot(bc_ref[at, STATE:], starts[block])
-        kinds = {name: [] for name in ("ds", "z", "dc", "low", "values", "dy")}
+        kinds = {name: [] for name in ("ds", "dc", "low", "dy")}
         for first in range(0, GROUP, ROWS_AT):
             local = slice(first, first + ROWS_AT)
             rows = slice(block * GROUP + first, block * GROUP + first + ROWS_AT)
@@ -413,28 +410,70 @@
                 scaled = step[local, lanes] * v
                 low = dy.astype(jnp.bfloat16).astype(jnp.float32)
                 inside = low * yi_ref[rows, lanes] - scaled.astype(jnp.bfloat16).astype(jnp.float32) * xi
-                ended = tail[local, lanes] * from_end[local, lanes]
                 inside = inside + dy * (entering[local, lanes] * outer[local, lanes])
-                pulled = xi + ended
                 high = inside.astype(jnp.bfloat16)
                 pieces["dc"].append(high)
                 pieces["low"].append((inside - high.astype(jnp.float32)).astype(jnp.bfloat16))
-                pieces["ds"].append((v * pulled).astype(jnp.bfloat16))
+                pieces["ds"].append((v * xi).astype(jnp.bfloat16))
+                pieces["dy"].append((entering[local, lanes] * dy).astype(jnp.bfloat16))
+                base_ref[rows, lanes] = step[local, lanes] * xi + ch_ref[0:1, lanes] * dy
+            for name in kinds:
+                kinds[name].append(jnp.concatenate(pieces[name], 1))
+        whole = {name: jnp.concatenate(parts, 0) for name, parts in kinds.items()}
+        ds_ref[at, :] += dot(whole["ds"], sums)
+        dc_ref[at, :] += dot(whole["dc"], sums) + dot(whole["low"], sums)
+        dmap_ref[at, STATE:] += dot_nt(whole["dy"], starts[block])
+
+
+def states_back_kernel(
+    base_ref, v_ref, slope_ref, slope_bc_ref, bc_ref, col_ref, dso_ref, sin_ref, made_ref, d1_ref,
+    kx_ref, ds0_ref, dc_ref, dmap0_ref, hp_ref, rate_ref,
+    dconv_ref, dconv_bc_ref, drate_ref, sum_ref,
+    ds_ref, z_ref, kd_ref, dmap_ref,
+):
+    turn = pl.program_id(0)
+    span = v_ref.shape[0]
+    count = span // GROUP
+
+    @pl.when(turn == 0)
+    def _():
+        ds_ref[...] = ds0_ref[...]
+        z_ref[...] = jnp.zeros_like(z_ref)
+        kd_ref[...] = jnp.zeros_like(kd_ref)
+        dmap_ref[...] = dmap0_ref[...]
+
+    sums = head_sums(turn * HEADS_AT)
+    pick = head_pick(turn * HEADS_AT, HEADS_AT)
+    end_grad = jnp.concatenate([dso_ref[pair] for pair in range(TILE // 128)], 1)
+    state = jnp.concatenate([sin_ref[pair] for pair in range(TILE // 128)], 1)
+    ends = [d1_ref[...] + kx_ref[1:2, :] * end_grad, end_grad]
+    starts = [state, kx_ref[0:1, :] * state + made_ref[...]]
+    for block in range(count):
+        at = slice(block * GROUP, (block + 1) * GROUP)
+        step = picked_heads(col_ref[1, at, :], pick)
+        tail = picked_heads(col_ref[3, at, :], pick)
+        from_end = dot(bc_ref[at, :STATE], ends[block])
+        kinds = {name: [] for name in ("ds", "z", "values")}
+        for first in range(0, GROUP, ROWS_AT):
+            local = slice(first, first + ROWS_AT)
+            rows = slice(block * GROUP + first, block * GROUP + first + ROWS_AT)
+            pieces = {name: [] for name in kinds}
+            for pair in range(TILE // 128):
+                lanes = slice(pair * 128, (pair + 1) * 128)
+                v = v_ref[rows, lanes]
+                scaled = step[local, lanes] * v
+                ended = tail[local, lanes] * from_end[local, lanes]
+                pieces["ds"].append((v * ended).astype(jnp.bfloat16))
                 pieces["z"].append((scaled * ended).astype(jnp.bfloat16))
                 pieces["values"].append((tail[local, lanes] * scaled).astype(jnp.bfloat16))
-                pieces["dy"].append((entering[local, lanes] * dy).astype(jnp.bfloat16))
-                grad = step[local, lanes] * pulled + ch_ref[0:1, lanes] * dy
-                conv = conv_rows(x_ref, w_ref, marks_ref, block * GROUP + first, ROWS_AT, lanes)
-                sig = sigmoid(conv)
-                dconv_ref[rows, lanes] = grad * (sig * (1.0 + conv * (1.0 - sig)))
+                grad = base_ref[rows, lanes] + step[local, lanes] * ended
+                dconv_ref[rows, lanes] = grad * slope_ref[rows, lanes]
             for name in kinds:
                 kinds[name].append(jnp.concatenate(pieces[name], 1))
         whole = {name: jnp.concatenate(parts, 0) for name, parts in kinds.items()}
         ds_ref[at, :] += dot(whole["ds"], sums)
         z_ref[at, :] += dot(whole["z"], sums)
-        dc_ref[at, :] += dot(whole["dc"], sums) + dot(whole["low"], sums)
         dmap_ref[at, :STATE] += dot_nt(whole["values"], ends[block])
-        dmap_ref[at, STATE:] += dot_nt(whole["dy"], starts[block])
         kept = kx_ref[block : block + 1, :] * jnp.sum(ends[block] * starts[block], 0, keepdims=True)
         kd_ref[block] += dot_exact(jnp.broadcast_to(kept, (8, TILE)), sums.astype(jnp.float32))
 
@@ -446,16 +485,13 @@
         bias_sum = jnp.zeros((1, 128), jnp.float32)
         decay_sum = jnp.zeros((1, 128), jnp.float32)
         for first, rows, lanes in chunks_of(span, MAPS):
-            conv = conv_rows(xbc_ref, wbc_ref, marks_ref, first, ROWS_AT, lanes)
-            sig = sigmoid(conv)
-            dconv_bc_ref[rows, lanes] = dmap_ref[rows, lanes] * (sig * (1.0 + conv * (1.0 - sig)))
+            dconv_bc_ref[rows, lanes] = dmap_ref[rows, lanes] * slope_bc_ref[rows, lanes]
         for block in range(count):
             rows = slice(block * GROUP, (block + 1) * GROUP)
-            z = z_ref[rows, :]
             da = dot_exact(after, dc_ref[rows, :]) + kd_ref[block, 0:1, :]
-            da = da + dot_exact(before, z)
+            da = da + dot_exact(before, z_ref[rows, :])
             ds = ds_ref[rows, :] + hp_ref[1:2, :] * da
-            drate = ds * sigmoid(rate_ref[rows, :] + hp_ref[0:1, :])
+            drate = ds * sigmoid(rate_ref[HALO + block * GROUP : HALO + (block + 1) * GROUP, :] + hp_ref[0:1, :])
             drate_ref[rows, :] = drate.astype(jnp.bfloat16)
             bias_sum = bias_sum + jnp.sum(drate, 0, keepdims=True)
             decay_sum = decay_sum + jnp.sum(da * hp_ref[1:2, :] * col_ref[1, rows, :], 0, keepdims=True)
@@ -463,7 +499,7 @@
 
 
 def conv_back_kernel(
-    dconv_ref, dconv_bc_ref, drate_ref, next_ref, x_ref, aux_ref, w_ref, dx_ref, sum_ref, ext_ref, marks_ref
+    dconv_ref, dconv_bc_ref, drate_ref, next_ref, x_ref, aux_ref, w_ref, dx_ref, sum_ref, marks_ref
 ):
     turn = pl.program_id(0)
     last = pl.num_programs(0) - 1
@@ -471,39 +507,42 @@
 
     @pl.when(turn == 0)
     def _():
-        keep_marks(marks_ref, aux_ref, (0, 1, 2, 6, 7, 8))
+        keep_marks(marks_ref, aux_ref, (6, 7, 8))
+
+    def tile(source_ref, width):
+        for pair in range(width // 128):
+            lanes = slice(pair * 128, (pair + 1) * 128)
+            sums = [jnp.zeros((8, 128), jnp.float32) for _ in range(KW + 1)]
+            weights = [jnp.broadcast_to(w_ref[tap : tap + 1, lanes], (8, 128)) for tap in range(KW)]
+            for first in range(0, span, ROWS_CONV):
+                rows = slice(first, first + ROWS_CONV)
+                following = next_ref if first + ROWS_CONV == span else source_ref
+                at = 0 if first + ROWS_CONV == span else first + ROWS_CONV
+                here = source_ref[rows, lanes]
+                whole = jnp.concatenate([here, following[at : at + 8, lanes]], 0)
+                x = x_ref[HALO + first : HALO + first + ROWS_CONV, lanes]
+                split = lambda v: v.reshape(ROWS_CONV // 8, 8, 128)
+                x8, here8 = split(x), split(here)
+                grad = weights[KW - 1] * here8
+                sums[KW] = sums[KW] + jnp.sum(here8, 0)
+                sums[KW - 1] = sums[KW - 1] + jnp.sum(here8 * x8, 0)
+                for ahead in range(1, KW):
+                    later = split(whole[ahead : ahead + ROWS_CONV] * marks_ref[ahead - 1, rows, :])
+                    tap = KW - 1 - ahead
+                    grad = grad + weights[tap] * later
+                    sums[tap] = sums[tap] + jnp.sum(later * x8, 0)
+                dx_ref[rows, lanes] = grad.reshape(ROWS_CONV, 128).astype(jnp.bfloat16)
+            sums = [jnp.sum(part, 0, keepdims=True) for part in sums]
+            sum_ref[:, lanes] = jnp.concatenate(sums + [jnp.zeros((3, 128), jnp.float32)], 0)
 
     @pl.when(turn < last)
     def _():
-        ext_ref[:span, :] = dconv_ref[...]
+        tile(dconv_ref, TILE)
 
     @pl.when(turn == last)
     def _():
-        ext_ref[:span, :MAPS] = dconv_bc_ref[...]
-
-    ext_ref[span:, :] = next_ref[...]
-    for pair in range(TILE // 128):
-        lanes = slice(pair * 128, (pair + 1) * 128)
-        sums = [jnp.zeros((8, 128), jnp.float32) for _ in range(KW + 1)]
-        for first in range(0, span, ROWS_AT):
-            rows = slice(first, first + ROWS_AT)
-            here = ext_ref[rows, lanes]
-            grad = w_ref[3:4, lanes] * here
-            for ahead in range(1, KW):
-                shifted_grad = ext_ref[first + ahead : first + ahead + ROWS_AT, lanes]
-                grad = grad + w_ref[3 - ahead : 4 - ahead, lanes] * (shifted_grad * marks_ref[2 + ahead, rows, :])
-            dx_ref[rows, lanes] = grad.astype(jnp.bfloat16)
-            for tap in range(KW):
-                term = here * x_ref[first + 5 + tap : first + 5 + tap + ROWS_AT, lanes]
-                if tap < KW - 1:
-                    term = term * marks_ref[tap, rows, :]
-                sums[tap] = sums[tap] + jnp.sum(term.reshape(-1, 8, 128), 0)
-            sums[KW] = sums[KW] + jnp.sum(here.reshape(-1, 8, 128), 0)
-        sums = [jnp.sum(part, 0, keepdims=True) for part in sums]
-        sum_ref[:, lanes] = jnp.concatenate(sums + [jnp.zeros((3, 128), jnp.float32)], 0)
-
-    @pl.when(turn == last)
-    def _():
+        tile(dconv_bc_ref, MAPS)
+        sum_ref[:, MAPS:] = jnp.zeros_like(sum_ref[:, MAPS:])
         dx_ref[:, MAPS : MAPS + 128] = drate_ref[...]
         dx_ref[:, MAPS + 128 :] = jnp.zeros_like(drate_ref)
 
@@ -534,10 +573,10 @@
                 out_ref[part] = split[:, part].reshape(size, rows.shape[1])
 
 
-def sums_kernel(counts, masks, *refs):
+def sums_kernel(counts, orders, *refs):
     pieces = len(counts)
     sends, keeps, out_ref, kept_ref = refs[:pieces], refs[pieces : 2 * pieces], refs[2 * pieces], refs[2 * pieces + 1]
-    stages = len(masks)
+    stages = len(orders[0])
     got = refs[2 * pieces + 2 : 2 * pieces + 2 + stages]
     load_sem, send_sem, recv_sem = refs[2 * pieces + 2 + stages :]
     chunks = sum(counts)
@@ -547,21 +586,34 @@
     def over(at, mask):
         return at + mask * (1 - 2 * lax.rem(at // mask, 2))
 
-    partners = []
-    for axis, even_mask, odd_mask in masks:
-        if axis == "rows":
-            partners.append({"seq": seq, "rows": over(row, even_mask)})
-        else:
-            one, two = over(seq, even_mask), over(seq, odd_mask)
-            partners.append({"seq": one + odd * (two - one), "rows": row})
+    routes = []
+    for masks in orders:
+        partners = []
+        for axis, even_mask, odd_mask in masks:
+            if axis == "rows":
+                partners.append((seq, over(row, even_mask)))
+            else:
+                one, two = over(seq, even_mask), over(seq, odd_mask)
+                partners.append((one + odd * (two - one), row))
+        routes.append(partners)
 
     barrier = pltpu.get_barrier_semaphore()
-    for partner in partners:
-        pl.semaphore_signal(barrier, inc=1, device_id=partner, device_id_type=pl.DeviceIdType.MESH)
+    for partner in routes[0]:
+        pl.semaphore_signal(
+            barrier,
+            inc=1,
+            device_id={"seq": partner[0], "rows": partner[1]},
+            device_id_type=pl.DeviceIdType.MESH,
+        )
     pl.semaphore_wait(barrier, stages)
+
+    def second(chunk):
+        return (EVERY - lax.rem(chunk, EVERY)) // EVERY
 
     def copy(stage, chunk, source=None):
         size = SUM_ROWS >> stage
+        other = second(chunk)
+        main, side = routes[0][stage], routes[1][stage]
         if source is None:
             source = kept_ref.at[chunk] if stage == 0 else kept_ref.at[chunk, pl.ds(size, size)]
         return pltpu.make_async_remote_copy(
@@ -569,7 +621,10 @@
             dst_ref=got[stage].at[chunk],
             send_sem=send_sem.at[stage, chunk],
             recv_sem=recv_sem.at[stage, chunk],
-            device_id=partners[stage],
+            device_id={
+                "seq": main[0] + other * (side[0] - main[0]),
+                "rows": main[1] + other * (side[1] - main[1]),
+            },
             device_id_type=pl.DeviceIdType.MESH,
         )
 
@@ -577,13 +632,21 @@
         return pltpu.make_async_copy(source, kept_ref.at[chunk], load_sem.at[chunk])
 
     def begin(chunk):
+        side = second(chunk)
+        inner = chunk - chunk // EVERY - 1
+
+        @pl.when((side == 1) & (chunk < chunks))
+        def _():
+            copy(0, chunk, sends[0].at[chunk // EVERY]).start()
+            load(chunk, keeps[0].at[chunk // EVERY]).start()
+
         base = 0
-        for count, send_ref, keep_ref in zip(counts, sends, keeps):
-
-            @pl.when((chunk >= base) & (chunk < base + count))
+        for count, send_ref, keep_ref in zip(counts[1:], sends[1:], keeps[1:]):
+
+            @pl.when((side == 0) & (inner >= base) & (inner < base + count))
             def _(base=base, send_ref=send_ref, keep_ref=keep_ref):
-                copy(0, chunk, send_ref.at[chunk - base]).start()
-                load(chunk, keep_ref.at[chunk - base]).start()
+                copy(0, chunk, send_ref.at[inner - base]).start()
+                load(chunk, keep_ref.at[inner - base]).start()
 
             base += count
 
@@ -623,6 +686,108 @@
     lax.fori_loop(0, chunks, ended, 0)
 
 
+def edge(weights, width, first):
+    row = lax.broadcasted_iota(jnp.int32, weights.shape, 0)
+    return jnp.where(first + row < width, weights, jnp.zeros_like(weights))
+
+
+def project_kernel(width, first_block, x_ref, before_ref, gain_ref, w_ref, normed_ref, out_ref, ext_ref):
+    turn = pl.program_id(0)
+    last = pl.num_programs(0) - 1
+
+    @pl.when(turn == 0)
+    def _():
+        def scaled(values):
+            scale = lax.rsqrt(jnp.mean(values * values, 1, keepdims=True) + EPS)
+            return (values * scale * gain_ref[...]).astype(jnp.bfloat16)
+
+        for first in range(0, x_ref.shape[0], ROWS_AT):
+            rows = slice(first, first + ROWS_AT)
+            normed_ref[rows, :] = scaled(x_ref[rows, :])
+        ext_ref[...] = jnp.concatenate([scaled(before_ref[...]), normed_ref[...]], 0)
+
+    @pl.when(turn < last)
+    def _():
+        out_ref[...] = dot_nt(ext_ref[...], w_ref[0])
+
+    @pl.when(turn == last)
+    def _():
+        out_ref[...] = dot_nt(ext_ref[...], edge(w_ref[0], width, (first_block + last) * TILE))
+
+
+def gate_kernel(normed_ref, w_ref, out_ref):
+    out_ref[...] = dot_nt(normed_ref[...], w_ref[0])
+
+
+def project_back_gate_kernel(dgate_ref, w_ref, out_ref):
+    @pl.when(pl.program_id(0) == 0)
+    def _():
+        out_ref[...] = dot(dgate_ref[...], w_ref[0])
+
+    @pl.when(pl.program_id(0) > 0)
+    def _():
+        out_ref[...] += dot(dgate_ref[...], w_ref[0])
+
+
+def project_back_kernel(
+    width, first_block, part_ref, dmixed_ref, w_ref, x_ref, grad_ref, gain_ref,
+    new_ref, low_ref, sum_ref,
+    acc_ref,
+):
+    turn = pl.program_id(0)
+    last = pl.num_programs(0) - 1
+
+    @pl.when(turn == 0)
+    def _():
+        acc_ref[...] = part_ref[...] + dot(dmixed_ref[...], w_ref[0])
+
+    @pl.when((turn > 0) & (turn < last))
+    def _():
+        acc_ref[...] += dot(dmixed_ref[...], w_ref[0])
+
+    @pl.when(turn == last)
+    def _():
+        acc_ref[...] += dot(dmixed_ref[...], edge(w_ref[0], width, (first_block + last) * TILE))
+        total = jnp.zeros((8, x_ref.shape[1]), jnp.float32)
+        for first in range(0, x_ref.shape[0], 16):
+            rows = slice(first, first + 16)
+            x = x_ref[rows, :]
+            grad = acc_ref[rows, :]
+            scale = lax.rsqrt(jnp.mean(x * x, 1, keepdims=True) + EPS)
+            pulled = grad * gain_ref[...]
+            cross = jnp.mean(pulled * x, 1, keepdims=True)
+            scaled = x * scale
+            total = total + grad[:8] * scaled[:8] + grad[8:] * scaled[8:]
+            new = grad_ref[rows, :] + (scale * pulled - x * (scale * scale * scale * cross))
+            new_ref[rows, :] = new
+            low_ref[rows, :] = new.astype(jnp.bfloat16)
+        sum_ref[...] = total
+
+
+def plain_weight_kernel(left_ref, right_ref, *refs):
+    out_ref = refs[-1]
+    out_ref[...] = dot(left_ref[...], right_ref[...], (((0,), (0,)), ((), ())))
+
+
+def sort_kernel(source_ref, values_ref, out_ref):
+    pick = (source_ref[...] == lane_iota((source_ref.shape[0], values_ref.shape[1]))).astype(jnp.bfloat16)
+    out_ref[...] = dot_nt(pick, values_ref[...]).astype(jnp.bfloat16)
+
+
+def assemble_kernel(outs, ins, total_ref, in_ref, all_out_ref, all_in_ref):
+    rows = total_ref.shape[1]
+    for level, parts in enumerate(outs):
+        for part, places in enumerate(parts):
+            for at, place in enumerate(places):
+                lanes = slice(at * 256, (at + 1) * 256)
+                all_out_ref[level, part * rows : (part + 1) * rows, lanes] = total_ref[place]
+    columns = all_in_ref.shape[2]
+    for at, place in enumerate(ins):
+        size = min(256, columns - at * 256)
+        all_in_ref[0, :, at * 256 : at * 256 + size] = total_ref[place, :, :size]
+    all_in_ref[1] = in_ref[:, :columns]
+
+
 def full(shape):
     return pl.BlockSpec(shape, lambda *at: (0,) * len(shape))
 
@@ -635,8 +800,9 @@
     return pltpu.VMEM(dims, dtype)
 
 
-def make_states(peers, mixed_ext, rate, aux, conv, hp):
-    span = rate.shape[0]
+def make_states(peers, mixed_ext, aux, conv, hp):
+    span = aux.shape[0]
+    rate = pl.BlockSpec((span + HALO, 128), lambda g: (0, CHANNELS // 128))
     groups = DI // TILE
     chunks = peers * 128 // DI
     tile = lambda rows: pl.BlockSpec((rows, TILE), lambda g: (0, g))
@@ -645,7 +811,7 @@
     return pcall(
         states_kernel,
         (groups,),
-        [tile(span + HALO), maps(span + HALO), full((span, 128)), full((span, 128)), tile(8), maps(8), full((8, 128))],
+        [tile(span + HALO), maps(span + HALO), rate, full((span, 128)), tile(8), maps(8), full((8, 128))],
         [
             tile(span),
             full((span, MAPS)),
@@ -654,6 +820,8 @@
             tile(STATE),
             tile(8),
             pl.BlockSpec(pay, lambda g: (g, 0, 0)),
+            tile(span),
+            full((span, MAPS)),
         ],
         [
             shape_of((span, DI)),
@@ -663,9 +831,11 @@
             shape_of((STATE, DI)),
             shape_of((8, DI)),
             shape_of((peers,) + pay[1:]),
+            shape_of((span, DI)),
+            shape_of((span, MAPS)),
         ],
         [vmem((span // GROUP, STATE, GROUP), jnp.bfloat16), vmem((KW - 1, span, 128))],
-        (mixed_ext, mixed_ext, rate, aux, conv, conv, hp),
+        (mixed_ext, mixed_ext, mixed_ext, aux, conv, conv, hp),
         flops=2 * span * DI * STATE,
         nbytes=12 * span * DI,
     )
@@ -759,28 +929,46 @@
     )
 
 
-def states_back(xi, values, dy, yi, mixed_ext, bc, col, dso, state_in, made, d1, kx, dbc, aux, conv, ch, hp, rate, after=()):
+def states_pre(xi, values, dy, yi, bc, col, state_in, made, kx, dbc, ch):
     span = values.shape[0]
-    groups = DI // TILE
     tile = lambda rows: pl.BlockSpec((rows, TILE), lambda g: (0, g))
-    maps = lambda rows: pl.BlockSpec((rows, MAPS), lambda g: (0, DI // MAPS))
     state = pl.BlockSpec((TILE // 128, STATE, 128), lambda g: (g, 0, 0))
-    small = full((span, 128))
+    small, maps = full((span, 128)), full((span, MAPS))
+    return pcall(
+        states_pre_kernel,
+        (DI // TILE,),
+        [
+            tile(span), tile(span), tile(span), tile(span), maps, full((4, span, 128)),
+            state, tile(STATE), tile(8), maps, tile(8),
+        ],
+        [tile(span), small, small, maps],
+        [shape_of((span, DI)), shape_of((span, 128)), shape_of((span, 128)), shape_of((span, MAPS))],
+        [],
+        (xi, values, dy, yi, bc, col, state_in, made, kx, dbc, ch),
+        flops=4 * span * DI * STATE,
+        nbytes=20 * span * DI,
+    )
+
+
+def states_back(base, values, slope, slope_bc, bc, col, dso, state_in, made, d1, kx, ds, dc, dmap, hp, mixed_ext):
+    span = values.shape[0]
+    tile = lambda rows: pl.BlockSpec((rows, TILE), lambda g: (0, g))
+    state = pl.BlockSpec((TILE // 128, STATE, 128), lambda g: (g, 0, 0))
+    small, maps = full((span, 128)), full((span, MAPS))
+    rate = pl.BlockSpec((span + HALO, 128), lambda g: (0, CHANNELS // 128))
     return pcall(
         states_back_kernel,
-        (groups,),
+        (DI // TILE,),
         [
-            tile(span), tile(span), tile(span), tile(span), tile(span + HALO), maps(span + HALO), full((span, MAPS)),
-            full((4, span, 128)), state, state, tile(STATE), tile(STATE), tile(8), full((span, MAPS)),
-            small, tile(8), maps(8), tile(8), full((8, 128)), small,
+            tile(span), tile(span), tile(span), maps, maps, full((4, span, 128)),
+            state, state, tile(STATE), tile(STATE), tile(8), small, small, maps, full((8, 128)), rate,
         ],
-        [tile(span), full((span, MAPS)), small, full((8, 128))],
+        [tile(span), maps, small, full((8, 128))],
         [shape_of((span, DI)), shape_of((span, MAPS)), shape_of((span, 128), jnp.bfloat16), shape_of((8, 128))],
-        [vmem((span, 128)), vmem((span, 128)), vmem((span, 128)), vmem((span // GROUP, 8, 128)), vmem((span, MAPS)), vmem((KW - 1, span, 128))],
-        (xi, values, dy, yi, mixed_ext, mixed_ext, bc, col, dso, state_in, made, d1, kx, dbc, aux, conv, conv, ch, hp, rate),
-        flops=8 * span * DI * STATE,
-        nbytes=20 * span * DI,
-        after=after,
+        [vmem((span, 128)), vmem((span, 128)), vmem((span // GROUP, 8, 128)), vmem((span, MAPS))],
+        (base, values, slope, slope_bc, bc, col, dso, state_in, made, d1, kx, ds, dc, dmap, hp, mixed_ext),
+        flops=4 * span * DI * STATE,
+        nbytes=16 * span * DI,
     )
 
 
@@ -796,12 +984,105 @@
             full((span, MAPS)), full((span, 128)), tile(HALO), tile(span + HALO), full((span, 128)), tile(8),
         ],
         [tile(span), tile(8)],
-        [shape_of((span, DI + TILE), jnp.bfloat16), shape_of((8, CHANNELS))],
-        [vmem((span + HALO, TILE)), vmem((2 * (KW - 1), span, 128))],
+        [shape_of((span, DI + TILE), jnp.bfloat16), shape_of((8, DI + TILE))],
+        [vmem((KW - 1, span, 128))],
         (dconv, dconv_bc, drate, following, mixed_ext, aux, conv),
         flops=8 * span * DI,
         nbytes=10 * span * DI,
         after=after,
+    )
+
+
+def project(depth, hidden, before, gain, weight):
+    span, width = hidden.shape
+    columns = weight.shape[1]
+    first, blocks = DI // TILE, pl.cdiv(columns - DI, TILE)
+    return pcall(
+        partial(project_kernel, columns, first),
+        (blocks,),
+        [
+            full((span, width)), full((HALO, width)), full((1, width)),
+            pl.BlockSpec((1, TILE, width), lambda g: (depth, first + g, 0)),
+        ],
+        [full((span, width)), pl.BlockSpec((span + HALO, TILE), lambda g: (0, g))],
+        [shape_of((span, width), jnp.bfloat16), shape_of((span + HALO, blocks * TILE))],
+        [vmem((span + HALO, width), jnp.bfloat16)],
+        (hidden, before, gain[None], weight),
+        flops=2 * span * width * blocks * TILE,
+        nbytes=4 * span * blocks * TILE,
+    )
+
+
+def project_gate(depth, normed, weight):
+    span, width = normed.shape
+    return pcall(
+        gate_kernel,
+        (DI // TILE,),
+        [full((span, width)), pl.BlockSpec((1, TILE, width), lambda g: (depth, g, 0))],
+        pl.BlockSpec((span, TILE), lambda g: (0, g)),
+        shape_of((span, DI)),
+        [],
+        (normed, weight),
+        flops=2 * span * width * DI,
+        nbytes=4 * span * DI,
+    )
+
+
+def project_back_gate(depth, dgate, weight, after=()):
+    span, width = dgate.shape[0], weight.shape[2]
+    return pcall(
+        project_back_gate_kernel,
+        (DI // TILE,),
+        [pl.BlockSpec((span, TILE), lambda g: (0, g)), pl.BlockSpec((1, TILE, width), lambda g: (depth, g, 0))],
+        full((span, width)),
+        shape_of((span, width)),
+        [],
+        (dgate, weight),
+        flops=2 * span * width * DI,
+        nbytes=2 * width * DI,
+        after=after,
+    )
+
+
+def project_back(depth, part, dmixed, weight, entry, gradient, gain, after=()):
+    span, width = entry.shape
+    columns = weight.shape[1]
+    first, blocks = DI // TILE, pl.cdiv(columns - DI, TILE)
+    return pcall(
+        partial(project_back_kernel, columns, first),
+        (blocks,),
+        [
+            full((span, width)),
+            pl.BlockSpec((span, TILE), lambda g: (0, g)),
+            pl.BlockSpec((1, TILE, width), lambda g: (depth, first + g, 0)),
+            full((span, width)), full((span, width)), full((1, width)),
+        ],
+        [full((span, width)), full((span, width)), full((8, width))],
+        [shape_of((span, width)), shape_of((span, width), jnp.bfloat16), shape_of((8, width))],
+        [vmem((span, width))],
+        (part, dmixed, weight, entry, gradient, gain[None]),
+        flops=2 * span * width * (columns - DI),
+        nbytes=4 * span * columns,
+        after=after,
+    )
+
+
+def plain_weight(left, right, first, tiles, total=None, after=()):
+    span, width = left.shape
+    columns = right.shape[1]
+    return pcall(
+        plain_weight_kernel,
+        (columns // 256,),
+        [full((span, width)), pl.BlockSpec((span, 256), lambda g: (0, g))]
+        + ([] if total is None else [pl.BlockSpec(memory_space=pltpu.HBM)]),
+        pl.BlockSpec((width, 256), lambda g: (0, first + g)),
+        shape_of((width, 256 * tiles)),
+        [],
+        (left, right) if total is None else (left, right, total),
+        flops=2 * span * width * columns,
+        nbytes=4 * width * columns,
+        after=after,
+        aliases={} if total is None else {2: 0},
     )
 
 
@@ -850,17 +1131,16 @@
     return aux, auxr
 
 
-def halving(count, rows):
-    def seq_masks(odd):
-        masks = [rows << bit for bit in range(count.bit_length() - 1)]
-        return masks[1::-1] + masks[2:] if odd else masks
-
-    return [1 << bit for bit in range(rows.bit_length() - 1)], seq_masks(False), seq_masks(True)
-
-
-def slab_order():
+def halving(count, rows, turned=False):
+    masks = [rows << bit for bit in range(count.bit_length() - 1)]
+    near, far = masks[:2], masks[2:]
+    pick = lambda pair: far + pair if turned else pair + far
+    return [1 << bit for bit in range(rows.bit_length() - 1)], pick(near), pick(near[::-1])
+
+
+def slab_order(turned=False):
     count, rows = lax.axis_size("seq"), lax.axis_size("rows")
-    row_masks, even, odd = halving(count, rows)
+    row_masks, even, odd = halving(count, rows, turned)
     stages = len(row_masks) + len(even)
     place = jnp.arange(count * rows, dtype=jnp.int32)
     bit = lambda stage: (place >> (stages - 1 - stage)) & 1
@@ -873,31 +1153,33 @@
     return slab
 
 
-def in_order(values, order):
-    width = values.shape[1]
+def in_order(values, order, after=()):
+    span, width = values.shape
     size = width // order.shape[0]
-    source = (order[:, None] * size + jnp.arange(size, dtype=jnp.int32)[None, :]).reshape(-1)
-    pick = (jnp.arange(width, dtype=jnp.int32)[:, None] == source[None, :]).astype(jnp.bfloat16)
-    return jnp.dot(values, pick, preferred_element_type=jnp.float32).astype(jnp.bfloat16)
-
-
-def in_order_rows(values, order):
-    width = values.shape[1]
-    size = width // order.shape[0]
-    source = (order[:, None] * size + jnp.arange(size, dtype=jnp.int32)[None, :]).reshape(-1)
-    pick = (source[:, None] == jnp.arange(width, dtype=jnp.int32)[None, :]).astype(jnp.bfloat16)
-    return jnp.einsum("ns,ts->nt", pick, values, preferred_element_type=jnp.float32).astype(jnp.bfloat16)
-
-
-def weight_sums(devices, left, right, after=()):
+    source = (order[:, None] * size + jnp.arange(size, dtype=jnp.int32)[None, :]).reshape(-1, 1)
+    return pcall(
+        sort_kernel,
+        (width // 256,),
+        [pl.BlockSpec((256, 1), lambda g: (g, 0)), full((span, width))],
+        pl.BlockSpec((256, span), lambda g: (g, 0)),
+        shape_of((width, span), jnp.bfloat16),
+        [],
+        (source, values),
+        flops=2 * span * width * width,
+        nbytes=4 * span * width,
+        after=after,
+    )
+
+
+def weight_sums(devices, left, right, first=0, tiles=None, after=()):
     width, span = left.shape
-    columns = right.shape[1]
+    columns = right.shape[1] if tiles is None else 256 * tiles
     slabs = width // 2 // SUM_ROWS
     out = pl.BlockSpec((slabs, SUM_ROWS, 256), lambda g: (g, 0, 0))
     return pcall(
         partial(weight_kernel, width // devices),
         (columns // 256,),
-        [full((width, span)), pl.BlockSpec((span, 256), lambda g: (0, g))],
+        [full((width, span)), pl.BlockSpec((span, 256), lambda g: (0, first + g))],
         [out, out],
         [shape_of((columns // 256 * slabs, SUM_ROWS, 256))] * 2,
         [],
@@ -910,17 +1192,19 @@
 
 def summed(parts, after=()):
     count, rows = lax.axis_size("seq"), lax.axis_size("rows")
-    row_masks, even, odd = halving(count, rows)
-    masks = [("rows", mask, mask) for mask in row_masks] + [("seq", one, two) for one, two in zip(even, odd)]
-    masks = [(axis, one // rows, two // rows) if axis == "seq" else (axis, one, two) for axis, one, two in masks]
+    orders = []
+    for turned in (False, True):
+        row_masks, even, odd = halving(count, rows, turned)
+        masks = [("rows", mask, mask) for mask in row_masks]
+        orders.append(masks + [("seq", one // rows, two // rows) for one, two in zip(even, odd)])
     counts = [send.shape[0] for send, _ in parts]
-    chunks, stages = sum(counts), len(masks)
+    chunks, stages = sum(counts), len(orders[0])
     last = SUM_ROWS >> (stages - 1)
     anywhere = pl.BlockSpec(memory_space=pltpu.HBM)
 
     def run(*refs):
         taken = 2 * len(parts)
-        sums_kernel(counts, masks, *refs[:taken], *refs[taken + len(after) :])
+        sums_kernel(counts, orders, *refs[:taken], *refs[taken + len(after) :])
 
     return pl.pallas_call(
         run,
@@ -935,48 +1219,14 @@
             pltpu.SemaphoreType.DMA((stages, chunks)),
         ],
         compiler_params=pltpu.CompilerParams(
-            vmem_limit_bytes=56 * 1024 * 1024, collective_id=0, has_side_effects=True
+            vmem_limit_bytes=VMEM_BYTES, collective_id=0, has_side_effects=True
         ),
         cost_estimate=pl.CostEstimate(flops=0, bytes_accessed=400 * 1024 * 1024, transcendentals=0),
     )(*[send for send, _ in parts], *[keep for _, keep in parts], *after)
 
 
-class Scatter:
-
-    def __init__(self, left, right):
-        half = left.shape[1] // 2
-        self.send = matmul_tn(left[:, half:], right)
-        self.keep = matmul_tn(left[:, :half], right)
-        count, rows = lax.axis_size("seq"), lax.axis_size("rows")
-        row_masks, even, odd = halving(count, rows)
-        self.devices = count * rows
-        self.stages = [(mask, mask) for mask in row_masks] + list(zip(even, odd))
-        self.share()
-
-    def share(self):
-        masks = self.stages.pop(0)
-        self.got = lax.ppermute(self.send, AXES, [(at, at ^ masks[at & 1]) for at in range(self.devices)])
-
-    def step(self):
-        if not self.stages:
-            if self.got is not None:
-                self.keep = self.keep + self.got
-            self.got = None
-            return (self.keep,)
-        half = self.keep.shape[0] // 2
-        self.send = self.keep[half:] + self.got[half:]
-        self.keep = self.keep[:half] + self.got[:half]
-        self.share()
-        return (self.send, self.keep)
-
-    def result(self):
-        while self.got is not None:
-            self.step()
-        return self.keep
-
-
-def steps(*scatters):
-    return sum((scatter.step() for scatter in scatters), ())
+def scattered(total):
+    return lax.psum_scatter(total, AXES, scatter_dimension=0, tiled=True)
 
 
 def matmul(a, b):
@@ -989,18 +1239,6 @@
 
 def matmul_nt(a, b):
     return jnp.einsum("tn,mn->tm", a, b, preferred_element_type=jnp.float32)
-
-
-def normalise(values, gain):
-    scale = lax.rsqrt(jnp.mean(values * values, -1, keepdims=True) + EPS)
-    return (values * scale * gain).astype(jnp.bfloat16)
-
-
-def normalise_back(values, gain, grad):
-    scale = lax.rsqrt(jnp.mean(values * values, -1, keepdims=True) + EPS)
-    gain_grad = jnp.sum(grad * values * scale, 0)
-    pulled = grad * gain
-    return scale * pulled - values * (scale**3 * jnp.mean(pulled * values, -1, keepdims=True)), gain_grad
 
 
 def padded(rows, width):
@@ -1026,97 +1264,113 @@
     peers = lax.axis_size("seq")
     aux, auxr = token_marks(lengths[0], span)
     order = slab_order()
+    in_weight = jnp.swapaxes(in_weight, 1, 2)
     hidden = inputs[0]
     saved = []
     for depth in range(LAYERS):
         conv = jnp.concatenate([conv_weight[depth].T, conv_bias[depth][None], jnp.zeros((3, CHANNELS), jnp.float32)])
+        conv = jnp.pad(conv, ((0, 0), (0, DI + TILE - CHANNELS)))
         hp = padded([dt_bias[depth], -jnp.exp(log_decay[depth])], 128)
         ch = padded([jnp.repeat(skip[depth], HEAD_DIM), gate_gain[depth]], DI)
-        gate_weight = in_weight[depth][:, :DI]
-        mixed_weight = in_weight[depth][:, DI : DI + CHANNELS]
-        rate_weight = jnp.pad(in_weight[depth][:, DI + CHANNELS :], ((0, 0), (0, 128 - HEADS)))
         before = shifted(hidden[span - HALO :], 1)
-        normed = normalise(hidden, norm_gain[depth])
-        normed_ext = jnp.concatenate([normalise(before, norm_gain[depth]), normed])
-        mixed_ext = matmul(normed_ext, mixed_weight)
-        rate = matmul(normed, rate_weight)
-        gate = matmul(normed, gate_weight)
-        values, bc, col, cumr, made, kx, pay = make_states(peers, mixed_ext, rate, aux, conv, hp)
+        normed, mixed_ext = project(depth, hidden, before, norm_gain[depth], in_weight)
+        values, bc, col, cumr, made, kx, pay, slope, slope_bc = make_states(peers, mixed_ext, aux, conv, hp)
         received = exchange(pay)
+        gate = project_gate(depth, normed, in_weight)
+        keeps = received[:, -8:]
+        waits = (gate,)
+        if depth:
+            ready = [in_order(values, by, after=(pay,)) for values, by in sorting]
+            waits += tuple(ready)
+        scanned = scan_states(received, keeps, False, after=waits)
+        state_in = exchange(scanned).reshape(DI // 128, STATE, 128)
         yi = inner(bc, values, col, cumr, aux, auxr)
-        keeps = received[:, -8:]
-        state_in = exchange(scan_states(received, keeps, False)).reshape(DI // 128, STATE, 128)
         y, out_low = finish(yi, values, gate, bc, col, state_in, made, kx, ch)
         saved.append(
-            (hidden, normed, mixed_ext, rate, gate, values, bc, col, cumr, made, kx, keeps, state_in, y, out_low, yi)
-            + (conv, hp, ch, gate_weight, mixed_weight, rate_weight)
+            (hidden, normed, mixed_ext, gate, values, bc, col, cumr, made, kx, keeps, state_in, y, out_low, yi)
+            + (slope, slope_bc, conv, hp, ch)
         )
+        sorting = [(out_low, order), (normed, order), (normed, slab_order(True))]
         hidden = hidden + matmul(out_low, out_weight[depth])
     gradient = cotangent[0]
+    grad_low = gradient.astype(jnp.bfloat16)
     devices = lax.axis_size(AXES)
     collected = [None] * LAYERS
-    big_out = [None] * LAYERS
-    big_in = [None] * LAYERS
-    early, late = (), ()
     for depth in reversed(range(LAYERS)):
-        entry, normed, mixed_ext, rate, gate, values, bc, col, cumr, made, kx, keeps, state_in, y, out_low, yi = saved[depth][:16]
-        conv, hp, ch, gate_weight, mixed_weight, rate_weight = saved[depth][16:]
-        normed_sorted = in_order(normed, order) if depth else in_order_rows(normed, order)
-        out_sorted = in_order(out_low, order) if depth else in_order_rows(out_low, order)
-        grad_low = gradient.astype(jnp.bfloat16)
+        entry, normed, mixed_ext, gate, values, bc, col, cumr, made, kx, keeps, state_in, y, out_low, yi = saved[depth][:15]
+        slope, slope_bc, conv, hp, ch = saved[depth][15:]
         dno = matmul_nt(grad_low, out_weight[depth])
-        waits = steps(*late)
-        dy, dgate, gate_sums, d1, pay = gate_back(peers, dno, y, gate, values, bc, col, kx, ch, after=waits)
+        dy, dgate, gate_sums, d1, pay = gate_back(peers, dno, y, gate, values, bc, col, kx, ch)
         received = exchange(pay)
         if depth:
-            early_now = Scatter(out_sorted, grad_low), Scatter(normed_sorted, dgate)
-            waits = sum(((part.send, part.keep) for part in early_now), ())
+            out_sorted = in_order(out_low, order, after=(pay,))
+            high_chunks = weight_sums(devices, out_sorted, grad_low)
+            waits = high_chunks[:1]
         else:
-            out_chunks = weight_sums(devices, out_sorted, grad_low)
+            out_sorted, normed_sorted, turned_sorted = ready
+            out_chunks = weight_sums(devices, out_sorted, grad_low, after=(pay,))
             gate_chunks = weight_sums(devices, normed_sorted, dgate, after=out_chunks[:1])
-            waits = (gate_chunks[0],) + steps(*early)
+            waits = (gate_chunks[0],)
         scanned = scan_states(received, keeps, True, after=waits)
         dso = exchange(scanned).reshape(DI // 128, STATE, 128)
-        if depth:
-            early = early_now
-        waits = steps(*early) if depth else steps(*late)
-        xi, dbc = inner_back(bc, values, dy, col, cumr, aux, auxr, after=waits)
-        waits = () if depth else steps(*early, *late)
+        tiles = (DI + DI + TILE) // 256
+        in_total = plain_weight(normed, dgate, 0, tiles, after=(scanned,)) if depth else None
+        xi, dbc = inner_back(bc, values, dy, col, cumr, aux, auxr, after=(in_total,) if depth else ())
+        base, ds, dc, dmap = states_pre(xi, values, dy, yi, bc, col, state_in, made, kx, dbc, ch)
         dconv, dconv_bc, drate, head_rows = states_back(
-            xi, values, dy, yi, mixed_ext, bc, col, dso, state_in, made, d1, kx, dbc, aux, conv, ch, hp, rate,
-            after=waits,
+            base, values, slope, slope_bc, bc, col, dso, state_in, made, d1, kx, ds, dc, dmap, hp, mixed_ext
         )
         following = shifted(jnp.concatenate([dconv[:HALO], dconv_bc[:HALO]], 1), -1)
-        waits = steps(*early) if depth else steps(*late)
-        dmixed, conv_sums = conv_back(dconv, dconv_bc, drate, following, mixed_ext, aux, conv, after=waits)
+        part = project_back_gate(depth, dgate, in_weight, after=(head_rows,))
+        dmixed, conv_sums = conv_back(dconv, dconv_bc, drate, following, mixed_ext, aux, conv, after=(part,))
         if depth:
-            late = (Scatter(normed_sorted, dmixed),)
+            in_total = plain_weight(normed, dmixed, DI // 256, tiles, in_total)
+            high_in = scattered(in_total)
+            waits = (in_total,)
         else:
-            rest_chunks = weight_sums(devices, normed_sorted, dmixed)
-        grad_normed = matmul_nt(dgate, gate_weight) + matmul_nt(
-            dmixed[:, : CHANNELS + HEADS], in_weight[depth][:, DI:]
+            others = [high_chunks, out_chunks, gate_chunks]
+            count = sum(part[0].shape[0] for part in others) + dmixed.shape[1] // 256
+            turned_tiles = pl.cdiv(count, EVERY)
+            waits = ()
+        gradient, grad_low, gain_sums = project_back(
+            depth, part, dmixed, in_weight, entry, gradient, norm_gain[depth], after=waits
         )
-        grad_hidden, gain_grad = normalise_back(entry, norm_gain[depth], grad_normed)
-        gradient = gradient + grad_hidden
+        if depth == 0:
+            turned_chunks = weight_sums(devices, turned_sorted, dmixed, 0, turned_tiles, after=(gain_sums,))
+            rest_tiles = dmixed.shape[1] // 256 - turned_tiles
+            rest_chunks = weight_sums(
+                devices, normed_sorted, dmixed, turned_tiles, rest_tiles, after=turned_chunks[:1]
+            )
+        gain_grad = jnp.sum(gain_sums, 0)
         collected[depth] = (
             gain_grad,
-            conv_sums[:KW].T,
-            conv_sums[KW],
+            conv_sums[:KW, :CHANNELS].T,
+            conv_sums[KW, :CHANNELS],
             gate_sums[0],
             head_rows[1, :HEADS],
             head_rows[0, :HEADS],
             jnp.sum(gate_sums[1].reshape(HEADS, HEAD_DIM), 1),
         )
-        if depth:
-            trio = early + late
-    big_out[1] = trio[0].result()
-    big_in[1] = jnp.concatenate([trio[1].result(), trio[2].result()[:, : CHANNELS + HEADS]], 1)
-    total = summed([out_chunks, gate_chunks, rest_chunks], after=(gradient, big_out[1], big_in[1]))
-    wide = lambda part: jnp.moveaxis(part, 0, 1).reshape(part.shape[1], -1)
-    n_out, n_gate = out_chunks[0].shape[0], gate_chunks[0].shape[0]
+    total = summed([turned_chunks, high_chunks, out_chunks, gate_chunks, rest_chunks], after=(gradient,))
+    places = list(range(total.shape[0]))
+    between = [place for place in places if place % EVERY]
+    n_out = out_chunks[0].shape[0]
+    n_gate = 2 * n_out + gate_chunks[0].shape[0]
     slabs = n_out * 256 // out_weight.shape[2]
-    big_out[0] = jnp.concatenate([wide(total[part:n_out:slabs]) for part in range(slabs)], 0)
-    big_in[0] = wide(total[n_out:])[:, : DI + CHANNELS + HEADS]
+    columns = between[2 * n_out : n_gate] + places[::EVERY] + between[n_gate:]
+    columns = columns[: pl.cdiv(in_weight.shape[1], 256)]
+    outs = [[between[first + part : first + n_out : slabs] for part in range(slabs)] for first in (n_out, 0)]
+    shapes = [(LAYERS, slabs * total.shape[1], out_weight.shape[2]), (LAYERS, high_in.shape[0], in_weight.shape[1])]
+    all_out, all_in = pcall(
+        partial(assemble_kernel, outs, columns),
+        (1,),
+        [full(total.shape), full(high_in.shape)],
+        [full(shape) for shape in shapes],
+        [shape_of(shape) for shape in shapes],
+        [],
+        (total, high_in),
+        nbytes=4 * 1024 * 1024,
+    )
     shares = [part.reshape(devices, -1) for sums in collected for part in sums[:4]]
     heads = jnp.concatenate([part for sums in collected for part in sums[4:]])
     table = jnp.concatenate(shares + [jnp.broadcast_to(heads, (devices,) + heads.shape)], 1)
@@ -1130,7 +1384,6 @@
         shape_of(table.shape[1:]),
         [],
         (table,),
-        after=(total,),
     ).reshape(-1)
     small = []
     at = 0
@@ -1151,14 +1404,14 @@
         hidden[None],
         gradient[None],
         norm_gain_grad,
-        jnp.stack(big_in),
+        all_in,
         conv_w_grad,
         conv_b_grad,
         decay_grad,
         bias_grad,
         skip_grad,
         gain_grad,
-        jnp.stack(big_out),
+        all_out,
     )
 
 

time: 755 us -> 735 us (0.974)
  Pallas kernels: 310 us -> 485 us
  matrix products: 113 us -> 26.1 us
  other arithmetic: 60.6 us -> 11.8 us
  blocking collectives: 33.2 us -> 0 us
  local copies, waits for them, and re-layouts: 59.5 us -> 38.1 us
  waiting for transfers between devices: 72.9 us -> 56.4 us
  between operations: 2.67 us -> 15 us
    pallas_call x22 -> x41, Pallas kernels: 179 us -> 333 us  [pcall(): pl.pallas_call(run, grid=grid, in_specs=list(in_specs) + [pl.BlockSpec(me...]
    add x16 -> x0, other arithmetic: 44.9 us -> none  [the longest x10 34.4 us: step(): self.keep = self.keep[:half] + self.got[:half]]
    dot_general x10 -> x0, matrix products: 38 us -> none  [the longest x6 22.6 us: matmul_tn(): return jnp.einsum('tn,tm->nm', a, b, preferred_element_type=jnp.float32)]
    all_to_all x1 -> x0, blocking collectives: 33.2 us -> none  [exchange(): return lax.all_to_all(parts, 'seq', split_axis=0, concat_axis=0, tiled=True)]
    ppermute x15 -> x0, waiting for transfers between devices: 31.5 us -> none  [share(): lax.ppermute(self.send, AXES, [(at, at ^ masks[at & 1]) for at in range(s...]
    dot_general x8 -> x2, matrix products: 40.2 us -> 12.3 us  [matmul(): return jnp.dot(a, b, preferred_element_type=jnp.float32)]
    ppermute x15 -> x0, starting transfers between devices: 27.4 us -> none  [share(): lax.ppermute(self.send, AXES, [(at, at ^ masks[at & 1]) for at in range(s...]
    pallas_call x1, Pallas kernels: 130 us -> 152 us  [summed(): pl.pallas_call(run, in_specs=[anywhere] * (2 * len(parts) + len(after)),...]
  transfers between devices with their start and end apart: 27 -> 14, of which waited for: 6 -> 6; matrix products, arithmetic and copies ran while one was open for 22% -> 8% of each run, Pallas kernels for 16% -> 51%
where the time goes in v6:
time: 735 us; the launch traced here: 723 us
  Pallas kernels  485 us (66%)
  starting transfers between devices  90.3 us (12%)
  waiting for transfers between devices  56.4 us (8%)
  local copies, waits for them, and re-layouts  38.1 us (5%)
  matrix products  26.1 us (4%)
  between operations  15 us (2%)
  other arithmetic  11.8 us (2%)
    pallas_call x41, Pallas kernels, pcall(): pl.pallas_call(run, grid=grid, in_specs=list(in_specs) + [pl.BlockSpec(me...  333 us
    pallas_call x1, Pallas kernels, summed(): pl.pallas_call(run, in_specs=[anywhere] * (2 * len(parts) + len(after)),...  152 us
    all_to_all x8, starting transfers between devices, exchange(): return lax.all_to_all(parts, 'seq', split_axis=0, concat_axis=0, tiled=True)  60.3 us
    all_to_all x8, waiting for transfers between devices, exchange(): return lax.all_to_all(parts, 'seq', split_axis=0, concat_axis=0, tiled=True)  56.3 us
    all_to_all x1, starting transfers between devices, local(): lax.all_to_all(table, AXES, split_axis=0, concat_axis=0, tiled=True)  20.5 us
  transfers between devices with their start and end apart: 14, of which 6 were waited for; matrix products, arithmetic and copies ran while one was open for 8% of the time, Pallas kernels for 51%

profile of v6, /device:TPU:1, one launch (start us, length us, event | category | flops | bytes accessed | tf_op | source)
XLA Modules:
  0.0 723.0 jit_solution(17581361704013032150)
XLA Ops:
  7.9 3.9 collective-permute-start
  21.3 9.1 %shard_map.203 = (bf16[512,1024]{1,0:T(8,128)(2,1)}, f32[520,2560]{1,0:T(8,128)}) custom-call(f32[512,1024]{1,0:T(8,128)} %bitcast.122, f32[8,1024]{1,0:T(8,128)} %copy-done.13, f32[1,1024]{1,0:T(1,128)} %get-tuple-element.201.refs_2_.refs_5_, bf16[2,4384,1024]{2,1,0:T(8,128)(2,1)} %bitcast.114), custom_call_target="tpu_custom_call" | custom-call | flops 2684354560 | bytes 5242880 | tf_op jit(solution)/shard_map/pallas_call | solution.py:44
  30.4 11.5 %shard_map.204 = (f32[512,2048]{1,0:T(8,128)}, f32[512,256]{1,0:T(8,128)}, f32[4,512,128]{2,1,0:T(8,128)}, f32[128,512]{1,0:T(8,128)}, f32[128,2048]{1,0:T(8,128...) custom-call(f32[520,2560]{1,0:T(8,128)} %get-tuple-element.88.refs_0_.refs_1_.refs_2_, ...), custom_call_target="tpu_custom_call" | custom-call | flops 268435456 | bytes 12582912 | tf_op jit(solution)/shard_map/pallas_call | solution.py:44
  41.8 5.7 all-to-all-start
  47.5 6.6 shard_map.206.refs_2_
  54.1 16.8 %all-to-all-done.refs_0_ = f32[16,136,128]{2,1,0:T(8,128)S(1)} async-done(((f32[16,136,128]{2,1,0:T(8,128)}), f32[16,136,128]{2,1,0:T(8,128)S(1)}, u32[]{:S(2)}, u32[]{:S(2)}) %all-to-all-start) | async-done | bytes 1114144 | tf_op jit(solution)/shard_map/all_to_all | solution.py:1106
  71.9 2.3 shard_map.207
  74.2 6.7 all-to-all-start.1
  82.4 6.9 shard_map.205.refs_0_.refs_3_
  89.4 13.8 %all-to-all-done.1.refs_5_.refs_6_.refs_7_ = f32[16,128,128]{2,1,0:T(8,128)S(1)} async-done(((f32[16,128,128]{2,1,0:T(8,128)}), f32[16,128,128]{2,1,0:T(8,128)S(1)}, u32[]{:S(2)}, u32[]{:S(2)}) %all-to-all-start.1) | async-done | bytes 1048608 | tf_op jit(solution)/shard_map/all_to_all | solution.py:1106
  104.1 8.9 %shard_map.208 = (f32[512,2048]{1,0:T(8,128)}, bf16[512,2048]{1,0:T(8,128)(2,1)}) custom-call(f32[512,2048]{1,0:T(8,128)} %shard_map.205.refs_0_.refs_3_, f32[512,2048]{1,0:T(8,128)} %get-tuple-element.90.refs_1_.refs_3_, f32[512,2048]{1,0:T(8,128)} %shard_map.206.refs_2_, f32[512,256]{1,0:T(8,128)} %get-tuple-element.89.refs_0_.refs_3_.refs_4_, ...), custom_call_target="tpu_custom_call" | custom-call | flops 268435456 | bytes 18874368 | tf_op jit(solution)/shard_map/pallas_call | solution.py:44
  113.0 5.8 fusion.12.refs_0_.refs_3_
  118.8 2.1 collective-permute-start.1
  122.7 9.2 %shard_map.209 = (bf16[512,1024]{1,0:T(8,128)(2,1)}, f32[520,2560]{1,0:T(8,128)}) custom-call(f32[512,1024]{1,0:T(8,128)} %copy-done.2, f32[8,1024]{1,0:T(8,128)} %copy-done.14, f32[1,1024]{1,0:T(1,128)} %get-tuple-element.200.refs_2_.refs_5_, bf16[2,4384,1024]{2,1,0:T(8,128)(2,1)} %bitcast.116), custom_call_target="tpu_custom_call" | custom-call | flops 2684354560 | bytes 5242880 | tf_op jit(solution)/shard_map/pallas_call | solution.py:44
  131.9 11.4 %shard_map.210 = (f32[512,2048]{1,0:T(8,128)}, f32[512,256]{1,0:T(8,128)}, f32[4,512,128]{2,1,0:T(8,128)}, f32[128,512]{1,0:T(8,128)}, f32[128,2048]{1,0:T(8,128...) custom-call(f32[520,2560]{1,0:T(8,128)} %get-tuple-element.98.refs_0_.refs_1_.refs_2_, ...), custom_call_target="tpu_custom_call" | custom-call | flops 268435456 | bytes 12582912 | tf_op jit(solution)/shard_map/pallas_call | solution.py:44
  143.3 9.0 %all-to-all-start.2 = ((f32[16,136,128]{2,1,0:T(8,128)}), f32[16,136,128]{2,1,0:T(8,128)S(1)}, u32[]{:S(2)}, u32[]{:S(2)}) async-start(f32[16,136,128]{2,1,0:T(8,128)} %get-tuple-element.104.refs_2_), calls=%async_computation.2 | async-start | bytes 2228224 | tf_op jit(solution)/shard_map/all_to_all | solution.py:1106
  155.2 2.0 add.148.refs_0_
  157.2 4.7 shard_map.214.refs_4_.refs_0_
  161.9 4.7 shard_map.215.refs_5_.refs_0_
  166.6 6.5 shard_map.212.refs_2_
  173.1 9.2 %shard_map.213.refs_3_.refs_0_ = bf16[2048,512]{1,0:T(8,128)(2,1)} custom-call(s32[2048,1]{1,0:T(8,128)} %add.148.refs_0_, bf16[512,2048]{1,0:T(8,128)(2,1)} %get-tuple-element.97.refs_1_, f32[16,136,128]{2,1,0:T(8,128)} %get-tuple-element.104.refs_2_), custom_call_target="tpu_custom_call" | custom-call | flops 4294967296 | bytes 4194304 | tf_op jit(solution)/shard_map/pallas_call | solution.py:44
  183.9 2.4 shard_map.216
  186.4 6.6 all-to-all-start.3
  193.8 6.6 fusion.refs_0_
  200.3 7.0 shard_map.211.refs_0_.refs_3_
  207.3 3.5 all-to-all-done.3.refs_5_.refs_6_.refs_7_
  211.8 8.9 %shard_map.217 = (f32[512,2048]{1,0:T(8,128)}, bf16[512,2048]{1,0:T(8,128)(2,1)}) custom-call(f32[512,2048]{1,0:T(8,128)} %shard_map.211.refs_0_.refs_3_, f32[512,2048]{1,0:T(8,128)} %get-tuple-element.100.refs_1_.refs_3_, f32[512,2048]{1,0:T(8,128)} %shard_map.212.refs_2_, f32[512,256]{1,0:T(8,128)} %get-tuple-element.99.refs_0_.refs_3_.refs_4_, ...), custom_call_target="tpu_custom_call" | custom-call | flops 268435456 | bytes 18874368 | tf_op jit(solution)/shard_map/pallas_call | solution.py:44
  220.7 12.3 %shard_map.218 = (f32[512,2048]{1,0:T(8,128)}, bf16[512,2048]{1,0:T(8,128)(2,1)}, f32[8,2048]{1,0:T(8,128)}, f32[128,2048]{1,0:T(8,128)}, f32[16,128,128]{2,1,0:T(8,128)}) custom-call(f32[512,2048]{1,0:T(8,128)} %fusion.refs_0_, f32[512,2048]{1,0:T(8,128)} %get-tuple-element.108.refs_1_, f32[512,2048]{1,0:T(8,128)} %shard_map.212.refs_2_, ...), custom_call_target="tpu_custom_call" | custom-call | flops 268435456 | bytes 23068672 | tf_op jit(solution)/shard_map/pallas_call | solution.py:44
  233.0 10.4 %all-to-all-start.4 = ((f32[16,128,128]{2,1,0:T(8,128)}), f32[16,128,128]{2,1,0:T(8,128)S(1)}, u32[]{:S(2)}, u32[]{:S(2)}) async-start(f32[16,128,128]{2,1,0:T(8,128)} %get-tuple-element.111.refs_2_), calls=%async_computation.4 | async-start | bytes 2097152 | tf_op jit(solution)/shard_map/all_to_all | solution.py:1106
  244.5 9.2 %shard_map.219.refs_0_ = bf16[2048,512]{1,0:T(8,128)(2,1)} custom-call(s32[2048,1]{1,0:T(8,128)} %add.148.refs_0_, bf16[512,2048]{1,0:T(8,128)(2,1)} %get-tuple-element.107.refs_1_, f32[16,128,128]{2,1,0:T(8,128)} %get-tuple-element.111.refs_2_), custom_call_target="tpu_custom_call" | custom-call | flops 4294967296 | bytes 4194304 | tf_op jit(solution)/shard_map/pallas_call | solution.py:44
  253.7 6.4 shard_map.220
  260.1 5.3 all-to-all-done.4.refs_0_
  266.4 2.3 shard_map.221.refs_2_
  268.6 6.9 all-to-all-start.5
  276.0 9.0 %shard_map.222.refs_7_.refs_2_ = f32[1024,4608]{1,0:T(8,128)} custom-call(bf16[512,1024]{1,0:T(8,128)(2,1)} %get-tuple-element.103.refs_0_, bf16[512,2048]{1,0:T(8,128)(2,1)} %get-tuple-element.109.refs_1_.refs_0_, f32[16,128,128]{2,1,0:T(8,128)} %shard_map.221.refs_2_), custom_call_target="tpu_custom_call" | custom-call | flops 2147483648 | bytes 8388608 | tf_op jit(solution)/shard_map/pallas_call | solution.py:44
  285.0 10.0 %shard_map.223 = (f32[512,2048]{1,0:T(8,128)}, f32[512,256]{1,0:T(8,128)}) custom-call(f32[512,256]{1,0:T(8,128)} %get-tuple-element.99.refs_0_.refs_3_.refs_4_, f32[512,2048]{1,0:T(8,128)} %get-tuple-element.100.refs_1_.refs_3_, f32[512,2048]{1,0:T(8,128)} %get-tuple-element.110.refs_2_, f32[4,512,128]{2,1,0:T(8,128)} %get-tuple-element.101.refs_2_.refs_4_.refs_5_.refs_3_, ...), custom_call_target="tpu_custom_call" | custom-call | flops 4294967296 | bytes 12582912 | tf_op jit(solution)/shard_map/pallas_call | solution.py:44
  295.0 12.9 %shard_map.224 = (f32[512,2048]{1,0:T(8,128)}, f32[512,128]{1,0:T(8,128)}, f32[512,128]{1,0:T(8,128)}, f32[512,256]{1,0:T(8,128)}) custom-call(f32[512,2048]{1,0:T(8,128)} %get-tuple-element.113.refs_0_, f32[512,2048]{1,0:T(8,128)} %get-tuple-element.100.refs_1_.refs_3_, f32[512,2048]{1,0:T(8,128)} %get-tuple-element.110.refs_2_, ...), custom_call_target="tpu_custom_call" | custom-call | flops 536870912 | bytes 20971520 | tf_op jit(solution)/shard_map/pallas_call | solution.py:44
  308.9 14.2 %shard_map.225 = (f32[512,2048]{1,0:T(8,128)}, f32[512,256]{1,0:T(8,128)}, bf16[512,128]{1,0:T(8,128)(2,1)}, f32[8,128]{1,0:T(8,128)}) custom-call(f32[512,2048]{1,0:T(8,128)} %get-tuple-element.115.refs_0_, f32[512,2048]{1,0:T(8,128)} %get-tuple-element.100.refs_1_.refs_3_, f32[512,2048]{1,0:T(8,128)} %get-tuple-element.116.refs_2_, ...), custom_call_target="tpu_custom_call" | custom-call | flops 536870912 | bytes 16777216 | tf_op jit(solution)/shard_map/pallas_call | solution.py:44
  326.2 6.4 shard_map.226.refs_7_.refs_0_
  333.3 9.1 %shard_map.227 = (bf16[512,2560]{1,0:T(8,128)(2,1)}, f32[8,2560]{1,0:T(8,128)}) custom-call(f32[512,2048]{1,0:T(8,128)} %get-tuple-element.123.refs_0_, f32[512,256]{1,0:T(8,128)} %get-tuple-element.124.refs_1_, bf16[512,128]{1,0:T(8,128)(2,1)} %get-tuple-element.125.refs_2_, f32[8,2304]{1,0:T(8,128)} %copy-done.12, ...), custom_call_target="tpu_custom_call" | custom-call | flops 8388608 | bytes 10485760 | tf_op jit(solution)/shard_map/pallas_call | solution.py:44
  342.4 10.8 %shard_map.228.refs_6_ = f32[1024,4608]{1,0:T(8,128)} custom-call(bf16[512,1024]{1,0:T(8,128)(2,1)} %get-tuple-element.103.refs_0_, bf16[512,2560]{1,0:T(8,128)(2,1)} %get-tuple-element.126.refs_1_, f32[1024,4608]{1,0:T(8,128)} %shard_map.222.refs_7_.refs_2_), custom_call_target="tpu_custom_call", output_to_operand_aliasing={{}: (2, {})} | custom-call | flops 2684354560 | bytes 10485760 | tf_op jit(solution)/shard_map/pallas_call | solution.py:44
  353.2 10.5 %shard_map.229 = (f32[512,1024]{1,0:T(8,128)}, bf16[512,1024]{1,0:T(8,128)(2,1)}, f32[8,1024]{1,0:T(8,128)}) custom-call(f32[512,1024]{1,0:T(8,128)} %shard_map.226.refs_7_.refs_0_, bf16[512,2560]{1,0:T(8,128)(2,1)} %get-tuple-element.126.refs_1_, bf16[2,4384,1024]{2,1,0:T(8,128)(2,1)} %bitcast.119, f32[512,1024]{1,0:T(8,128)} %copy-done.2, ...), custom_call_target="tpu_custom_call" | custom-call | flops 2449473536 | bytes 8978432 | tf_op jit(solution)/shard_map/pallas_call | solution.py:44
  363.7 7.2 %fusion.4.refs_0_ = f32[512,2048]{1,0:T(8,128)} fusion(bf16[512,1024]{1,0:T(8,128)(2,1)} %get-tuple-element.127.refs_1_, bf16[2,2048,1024]{2,1,0:T(8,128)(2,1)} %param.22), kind=kOutput, calls=%fused_computation.4 | convolution fusion | flops 2147483648 | bytes 9437184 | tf_op jit(solution)/shard_map/tn,mn->tm/dot_general | solution.py:1241
  370.9 13.0 %shard_map.230 = (f32[512,2048]{1,0:T(8,128)}, bf16[512,2048]{1,0:T(8,128)(2,1)}, f32[8,2048]{1,0:T(8,128)}, f32[128,2048]{1,0:T(8,128)}, f32[16,128,128]{2,1,0:T(8,128)}) custom-call(f32[512,2048]{1,0:T(8,128)} %fusion.4.refs_0_, f32[512,2048]{1,0:T(8,128)} %get-tuple-element.128.refs_1_, f32[512,2048]{1,0:T(8,128)} %shard_map.206.refs_2_, ...), custom_call_target="tpu_custom_call" | custom-call | flops 268435456 | bytes 23068672 | tf_op jit(solution)/shard_map/pallas_call | solution.py:44
  383.9 7.7 %all-to-all-start.6 = ((f32[16,128,128]{2,1,0:T(8,128)}), f32[16,128,128]{2,1,0:T(8,128)S(1)}, u32[]{:S(2)}, u32[]{:S(2)}) async-start(f32[16,128,128]{2,1,0:T(8,128)} %get-tuple-element.136.refs_2_), calls=%async_computation.6 | async-start | bytes 2097152 | tf_op jit(solution)/shard_map/all_to_all | solution.py:1106
  391.7 6.7 shard_map.233
  398.3 8.4 %shard_map.234 = (f32[8,512,256]{2,1,0:T(8,128)}, f32[8,512,256]{2,1,0:T(8,128)}) custom-call(bf16[1024,512]{1,0:T(8,128)(2,1)} %shard_map.214.refs_4_.refs_0_, bf16[512,2048]{1,0:T(8,128)(2,1)} %get-tuple-element.129.refs_1_.refs_0_, f32[8,512,256]{2,1,0:T(8,128)} %get-tuple-element.137.refs_2_), custom_call_target="tpu_custom_call" | custom-call | flops 2147483648 | bytes 8388608 | tf_op jit(solution)/shard_map/pallas_call | solution.py:44
  406.8 6.3 all-to-all-done.6.refs_0_
  414.0 2.3 shard_map.235
  416.3 7.4 %all-to-all-start.7 = ((f32[16,128,128]{2,1,0:T(8,128)}), f32[16,128,128]{2,1,0:T(8,128)S(1)}, u32[]{:S(2)}, u32[]{:S(2)}) async-start(f32[16,128,128]{2,1,0:T(8,128)} %shard_map.235), calls=%async_computation.7 | async-start | bytes 2097152 | tf_op jit(solution)/shard_map/all_to_all | solution.py:1106
  427.9 10.0 %shard_map.231 = (f32[512,2048]{1,0:T(8,128)}, f32[512,256]{1,0:T(8,128)}) custom-call(f32[512,256]{1,0:T(8,128)} %get-tuple-element.89.refs_0_.refs_3_.refs_4_, f32[512,2048]{1,0:T(8,128)} %get-tuple-element.90.refs_1_.refs_3_, f32[512,2048]{1,0:T(8,128)} %get-tuple-element.130.refs_2_, f32[4,512,128]{2,1,0:T(8,128)} %get-tuple-element.91.refs_2_.refs_4_.refs_5_.refs_3_, ...), custom_call_target="tpu_custom_call" | custom-call | flops 4294967296 | bytes 12582912 | tf_op jit(solution)/shard_map/pallas_call | solution.py:44
  437.9 13.2 %shard_map.232 = (f32[512,2048]{1,0:T(8,128)}, f32[512,128]{1,0:T(8,128)}, f32[512,128]{1,0:T(8,128)}, f32[512,256]{1,0:T(8,128)}) custom-call(f32[512,2048]{1,0:T(8,128)} %get-tuple-element.131.refs_0_, f32[512,2048]{1,0:T(8,128)} %get-tuple-element.90.refs_1_.refs_3_, f32[512,2048]{1,0:T(8,128)} %get-tuple-element.130.refs_2_, ...), custom_call_target="tpu_custom_call" | custom-call | flops 536870912 | bytes 20971520 | tf_op jit(solution)/shard_map/pallas_call | solution.py:44
  451.2 10.7 %all-to-all-done.7.refs_6_ = f32[16,128,128]{2,1,0:T(8,128)S(1)} async-done(((f32[16,128,128]{2,1,0:T(8,128)}), f32[16,128,128]{2,1,0:T(8,128)S(1)}, u32[]{:S(2)}, u32[]{:S(2)}) %all-to-all-start.7) | async-done | bytes 1048608 | tf_op jit(solution)/shard_map/all_to_all | solution.py:1106
  462.8 14.7 %shard_map.236 = (f32[512,2048]{1,0:T(8,128)}, f32[512,256]{1,0:T(8,128)}, bf16[512,128]{1,0:T(8,128)(2,1)}, f32[8,128]{1,0:T(8,128)}) custom-call(f32[512,2048]{1,0:T(8,128)} %get-tuple-element.133.refs_0_, f32[512,2048]{1,0:T(8,128)} %get-tuple-element.90.refs_1_.refs_3_, f32[512,2048]{1,0:T(8,128)} %get-tuple-element.134.refs_2_, ...), custom_call_target="tpu_custom_call" | custom-call | flops 536870912 | bytes 16777216 | tf_op jit(solution)/shard_map/pallas_call | solution.py:44
  481.4 6.6 shard_map.237.refs_7_.refs_0_
  488.7 9.4 %shard_map.238 = (bf16[512,2560]{1,0:T(8,128)(2,1)}, f32[8,2560]{1,0:T(8,128)}) custom-call(f32[512,2048]{1,0:T(8,128)} %get-tuple-element.144.refs_0_, f32[512,256]{1,0:T(8,128)} %get-tuple-element.145.refs_1_, bf16[512,128]{1,0:T(8,128)(2,1)} %get-tuple-element.146.refs_2_, f32[8,2304]{1,0:T(8,128)} %copy-done.11, ...), custom_call_target="tpu_custom_call" | custom-call | flops 8388608 | bytes 10485760 | tf_op jit(solution)/shard_map/pallas_call | solution.py:44
  498.1 10.7 %shard_map.239 = (f32[512,1024]{1,0:T(8,128)}, bf16[512,1024]{1,0:T(8,128)(2,1)}, f32[8,1024]{1,0:T(8,128)}) custom-call(f32[512,1024]{1,0:T(8,128)} %shard_map.237.refs_7_.refs_0_, bf16[512,2560]{1,0:T(8,128)(2,1)} %get-tuple-element.147.refs_1_, bf16[2,4384,1024]{2,1,0:T(8,128)(2,1)} %bitcast.121, f32[512,1024]{1,0:T(8,128)} %bitcast.123, ...), custom_call_target="tpu_custom_call" | custom-call | flops 2449473536 | bytes 8978432 | tf_op jit(solution)/shard_map/pallas_call | solution.py:44
  511.5 20.5 %all-to-all-start.8 = ((f32[32,1,1152]{2,1,0:T(1,128)}), f32[32,1,1152]{2,1,0:T(1,128)S(1)}, u32[]{:S(2)}, u32[]{:S(2)}) async-start(f32[32,1,1152]{2,1,0:T(1,128)} %copy.57), calls=%async_computation.8 | async-start | bytes 294912 | tf_op jit(solution)/shard_map/all_to_all | solution.py:1378
  532.1 6.5 add_bitcast_fusion
  538.6 7.5 %shard_map.241 = (f32[7,512,256]{2,1,0:T(8,128)}, f32[7,512,256]{2,1,0:T(8,128)}) custom-call(bf16[1024,512]{1,0:T(8,128)(2,1)} %shard_map.215.refs_5_.refs_0_, bf16[512,2560]{1,0:T(8,128)(2,1)} %get-tuple-element.147.refs_1_, f32[8,1024]{1,0:T(8,128)} %get-tuple-element.150.refs_2_), custom_call_target="tpu_custom_call" | custom-call | flops 1879048192 | bytes 7340032 | tf_op jit(solution)/shard_map/pallas_call | solution.py:44
  546.1 4.2 shard_map.242
  550.3 152.2 %shard_map.243.refs_0_ = f32[34,32,256]{2,1,0:T(8,128)} custom-call(f32[7,512,256]{2,1,0:T(8,128)} %get-tuple-element.156.refs_2_.refs_0_, f32[8,512,256]{2,1,0:T(8,128)} %get-tuple-element.112.refs_2_.refs_1_, f32[8,512,256]{2,1,0:T(8,128)} %get-tuple-element.137.refs_2_, f32[8,512,256]{2,1,0:T(8,128)} %get-tuple-element.138.refs_2_.refs_3_, ...), custom_call_target="tpu_custom_call" | custom-call | bytes 419430400 | tf_op jit(solution)/shard_map/pallas_call | solution.py:1209
  703.6 1.6 shard_map.240
  713.1 2.6 shard_map.244
  (154 shorter events, 51.4 us)
Async XLA Ops:
  7.9 12.8 %collective-permute-start = (f32[8,1024]{1,0:T(8,128)S(1)}, f32[8,1024]{1,0:T(8,128)S(1)}, u32[]{:S(2)}, u32[]{:S(2)}) collective-permute-start(f32[8,1024]{1,0:T(8,128)S(1)} %slice_bitcast_fusion.4), channel_id=1, source_target_pairs={{0,2},{2,4},{4,6},{6,8},{8,10},{10,12},{12,14},{14,16},{16,18},{18... | collective-permute-start | bytes 98312 | tf_op jit(solution)/shard_map/ppermute | solution.py:1112
  20.7 0.6 copy-start.13
  41.8 29.1 %all-to-all-start = ((f32[16,136,128]{2,1,0:T(8,128)}), f32[16,136,128]{2,1,0:T(8,128)S(1)}, u32[]{:S(2)}, u32[]{:S(2)}) async-start(f32[16,136,128]{2,1,0:T(8,128)} %get-tuple-element.94), calls=%async_computation | async-start | bytes 2228224 | tf_op jit(solution)/shard_map/all_to_all | solution.py:1106
  70.9 1.0 copy-start.5
  71.9 9.1 %copy-start.19 = (f32[2,32]{1,0:T(2,128)S(1)}, f32[2,32]{1,0:T(2,128)}, u32[]{:S(2)}) copy-start(f32[2,32]{1,0:T(2,128)} %param.20) | copy-start | bytes 772
  71.9 9.2 %copy-start.18 = (f32[2,2048]{1,0:T(2,128)S(1)}, f32[2,2048]{1,0:T(2,128)}, u32[]{:S(2)}) copy-start(f32[2,2048]{1,0:T(2,128)} %param.21) | copy-start | bytes 49156
  74.2 28.9 %all-to-all-start.1 = ((f32[16,128,128]{2,1,0:T(8,128)}), f32[16,128,128]{2,1,0:T(8,128)S(1)}, u32[]{:S(2)}, u32[]{:S(2)}) async-start(f32[16,128,128]{2,1,0:T(8,128)} %shard_map.207), calls=%async_computation.1 | async-start | bytes 2097152 | tf_op jit(solution)/shard_map/all_to_all | solution.py:1106
  103.1 1.0 copy-start
  118.8 3.3 copy-start.2
  118.8 3.3 collective-permute-start.1
  122.1 0.6 copy-start.14
  143.3 39.1 %all-to-all-start.2 = ((f32[16,136,128]{2,1,0:T(8,128)}), f32[16,136,128]{2,1,0:T(8,128)S(1)}, u32[]{:S(2)}, u32[]{:S(2)}) async-start(f32[16,136,128]{2,1,0:T(8,128)} %get-tuple-element.104.refs_2_), calls=%async_computation.2 | async-start | bytes 2228224 | tf_op jit(solution)/shard_map/all_to_all | solution.py:1106
  182.3 1.0 copy-start.6
  183.9 9.8 %copy-start.4 = (f32[1,512,1024]{2,1,0:T(8,128)S(1)}, f32[1,512,1024]{2,1,0:T(8,128)}, u32[]{:S(2)}) copy-start(f32[1,512,1024]{2,1,0:T(8,128)} %param.23) | copy-start | bytes 6291460
  186.4 24.5 %all-to-all-start.3 = ((f32[16,128,128]{2,1,0:T(8,128)}), f32[16,128,128]{2,1,0:T(8,128)S(1)}, u32[]{:S(2)}, u32[]{:S(2)}) async-start(f32[16,128,128]{2,1,0:T(8,128)} %shard_map.216), calls=%async_computation.3 | async-start | bytes 2097152 | tf_op jit(solution)/shard_map/all_to_all | solution.py:1106
  210.8 1.0 copy-start.1
  233.0 32.4 %all-to-all-start.4 = ((f32[16,128,128]{2,1,0:T(8,128)}), f32[16,128,128]{2,1,0:T(8,128)S(1)}, u32[]{:S(2)}, u32[]{:S(2)}) async-start(f32[16,128,128]{2,1,0:T(8,128)} %get-tuple-element.111.refs_2_), calls=%async_computation.4 | async-start | bytes 2097152 | tf_op jit(solution)/shard_map/all_to_all | solution.py:1106
  265.4 1.0 copy-start.9
  268.6 39.3 %all-to-all-start.5 = ((f32[16,128,128]{2,1,0:T(8,128)}), f32[16,128,128]{2,1,0:T(8,128)S(1)}, u32[]{:S(2)}, u32[]{:S(2)}) async-start(f32[16,128,128]{2,1,0:T(8,128)} %shard_map.221.refs_2_), calls=%async_computation.5 | async-start | bytes 2097152 | tf_op jit(solution)/shard_map/all_to_all | solution.py:1106
  275.6 437.5 %reduce-scatter.2.cloned.1.call-start = ((), (), s32[]{:S(2)}) async-start(), calls=%async_computation.10 | async-start | bytes 19464192 | tf_op jit(solution)/shard_map/reduce_scatter | solution.py:1229
  307.9 1.0 copy-start.8
  324.7 7.9 %collective-permute-start.2 = (f32[8,2304]{1,0:T(8,128)S(1)}, f32[8,2304]{1,0:T(8,128)S(1)}, u32[]{:S(2)}, u32[]{:S(2)}) collective-permute-start(f32[8,2304]{1,0:T(8,128)S(1)} %pad_maximum_fusion), channel_id=1, source_target_pairs={{2,0},{4,2},{6,4},{8,6},{10,8},{12,10},{14,12},{16,14},{18,16},{20... | collective-permute-start | bytes 221192 | tf_op jit(solution)/shard_map/ppermute | solution.py:1112
  332.6 0.6 copy-start.12
  383.9 29.1 %all-to-all-start.6 = ((f32[16,128,128]{2,1,0:T(8,128)}), f32[16,128,128]{2,1,0:T(8,128)S(1)}, u32[]{:S(2)}, u32[]{:S(2)}) async-start(f32[16,128,128]{2,1,0:T(8,128)} %get-tuple-element.136.refs_2_), calls=%async_computation.6 | async-start | bytes 2097152 | tf_op jit(solution)/shard_map/all_to_all | solution.py:1106
  413.1 1.0 copy-start.10
  414.0 11.7 %copy-start.15 = (f32[8,1024]{1,0:T(8,128)S(1)}, f32[8,1024]{1,0:T(8,128)}, u32[]{:S(2)}) copy-start(f32[8,1024]{1,0:T(8,128)} %get-tuple-element.153) | copy-start | bytes 98308
  414.0 11.8 %copy-start.16 = (f32[8,2560]{1,0:T(8,128)S(1)}, f32[8,2560]{1,0:T(8,128)}, u32[]{:S(2)}) copy-start(f32[8,2560]{1,0:T(8,128)} %get-tuple-element.154) | copy-start | bytes 245764
  416.3 45.5 %all-to-all-start.7 = ((f32[16,128,128]{2,1,0:T(8,128)}), f32[16,128,128]{2,1,0:T(8,128)S(1)}, u32[]{:S(2)}, u32[]{:S(2)}) async-start(f32[16,128,128]{2,1,0:T(8,128)} %shard_map.235), calls=%async_computation.7 | async-start | bytes 2097152 | tf_op jit(solution)/shard_map/all_to_all | solution.py:1106
  461.8 1.0 copy-start.7
  479.1 9.0 %collective-permute-start.3 = (f32[8,2304]{1,0:T(8,128)S(1)}, f32[8,2304]{1,0:T(8,128)S(1)}, u32[]{:S(2)}, u32[]{:S(2)}) collective-permute-start(f32[8,2304]{1,0:T(8,128)S(1)} %pad_maximum_fusion.1), channel_id=1, source_target_pairs={{2,0},{4,2},{6,4},{8,6},{10,8},{12,10},{14,12},{16,14},{18,16},{20... | collective-permute-start | bytes 221192 | tf_op jit(solution)/shard_map/ppermute | solution.py:1112
  488.0 0.6 copy-start.11
  498.1 11.6 %copy-start.17 = (f32[8,2560]{1,0:T(8,128)S(1)}, f32[8,2560]{1,0:T(8,128)}, u32[]{:S(2)}) copy-start(f32[8,2560]{1,0:T(8,128)} %get-tuple-element.151) | copy-start | bytes 245764
  498.1 34.0 %copy-start.3 = (f32[512,1024]{1,0:T(8,128)S(1)}, f32[512,1024]{1,0:T(8,128)}, u32[]{:S(2)}) copy-start(f32[512,1024]{1,0:T(8,128)} %copy-done.2) | copy-start | bytes 6291460
  511.5 191.0 %all-to-all-start.8 = ((f32[32,1,1152]{2,1,0:T(1,128)}), f32[32,1,1152]{2,1,0:T(1,128)S(1)}, u32[]{:S(2)}, u32[]{:S(2)}) async-start(f32[32,1,1152]{2,1,0:T(1,128)} %copy.57), calls=%async_computation.8 | async-start | bytes 294912 | tf_op jit(solution)/shard_map/all_to_all | solution.py:1378
Sparse Core Ops, SparseCore 0:
  353.3 253.4 reduce-scatter.1

commit v7 on v6

--- a/solution.py
+++ b/solution.py
@@ -12,6 +12,7 @@
 HEAD_DIM = 64
 HEADS = DI // HEAD_DIM
 KW = 4
+SMALL_ROWS = 6 + KW
 GROUP = 256
 LAYERS = 2
 CHANNELS = DI + 2 * STATE
@@ -556,10 +557,6 @@
         carried = keep_ref[peer, 0:1, :] * carried + in_ref[peer, :rows, :]
 
 
-def total_kernel(in_ref, out_ref):
-    out_ref[...] = jnp.sum(in_ref[...], 0)
-
-
 def weight_kernel(each, left_ref, right_ref, send_ref, keep_ref):
     slabs, size = send_ref.shape[0], SUM_ROWS
     total = dot(left_ref[...], right_ref[...])
@@ -786,6 +783,22 @@
         size = min(256, columns - at * 256)
         all_in_ref[0, :, at * 256 : at * 256 + size] = total_ref[place, :, :size]
     all_in_ref[1] = in_ref[:, :columns]
+
+
+def small_kernel(in_ref, gain_ref, conv_ref, bias_ref, decay_ref, dt_ref, skip_ref, gate_ref):
+    total = jnp.sum(in_ref[...], 0)
+    for level in range(LAYERS):
+        at = SMALL_ROWS * level
+        row = lambda place, ref: total[at + place : at + place + 1, : ref.shape[1]]
+        here = slice(level, level + 1)
+        gain_ref[here, :] = row(0, gain_ref)
+        taps = jnp.concatenate([total[at + 1 : at + 1 + KW], jnp.zeros((128 - KW, 128), jnp.float32)], 0)
+        conv_ref[level] = taps.T[: conv_ref.shape[1], :KW]
+        bias_ref[here, :] = row(1 + KW, bias_ref)
+        gate_ref[here, :] = row(2 + KW, gate_ref)
+        decay_ref[here, :] = row(3 + KW, decay_ref)
+        dt_ref[here, :] = row(4 + KW, dt_ref)
+        skip_ref[here, :] = row(5 + KW, skip_ref)
 
 
 def full(shape):
@@ -1342,14 +1355,18 @@
                 devices, normed_sorted, dmixed, turned_tiles, rest_tiles, after=turned_chunks[:1]
             )
         gain_grad = jnp.sum(gain_sums, 0)
-        collected[depth] = (
-            gain_grad,
-            conv_sums[:KW, :CHANNELS].T,
-            conv_sums[KW, :CHANNELS],
-            gate_sums[0],
-            head_rows[1, :HEADS],
-            head_rows[0, :HEADS],
-            jnp.sum(gate_sums[1].reshape(HEADS, HEAD_DIM), 1),
+        spread = lambda part: jnp.moveaxis(part.reshape(part.shape[0], devices, -1), 0, 1)
+        widened = lambda part: jnp.pad(part, ((0, 0), (0, 0), (0, 128 - part.shape[2])))
+        skip_sums = jnp.sum(gate_sums[1].reshape(HEADS, HEAD_DIM), 1)
+        heads = jnp.stack([head_rows[1], head_rows[0], jnp.pad(skip_sums, (0, 128 - HEADS))])
+        collected[depth] = jnp.concatenate(
+            [
+                widened(spread(gain_grad[None])),
+                widened(spread(conv_sums[: KW + 1, :CHANNELS])),
+                widened(spread(gate_sums[:1])),
+                jnp.broadcast_to(heads, (devices,) + heads.shape),
+            ],
+            1,
         )
     total = summed([turned_chunks, high_chunks, out_chunks, gate_chunks, rest_chunks], after=(gradient,))
     places = list(range(total.shape[0]))
@@ -1371,35 +1388,21 @@
         (total, high_in),
         nbytes=4 * 1024 * 1024,
     )
-    shares = [part.reshape(devices, -1) for sums in collected for part in sums[:4]]
-    heads = jnp.concatenate([part for sums in collected for part in sums[4:]])
-    table = jnp.concatenate(shares + [jnp.broadcast_to(heads, (devices,) + heads.shape)], 1)
-    table = jnp.pad(table, ((0, 0), (0, -table.shape[1] % 128)))
-    table = lax.all_to_all(table, AXES, split_axis=0, concat_axis=0, tiled=True).reshape(devices, -1, 128)
-    table = pcall(
-        total_kernel,
+    table = jnp.concatenate(collected, 1)
+    table = jnp.pad(table, ((0, 0), (0, -table.shape[1] % 8), (0, 0)))
+    table = lax.all_to_all(table, AXES, split_axis=0, concat_axis=0, tiled=True)
+    mine = lambda whole: (LAYERS, whole.shape[1] // devices) + whole.shape[2:]
+    shapes = [mine(norm_gain), mine(conv_weight), mine(conv_bias)] + [(LAYERS, HEADS)] * 3 + [mine(gate_gain)]
+    norm_gain_grad, conv_w_grad, conv_b_grad, decay_grad, bias_grad, skip_grad, gain_grad = pcall(
+        small_kernel,
         (1,),
         [full(table.shape)],
-        full(table.shape[1:]),
-        shape_of(table.shape[1:]),
+        [full(shape) for shape in shapes],
+        [shape_of(shape) for shape in shapes],
         [],
         (table,),
-    ).reshape(-1)
-    small = []
-    at = 0
-    for sums in collected:
-        row = []
-        for part in sums[:4]:
-            size = part.size // devices
-            row.append(table[at : at + size].reshape((part.shape[0] // devices,) + part.shape[1:]))
-            at += size
-        small.append(row)
-    for row in small:
-        for _ in range(3):
-            row.append(table[at : at + HEADS])
-            at += HEADS
-    stacked = [jnp.stack([small[level][member] for level in range(LAYERS)]) for member in range(7)]
-    norm_gain_grad, conv_w_grad, conv_b_grad, gain_grad, decay_grad, bias_grad, skip_grad = stacked
+        nbytes=4 * table.size,
+    )
     return (
         hidden[None],
         gradient[None],

time: 735 us -> 731 us (level)
  transfers between devices with their start and end apart: 14 -> 14, of which waited for: 6 -> 6; matrix products, arithmetic and copies ran while one was open for 8% -> 7% of each run, Pallas kernels for 51% -> 52%
where the time goes in v7:
time: 731 us; the launch traced here: 719 us
  Pallas kernels  487 us (67%)
  starting transfers between devices  90.3 us (12%)
  waiting for transfers between devices  57 us (8%)
  local copies, waits for them, and re-layouts  35.5 us (5%)
  matrix products  26.2 us (4%)
  between operations  15 us (2%)
  other arithmetic  7.46 us (1%)
    pallas_call x41, Pallas kernels, pcall(): pl.pallas_call(run, grid=grid, in_specs=list(in_specs) + [pl.BlockSpec(me...  333 us
    pallas_call x1, Pallas kernels, summed(): pl.pallas_call(run, in_specs=[anywhere] * (2 * len(parts) + len(after)),...  154 us
    all_to_all x8, starting transfers between devices, exchange(): return lax.all_to_all(parts, 'seq', split_axis=0, concat_axis=0, tiled=True)  60.3 us
    all_to_all x8, waiting for transfers between devices, exchange(): return lax.all_to_all(parts, 'seq', split_axis=0, concat_axis=0, tiled=True)  57 us
    all_to_all x1, starting transfers between devices, local(): table = lax.all_to_all(table, AXES, split_axis=0, concat_axis=0, tiled=True)  20.6 us
  transfers between devices with their start and end apart: 14, of which 6 were waited for; matrix products, arithmetic and copies ran while one was open for 7% of the time, Pallas kernels for 52%

profile of v7, /device:TPU:1, one launch (start us, length us, event | category | flops | bytes accessed | tf_op | source)
XLA Modules:
  0.0 718.7 jit_solution(15589410172205994134)
XLA Ops:
  7.9 3.9 collective-permute-start
  21.3 9.0 %shard_map.203 = (bf16[512,1024]{1,0:T(8,128)(2,1)}, f32[520,2560]{1,0:T(8,128)}) custom-call(f32[512,1024]{1,0:T(8,128)} %bitcast.93, f32[8,1024]{1,0:T(8,128)} %copy-done.15, f32[1,1024]{1,0:T(1,128)} %get-tuple-element.234.refs_2_.refs_5_, bf16[2,4384,1024]{2,1,0:T(8,128)(2,1)} %bitcast.85), custom_call_target="tpu_custom_call" | custom-call | flops 2684354560 | bytes 5242880 | tf_op jit(solution)/shard_map/pallas_call | solution.py:45
  30.4 11.4 %shard_map.204 = (f32[512,2048]{1,0:T(8,128)}, f32[512,256]{1,0:T(8,128)}, f32[4,512,128]{2,1,0:T(8,128)}, f32[128,512]{1,0:T(8,128)}, f32[128,2048]{1,0:T(8,128...) custom-call(f32[520,2560]{1,0:T(8,128)} %get-tuple-element.95.refs_0_.refs_1_.refs_2_, ...), custom_call_target="tpu_custom_call" | custom-call | flops 268435456 | bytes 12582912 | tf_op jit(solution)/shard_map/pallas_call | solution.py:45
  41.8 5.7 all-to-all-start
  47.5 6.5 shard_map.206.refs_2_
  54.0 16.9 %all-to-all-done.refs_0_ = f32[16,136,128]{2,1,0:T(8,128)S(1)} async-done(((f32[16,136,128]{2,1,0:T(8,128)}), f32[16,136,128]{2,1,0:T(8,128)S(1)}, u32[]{:S(2)}, u32[]{:S(2)}) %all-to-all-start) | async-done | bytes 1114144 | tf_op jit(solution)/shard_map/all_to_all | solution.py:1119
  71.9 2.3 shard_map.207
  74.2 6.7 all-to-all-start.1
  82.4 6.9 shard_map.205.refs_0_.refs_3_
  89.3 13.8 %all-to-all-done.1.refs_5_.refs_6_.refs_7_ = f32[16,128,128]{2,1,0:T(8,128)S(1)} async-done(((f32[16,128,128]{2,1,0:T(8,128)}), f32[16,128,128]{2,1,0:T(8,128)S(1)}, u32[]{:S(2)}, u32[]{:S(2)}) %all-to-all-start.1) | async-done | bytes 1048608 | tf_op jit(solution)/shard_map/all_to_all | solution.py:1119
  104.0 8.9 %shard_map.208 = (f32[512,2048]{1,0:T(8,128)}, bf16[512,2048]{1,0:T(8,128)(2,1)}) custom-call(f32[512,2048]{1,0:T(8,128)} %shard_map.205.refs_0_.refs_3_, f32[512,2048]{1,0:T(8,128)} %get-tuple-element.97.refs_1_.refs_3_, f32[512,2048]{1,0:T(8,128)} %shard_map.206.refs_2_, f32[512,256]{1,0:T(8,128)} %get-tuple-element.96.refs_0_.refs_3_.refs_4_, ...), custom_call_target="tpu_custom_call" | custom-call | flops 268435456 | bytes 18874368 | tf_op jit(solution)/shard_map/pallas_call | solution.py:45
  112.9 5.8 fusion.12.refs_0_.refs_3_
  118.8 2.1 collective-permute-start.1
  122.7 9.1 %shard_map.209 = (bf16[512,1024]{1,0:T(8,128)(2,1)}, f32[520,2560]{1,0:T(8,128)}) custom-call(f32[512,1024]{1,0:T(8,128)} %copy-done.2, f32[8,1024]{1,0:T(8,128)} %copy-done.16, f32[1,1024]{1,0:T(1,128)} %get-tuple-element.233.refs_2_.refs_5_, bf16[2,4384,1024]{2,1,0:T(8,128)(2,1)} %bitcast.87), custom_call_target="tpu_custom_call" | custom-call | flops 2684354560 | bytes 5242880 | tf_op jit(solution)/shard_map/pallas_call | solution.py:45
  131.8 11.4 %shard_map.210 = (f32[512,2048]{1,0:T(8,128)}, f32[512,256]{1,0:T(8,128)}, f32[4,512,128]{2,1,0:T(8,128)}, f32[128,512]{1,0:T(8,128)}, f32[128,2048]{1,0:T(8,128...) custom-call(f32[520,2560]{1,0:T(8,128)} %get-tuple-element.105.refs_0_.refs_1_.refs_2, ...), custom_call_target="tpu_custom_call" | custom-call | flops 268435456 | bytes 12582912 | tf_op jit(solution)/shard_map/pallas_call | solution.py:45
  143.2 9.0 %all-to-all-start.2 = ((f32[16,136,128]{2,1,0:T(8,128)}), f32[16,136,128]{2,1,0:T(8,128)S(1)}, u32[]{:S(2)}, u32[]{:S(2)}) async-start(f32[16,136,128]{2,1,0:T(8,128)} %get-tuple-element.111.refs_2_), calls=%async_computation.2 | async-start | bytes 2228224 | tf_op jit(solution)/shard_map/all_to_all | solution.py:1119
  155.2 2.0 add.164.refs_0_
  157.2 4.7 shard_map.214.refs_4_.refs_0_
  161.9 4.7 shard_map.215.refs_5_.refs_0_
  166.6 6.5 shard_map.212.refs_2_
  173.1 9.2 %shard_map.213.refs_3_.refs_0_ = bf16[2048,512]{1,0:T(8,128)(2,1)} custom-call(s32[2048,1]{1,0:T(8,128)} %add.164.refs_0_, bf16[512,2048]{1,0:T(8,128)(2,1)} %get-tuple-element.104.refs_1_, f32[16,136,128]{2,1,0:T(8,128)} %get-tuple-element.111.refs_2_), custom_call_target="tpu_custom_call" | custom-call | flops 4294967296 | bytes 4194304 | tf_op jit(solution)/shard_map/pallas_call | solution.py:45
  183.9 2.4 shard_map.216
  186.4 6.6 all-to-all-start.3
  193.8 6.6 fusion.refs_0_
  200.3 7.0 shard_map.211.refs_0_.refs_3_
  207.3 3.5 all-to-all-done.3.refs_5_.refs_6_.refs_7_
  211.8 8.9 %shard_map.217 = (f32[512,2048]{1,0:T(8,128)}, bf16[512,2048]{1,0:T(8,128)(2,1)}) custom-call(f32[512,2048]{1,0:T(8,128)} %shard_map.211.refs_0_.refs_3_, f32[512,2048]{1,0:T(8,128)} %get-tuple-element.107.refs_1_.refs_3_, f32[512,2048]{1,0:T(8,128)} %shard_map.212.refs_2_, f32[512,256]{1,0:T(8,128)} %get-tuple-element.106.refs_0_.refs_3_.refs_4_, ...), custom_call_target="tpu_custom_call" | custom-call | flops 268435456 | bytes 18874368 | tf_op jit(solution)/shard_map/pallas_call | solution.py:45
  220.7 12.2 %shard_map.218 = (f32[512,2048]{1,0:T(8,128)}, bf16[512,2048]{1,0:T(8,128)(2,1)}, f32[8,2048]{1,0:T(8,128)}, f32[128,2048]{1,0:T(8,128)}, f32[16,128,128]{2,1,0:T(8,128)}) custom-call(f32[512,2048]{1,0:T(8,128)} %fusion.refs_0_, f32[512,2048]{1,0:T(8,128)} %get-tuple-element.115.refs_1_, f32[512,2048]{1,0:T(8,128)} %shard_map.212.refs_2_, ...), custom_call_target="tpu_custom_call" | custom-call | flops 268435456 | bytes 23068672 | tf_op jit(solution)/shard_map/pallas_call | solution.py:45
  232.9 10.4 %all-to-all-start.4 = ((f32[16,128,128]{2,1,0:T(8,128)}), f32[16,128,128]{2,1,0:T(8,128)S(1)}, u32[]{:S(2)}, u32[]{:S(2)}) async-start(f32[16,128,128]{2,1,0:T(8,128)} %get-tuple-element.118.refs_2_), calls=%async_computation.4 | async-start | bytes 2097152 | tf_op jit(solution)/shard_map/all_to_all | solution.py:1119
  244.4 9.2 %shard_map.219.refs_0_ = bf16[2048,512]{1,0:T(8,128)(2,1)} custom-call(s32[2048,1]{1,0:T(8,128)} %add.164.refs_0_, bf16[512,2048]{1,0:T(8,128)(2,1)} %get-tuple-element.114.refs_1_, f32[16,128,128]{2,1,0:T(8,128)} %get-tuple-element.118.refs_2_), custom_call_target="tpu_custom_call" | custom-call | flops 4294967296 | bytes 4194304 | tf_op jit(solution)/shard_map/pallas_call | solution.py:45
  253.6 6.4 shard_map.220
  260.0 5.3 all-to-all-done.4.refs_0_
  266.3 2.3 shard_map.221.refs_2_
  268.5 6.9 all-to-all-start.5
  275.9 9.0 %shard_map.222.refs_7_.refs_2_ = f32[1024,4608]{1,0:T(8,128)} custom-call(bf16[512,1024]{1,0:T(8,128)(2,1)} %get-tuple-element.110.refs_0_, bf16[512,2048]{1,0:T(8,128)(2,1)} %get-tuple-element.116.refs_1_.refs_0_, f32[16,128,128]{2,1,0:T(8,128)} %shard_map.221.refs_2_), custom_call_target="tpu_custom_call" | custom-call | flops 2147483648 | bytes 8388608 | tf_op jit(solution)/shard_map/pallas_call | solution.py:45
  284.9 10.0 %shard_map.223 = (f32[512,2048]{1,0:T(8,128)}, f32[512,256]{1,0:T(8,128)}) custom-call(f32[512,256]{1,0:T(8,128)} %get-tuple-element.106.refs_0_.refs_3_.refs_4_, f32[512,2048]{1,0:T(8,128)} %get-tuple-element.107.refs_1_.refs_3_, f32[512,2048]{1,0:T(8,128)} %get-tuple-element.117.refs_2_, f32[4,512,128]{2,1,0:T(8,128)} %get-tuple-element.108.refs_2_.refs_4_.refs_5_.refs_3_, ...), custom_call_target="tpu_custom_call" | custom-call | flops 4294967296 | bytes 12582912 | tf_op jit(solution)/shard_map/pallas_call | solution.py:45
  294.9 13.0 %shard_map.224 = (f32[512,2048]{1,0:T(8,128)}, f32[512,128]{1,0:T(8,128)}, f32[512,128]{1,0:T(8,128)}, f32[512,256]{1,0:T(8,128)}) custom-call(f32[512,2048]{1,0:T(8,128)} %get-tuple-element.120.refs_0_, f32[512,2048]{1,0:T(8,128)} %get-tuple-element.107.refs_1_.refs_3_, f32[512,2048]{1,0:T(8,128)} %get-tuple-element.117.refs_2_, ...), custom_call_target="tpu_custom_call" | custom-call | flops 536870912 | bytes 20971520 | tf_op jit(solution)/shard_map/pallas_call | solution.py:45
  308.9 14.3 %shard_map.225 = (f32[512,2048]{1,0:T(8,128)}, f32[512,256]{1,0:T(8,128)}, bf16[512,128]{1,0:T(8,128)(2,1)}, f32[8,128]{1,0:T(8,128)}) custom-call(f32[512,2048]{1,0:T(8,128)} %get-tuple-element.122.refs_0_, f32[512,2048]{1,0:T(8,128)} %get-tuple-element.107.refs_1_.refs_3_, f32[512,2048]{1,0:T(8,128)} %get-tuple-element.123.refs_2_, ...), custom_call_target="tpu_custom_call" | custom-call | flops 536870912 | bytes 16777216 | tf_op jit(solution)/shard_map/pallas_call | solution.py:45
  326.2 6.4 shard_map.226.refs_7_.refs_0_
  333.3 9.1 %shard_map.227 = (bf16[512,2560]{1,0:T(8,128)(2,1)}, f32[8,2560]{1,0:T(8,128)}) custom-call(f32[512,2048]{1,0:T(8,128)} %get-tuple-element.130.refs_0_, f32[512,256]{1,0:T(8,128)} %get-tuple-element.131.refs_1_, bf16[512,128]{1,0:T(8,128)(2,1)} %get-tuple-element.132.refs_2_, f32[8,2304]{1,0:T(8,128)} %copy-done.13, ...), custom_call_target="tpu_custom_call" | custom-call | flops 8388608 | bytes 10485760 | tf_op jit(solution)/shard_map/pallas_call | solution.py:45
  342.4 10.8 %shard_map.228.refs_6_ = f32[1024,4608]{1,0:T(8,128)} custom-call(bf16[512,1024]{1,0:T(8,128)(2,1)} %get-tuple-element.110.refs_0_, bf16[512,2560]{1,0:T(8,128)(2,1)} %get-tuple-element.133.refs_1_, f32[1024,4608]{1,0:T(8,128)} %shard_map.222.refs_7_.refs_2_), custom_call_target="tpu_custom_call", output_to_operand_aliasing={{}: (2, {})} | custom-call | flops 2684354560 | bytes 10485760 | tf_op jit(solution)/shard_map/pallas_call | solution.py:45
  353.2 10.5 %shard_map.229 = (f32[512,1024]{1,0:T(8,128)}, bf16[512,1024]{1,0:T(8,128)(2,1)}, f32[8,1024]{1,0:T(8,128)}) custom-call(f32[512,1024]{1,0:T(8,128)} %shard_map.226.refs_7_.refs_0_, bf16[512,2560]{1,0:T(8,128)(2,1)} %get-tuple-element.133.refs_1_, bf16[2,4384,1024]{2,1,0:T(8,128)(2,1)} %bitcast.90, f32[512,1024]{1,0:T(8,128)} %copy-done.2, ...), custom_call_target="tpu_custom_call" | custom-call | flops 2449473536 | bytes 8978432 | tf_op jit(solution)/shard_map/pallas_call | solution.py:45
  363.7 7.3 %fusion.4.refs_0_ = f32[512,2048]{1,0:T(8,128)} fusion(bf16[512,1024]{1,0:T(8,128)(2,1)} %get-tuple-element.134.refs_1_, bf16[2,2048,1024]{2,1,0:T(8,128)(2,1)} %param.22), kind=kOutput, calls=%fused_computation.4 | convolution fusion | flops 2147483648 | bytes 9437184 | tf_op jit(solution)/shard_map/tn,mn->tm/dot_general | solution.py:1254
  371.0 13.0 %shard_map.230 = (f32[512,2048]{1,0:T(8,128)}, bf16[512,2048]{1,0:T(8,128)(2,1)}, f32[8,2048]{1,0:T(8,128)}, f32[128,2048]{1,0:T(8,128)}, f32[16,128,128]{2,1,0:T(8,128)}) custom-call(f32[512,2048]{1,0:T(8,128)} %fusion.4.refs_0_, f32[512,2048]{1,0:T(8,128)} %get-tuple-element.135.refs_1_, f32[512,2048]{1,0:T(8,128)} %shard_map.206.refs_2_, ...), custom_call_target="tpu_custom_call" | custom-call | flops 268435456 | bytes 23068672 | tf_op jit(solution)/shard_map/pallas_call | solution.py:45
  383.9 7.7 %all-to-all-start.6 = ((f32[16,128,128]{2,1,0:T(8,128)}), f32[16,128,128]{2,1,0:T(8,128)S(1)}, u32[]{:S(2)}, u32[]{:S(2)}) async-start(f32[16,128,128]{2,1,0:T(8,128)} %get-tuple-element.143.refs_2_), calls=%async_computation.6 | async-start | bytes 2097152 | tf_op jit(solution)/shard_map/all_to_all | solution.py:1119
  391.6 6.7 shard_map.233
  398.4 8.5 %shard_map.234 = (f32[8,512,256]{2,1,0:T(8,128)}, f32[8,512,256]{2,1,0:T(8,128)}) custom-call(bf16[1024,512]{1,0:T(8,128)(2,1)} %shard_map.214.refs_4_.refs_0_, bf16[512,2048]{1,0:T(8,128)(2,1)} %get-tuple-element.136.refs_1_.refs_0_, f32[8,512,256]{2,1,0:T(8,128)} %get-tuple-element.144.refs_2_), custom_call_target="tpu_custom_call" | custom-call | flops 2147483648 | bytes 8388608 | tf_op jit(solution)/shard_map/pallas_call | solution.py:45
  406.8 6.2 all-to-all-done.6.refs_0_
  414.0 2.3 shard_map.235
  416.3 7.4 %all-to-all-start.7 = ((f32[16,128,128]{2,1,0:T(8,128)}), f32[16,128,128]{2,1,0:T(8,128)S(1)}, u32[]{:S(2)}, u32[]{:S(2)}) async-start(f32[16,128,128]{2,1,0:T(8,128)} %shard_map.235), calls=%async_computation.7 | async-start | bytes 2097152 | tf_op jit(solution)/shard_map/all_to_all | solution.py:1119
  427.3 10.1 %shard_map.231 = (f32[512,2048]{1,0:T(8,128)}, f32[512,256]{1,0:T(8,128)}) custom-call(f32[512,256]{1,0:T(8,128)} %get-tuple-element.96.refs_0_.refs_3_.refs_4_, f32[512,2048]{1,0:T(8,128)} %get-tuple-element.97.refs_1_.refs_3_, f32[512,2048]{1,0:T(8,128)} %get-tuple-element.137.refs_2_, f32[4,512,128]{2,1,0:T(8,128)} %get-tuple-element.98.refs_2_.refs_4_.refs_5_.refs_3_, ...), custom_call_target="tpu_custom_call" | custom-call | flops 4294967296 | bytes 12582912 | tf_op jit(solution)/shard_map/pallas_call | solution.py:45
  437.4 13.1 %shard_map.232 = (f32[512,2048]{1,0:T(8,128)}, f32[512,128]{1,0:T(8,128)}, f32[512,128]{1,0:T(8,128)}, f32[512,256]{1,0:T(8,128)}) custom-call(f32[512,2048]{1,0:T(8,128)} %get-tuple-element.138.refs_0_, f32[512,2048]{1,0:T(8,128)} %get-tuple-element.97.refs_1_.refs_3_, f32[512,2048]{1,0:T(8,128)} %get-tuple-element.137.refs_2_, ...), custom_call_target="tpu_custom_call" | custom-call | flops 536870912 | bytes 20971520 | tf_op jit(solution)/shard_map/pallas_call | solution.py:45
  450.5 11.3 %all-to-all-done.7.refs_6_ = f32[16,128,128]{2,1,0:T(8,128)S(1)} async-done(((f32[16,128,128]{2,1,0:T(8,128)}), f32[16,128,128]{2,1,0:T(8,128)S(1)}, u32[]{:S(2)}, u32[]{:S(2)}) %all-to-all-start.7) | async-done | bytes 1048608 | tf_op jit(solution)/shard_map/all_to_all | solution.py:1119
  462.8 14.7 %shard_map.236 = (f32[512,2048]{1,0:T(8,128)}, f32[512,256]{1,0:T(8,128)}, bf16[512,128]{1,0:T(8,128)(2,1)}, f32[8,128]{1,0:T(8,128)}) custom-call(f32[512,2048]{1,0:T(8,128)} %get-tuple-element.140.refs_0_, f32[512,2048]{1,0:T(8,128)} %get-tuple-element.97.refs_1_.refs_3_, f32[512,2048]{1,0:T(8,128)} %get-tuple-element.141.refs_2_, ...), custom_call_target="tpu_custom_call" | custom-call | flops 536870912 | bytes 16777216 | tf_op jit(solution)/shard_map/pallas_call | solution.py:45
  480.6 6.6 shard_map.237.refs_7_.refs_0_
  488.6 9.3 %shard_map.238 = (bf16[512,2560]{1,0:T(8,128)(2,1)}, f32[8,2560]{1,0:T(8,128)}) custom-call(f32[512,2048]{1,0:T(8,128)} %get-tuple-element.151.refs_0_, f32[512,256]{1,0:T(8,128)} %get-tuple-element.152.refs_1_, bf16[512,128]{1,0:T(8,128)(2,1)} %get-tuple-element.153.refs_2_, f32[8,2304]{1,0:T(8,128)} %copy-done.12, ...), custom_call_target="tpu_custom_call" | custom-call | flops 8388608 | bytes 10485760 | tf_op jit(solution)/shard_map/pallas_call | solution.py:45
  498.9 10.7 %shard_map.239 = (f32[512,1024]{1,0:T(8,128)}, bf16[512,1024]{1,0:T(8,128)(2,1)}, f32[8,1024]{1,0:T(8,128)}) custom-call(f32[512,1024]{1,0:T(8,128)} %shard_map.237.refs_7_.refs_0_, bf16[512,2560]{1,0:T(8,128)(2,1)} %get-tuple-element.154.refs_1_, bf16[2,4384,1024]{2,1,0:T(8,128)(2,1)} %bitcast.92, f32[512,1024]{1,0:T(8,128)} %bitcast.94, ...), custom_call_target="tpu_custom_call" | custom-call | flops 2449473536 | bytes 8978432 | tf_op jit(solution)/shard_map/pallas_call | solution.py:45
  511.9 20.6 %all-to-all-start.8 = ((f32[32,24,128]{2,1,0:T(8,128)}), f32[32,24,128]{2,1,0:T(8,128)S(1)}, u32[]{:S(2)}, u32[]{:S(2)}) async-start(f32[32,24,128]{2,1,0:T(8,128)} %pad.88), calls=%async_computation.8 | async-start | bytes 786432 | tf_op jit(solution)/shard_map/all_to_all | solution.py:1393
  532.5 6.5 add_bitcast_fusion
  539.0 7.5 %shard_map.241 = (f32[7,512,256]{2,1,0:T(8,128)}, f32[7,512,256]{2,1,0:T(8,128)}) custom-call(bf16[1024,512]{1,0:T(8,128)(2,1)} %shard_map.215.refs_5_.refs_0_, bf16[512,2560]{1,0:T(8,128)(2,1)} %get-tuple-element.154.refs_1_, f32[8,1024]{1,0:T(8,128)} %get-tuple-element.157.refs_2_), custom_call_target="tpu_custom_call" | custom-call | flops 1879048192 | bytes 7340032 | tf_op jit(solution)/shard_map/pallas_call | solution.py:45
  546.5 4.2 shard_map.242
  550.7 154.0 %shard_map.243.refs_0_ = f32[34,32,256]{2,1,0:T(8,128)} custom-call(f32[7,512,256]{2,1,0:T(8,128)} %get-tuple-element.164.refs_2_.refs_0_, f32[8,512,256]{2,1,0:T(8,128)} %get-tuple-element.119.refs_2_.refs_1_, f32[8,512,256]{2,1,0:T(8,128)} %get-tuple-element.144.refs_2_, f32[8,512,256]{2,1,0:T(8,128)} %get-tuple-element.145.refs_2_.refs_3_, ...), custom_call_target="tpu_custom_call" | custom-call | bytes 419430400 | tf_op jit(solution)/shard_map/pallas_call | solution.py:1222
  705.5 1.8 shard_map.240
  708.8 2.6 shard_map.244
  (143 shorter events, 44.4 us)
Async XLA Ops:
  7.9 12.8 %collective-permute-start = (f32[8,1024]{1,0:T(8,128)S(1)}, f32[8,1024]{1,0:T(8,128)S(1)}, u32[]{:S(2)}, u32[]{:S(2)}) collective-permute-start(f32[8,1024]{1,0:T(8,128)S(1)} %slice_bitcast_fusion.2), channel_id=1, source_target_pairs={{0,2},{2,4},{4,6},{6,8},{8,10},{10,12},{12,14},{14,16},{16,18},{18... | collective-permute-start | bytes 98312 | tf_op jit(solution)/shard_map/ppermute | solution.py:1125
  20.7 0.6 copy-start.15
  41.8 29.1 %all-to-all-start = ((f32[16,136,128]{2,1,0:T(8,128)}), f32[16,136,128]{2,1,0:T(8,128)S(1)}, u32[]{:S(2)}, u32[]{:S(2)}) async-start(f32[16,136,128]{2,1,0:T(8,128)} %get-tuple-element.101), calls=%async_computation | async-start | bytes 2228224 | tf_op jit(solution)/shard_map/all_to_all | solution.py:1119
  70.8 1.0 copy-start.5
  71.9 9.1 %copy-start.19 = (f32[2,32]{1,0:T(2,128)S(1)}, f32[2,32]{1,0:T(2,128)}, u32[]{:S(2)}) copy-start(f32[2,32]{1,0:T(2,128)} %param.20) | copy-start | bytes 772
  71.9 9.2 %copy-start.18 = (f32[2,2048]{1,0:T(2,128)S(1)}, f32[2,2048]{1,0:T(2,128)}, u32[]{:S(2)}) copy-start(f32[2,2048]{1,0:T(2,128)} %param.21) | copy-start | bytes 49156
  74.2 28.9 %all-to-all-start.1 = ((f32[16,128,128]{2,1,0:T(8,128)}), f32[16,128,128]{2,1,0:T(8,128)S(1)}, u32[]{:S(2)}, u32[]{:S(2)}) async-start(f32[16,128,128]{2,1,0:T(8,128)} %shard_map.207), calls=%async_computation.1 | async-start | bytes 2097152 | tf_op jit(solution)/shard_map/all_to_all | solution.py:1119
  103.1 1.0 copy-start
  118.7 3.3 copy-start.2
  118.8 3.3 collective-permute-start.1
  122.1 0.6 copy-start.16
  143.2 39.1 %all-to-all-start.2 = ((f32[16,136,128]{2,1,0:T(8,128)}), f32[16,136,128]{2,1,0:T(8,128)S(1)}, u32[]{:S(2)}, u32[]{:S(2)}) async-start(f32[16,136,128]{2,1,0:T(8,128)} %get-tuple-element.111.refs_2_), calls=%async_computation.2 | async-start | bytes 2228224 | tf_op jit(solution)/shard_map/all_to_all | solution.py:1119
  182.3 1.0 copy-start.6
  183.9 9.8 %copy-start.4 = (f32[1,512,1024]{2,1,0:T(8,128)S(1)}, f32[1,512,1024]{2,1,0:T(8,128)}, u32[]{:S(2)}) copy-start(f32[1,512,1024]{2,1,0:T(8,128)} %param.23) | copy-start | bytes 6291460
  186.4 24.5 %all-to-all-start.3 = ((f32[16,128,128]{2,1,0:T(8,128)}), f32[16,128,128]{2,1,0:T(8,128)S(1)}, u32[]{:S(2)}, u32[]{:S(2)}) async-start(f32[16,128,128]{2,1,0:T(8,128)} %shard_map.216), calls=%async_computation.3 | async-start | bytes 2097152 | tf_op jit(solution)/shard_map/all_to_all | solution.py:1119
  210.8 1.0 copy-start.1
  232.9 32.4 %all-to-all-start.4 = ((f32[16,128,128]{2,1,0:T(8,128)}), f32[16,128,128]{2,1,0:T(8,128)S(1)}, u32[]{:S(2)}, u32[]{:S(2)}) async-start(f32[16,128,128]{2,1,0:T(8,128)} %get-tuple-element.118.refs_2_), calls=%async_computation.4 | async-start | bytes 2097152 | tf_op jit(solution)/shard_map/all_to_all | solution.py:1119
  265.3 1.0 copy-start.9
  268.5 39.3 %all-to-all-start.5 = ((f32[16,128,128]{2,1,0:T(8,128)}), f32[16,128,128]{2,1,0:T(8,128)S(1)}, u32[]{:S(2)}, u32[]{:S(2)}) async-start(f32[16,128,128]{2,1,0:T(8,128)} %shard_map.221.refs_2_), calls=%async_computation.5 | async-start | bytes 2097152 | tf_op jit(solution)/shard_map/all_to_all | solution.py:1119
  275.5 433.3 %reduce-scatter.2.cloned.1.call-start = ((), (), s32[]{:S(2)}) async-start(), calls=%async_computation.10 | async-start | bytes 19464192 | tf_op jit(solution)/shard_map/reduce_scatter | solution.py:1242
  307.9 1.0 copy-start.8
  324.8 7.9 %collective-permute-start.2 = (f32[8,2304]{1,0:T(8,128)S(1)}, f32[8,2304]{1,0:T(8,128)S(1)}, u32[]{:S(2)}, u32[]{:S(2)}) collective-permute-start(f32[8,2304]{1,0:T(8,128)S(1)} %pad_maximum_fusion), channel_id=1, source_target_pairs={{2,0},{4,2},{6,4},{8,6},{10,8},{12,10},{14,12},{16,14},{18,16},{20... | collective-permute-start | bytes 221192 | tf_op jit(solution)/shard_map/ppermute | solution.py:1125
  332.7 0.6 copy-start.13
  383.9 29.1 %all-to-all-start.6 = ((f32[16,128,128]{2,1,0:T(8,128)}), f32[16,128,128]{2,1,0:T(8,128)S(1)}, u32[]{:S(2)}, u32[]{:S(2)}) async-start(f32[16,128,128]{2,1,0:T(8,128)} %get-tuple-element.143.refs_2_), calls=%async_computation.6 | async-start | bytes 2097152 | tf_op jit(solution)/shard_map/all_to_all | solution.py:1119
  413.0 1.0 copy-start.10
  414.0 11.7 %copy-start.14 = (f32[8,2560]{1,0:T(8,128)S(1)}, f32[8,2560]{1,0:T(8,128)}, u32[]{:S(2)}) copy-start(f32[8,2560]{1,0:T(8,128)} %get-tuple-element.161) | copy-start | bytes 245764
  414.0 11.7 %copy-start.17 = (f32[8,1024]{1,0:T(8,128)S(1)}, f32[8,1024]{1,0:T(8,128)}, u32[]{:S(2)}) copy-start(f32[8,1024]{1,0:T(8,128)} %get-tuple-element.160) | copy-start | bytes 98308
  416.3 45.5 %all-to-all-start.7 = ((f32[16,128,128]{2,1,0:T(8,128)}), f32[16,128,128]{2,1,0:T(8,128)S(1)}, u32[]{:S(2)}, u32[]{:S(2)}) async-start(f32[16,128,128]{2,1,0:T(8,128)} %shard_map.235), calls=%async_computation.7 | async-start | bytes 2097152 | tf_op jit(solution)/shard_map/all_to_all | solution.py:1119
  461.8 1.0 copy-start.7
  479.1 8.9 %collective-permute-start.3 = (f32[8,2304]{1,0:T(8,128)S(1)}, f32[8,2304]{1,0:T(8,128)S(1)}, u32[]{:S(2)}, u32[]{:S(2)}) collective-permute-start(f32[8,2304]{1,0:T(8,128)S(1)} %pad_maximum_fusion.1), channel_id=1, source_target_pairs={{2,0},{4,2},{6,4},{8,6},{10,8},{12,10},{14,12},{16,14},{18,16},{20... | collective-permute-start | bytes 221192 | tf_op jit(solution)/shard_map/ppermute | solution.py:1125
  488.0 0.6 copy-start.12
  498.9 33.6 %copy-start.3 = (f32[512,1024]{1,0:T(8,128)S(1)}, f32[512,1024]{1,0:T(8,128)}, u32[]{:S(2)}) copy-start(f32[512,1024]{1,0:T(8,128)} %copy-done.2) | copy-start | bytes 6291460
  511.9 192.8 %all-to-all-start.8 = ((f32[32,24,128]{2,1,0:T(8,128)}), f32[32,24,128]{2,1,0:T(8,128)S(1)}, u32[]{:S(2)}, u32[]{:S(2)}) async-start(f32[32,24,128]{2,1,0:T(8,128)} %pad.88), calls=%async_computation.8 | async-start | bytes 786432 | tf_op jit(solution)/shard_map/all_to_all | solution.py:1393
  704.7 0.7 copy-start.11
Sparse Core Ops, SparseCore 0:
  353.3 259.8 reduce-scatter.1

commit v8 on v7

--- a/solution.py
+++ b/solution.py
@@ -23,7 +23,7 @@
 SUM_ROWS = 512
 LAG = 3
 AHEAD = 6
-EVERY = 5
+EVERY = 6
 HALO = 8
 HALF = 128
 LOG2E = 1.4426950408889634

time: 731 us -> 734 us (level)
  no operation moved by 1% of the time
where the time goes in v8:
time: 734 us; the launch traced here: 721 us
  Pallas kernels  490 us (67%)
  starting transfers between devices  90.3 us (12%)
  waiting for transfers between devices  57 us (8%)
  local copies, waits for them, and re-layouts  35.5 us (5%)
  matrix products  26.2 us (4%)
  between operations  15 us (2%)
  other arithmetic  7.46 us (1%)
    pallas_call x41, Pallas kernels, pcall(): pl.pallas_call(run, grid=grid, in_specs=list(in_specs) + [pl.BlockSpec(me...  333 us
    pallas_call x1, Pallas kernels, summed(): pl.pallas_call(run, in_specs=[anywhere] * (2 * len(parts) + len(after)),...  157 us
    all_to_all x8, starting transfers between devices, exchange(): return lax.all_to_all(parts, 'seq', split_axis=0, concat_axis=0, tiled=True)  60.3 us
    all_to_all x8, waiting for transfers between devices, exchange(): return lax.all_to_all(parts, 'seq', split_axis=0, concat_axis=0, tiled=True)  57 us
    all_to_all x1, starting transfers between devices, local(): table = lax.all_to_all(table, AXES, split_axis=0, concat_axis=0, tiled=True)  20.6 us
  transfers between devices with their start and end apart: 14, of which 6 were waited for; matrix products, arithmetic and copies ran while one was open for 7% of the time, Pallas kernels for 52%

profile of v8, /device:TPU:1, one launch (start us, length us, event | category | flops | bytes accessed | tf_op | source)
XLA Modules:
  0.0 721.0 jit_solution(1535159942604048030)
XLA Ops:
  7.9 3.9 collective-permute-start
  21.3 9.0 %shard_map.203 = (bf16[512,1024]{1,0:T(8,128)(2,1)}, f32[520,2560]{1,0:T(8,128)}) custom-call(f32[512,1024]{1,0:T(8,128)} %bitcast.93, f32[8,1024]{1,0:T(8,128)} %copy-done.15, f32[1,1024]{1,0:T(1,128)} %get-tuple-element.234.refs_2_.refs_5_, bf16[2,4384,1024]{2,1,0:T(8,128)(2,1)} %bitcast.85), custom_call_target="tpu_custom_call" | custom-call | flops 2684354560 | bytes 5242880 | tf_op jit(solution)/shard_map/pallas_call | solution.py:45
  30.4 11.4 %shard_map.204 = (f32[512,2048]{1,0:T(8,128)}, f32[512,256]{1,0:T(8,128)}, f32[4,512,128]{2,1,0:T(8,128)}, f32[128,512]{1,0:T(8,128)}, f32[128,2048]{1,0:T(8,128...) custom-call(f32[520,2560]{1,0:T(8,128)} %get-tuple-element.95.refs_0_.refs_1_.refs_2_, ...), custom_call_target="tpu_custom_call" | custom-call | flops 268435456 | bytes 12582912 | tf_op jit(solution)/shard_map/pallas_call | solution.py:45
  41.8 5.7 all-to-all-start
  47.5 6.5 shard_map.206.refs_2_
  54.0 16.9 %all-to-all-done.refs_0_ = f32[16,136,128]{2,1,0:T(8,128)S(1)} async-done(((f32[16,136,128]{2,1,0:T(8,128)}), f32[16,136,128]{2,1,0:T(8,128)S(1)}, u32[]{:S(2)}, u32[]{:S(2)}) %all-to-all-start) | async-done | bytes 1114144 | tf_op jit(solution)/shard_map/all_to_all | solution.py:1119
  71.9 2.3 shard_map.207
  74.2 6.7 all-to-all-start.1
  82.4 6.9 shard_map.205.refs_0_.refs_3_
  89.3 13.8 %all-to-all-done.1.refs_5_.refs_6_.refs_7_ = f32[16,128,128]{2,1,0:T(8,128)S(1)} async-done(((f32[16,128,128]{2,1,0:T(8,128)}), f32[16,128,128]{2,1,0:T(8,128)S(1)}, u32[]{:S(2)}, u32[]{:S(2)}) %all-to-all-start.1) | async-done | bytes 1048608 | tf_op jit(solution)/shard_map/all_to_all | solution.py:1119
  104.0 8.9 %shard_map.208 = (f32[512,2048]{1,0:T(8,128)}, bf16[512,2048]{1,0:T(8,128)(2,1)}) custom-call(f32[512,2048]{1,0:T(8,128)} %shard_map.205.refs_0_.refs_3_, f32[512,2048]{1,0:T(8,128)} %get-tuple-element.97.refs_1_.refs_3_, f32[512,2048]{1,0:T(8,128)} %shard_map.206.refs_2_, f32[512,256]{1,0:T(8,128)} %get-tuple-element.96.refs_0_.refs_3_.refs_4_, ...), custom_call_target="tpu_custom_call" | custom-call | flops 268435456 | bytes 18874368 | tf_op jit(solution)/shard_map/pallas_call | solution.py:45
  112.9 5.8 fusion.12.refs_0_.refs_3_
  118.8 2.1 collective-permute-start.1
  122.7 9.1 %shard_map.209 = (bf16[512,1024]{1,0:T(8,128)(2,1)}, f32[520,2560]{1,0:T(8,128)}) custom-call(f32[512,1024]{1,0:T(8,128)} %copy-done.2, f32[8,1024]{1,0:T(8,128)} %copy-done.16, f32[1,1024]{1,0:T(1,128)} %get-tuple-element.233.refs_2_.refs_5_, bf16[2,4384,1024]{2,1,0:T(8,128)(2,1)} %bitcast.87), custom_call_target="tpu_custom_call" | custom-call | flops 2684354560 | bytes 5242880 | tf_op jit(solution)/shard_map/pallas_call | solution.py:45
  131.8 11.4 %shard_map.210 = (f32[512,2048]{1,0:T(8,128)}, f32[512,256]{1,0:T(8,128)}, f32[4,512,128]{2,1,0:T(8,128)}, f32[128,512]{1,0:T(8,128)}, f32[128,2048]{1,0:T(8,128...) custom-call(f32[520,2560]{1,0:T(8,128)} %get-tuple-element.105.refs_0_.refs_1_.refs_2, ...), custom_call_target="tpu_custom_call" | custom-call | flops 268435456 | bytes 12582912 | tf_op jit(solution)/shard_map/pallas_call | solution.py:45
  143.2 9.0 %all-to-all-start.2 = ((f32[16,136,128]{2,1,0:T(8,128)}), f32[16,136,128]{2,1,0:T(8,128)S(1)}, u32[]{:S(2)}, u32[]{:S(2)}) async-start(f32[16,136,128]{2,1,0:T(8,128)} %get-tuple-element.111.refs_2_), calls=%async_computation.2 | async-start | bytes 2228224 | tf_op jit(solution)/shard_map/all_to_all | solution.py:1119
  155.2 2.0 add.164.refs_0_
  157.2 4.7 shard_map.214.refs_4_.refs_0_
  161.9 4.7 shard_map.215.refs_5_.refs_0_
  166.6 6.5 shard_map.212.refs_2_
  173.1 9.2 %shard_map.213.refs_3_.refs_0_ = bf16[2048,512]{1,0:T(8,128)(2,1)} custom-call(s32[2048,1]{1,0:T(8,128)} %add.164.refs_0_, bf16[512,2048]{1,0:T(8,128)(2,1)} %get-tuple-element.104.refs_1_, f32[16,136,128]{2,1,0:T(8,128)} %get-tuple-element.111.refs_2_), custom_call_target="tpu_custom_call" | custom-call | flops 4294967296 | bytes 4194304 | tf_op jit(solution)/shard_map/pallas_call | solution.py:45
  183.9 2.4 shard_map.216
  186.4 6.6 all-to-all-start.3
  193.8 6.6 fusion.refs_0_
  200.3 7.0 shard_map.211.refs_0_.refs_3_
  207.3 3.5 all-to-all-done.3.refs_5_.refs_6_.refs_7_
  211.8 8.9 %shard_map.217 = (f32[512,2048]{1,0:T(8,128)}, bf16[512,2048]{1,0:T(8,128)(2,1)}) custom-call(f32[512,2048]{1,0:T(8,128)} %shard_map.211.refs_0_.refs_3_, f32[512,2048]{1,0:T(8,128)} %get-tuple-element.107.refs_1_.refs_3_, f32[512,2048]{1,0:T(8,128)} %shard_map.212.refs_2_, f32[512,256]{1,0:T(8,128)} %get-tuple-element.106.refs_0_.refs_3_.refs_4_, ...), custom_call_target="tpu_custom_call" | custom-call | flops 268435456 | bytes 18874368 | tf_op jit(solution)/shard_map/pallas_call | solution.py:45
  220.7 12.2 %shard_map.218 = (f32[512,2048]{1,0:T(8,128)}, bf16[512,2048]{1,0:T(8,128)(2,1)}, f32[8,2048]{1,0:T(8,128)}, f32[128,2048]{1,0:T(8,128)}, f32[16,128,128]{2,1,0:T(8,128)}) custom-call(f32[512,2048]{1,0:T(8,128)} %fusion.refs_0_, f32[512,2048]{1,0:T(8,128)} %get-tuple-element.115.refs_1_, f32[512,2048]{1,0:T(8,128)} %shard_map.212.refs_2_, ...), custom_call_target="tpu_custom_call" | custom-call | flops 268435456 | bytes 23068672 | tf_op jit(solution)/shard_map/pallas_call | solution.py:45
  232.9 10.4 %all-to-all-start.4 = ((f32[16,128,128]{2,1,0:T(8,128)}), f32[16,128,128]{2,1,0:T(8,128)S(1)}, u32[]{:S(2)}, u32[]{:S(2)}) async-start(f32[16,128,128]{2,1,0:T(8,128)} %get-tuple-element.118.refs_2_), calls=%async_computation.4 | async-start | bytes 2097152 | tf_op jit(solution)/shard_map/all_to_all | solution.py:1119
  244.4 9.2 %shard_map.219.refs_0_ = bf16[2048,512]{1,0:T(8,128)(2,1)} custom-call(s32[2048,1]{1,0:T(8,128)} %add.164.refs_0_, bf16[512,2048]{1,0:T(8,128)(2,1)} %get-tuple-element.114.refs_1_, f32[16,128,128]{2,1,0:T(8,128)} %get-tuple-element.118.refs_2_), custom_call_target="tpu_custom_call" | custom-call | flops 4294967296 | bytes 4194304 | tf_op jit(solution)/shard_map/pallas_call | solution.py:45
  253.6 6.4 shard_map.220
  260.0 5.3 all-to-all-done.4.refs_0_
  266.3 2.3 shard_map.221.refs_2_
  268.5 6.9 all-to-all-start.5
  275.9 9.0 %shard_map.222.refs_7_.refs_2_ = f32[1024,4608]{1,0:T(8,128)} custom-call(bf16[512,1024]{1,0:T(8,128)(2,1)} %get-tuple-element.110.refs_0_, bf16[512,2048]{1,0:T(8,128)(2,1)} %get-tuple-element.116.refs_1_.refs_0_, f32[16,128,128]{2,1,0:T(8,128)} %shard_map.221.refs_2_), custom_call_target="tpu_custom_call" | custom-call | flops 2147483648 | bytes 8388608 | tf_op jit(solution)/shard_map/pallas_call | solution.py:45
  284.9 10.0 %shard_map.223 = (f32[512,2048]{1,0:T(8,128)}, f32[512,256]{1,0:T(8,128)}) custom-call(f32[512,256]{1,0:T(8,128)} %get-tuple-element.106.refs_0_.refs_3_.refs_4_, f32[512,2048]{1,0:T(8,128)} %get-tuple-element.107.refs_1_.refs_3_, f32[512,2048]{1,0:T(8,128)} %get-tuple-element.117.refs_2_, f32[4,512,128]{2,1,0:T(8,128)} %get-tuple-element.108.refs_2_.refs_4_.refs_5_.refs_3_, ...), custom_call_target="tpu_custom_call" | custom-call | flops 4294967296 | bytes 12582912 | tf_op jit(solution)/shard_map/pallas_call | solution.py:45
  294.9 13.0 %shard_map.224 = (f32[512,2048]{1,0:T(8,128)}, f32[512,128]{1,0:T(8,128)}, f32[512,128]{1,0:T(8,128)}, f32[512,256]{1,0:T(8,128)}) custom-call(f32[512,2048]{1,0:T(8,128)} %get-tuple-element.120.refs_0_, f32[512,2048]{1,0:T(8,128)} %get-tuple-element.107.refs_1_.refs_3_, f32[512,2048]{1,0:T(8,128)} %get-tuple-element.117.refs_2_, ...), custom_call_target="tpu_custom_call" | custom-call | flops 536870912 | bytes 20971520 | tf_op jit(solution)/shard_map/pallas_call | solution.py:45
  308.9 14.3 %shard_map.225 = (f32[512,2048]{1,0:T(8,128)}, f32[512,256]{1,0:T(8,128)}, bf16[512,128]{1,0:T(8,128)(2,1)}, f32[8,128]{1,0:T(8,128)}) custom-call(f32[512,2048]{1,0:T(8,128)} %get-tuple-element.122.refs_0_, f32[512,2048]{1,0:T(8,128)} %get-tuple-element.107.refs_1_.refs_3_, f32[512,2048]{1,0:T(8,128)} %get-tuple-element.123.refs_2_, ...), custom_call_target="tpu_custom_call" | custom-call | flops 536870912 | bytes 16777216 | tf_op jit(solution)/shard_map/pallas_call | solution.py:45
  326.2 6.4 shard_map.226.refs_7_.refs_0_
  333.3 9.1 %shard_map.227 = (bf16[512,2560]{1,0:T(8,128)(2,1)}, f32[8,2560]{1,0:T(8,128)}) custom-call(f32[512,2048]{1,0:T(8,128)} %get-tuple-element.130.refs_0_, f32[512,256]{1,0:T(8,128)} %get-tuple-element.131.refs_1_, bf16[512,128]{1,0:T(8,128)(2,1)} %get-tuple-element.132.refs_2_, f32[8,2304]{1,0:T(8,128)} %copy-done.13, ...), custom_call_target="tpu_custom_call" | custom-call | flops 8388608 | bytes 10485760 | tf_op jit(solution)/shard_map/pallas_call | solution.py:45
  342.4 10.8 %shard_map.228.refs_6_ = f32[1024,4608]{1,0:T(8,128)} custom-call(bf16[512,1024]{1,0:T(8,128)(2,1)} %get-tuple-element.110.refs_0_, bf16[512,2560]{1,0:T(8,128)(2,1)} %get-tuple-element.133.refs_1_, f32[1024,4608]{1,0:T(8,128)} %shard_map.222.refs_7_.refs_2_), custom_call_target="tpu_custom_call", output_to_operand_aliasing={{}: (2, {})} | custom-call | flops 2684354560 | bytes 10485760 | tf_op jit(solution)/shard_map/pallas_call | solution.py:45
  353.2 10.5 %shard_map.229 = (f32[512,1024]{1,0:T(8,128)}, bf16[512,1024]{1,0:T(8,128)(2,1)}, f32[8,1024]{1,0:T(8,128)}) custom-call(f32[512,1024]{1,0:T(8,128)} %shard_map.226.refs_7_.refs_0_, bf16[512,2560]{1,0:T(8,128)(2,1)} %get-tuple-element.133.refs_1_, bf16[2,4384,1024]{2,1,0:T(8,128)(2,1)} %bitcast.90, f32[512,1024]{1,0:T(8,128)} %copy-done.2, ...), custom_call_target="tpu_custom_call" | custom-call | flops 2449473536 | bytes 8978432 | tf_op jit(solution)/shard_map/pallas_call | solution.py:45
  363.7 7.3 %fusion.4.refs_0_ = f32[512,2048]{1,0:T(8,128)} fusion(bf16[512,1024]{1,0:T(8,128)(2,1)} %get-tuple-element.134.refs_1_, bf16[2,2048,1024]{2,1,0:T(8,128)(2,1)} %param.22), kind=kOutput, calls=%fused_computation.4 | convolution fusion | flops 2147483648 | bytes 9437184 | tf_op jit(solution)/shard_map/tn,mn->tm/dot_general | solution.py:1254
  371.0 13.0 %shard_map.230 = (f32[512,2048]{1,0:T(8,128)}, bf16[512,2048]{1,0:T(8,128)(2,1)}, f32[8,2048]{1,0:T(8,128)}, f32[128,2048]{1,0:T(8,128)}, f32[16,128,128]{2,1,0:T(8,128)}) custom-call(f32[512,2048]{1,0:T(8,128)} %fusion.4.refs_0_, f32[512,2048]{1,0:T(8,128)} %get-tuple-element.135.refs_1_, f32[512,2048]{1,0:T(8,128)} %shard_map.206.refs_2_, ...), custom_call_target="tpu_custom_call" | custom-call | flops 268435456 | bytes 23068672 | tf_op jit(solution)/shard_map/pallas_call | solution.py:45
  383.9 7.7 %all-to-all-start.6 = ((f32[16,128,128]{2,1,0:T(8,128)}), f32[16,128,128]{2,1,0:T(8,128)S(1)}, u32[]{:S(2)}, u32[]{:S(2)}) async-start(f32[16,128,128]{2,1,0:T(8,128)} %get-tuple-element.143.refs_2_), calls=%async_computation.6 | async-start | bytes 2097152 | tf_op jit(solution)/shard_map/all_to_all | solution.py:1119
  391.6 6.7 shard_map.233
  398.4 8.5 %shard_map.234 = (f32[8,512,256]{2,1,0:T(8,128)}, f32[8,512,256]{2,1,0:T(8,128)}) custom-call(bf16[1024,512]{1,0:T(8,128)(2,1)} %shard_map.214.refs_4_.refs_0_, bf16[512,2048]{1,0:T(8,128)(2,1)} %get-tuple-element.136.refs_1_.refs_0_, f32[8,512,256]{2,1,0:T(8,128)} %get-tuple-element.144.refs_2_), custom_call_target="tpu_custom_call" | custom-call | flops 2147483648 | bytes 8388608 | tf_op jit(solution)/shard_map/pallas_call | solution.py:45
  406.8 6.2 all-to-all-done.6.refs_0_
  414.0 2.3 shard_map.235
  416.3 7.4 %all-to-all-start.7 = ((f32[16,128,128]{2,1,0:T(8,128)}), f32[16,128,128]{2,1,0:T(8,128)S(1)}, u32[]{:S(2)}, u32[]{:S(2)}) async-start(f32[16,128,128]{2,1,0:T(8,128)} %shard_map.235), calls=%async_computation.7 | async-start | bytes 2097152 | tf_op jit(solution)/shard_map/all_to_all | solution.py:1119
  427.3 10.1 %shard_map.231 = (f32[512,2048]{1,0:T(8,128)}, f32[512,256]{1,0:T(8,128)}) custom-call(f32[512,256]{1,0:T(8,128)} %get-tuple-element.96.refs_0_.refs_3_.refs_4_, f32[512,2048]{1,0:T(8,128)} %get-tuple-element.97.refs_1_.refs_3_, f32[512,2048]{1,0:T(8,128)} %get-tuple-element.137.refs_2_, f32[4,512,128]{2,1,0:T(8,128)} %get-tuple-element.98.refs_2_.refs_4_.refs_5_.refs_3_, ...), custom_call_target="tpu_custom_call" | custom-call | flops 4294967296 | bytes 12582912 | tf_op jit(solution)/shard_map/pallas_call | solution.py:45
  437.4 13.1 %shard_map.232 = (f32[512,2048]{1,0:T(8,128)}, f32[512,128]{1,0:T(8,128)}, f32[512,128]{1,0:T(8,128)}, f32[512,256]{1,0:T(8,128)}) custom-call(f32[512,2048]{1,0:T(8,128)} %get-tuple-element.138.refs_0_, f32[512,2048]{1,0:T(8,128)} %get-tuple-element.97.refs_1_.refs_3_, f32[512,2048]{1,0:T(8,128)} %get-tuple-element.137.refs_2_, ...), custom_call_target="tpu_custom_call" | custom-call | flops 536870912 | bytes 20971520 | tf_op jit(solution)/shard_map/pallas_call | solution.py:45
  450.5 11.3 %all-to-all-done.7.refs_6_ = f32[16,128,128]{2,1,0:T(8,128)S(1)} async-done(((f32[16,128,128]{2,1,0:T(8,128)}), f32[16,128,128]{2,1,0:T(8,128)S(1)}, u32[]{:S(2)}, u32[]{:S(2)}) %all-to-all-start.7) | async-done | bytes 1048608 | tf_op jit(solution)/shard_map/all_to_all | solution.py:1119
  462.8 14.7 %shard_map.236 = (f32[512,2048]{1,0:T(8,128)}, f32[512,256]{1,0:T(8,128)}, bf16[512,128]{1,0:T(8,128)(2,1)}, f32[8,128]{1,0:T(8,128)}) custom-call(f32[512,2048]{1,0:T(8,128)} %get-tuple-element.140.refs_0_, f32[512,2048]{1,0:T(8,128)} %get-tuple-element.97.refs_1_.refs_3_, f32[512,2048]{1,0:T(8,128)} %get-tuple-element.141.refs_2_, ...), custom_call_target="tpu_custom_call" | custom-call | flops 536870912 | bytes 16777216 | tf_op jit(solution)/shard_map/pallas_call | solution.py:45
  480.6 6.6 shard_map.237.refs_7_.refs_0_
  488.6 9.3 %shard_map.238 = (bf16[512,2560]{1,0:T(8,128)(2,1)}, f32[8,2560]{1,0:T(8,128)}) custom-call(f32[512,2048]{1,0:T(8,128)} %get-tuple-element.151.refs_0_, f32[512,256]{1,0:T(8,128)} %get-tuple-element.152.refs_1_, bf16[512,128]{1,0:T(8,128)(2,1)} %get-tuple-element.153.refs_2_, f32[8,2304]{1,0:T(8,128)} %copy-done.12, ...), custom_call_target="tpu_custom_call" | custom-call | flops 8388608 | bytes 10485760 | tf_op jit(solution)/shard_map/pallas_call | solution.py:45
  498.9 10.7 %shard_map.239 = (f32[512,1024]{1,0:T(8,128)}, bf16[512,1024]{1,0:T(8,128)(2,1)}, f32[8,1024]{1,0:T(8,128)}) custom-call(f32[512,1024]{1,0:T(8,128)} %shard_map.237.refs_7_.refs_0_, bf16[512,2560]{1,0:T(8,128)(2,1)} %get-tuple-element.154.refs_1_, bf16[2,4384,1024]{2,1,0:T(8,128)(2,1)} %bitcast.92, f32[512,1024]{1,0:T(8,128)} %bitcast.94, ...), custom_call_target="tpu_custom_call" | custom-call | flops 2449473536 | bytes 8978432 | tf_op jit(solution)/shard_map/pallas_call | solution.py:45
  511.9 20.6 %all-to-all-start.8 = ((f32[32,24,128]{2,1,0:T(8,128)}), f32[32,24,128]{2,1,0:T(8,128)S(1)}, u32[]{:S(2)}, u32[]{:S(2)}) async-start(f32[32,24,128]{2,1,0:T(8,128)} %pad.88), calls=%async_computation.8 | async-start | bytes 786432 | tf_op jit(solution)/shard_map/all_to_all | solution.py:1393
  532.5 6.5 add_bitcast_fusion
  539.0 6.5 shard_map.241
  545.5 5.0 shard_map.242
  550.5 156.6 %shard_map.243.refs_0_ = f32[34,32,256]{2,1,0:T(8,128)} custom-call(f32[6,512,256]{2,1,0:T(8,128)} %get-tuple-element.164.refs_2_.refs_0_, f32[8,512,256]{2,1,0:T(8,128)} %get-tuple-element.119.refs_2_.refs_1_, f32[8,512,256]{2,1,0:T(8,128)} %get-tuple-element.144.refs_2_, f32[8,512,256]{2,1,0:T(8,128)} %get-tuple-element.145.refs_2_.refs_3_, ...), custom_call_target="tpu_custom_call" | custom-call | bytes 419430400 | tf_op jit(solution)/shard_map/pallas_call | solution.py:1222
  707.8 1.8 shard_map.240
  711.1 2.6 shard_map.244
  (143 shorter events, 44.4 us)
Async XLA Ops:
  7.9 12.8 %collective-permute-start = (f32[8,1024]{1,0:T(8,128)S(1)}, f32[8,1024]{1,0:T(8,128)S(1)}, u32[]{:S(2)}, u32[]{:S(2)}) collective-permute-start(f32[8,1024]{1,0:T(8,128)S(1)} %slice_bitcast_fusion.2), channel_id=1, source_target_pairs={{0,2},{2,4},{4,6},{6,8},{8,10},{10,12},{12,14},{14,16},{16,18},{18... | collective-permute-start | bytes 98312 | tf_op jit(solution)/shard_map/ppermute | solution.py:1125
  20.7 0.6 copy-start.15
  41.8 29.1 %all-to-all-start = ((f32[16,136,128]{2,1,0:T(8,128)}), f32[16,136,128]{2,1,0:T(8,128)S(1)}, u32[]{:S(2)}, u32[]{:S(2)}) async-start(f32[16,136,128]{2,1,0:T(8,128)} %get-tuple-element.101), calls=%async_computation | async-start | bytes 2228224 | tf_op jit(solution)/shard_map/all_to_all | solution.py:1119
  70.8 1.0 copy-start.5
  71.9 9.1 %copy-start.19 = (f32[2,32]{1,0:T(2,128)S(1)}, f32[2,32]{1,0:T(2,128)}, u32[]{:S(2)}) copy-start(f32[2,32]{1,0:T(2,128)} %param.20) | copy-start | bytes 772
  71.9 9.2 %copy-start.18 = (f32[2,2048]{1,0:T(2,128)S(1)}, f32[2,2048]{1,0:T(2,128)}, u32[]{:S(2)}) copy-start(f32[2,2048]{1,0:T(2,128)} %param.21) | copy-start | bytes 49156
  74.2 28.9 %all-to-all-start.1 = ((f32[16,128,128]{2,1,0:T(8,128)}), f32[16,128,128]{2,1,0:T(8,128)S(1)}, u32[]{:S(2)}, u32[]{:S(2)}) async-start(f32[16,128,128]{2,1,0:T(8,128)} %shard_map.207), calls=%async_computation.1 | async-start | bytes 2097152 | tf_op jit(solution)/shard_map/all_to_all | solution.py:1119
  103.1 1.0 copy-start
  118.7 3.3 copy-start.2
  118.8 3.3 collective-permute-start.1
  122.1 0.6 copy-start.16
  143.2 39.1 %all-to-all-start.2 = ((f32[16,136,128]{2,1,0:T(8,128)}), f32[16,136,128]{2,1,0:T(8,128)S(1)}, u32[]{:S(2)}, u32[]{:S(2)}) async-start(f32[16,136,128]{2,1,0:T(8,128)} %get-tuple-element.111.refs_2_), calls=%async_computation.2 | async-start | bytes 2228224 | tf_op jit(solution)/shard_map/all_to_all | solution.py:1119
  182.3 1.0 copy-start.6
  183.9 9.8 %copy-start.4 = (f32[1,512,1024]{2,1,0:T(8,128)S(1)}, f32[1,512,1024]{2,1,0:T(8,128)}, u32[]{:S(2)}) copy-start(f32[1,512,1024]{2,1,0:T(8,128)} %param.23) | copy-start | bytes 6291460
  186.4 24.5 %all-to-all-start.3 = ((f32[16,128,128]{2,1,0:T(8,128)}), f32[16,128,128]{2,1,0:T(8,128)S(1)}, u32[]{:S(2)}, u32[]{:S(2)}) async-start(f32[16,128,128]{2,1,0:T(8,128)} %shard_map.216), calls=%async_computation.3 | async-start | bytes 2097152 | tf_op jit(solution)/shard_map/all_to_all | solution.py:1119
  210.8 1.0 copy-start.1
  232.9 32.4 %all-to-all-start.4 = ((f32[16,128,128]{2,1,0:T(8,128)}), f32[16,128,128]{2,1,0:T(8,128)S(1)}, u32[]{:S(2)}, u32[]{:S(2)}) async-start(f32[16,128,128]{2,1,0:T(8,128)} %get-tuple-element.118.refs_2_), calls=%async_computation.4 | async-start | bytes 2097152 | tf_op jit(solution)/shard_map/all_to_all | solution.py:1119
  265.3 1.0 copy-start.9
  268.5 39.3 %all-to-all-start.5 = ((f32[16,128,128]{2,1,0:T(8,128)}), f32[16,128,128]{2,1,0:T(8,128)S(1)}, u32[]{:S(2)}, u32[]{:S(2)}) async-start(f32[16,128,128]{2,1,0:T(8,128)} %shard_map.221.refs_2_), calls=%async_computation.5 | async-start | bytes 2097152 | tf_op jit(solution)/shard_map/all_to_all | solution.py:1119
  275.5 435.7 %reduce-scatter.2.cloned.1.call-start = ((), (), s32[]{:S(2)}) async-start(), calls=%async_computation.10 | async-start | bytes 19464192 | tf_op jit(solution)/shard_map/reduce_scatter | solution.py:1242
  307.9 1.0 copy-start.8
  324.8 7.9 %collective-permute-start.2 = (f32[8,2304]{1,0:T(8,128)S(1)}, f32[8,2304]{1,0:T(8,128)S(1)}, u32[]{:S(2)}, u32[]{:S(2)}) collective-permute-start(f32[8,2304]{1,0:T(8,128)S(1)} %pad_maximum_fusion), channel_id=1, source_target_pairs={{2,0},{4,2},{6,4},{8,6},{10,8},{12,10},{14,12},{16,14},{18,16},{20... | collective-permute-start | bytes 221192 | tf_op jit(solution)/shard_map/ppermute | solution.py:1125
  332.7 0.6 copy-start.13
  383.9 29.1 %all-to-all-start.6 = ((f32[16,128,128]{2,1,0:T(8,128)}), f32[16,128,128]{2,1,0:T(8,128)S(1)}, u32[]{:S(2)}, u32[]{:S(2)}) async-start(f32[16,128,128]{2,1,0:T(8,128)} %get-tuple-element.143.refs_2_), calls=%async_computation.6 | async-start | bytes 2097152 | tf_op jit(solution)/shard_map/all_to_all | solution.py:1119
  413.0 1.0 copy-start.10
  414.0 11.7 %copy-start.14 = (f32[8,2560]{1,0:T(8,128)S(1)}, f32[8,2560]{1,0:T(8,128)}, u32[]{:S(2)}) copy-start(f32[8,2560]{1,0:T(8,128)} %get-tuple-element.161) | copy-start | bytes 245764
  414.0 11.7 %copy-start.17 = (f32[8,1024]{1,0:T(8,128)S(1)}, f32[8,1024]{1,0:T(8,128)}, u32[]{:S(2)}) copy-start(f32[8,1024]{1,0:T(8,128)} %get-tuple-element.160) | copy-start | bytes 98308
  416.3 45.5 %all-to-all-start.7 = ((f32[16,128,128]{2,1,0:T(8,128)}), f32[16,128,128]{2,1,0:T(8,128)S(1)}, u32[]{:S(2)}, u32[]{:S(2)}) async-start(f32[16,128,128]{2,1,0:T(8,128)} %shard_map.235), calls=%async_computation.7 | async-start | bytes 2097152 | tf_op jit(solution)/shard_map/all_to_all | solution.py:1119
  461.8 1.0 copy-start.7
  479.1 8.9 %collective-permute-start.3 = (f32[8,2304]{1,0:T(8,128)S(1)}, f32[8,2304]{1,0:T(8,128)S(1)}, u32[]{:S(2)}, u32[]{:S(2)}) collective-permute-start(f32[8,2304]{1,0:T(8,128)S(1)} %pad_maximum_fusion.1), channel_id=1, source_target_pairs={{2,0},{4,2},{6,4},{8,6},{10,8},{12,10},{14,12},{16,14},{18,16},{20... | collective-permute-start | bytes 221192 | tf_op jit(solution)/shard_map/ppermute | solution.py:1125
  488.0 0.6 copy-start.12
  498.9 33.6 %copy-start.3 = (f32[512,1024]{1,0:T(8,128)S(1)}, f32[512,1024]{1,0:T(8,128)}, u32[]{:S(2)}) copy-start(f32[512,1024]{1,0:T(8,128)} %copy-done.2) | copy-start | bytes 6291460
  511.9 195.2 %all-to-all-start.8 = ((f32[32,24,128]{2,1,0:T(8,128)}), f32[32,24,128]{2,1,0:T(8,128)S(1)}, u32[]{:S(2)}, u32[]{:S(2)}) async-start(f32[32,24,128]{2,1,0:T(8,128)} %pad.88), calls=%async_computation.8 | async-start | bytes 786432 | tf_op jit(solution)/shard_map/all_to_all | solution.py:1393
  707.0 0.7 copy-start.11
Sparse Core Ops, SparseCore 0:
  353.3 258.5 reduce-scatter.1
